TPU v7x, 32 devices: a whole 2x2x4 slice. The times are simulated.
32 devices in a mesh: gx: 16 (over z, x, core), gy: 2 (over y).
Axes of the slice: x: 2, y: 2, z: 4, core: 2. Of those that a mesh axis runs over, the one named last changes fastest.
Arguments:
- flow_field: bfloat16 [64, 32, 64, 128], P('gx', 'gy'), may hold values from -6 to 6
- spectral_weight: bfloat16 [512, 64, 2, 64, 128], P(('gy', 'gx')), may hold values from -1 to 1
- conv_weight: bfloat16 [3, 3, 3, 128, 128], replicated, may hold values from -0.109375 to 0.109375
- channel_bias: float32 [128], replicated, may hold values from -3 to 3
Outputs:
- activated: bfloat16 [64, 32, 64, 128], P('gx', 'gy')
All inputs are finite; a program needn't handle non-finite values.
Results may differ from a plain program's by a relative error of at most 0.018.
Values may be sent and summed in bfloat16 or wider, within the bound.
No kernel may reach another device: no remote copies, remote signals or barrier semaphores. Data moves between devices by JAX's collectives and lax.ppermute only.
A program may use at most 128 MiB of HBM per device.

v0:
```python
import math

import jax
import jax.numpy as jnp
from jax import lax
from jax.sharding import PartitionSpec as P

MX = 64
MY = 16
MZ = 16


def with_halo(array, sides, width):
    for axis, dim in sides:
        size, length = (lax.axis_size(axis), array.shape[dim])
        up = [(i, (i + 1) % size) for i in range(size - 1)]
        down = [(j, i) for i, j in up]
        last = lax.slice_in_dim(array, length - width, length, axis=dim)
        initial = lax.slice_in_dim(array, 0, width, axis=dim)
        before = lax.ppermute(last, axis, up)
        after = lax.ppermute(initial, axis, down)
        array = jnp.concatenate([before, array, after], axis=dim)
    return array


def signed_modes(mode_count):
    position = jnp.arange(mode_count, dtype=jnp.int32)
    return jnp.where(position < mode_count // 2, position, position - mode_count)


def angle_grid(first, second, length):
    phase_turns = first[:, None] * second[None, :] % length
    return phase_turns.astype(jnp.float32) * (2.0 * math.pi / length)


def real_table(first, second, length, factor):
    angles = angle_grid(first, second, length)
    return jnp.stack([jnp.cos(angles) * factor, -jnp.sin(angles) * factor])


def complex_table(first, second, length, factor, direction):
    angles = angle_grid(first, second, length)
    cosine = jnp.cos(angles) * factor
    sine_part = jnp.sin(angles) * factor
    return jnp.stack(
        [jnp.stack([cosine, direction * sine_part]), jnp.stack([-direction * sine_part, cosine])]
    )


def spectral_part(flow_field, spectral_weight):
    highest = lax.Precision.HIGHEST
    cells_x, cells_y, cells_z, channels = flow_field.shape
    count_x = lax.axis_size("gx")
    count_y = lax.axis_size("gy")
    full_x = cells_x * count_x
    full_y = cells_y * count_y
    item_count = spectral_weight.shape[0]
    local_y = lax.axis_index("gy") * cells_y + jnp.arange(cells_y, dtype=jnp.int32)
    grid_x = jnp.arange(full_x, dtype=jnp.int32)
    grid_z = jnp.arange(cells_z, dtype=jnp.int32)
    modes_z = jnp.arange(MZ, dtype=jnp.int32)
    forward_z = real_table(grid_z, modes_z, cells_z, cells_z ** (-0.5)).astype(jnp.bfloat16)
    z_spectrum = jnp.einsum(
        "xyzc,pzk->pxykc", flow_field, forward_z, preferred_element_type=jnp.float32
    )
    columns = lax.all_to_all(
        z_spectrum.astype(jnp.bfloat16), "gy", split_axis=4, concat_axis=2, tiled=True
    ).astype(z_spectrum.dtype)
    whole_y = jnp.arange(full_y, dtype=jnp.int32)
    forward_full = complex_table(whole_y, signed_modes(MY), full_y, full_y ** (-0.5), -1.0)
    y_spectrum = jnp.einsum("pxykc,pqyj->qxjkc", columns, forward_full, precision=highest)
    owned = lax.all_to_all(
        y_spectrum.astype(jnp.bfloat16), "gy", split_axis=2, concat_axis=4, tiled=True
    ).astype(y_spectrum.dtype)
    owned_modes = owned.reshape(2, cells_x, count_x, item_count, channels // 2)
    gathered_rows = lax.all_to_all(
        owned_modes.astype(jnp.bfloat16), "gx", split_axis=2, concat_axis=1, tiled=True
    ).astype(owned_modes.dtype)
    gathered_rows = gathered_rows.reshape(2, full_x, item_count, channels // 2)
    forward_x = complex_table(grid_x, signed_modes(MX), full_x, full_x ** (-0.5), -1.0)
    x_spectrum = jnp.einsum("pxjc,pqxm->qmjc", gathered_rows, forward_x, precision=highest).astype(
        jnp.bfloat16
    )
    products = jnp.einsum(
        "pmjc,jmqco->pqmjo", x_spectrum, spectral_weight, preferred_element_type=jnp.float32
    )
    mixed_modes = jnp.stack([products[0, 0] - products[1, 1], products[0, 1] + products[1, 0]])
    backward_x = complex_table(signed_modes(MX), grid_x, full_x, MX ** (-0.5), 1.0)
    inverse_x = jnp.einsum("pmjc,pqmx->qxjc", mixed_modes, backward_x, precision=highest)
    inverse_x = inverse_x.reshape(2, full_x, 1, item_count, channels)
    returned = lax.all_to_all(
        inverse_x.astype(jnp.bfloat16), "gx", split_axis=1, concat_axis=2, tiled=True
    ).astype(inverse_x.dtype)
    band_rows = MY // count_y
    summed = returned.reshape(2, cells_x, band_rows * MZ, 2, channels).sum(axis=3)
    summed = summed.reshape(2, cells_x, band_rows, MZ, channels)
    coefficients = lax.all_gather(summed.astype(jnp.bfloat16), "gy", axis=2, tiled=True).astype(
        summed.dtype
    )
    backward_y = complex_table(signed_modes(MY), local_y, full_y, MY ** (-0.5), 1.0)
    y_inverse = jnp.einsum("pxjkc,pqjy->qxykc", coefficients, backward_y, precision=highest).astype(
        jnp.bfloat16
    )
    backward_z = real_table(modes_z, grid_z, cells_z, MZ ** (-0.5)).astype(jnp.bfloat16)
    return jnp.einsum("pxykc,pkz->xyzc", y_inverse, backward_z, preferred_element_type=jnp.float32)


def convolve(flow_field, conv_weight):
    cells_x, cells_y, cells_z, channels = flow_field.shape
    padded = with_halo(flow_field, (("gx", 0), ("gy", 1)), 1)
    padded = jnp.pad(padded, ((0, 0), (0, 0), (1, 1), (0, 0)))
    stacked = jnp.concatenate(
        [padded[:, :, 0:cells_z], padded[:, :, 1 : cells_z + 1], padded[:, :, 2 : cells_z + 2]],
        axis=3,
    )
    kernel = conv_weight.reshape(3, 3, 3 * channels, channels)
    accumulated = jnp.zeros((cells_x, cells_y, cells_z, channels), jnp.float32)
    for shift_x in range(3):
        for shift_y in range(3):
            accumulated = accumulated + jnp.dot(
                stacked[shift_x : shift_x + cells_x, shift_y : shift_y + cells_y],
                kernel[shift_x, shift_y],
                preferred_element_type=jnp.float32,
            )
    return accumulated


def body(flow_field, spectral_weight, conv_weight, channel_bias):
    convolved = convolve(flow_field, conv_weight)
    spectral = spectral_part(flow_field, spectral_weight)
    return jax.nn.gelu(spectral + convolved + channel_bias, approximate=True).astype(jnp.bfloat16)


def solution(mesh):
    placed = (P("gx", "gy", None, None), P(("gy", "gx"), None, None, None, None), P(), P())
    return jax.shard_map(
        body, mesh=mesh, in_specs=placed, out_specs=P("gx", "gy", None, None), check_vma=False
    )
```

profile of v0, /device:TPU:0, one launch (start us, length us, event | category | flops | bytes accessed | tf_op | source)
XLA Modules:
  0.0 136.2 jit_solution(9942999487540331168)
XLA Ops:
  0.1 1.5 %fusion.28 = bf16[2,4,16,16,128]{4,3,2,1,0:T(8,128)(2,1)S(1)} fusion(bf16[4,16,64,128]{3,2,1,0:T(8,128)(2,1)} %param.4, bf16[1,64,16]{1,2,0:T(8,128)(2,1)S(1)} %get-tuple-element.34, bf16[1,64,16]{1,2,0:T(8,128)(2,1)S(1)} %get-tuple-element.35), kind=kOutput, calls=%fused_computation.36 | convolution fusion | flops 33824768 | bytes 1576960 | tf_op jit(solution)/shard_map/xyzc,pzk->pxykc/dot_general | solution.py:63
  1.6 6.4 %copy.43 = bf16[2,4,16,16,128]{3,2,1,0,4:T(8,128)(2,1)} copy(bf16[2,4,16,16,128]{4,3,2,1,0:T(8,128)(2,1)S(1)} %fusion.28) | data formatting | bytes 1048576 | tf_op jit(solution)/shard_map/convert_element_type | solution.py:67
  8.0 6.7 %reshape.844 = bf16[2,2,65536]{2,1,0:T(2,128)(2,1)} reshape(bf16[128,2,4,16,16]{4,3,2,1,0:T(8,128)(2,1)} %bitcast.224) | data formatting | bytes 1048576
  14.7 4.2 %all-to-all-start = ((bf16[2,2,65536]{2,1,0:T(2,128)(2,1)}), bf16[2,2,65536]{2,1,0:T(2,128)(2,1)S(1)}, u32[]{:S(2)}, u32[]{:S(2)}) async-start(bf16[2,2,65536]{2,1,0:T(2,128)(2,1)} %reshape.844), calls=%async_computation | async-start | bytes 1048576 | tf_op jit(solution)/shard_map/all_to_all | solution.py:66
  19.0 1.6 %collective-permute-start = (bf16[1,16,64,128]{3,2,1,0:T(8,128)(2,1)S(1)}, bf16[1,16,64,128]{3,2,1,0:T(8,128)(2,1)S(1)}, u32[]{:S(2)}, u32[]{:S(2)}) collective-permute-start(bf16[1,16,64,128]{3,2,1,0:T(8,128)(2,1)S(1)} %get-tuple-element.13), channel_id=1, source_target_pairs={{0,2},{2,4},{4,6},{6,8},{8,10},{10,12},{12,14},{14,16},{16,18},{18... | collective-permute-start | bytes 786440 | tf_op jit(solution)/shard_map/ppermute | solution.py:20
  20.6 1.3 collective-permute-start.1
  22.1 0.3 broadcast_multiply_fusion.3
  22.6 0.7 maximum_bitcast_fusion.5
  23.2 0.7 maximum_bitcast_fusion.3
  23.9 3.7 %all-to-all-done = bf16[2,2,65536]{2,1,0:T(2,128)(2,1)S(1)} async-done(((bf16[2,2,65536]{2,1,0:T(2,128)(2,1)}), bf16[2,2,65536]{2,1,0:T(2,128)(2,1)S(1)}, u32[]{:S(2)}, u32[]{:S(2)}) %all-to-all-start) | async-done | bytes 524320 | tf_op jit(solution)/shard_map/all_to_all | solution.py:66
  27.7 4.1 %reshape.845 = bf16[128,2,4,16,16]{4,3,2,1,0:T(8,128)(2,1)} reshape(bf16[2,2,65536]{2,1,0:T(2,128)(2,1)S(1)} %all-to-all-done) | data formatting | bytes 1048576
  31.8 7.3 %copy.44 = bf16[2,4,16,16,2,64]{5,2,4,0,3,1:T(8,128)(2,1)} copy(bf16[2,4,16,16,2,64]{3,2,1,0,5,4:T(8,128)(2,1)} %bitcast.223) | data formatting | bytes 1048576 | tf_op jit(solution)/shard_map/all_to_all | solution.py:66
  39.4 1.7 %collective-permute-start.2 = (bf16[6,1,64,128]{3,2,1,0:T(8,128)(2,1)S(1)}, bf16[6,1,64,128]{3,2,1,0:T(8,128)(2,1)S(1)}, u32[]{:S(2)}, u32[]{:S(2)}) collective-permute-start(bf16[6,1,64,128]{3,2,1,0:T(8,128)(2,1)S(1)} %get-tuple-element.10), channel_id=1, source_target_pairs={{0,1},{2,3},{4,5},{6,7},{8,9},{10,11},{12,13},{14,15},{16,17},{18,... | collective-permute-start | bytes 294920 | tf_op jit(solution)/shard_map/ppermute | solution.py:20
  41.1 1.3 collective-permute-start.3
  42.4 0.6 fusion.27
  43.2 1.1 reshape.846
  44.3 3.9 %all-to-all-start.1 = ((bf16[2,2,32768]{2,1,0:T(2,128)(2,1)}), bf16[2,2,32768]{2,1,0:T(2,128)(2,1)S(1)}, u32[]{:S(2)}, u32[]{:S(2)}) async-start(bf16[2,2,32768]{2,1,0:T(2,128)(2,1)} %reshape.846), calls=%async_computation.1 | async-start | bytes 524288 | tf_op jit(solution)/shard_map/all_to_all | solution.py:72
  48.2 1.2 fusion.16
  49.5 0.9 fusion.100
  50.4 0.9 pad_maximum_fusion
  51.3 0.3 copy-done.7
  51.6 2.6 %fusion.41 = f32[4,16,64,128]{3,2,1,0:T(8,128)} fusion(bf16[6,18,64,384]{3,2,1,0:T(8,128)(2,1)S(1)} %pad_maximum_fusion, bf16[3,3,384,128]{3,2,1,0:T(8,128)(2,1)S(1)} %bitcast.239), kind=kOutput, calls=%fused_computation.56 | convolution fusion | flops 402653184 | bytes 7503872 | tf_op jit(solution)/shard_map/dot_general | solution.py:120
  54.2 2.3 %fusion.42 = f32[4,16,64,128]{3,2,1,0:T(8,128)} fusion(bf16[6,18,64,384]{3,2,1,0:T(8,128)(2,1)S(1)} %pad_maximum_fusion, bf16[3,3,384,128]{3,2,1,0:T(8,128)(2,1)S(1)} %bitcast.240), kind=kOutput, calls=%fused_computation.58 | convolution fusion | flops 402653184 | bytes 7503872 | tf_op jit(solution)/shard_map/dot_general | solution.py:120
  56.5 2.3 %fusion.43 = f32[4,16,64,128]{3,2,1,0:T(8,128)} fusion(bf16[6,18,64,384]{3,2,1,0:T(8,128)(2,1)S(1)} %pad_maximum_fusion, bf16[3,3,384,128]{3,2,1,0:T(8,128)(2,1)S(1)} %bitcast.241), kind=kOutput, calls=%fused_computation.60 | convolution fusion | flops 402653184 | bytes 7503872 | tf_op jit(solution)/shard_map/dot_general | solution.py:120
  58.9 0.3 reshape.847
  59.2 0.5 copy.46
  59.8 1.1 reshape.848
  60.9 7.9 %all-to-all-start.2 = ((bf16[16,2,4096]{2,1,0:T(2,128)(2,1)}), bf16[16,2,4096]{2,1,0:T(2,128)(2,1)S(1)}, u32[]{:S(2)}, u32[]{:S(2)}) async-start(bf16[16,2,4096]{2,1,0:T(2,128)(2,1)} %reshape.848), calls=%async_computation.2 | async-start | bytes 524288 | tf_op jit(solution)/shard_map/all_to_all | solution.py:76
  68.8 4.3 %fusion.44 = f32[4,16,64,128]{3,2,1,0:T(8,128)} fusion(bf16[6,18,64,384]{3,2,1,0:T(8,128)(2,1)} %copy-done, bf16[3,3,384,128]{3,2,1,0:T(8,128)(2,1)S(1)} %bitcast.242), kind=kOutput, calls=%fused_computation.62 | convolution fusion | flops 402653184 | bytes 7503872 | tf_op jit(solution)/shard_map/dot_general | solution.py:120
  73.2 2.3 %fusion.45 = f32[4,16,64,128]{3,2,1,0:T(8,128)} fusion(bf16[6,18,64,384]{3,2,1,0:T(8,128)(2,1)S(1)} %copy-done.1, bf16[3,3,384,128]{3,2,1,0:T(8,128)(2,1)S(1)} %bitcast.243), kind=kOutput, calls=%fused_computation.64 | convolution fusion | flops 402653184 | bytes 7503872 | tf_op jit(solution)/shard_map/dot_general | solution.py:120
  75.5 3.3 %all-to-all-done.2 = bf16[16,2,4096]{2,1,0:T(2,128)(2,1)S(1)} async-done(((bf16[16,2,4096]{2,1,0:T(2,128)(2,1)}), bf16[16,2,4096]{2,1,0:T(2,128)(2,1)S(1)}, u32[]{:S(2)}, u32[]{:S(2)}) %all-to-all-start.2) | async-done | bytes 262176 | tf_op jit(solution)/shard_map/all_to_all | solution.py:76
  78.9 0.3 reshape.849
  79.3 0.6 fusion.24
  79.9 12.9 %fusion.17 = f32[2,2,64,16,128]{4,0,1,3,2:T(2,128)S(1)} fusion(bf16[16,64,2,64,128]{4,3,2,1,0:T(8,128)(2,1)} %param.5, bf16[2,64,16,64,1]{3,1,2,0,4:T(8,128)(2,1)S(1)} %fusion.24), kind=kOutput, calls=%fused_computation.22 | convolution fusion | flops 67108864 | bytes 35913728 | tf_op jit(solution)/shard_map/pmjc,jmqco->pqmjo/dot_general | solution.py:84
  92.8 1.3 fusion.99
  94.3 0.7 copy-done.10
  95.0 1.3 fusion.26
  96.3 1.1 copy.56
  97.5 4.0 %all-to-all-start.3 = ((bf16[2,64,1,16,128]{4,3,0,2,1:T(8,128)(2,1)}), bf16[2,64,1,16,128]{4,3,0,2,1:T(8,128)(2,1)S(1)}, u32[]{:S(2)}, u32[]{:S(2)}) async-start(bf16[2,64,1,16,128]{4,3,0,2,1:T(8,128)(2,1)} %copy.56), calls=%async_computation.3 | async-start | bytes 1048576 | tf_op jit(solution)/shard_map/all_to_all | solution.py:91
  101.4 4.4 %fusion.46 = f32[4,16,64,128]{3,2,1,0:T(8,128)} fusion(bf16[6,18,64,384]{3,2,1,0:T(8,128)(2,1)} %copy-done, bf16[3,3,384,128]{3,2,1,0:T(8,128)(2,1)S(1)} %bitcast.244), kind=kOutput, calls=%fused_computation.66 | convolution fusion | flops 402653184 | bytes 7503872 | tf_op jit(solution)/shard_map/dot_general | solution.py:120
  105.8 4.2 %fusion.47 = f32[4,16,64,128]{3,2,1,0:T(8,128)} fusion(bf16[6,18,64,384]{3,2,1,0:T(8,128)(2,1)} %copy-done, bf16[3,3,384,128]{3,2,1,0:T(8,128)(2,1)S(1)} %bitcast.245), kind=kOutput, calls=%fused_computation.68 | convolution fusion | flops 402653184 | bytes 7503872 | tf_op jit(solution)/shard_map/dot_general | solution.py:120
  110.0 2.3 %fusion.48 = f32[4,16,64,128]{3,2,1,0:T(8,128)} fusion(bf16[6,18,64,384]{3,2,1,0:T(8,128)(2,1)S(1)} %bitcast.222, bf16[3,3,384,128]{3,2,1,0:T(8,128)(2,1)S(1)} %bitcast.246), kind=kOutput, calls=%fused_computation.70 | convolution fusion | flops 402653184 | bytes 7503872 | tf_op jit(solution)/shard_map/dot_general | solution.py:120
  112.3 3.3 %all-to-all-done.3 = bf16[2,64,1,16,128]{4,3,0,2,1:T(8,128)(2,1)S(1)} async-done(((bf16[2,64,1,16,128]{4,3,0,2,1:T(8,128)(2,1)}), bf16[2,64,1,16,128]{4,3,0,2,1:T(8,128)(2,1)S(1)}, u32[]{:S(2)}, u32[]{:S(2)}) %all-to-all-start.3) | async-done | bytes 524320 | tf_op jit(solution)/shard_map/all_to_all | solution.py:91
  115.7 1.4 %reduce = bf16[2,4,128,128]{3,2,1,0:T(8,128)(2,1)S(1)} reduce(bf16[2,4,128,2,128]{4,3,2,1,0:T(2,128)(2,1)S(1)} %bitcast.230, bf16[]{:T(256)} %constant.106.clone.1), dimensions={3}, to_apply=%region_0.1.clone | reduce | flops 131072 | bytes 786434 | tf_op jit(solution)/shard_map/reduce_sum | solution.py:95
  117.2 9.7 %all_gather.3 = bf16[2,4,16,16,128]{4,2,0,3,1:T(8,128)(2,1)S(1)} all-gather(bf16[2,4,8,16,128]{4,2,0,3,1:T(8,128)(2,1)S(1)} %copy.59), channel_id=1, replica_groups=mesh['gx'=16,'gy'=2] {'gy'}, dimensions={2}, use_global_device_ids=true | all-gather | bytes 786432 | tf_op jit(solution)/shard_map/all_gather | solution.py:97
  126.9 0.6 fusion.25
  127.5 0.5 fusion.35
  128.0 8.2 %fusion.13 = bf16[4,16,64,128]{3,2,1,0:T(8,128)(2,1)} fusion(f32[64,4,16,128,1]{3,0,4,2,1:T(8,128)S(1)} %fusion.35, f32[4,16,64,128]{3,2,1,0:T(8,128)S(1)} %copy-done.2, f32[4,16,64,128]{3,2,1,0:T(8,128)S(1)} %copy-done.3, f32[4,16,64,128]{3,2,1,0:T(8,128)S(1)} %copy-done.4, f32[4,16,64,128]{3,2,1,0:T(8,128)} %fusion.44, f32[4,16,64,128]{3,2,1,0:T(8,128)} %fusion.45, ...), kind=kOutput, calls=%fused_computation.17 | convolution fusion | flops 412614656 | bytes 25330176 | tf_op jit(solution)/shard_map/dot_general | solution.py:120
  (55 shorter events, 1.3 us)
Async XLA Ops:
  8.0 10.9 %copy-start.5 = (bf16[4,16,64,128]{3,2,1,0:T(8,128)(2,1)S(1)}, bf16[4,16,64,128]{3,2,1,0:T(8,128)(2,1)}, u32[]{:S(2)}) copy-start(bf16[4,16,64,128]{3,2,1,0:T(8,128)(2,1)} %param.4) | copy-start | bytes 3145732
  14.7 13.0 %all-to-all-start = ((bf16[2,2,65536]{2,1,0:T(2,128)(2,1)}), bf16[2,2,65536]{2,1,0:T(2,128)(2,1)S(1)}, u32[]{:S(2)}, u32[]{:S(2)}) async-start(bf16[2,2,65536]{2,1,0:T(2,128)(2,1)} %reshape.844), calls=%async_computation | async-start | bytes 1048576 | tf_op jit(solution)/shard_map/all_to_all | solution.py:66
  19.0 20.1 %collective-permute-start = (bf16[1,16,64,128]{3,2,1,0:T(8,128)(2,1)S(1)}, bf16[1,16,64,128]{3,2,1,0:T(8,128)(2,1)S(1)}, u32[]{:S(2)}, u32[]{:S(2)}) collective-permute-start(bf16[1,16,64,128]{3,2,1,0:T(8,128)(2,1)S(1)} %get-tuple-element.13), channel_id=1, source_target_pairs={{0,2},{2,4},{4,6},{6,8},{8,10},{10,12},{12,14},{14,16},{16,18},{18... | collective-permute-start | bytes 786440 | tf_op jit(solution)/shard_map/ppermute | solution.py:20
  20.6 18.7 %collective-permute-start.1 = (bf16[1,16,64,128]{3,2,1,0:T(8,128)(2,1)S(1)}, bf16[1,16,64,128]{3,2,1,0:T(8,128)(2,1)S(1)}, u32[]{:S(2)}, u32[]{:S(2)}) collective-permute-start(bf16[1,16,64,128]{3,2,1,0:T(8,128)(2,1)S(1)} %get-tuple-element.12), channel_id=1, source_target_pairs={{2,0},{4,2},{6,4},{8,6},{10,8},{12,10},{14,12},{16,14},{18,16},{20... | collective-permute-start | bytes 786440 | tf_op jit(solution)/shard_map/ppermute | solution.py:21
  39.1 3.3 %copy-start.6 = (bf16[2,4,16,16,2,64]{5,2,4,0,3,1:T(8,128)(2,1)S(1)}, bf16[2,4,16,16,2,64]{5,2,4,0,3,1:T(8,128)(2,1)}, u32[]{:S(2)}) copy-start(bf16[2,4,16,16,2,64]{5,2,4,0,3,1:T(8,128)(2,1)} %copy.44) | copy-start | bytes 1572868
  39.4 8.8 %collective-permute-start.2 = (bf16[6,1,64,128]{3,2,1,0:T(8,128)(2,1)S(1)}, bf16[6,1,64,128]{3,2,1,0:T(8,128)(2,1)S(1)}, u32[]{:S(2)}, u32[]{:S(2)}) collective-permute-start(bf16[6,1,64,128]{3,2,1,0:T(8,128)(2,1)S(1)} %get-tuple-element.10), channel_id=1, source_target_pairs={{0,1},{2,3},{4,5},{6,7},{8,9},{10,11},{12,13},{14,15},{16,17},{18,... | collective-permute-start | bytes 294920 | tf_op jit(solution)/shard_map/ppermute | solution.py:20
  41.1 7.1 %collective-permute-start.3 = (bf16[6,1,64,128]{3,2,1,0:T(8,128)(2,1)S(1)}, bf16[6,1,64,128]{3,2,1,0:T(8,128)(2,1)S(1)}, u32[]{:S(2)}, u32[]{:S(2)}) collective-permute-start(bf16[6,1,64,128]{3,2,1,0:T(8,128)(2,1)S(1)} %get-tuple-element.11), channel_id=1, source_target_pairs={{1,0},{3,2},{5,4},{7,6},{9,8},{11,10},{13,12},{15,14},{17,16},{19,... | collective-permute-start | bytes 294920 | tf_op jit(solution)/shard_map/ppermute | solution.py:21
  44.3 14.6 %all-to-all-start.1 = ((bf16[2,2,32768]{2,1,0:T(2,128)(2,1)}), bf16[2,2,32768]{2,1,0:T(2,128)(2,1)S(1)}, u32[]{:S(2)}, u32[]{:S(2)}) async-start(bf16[2,2,32768]{2,1,0:T(2,128)(2,1)} %reshape.846), calls=%async_computation.1 | async-start | bytes 524288 | tf_op jit(solution)/shard_map/all_to_all | solution.py:72
  50.4 1.2 copy-start.7
  51.3 5.3 %copy-start = (bf16[6,18,64,384]{3,2,1,0:T(8,128)(2,1)}, bf16[6,18,64,384]{3,2,1,0:T(8,128)(2,1)S(1)}, u32[]{:S(2)}) copy-start(bf16[6,18,64,384]{3,2,1,0:T(8,128)(2,1)S(1)} %pad_maximum_fusion) | copy-start | bytes 15925252
  60.9 17.9 %all-to-all-start.2 = ((bf16[16,2,4096]{2,1,0:T(2,128)(2,1)}), bf16[16,2,4096]{2,1,0:T(2,128)(2,1)S(1)}, u32[]{:S(2)}, u32[]{:S(2)}) async-start(bf16[16,2,4096]{2,1,0:T(2,128)(2,1)} %reshape.848), calls=%async_computation.2 | async-start | bytes 524288 | tf_op jit(solution)/shard_map/all_to_all | solution.py:76
  68.8 4.4 %copy-start.1 = (bf16[6,18,64,384]{3,2,1,0:T(8,128)(2,1)S(1)}, bf16[6,18,64,384]{3,2,1,0:T(8,128)(2,1)}, u32[]{:S(2)}) copy-start(bf16[6,18,64,384]{3,2,1,0:T(8,128)(2,1)} %copy-done) | copy-start | bytes 15925252
  73.2 6.1 %copy-start.8 = (f32[1,2,64,64]{2,3,0,1:T(8,128)S(1)}, f32[1,2,64,64]{2,3,0,1:T(8,128)}, u32[]{:S(2)}) copy-start(f32[1,2,64,64]{2,3,0,1:T(8,128)} %get-tuple-element.16) | copy-start | bytes 98308
  73.2 6.1 %copy-start.9 = (f32[1,2,64,64]{2,3,0,1:T(8,128)S(1)}, f32[1,2,64,64]{2,3,0,1:T(8,128)}, u32[]{:S(2)}) copy-start(f32[1,2,64,64]{2,3,0,1:T(8,128)} %get-tuple-element.17) | copy-start | bytes 98308
  94.1 0.8 copy-start.10
  94.1 0.9 copy-start.11
  97.5 12.5 %slice-start = ((s8[5308416]{0:T(1024)(128)(4,1)}), s8[1114112]{0:T(1024)(128)(4,1)S(1)}, s32[]{:S(2)}) async-start(s8[5308416]{0:T(1024)(128)(4,1)} %bitcast.221), calls=%async_computation.4 | async-start | bytes 2228224
  97.5 18.1 %all-to-all-start.3 = ((bf16[2,64,1,16,128]{4,3,0,2,1:T(8,128)(2,1)}), bf16[2,64,1,16,128]{4,3,0,2,1:T(8,128)(2,1)S(1)}, u32[]{:S(2)}, u32[]{:S(2)}) async-start(bf16[2,64,1,16,128]{4,3,0,2,1:T(8,128)(2,1)} %copy.56), calls=%async_computation.3 | async-start | bytes 1048576 | tf_op jit(solution)/shard_map/all_to_all | solution.py:91
  101.4 8.6 %slice-start.1 = ((s8[5308416]{0:T(1024)(128)(4,1)}), s8[4194304]{0:T(1024)(128)(4,1)S(1)}, s32[]{:S(2)}) async-start(s8[5308416]{0:T(1024)(128)(4,1)} %bitcast.221), calls=%async_computation.5 | async-start | bytes 8388608
  115.6 12.3 %copy-start.4 = (f32[4,16,64,128]{3,2,1,0:T(8,128)S(1)}, f32[4,16,64,128]{3,2,1,0:T(8,128)}, u32[]{:S(2)}) copy-start(f32[4,16,64,128]{3,2,1,0:T(8,128)} %fusion.43) | copy-start | bytes 6291460
  117.2 10.8 %copy-start.2 = (f32[4,16,64,128]{3,2,1,0:T(8,128)S(1)}, f32[4,16,64,128]{3,2,1,0:T(8,128)}, u32[]{:S(2)}) copy-start(f32[4,16,64,128]{3,2,1,0:T(8,128)} %fusion.41) | copy-start | bytes 6291460
  117.2 10.8 %copy-start.3 = (f32[4,16,64,128]{3,2,1,0:T(8,128)S(1)}, f32[4,16,64,128]{3,2,1,0:T(8,128)}, u32[]{:S(2)}) copy-start(f32[4,16,64,128]{3,2,1,0:T(8,128)} %fusion.42) | copy-start | bytes 6291460
  117.2 10.8 %copy-start.12 = (f32[128]{0:T(128)S(1)}, f32[128]{0:T(128)}, u32[]{:S(2)}) copy-start(f32[128]{0:T(128)} %param.7) | copy-start | bytes 1540
where the time goes:
time: 137 us; the launch traced here: 136 us
  matrix products  51.1 us (37%)
  local copies, waits for them, and re-layouts  31.7 us (23%)
  starting transfers between devices  26 us (19%)
  waiting for transfers between devices  10.4 us (8%)
  blocking collectives  9.67 us (7%)
  other arithmetic  6.95 us (5%)
    dot_general x9, matrix products, convolve(): jnp.dot(stacked[shift_x:shift_x + cells_x, shift_y:shift_y + cells_y], ke...  33 us
    unnamed x38, local copies, waits for them, and re-layouts  14.9 us
    dot_general x1, matrix products, spectral_part(): jnp.einsum('pmjc,jmqco->pqmjo', x_spectrum, spectral_weight, preferred_el...  12.9 us
    all_gather x1, blocking collectives, spectral_part(): lax.all_gather(summed.astype(jnp.bfloat16), 'gy', axis=2, tiled=True)  9.67 us
    all_to_all x1, starting transfers between devices, spectral_part(): lax.all_to_all(owned_modes.astype(jnp.bfloat16), 'gx', split_axis=2, conc...  7.89 us
    all_to_all x1, local copies, waits for them, and re-layouts, spectral_part(): lax.all_to_all(z_spectrum.astype(jnp.bfloat16), 'gy', split_axis=4, conca...  7.32 us
    convert_element_type x1, local copies, waits for them, and re-layouts, spectral_part(): z_spectrum.astype(jnp.bfloat16)  6.43 us
    all_to_all x1, starting transfers between devices, spectral_part(): lax.all_to_all(z_spectrum.astype(jnp.bfloat16), 'gy', split_axis=4, conca...  4.23 us
  transfers between devices with their start and end apart: 8, of which 3 were waited for; matrix products, arithmetic and copies ran while one was open for 32% of the time, Pallas kernels for 0%

commit v1 on v0

--- a/solution.py
+++ b/solution.py
@@ -1,8 +1,12 @@
+import functools
 import math
 
 import jax
 import jax.numpy as jnp
+import numpy as np
 from jax import lax
+from jax.experimental import pallas as pl
+from jax.experimental.pallas import tpu as pltpu
 from jax.sharding import PartitionSpec as P
 
 MX = 64
@@ -10,17 +14,353 @@
 MZ = 16
 
 
-def with_halo(array, sides, width):
-    for axis, dim in sides:
-        size, length = (lax.axis_size(axis), array.shape[dim])
-        up = [(i, (i + 1) % size) for i in range(size - 1)]
-        down = [(j, i) for i, j in up]
-        last = lax.slice_in_dim(array, length - width, length, axis=dim)
-        initial = lax.slice_in_dim(array, 0, width, axis=dim)
-        before = lax.ppermute(last, axis, up)
-        after = lax.ppermute(initial, axis, down)
-        array = jnp.concatenate([before, array, after], axis=dim)
-    return array
+def frequencies(mode_count):
+    position = np.arange(mode_count)
+    return np.where(position < mode_count // 2, position, position - mode_count)
+
+
+def wave(first, second, length, factor):
+    turns = (np.asarray(first)[:, None] * np.asarray(second)[None, :]) % length
+    angles = turns * (2.0 * math.pi / length)
+    return (np.cos(angles) + 1j * np.sin(angles)) * factor
+
+
+def rounded(values):
+    return values.astype(np.float32).astype(jnp.bfloat16).astype(np.float64)
+
+
+def item_modes(shards_x, shards_y, pairs):
+    index = np.arange(shards_y * shards_x * pairs).reshape(shards_y, shards_x, pairs)
+    return index // MZ, index % MZ
+
+
+def forward_yz_table(shards_x, shards_y, pairs, cells_y, cells_z):
+    full_y = shards_y * cells_y
+    turn_z = wave(np.arange(MZ), np.arange(cells_z), cells_z, cells_z**-0.5)
+    turn_z = rounded(turn_z.real) - 1j * rounded(turn_z.imag)
+    turn_y = np.conj(wave(frequencies(MY), np.arange(full_y), full_y, full_y**-0.5))
+    mode_y, mode_z = item_modes(shards_x, shards_y, pairs)
+    table = np.empty(
+        (shards_y, shards_y, shards_x, pairs, 2, cells_y, cells_z), np.float32
+    )
+    for own in range(shards_y):
+        rows = turn_y[:, own * cells_y : (own + 1) * cells_y]
+        for step in range(shards_y):
+            owner = (own + step) % shards_y
+            product = rows[mode_y[owner]][..., :, None] * turn_z[mode_z[owner]][..., None, :]
+            table[own, step, :, :, 0] = product.real
+            table[own, step, :, :, 1] = product.imag
+    return table.reshape(
+        shards_y, shards_y, shards_x * pairs * 2, cells_y * cells_z
+    ).astype(jnp.bfloat16)
+
+
+def backward_yz_table(shards_x, shards_y, pairs, cells_y, cells_z):
+    full_y = shards_y * cells_y
+    turn_z = wave(np.arange(MZ), np.arange(cells_z), cells_z, MZ**-0.5)
+    turn_z = rounded(turn_z.real) + 1j * rounded(turn_z.imag)
+    turn_y = wave(frequencies(MY), np.arange(full_y), full_y, MY**-0.5)
+    mode_y, mode_z = item_modes(shards_x, shards_y, pairs)
+    table = np.empty(
+        (shards_y, shards_y, cells_y, cells_z, shards_x, pairs, 2), np.float32
+    )
+    for own in range(shards_y):
+        rows = turn_y[:, own * cells_y : (own + 1) * cells_y]
+        for step in range(shards_y):
+            owner = (own - step) % shards_y
+            product = rows[mode_y[owner]][..., :, None] * turn_z[mode_z[owner]][..., None, :]
+            product = np.moveaxis(product, (2, 3), (0, 1))
+            table[own, step, ..., 0] = product.real
+            table[own, step, ..., 1] = -product.imag
+    return table.reshape(
+        shards_y, shards_y, cells_y * cells_z, shards_x * pairs * 2
+    ).astype(jnp.bfloat16)
+
+
+def forward_x_table(full_x, pairs):
+    turn = np.conj(wave(frequencies(MX), np.arange(full_x), full_x, full_x**-0.5))
+    parts = np.empty((2, MX, 2, full_x, pairs, 2), np.float32)
+    cosine, sine = turn.real[:, :, None], turn.imag[:, :, None]
+    parts[0, :, 0, :, :, 0], parts[0, :, 0, :, :, 1] = cosine, -sine
+    parts[0, :, 1, :, :, 0], parts[0, :, 1, :, :, 1] = sine, cosine
+    parts[1, :, 0] = -parts[0, :, 1]
+    parts[1, :, 1] = parts[0, :, 0]
+    return parts.reshape(2 * MX * 2, full_x * pairs * 2).astype(jnp.bfloat16)
+
+
+def backward_x_table(full_x, pairs):
+    turn = wave(frequencies(MX), np.arange(full_x), full_x, MX**-0.5).T
+    parts = np.empty((full_x, pairs, 2, MX, 2), np.float32)
+    cosine, sine = turn.real[:, None, :], turn.imag[:, None, :]
+    parts[:, :, 0, :, 0], parts[:, :, 0, :, 1] = cosine, -sine
+    parts[:, :, 1, :, 0], parts[:, :, 1, :, 1] = sine, cosine
+    return parts.reshape(full_x * pairs * 2, MX * 2).astype(jnp.bfloat16)
+
+
+def dot(left, right):
+    return jnp.dot(left, right, preferred_element_type=jnp.float32)
+
+
+def forward_kernel(own_ref, table_ref, flow_ref, out_ref):
+    cells_x = flow_ref.shape[0]
+    shards_x, _, rows, channels = out_ref.shape
+    width = 2 if cells_x % 2 == 0 else 1
+    for x in range(0, cells_x, width):
+        columns = [flow_ref[x + i] for i in range(width)]
+        result = dot(table_ref[0, 0], jnp.concatenate(columns, axis=1))
+        for i in range(width):
+            part = result[:, i * channels : (i + 1) * channels]
+            out_ref[:, x + i] = part.astype(out_ref.dtype).reshape(shards_x, rows, channels)
+
+
+def forward_yz(own_y, table, flow, step, shards_x):
+    cells_x, positions, channels = flow.shape
+    rows = table.shape[2]
+    return pl.pallas_call(
+        forward_kernel,
+        grid_spec=pltpu.PrefetchScalarGridSpec(
+            num_scalar_prefetch=1,
+            grid=(1,),
+            in_specs=[
+                pl.BlockSpec((1, 1, rows, positions), lambda i, own: (own[0], step, 0, 0)),
+                pl.BlockSpec((cells_x, positions, channels), lambda i, own: (0, 0, 0)),
+            ],
+            out_specs=pl.BlockSpec(
+                (shards_x, cells_x, rows // shards_x, channels), lambda i, own: (0, 0, 0, 0)
+            ),
+        ),
+        out_shape=jax.ShapeDtypeStruct(
+            (shards_x, cells_x, rows // shards_x, channels), jnp.bfloat16
+        ),
+        compiler_params=pltpu.CompilerParams(vmem_limit_bytes=24 << 20),
+        cost_estimate=pl.CostEstimate(
+            flops=4 * rows * positions * cells_x * channels,
+            bytes_accessed=2 * positions * (rows + cells_x * channels),
+            transcendentals=0,
+        ),
+    )(own_y, table, flow)
+
+
+def mixing_kernel(rows_ref, forward_ref, backward_ref, weight_ref, out_ref, left, mixed, total):
+    pair = pl.program_id(0)
+    pairs = pl.num_programs(0)
+    spectrum_rows = mixed.shape[0]
+    channels = rows_ref.shape[1]
+    half = channels // 2
+
+    def owned(shape, axis):
+        index = lax.broadcasted_iota(jnp.int32, shape, axis)
+        return lax.rem(lax.div(index, 2), out_ref.shape[1] // 2) == pair
+
+    table = forward_ref[...]
+    table = jnp.where(owned(table.shape, 1), table, jnp.zeros_like(table))
+    both = dot(table, rows_ref[...])
+    value, turned = both[:spectrum_rows], both[spectrum_rows:]
+    low = lax.broadcasted_iota(jnp.int32, value.shape, 1) < half
+    first = jnp.where(low, value, pltpu.roll(turned, half, axis=1))
+    second = jnp.where(low, pltpu.roll(value, half, axis=1), turned)
+    left[:, :channels] = first.astype(left.dtype)
+    left[:, channels:] = second.astype(left.dtype)
+
+    group = 16
+    row = lax.broadcasted_iota(jnp.int32, (group, channels), 0) // 2
+
+    def mix(step, carry):
+        start = pl.multiple_of(step * group, group)
+        lhs = left[pl.ds(start, group), :]
+        gathered = jnp.zeros((group, channels), jnp.float32)
+        for i in range(0, group // 2, 2):
+            mode = step * (group // 2) + i
+            tiles = [
+                jnp.concatenate([weight_ref[0, mode + k], weight_ref[1, mode + k]], axis=0)
+                for k in range(2)
+            ]
+            product = dot(lhs, jnp.concatenate(tiles, axis=1))
+            for k in range(2):
+                gathered = jnp.where(
+                    row == i + k, product[:, k * channels : (k + 1) * channels], gathered
+                )
+        mixed[pl.ds(start, group), :] = gathered.astype(mixed.dtype)
+        return carry
+
+    lax.fori_loop(0, spectrum_rows // group, mix, 0)
+
+    table = backward_ref[...]
+    table = jnp.where(owned(table.shape, 0), table, jnp.zeros_like(table))
+    added = dot(table, mixed[...])
+
+    @pl.when(pair == 0)
+    def _():
+        total[...] = added
+
+    @pl.when(pair > 0)
+    def _():
+        total[...] += added
+
+    @pl.when(pair == pairs - 1)
+    def _():
+        out_ref[...] = total[...].reshape(out_ref.shape).astype(out_ref.dtype)
+
+
+def mixing(rows, forward_x, backward_x, weight, pairs):
+    row_count, channels = rows.shape
+    full_x = row_count // (2 * pairs)
+    depth = weight.shape[2]
+    whole = lambda i: (0, 0)
+    return pl.pallas_call(
+        mixing_kernel,
+        grid=(pairs,),
+        in_specs=[
+            pl.BlockSpec(rows.shape, whole),
+            pl.BlockSpec(forward_x.shape, whole),
+            pl.BlockSpec(backward_x.shape, whole),
+            pl.BlockSpec((2, MX, depth, channels), lambda i: (i, 0, 0, 0)),
+        ],
+        out_specs=pl.BlockSpec((full_x, 2 * pairs, channels), lambda i: (0, 0, 0)),
+        out_shape=jax.ShapeDtypeStruct((full_x, 2 * pairs, channels), jnp.bfloat16),
+        scratch_shapes=[
+            pltpu.VMEM((2 * MX, 2 * channels), jnp.bfloat16),
+            pltpu.VMEM((2 * MX, channels), jnp.bfloat16),
+            pltpu.VMEM((row_count, channels), jnp.float32),
+        ],
+        compiler_params=pltpu.CompilerParams(vmem_limit_bytes=40 << 20),
+        cost_estimate=pl.CostEstimate(
+            flops=8 * weight.size, bytes_accessed=2 * weight.size, transcendentals=0
+        ),
+    )(rows, forward_x, backward_x, weight)
+
+
+def final_kernel(own_ref, table_ref, *refs):
+    *coefficient_refs, convolved_ref, bias_ref, out_ref = refs
+    cells_x, cells_y, cells_z, channels = out_ref.shape
+    width = 2 if cells_x % 2 == 0 else 1
+    bias = bias_ref[...]
+    for x in range(0, cells_x, width):
+        total = None
+        for step, ref in enumerate(coefficient_refs):
+            depth = ref.shape[0] * ref.shape[2]
+            columns = [ref[:, x + i].reshape(depth, channels) for i in range(width)]
+            product = dot(table_ref[0, step], jnp.concatenate(columns, axis=1))
+            total = product if total is None else total + product
+        for i in range(width):
+            spectral = total[:, i * channels : (i + 1) * channels]
+            spectral = spectral.reshape(cells_y, cells_z, channels)
+            value = spectral + convolved_ref[x + i].astype(jnp.float32) + bias
+            out_ref[x + i] = jax.nn.gelu(value, approximate=True).astype(out_ref.dtype)
+
+
+def final(own_y, table, coefficients, convolved, bias):
+    cells_x, cells_y, cells_z, channels = convolved.shape
+    parts = 4 if cells_y % 4 == 0 else 1
+    rows = cells_y // parts * cells_z
+    block = (cells_x, cells_y // parts, cells_z, channels)
+    depth = table.shape[3]
+    return pl.pallas_call(
+        final_kernel,
+        grid_spec=pltpu.PrefetchScalarGridSpec(
+            num_scalar_prefetch=1,
+            grid=(parts,),
+            in_specs=[
+                pl.BlockSpec((1, table.shape[1], rows, depth), lambda i, own: (own[0], 0, i, 0)),
+                *(pl.BlockSpec(c.shape, lambda i, own: (0, 0, 0, 0)) for c in coefficients),
+                pl.BlockSpec(block, lambda i, own: (0, i, 0, 0)),
+                pl.BlockSpec((1, channels), lambda i, own: (0, 0)),
+            ],
+            out_specs=pl.BlockSpec(block, lambda i, own: (0, i, 0, 0)),
+        ),
+        out_shape=jax.ShapeDtypeStruct(convolved.shape, jnp.bfloat16),
+        compiler_params=pltpu.CompilerParams(vmem_limit_bytes=24 << 20),
+        cost_estimate=pl.CostEstimate(
+            flops=2 * table.shape[1] * table.shape[2] * depth * cells_x * channels,
+            bytes_accessed=6 * convolved.size,
+            transcendentals=convolved.size,
+        ),
+    )(own_y, table, *coefficients, convolved, bias)
+
+
+def convolution_kernel(
+    own_ref, flow_ref, left_ref, right_ref, front_ref, back_ref, weight_ref, out_ref, stacked
+):
+    cells_x, cells_y, cells_z, channels = flow_ref.shape
+    shards_y = own_ref[1]
+    own_y = own_ref[0]
+    z = lax.broadcasted_iota(jnp.int32, (cells_z, channels), 0)
+
+    def place(x, y, cells):
+        wide = cells.astype(jnp.float32)
+        before = jnp.where(z == 0, 0.0, pltpu.roll(wide, 1, axis=0))
+        after = jnp.where(z == cells_z - 1, 0.0, pltpu.roll(wide, cells_z - 1, axis=0))
+        stacked[x, y, :, :channels] = before.astype(stacked.dtype)
+        stacked[x, y, :, channels : 2 * channels] = cells
+        stacked[x, y, :, 2 * channels :] = after.astype(stacked.dtype)
+
+    def inner(x, read):
+        def one(y, carry):
+            place(x, y + 1, read(y))
+            return carry
+
+        lax.fori_loop(0, cells_y, one, 0, unroll=2)
+
+    inner(0, lambda y: left_ref[0, y])
+    inner(cells_x + 1, lambda y: right_ref[0, y])
+    for x in range(cells_x):
+        inner(x + 1, lambda y, x=x: flow_ref[x, y])
+
+    blank = jnp.zeros((cells_x + 2, cells_z, 3 * channels), stacked.dtype)
+
+    @pl.when(own_y > 0)
+    def _():
+        for x in range(cells_x + 2):
+            place(x, 0, front_ref[x, 0])
+
+    @pl.when(own_y == 0)
+    def _():
+        stacked[:, 0] = blank
+
+    @pl.when(own_y < shards_y - 1)
+    def _():
+        for x in range(cells_x + 2):
+            place(x, cells_y + 1, back_ref[x, 0])
+
+    @pl.when(own_y == shards_y - 1)
+    def _():
+        stacked[:, cells_y + 1] = blank
+
+    rows = 4 if cells_y % 4 == 0 else 1
+
+    def chunk(index, carry):
+        x = index // (cells_y // rows)
+        y = index % (cells_y // rows) * rows
+        total = jnp.zeros((rows * cells_z, channels), jnp.float32)
+        for a in range(3):
+            for b in range(3):
+                block = stacked[x + a, pl.ds(y + b, rows)]
+                total = total + dot(block.reshape(rows * cells_z, 3 * channels), weight_ref[a, b])
+        out_ref[x, pl.ds(y, rows)] = total.reshape(rows, cells_z, channels).astype(out_ref.dtype)
+        return carry
+
+    lax.fori_loop(0, cells_x * (cells_y // rows), chunk, 0)
+
+
+def convolution(own_y, shards_y, flow, left, right, front, back, weight):
+    cells_x, cells_y, cells_z, channels = flow.shape
+    scalars = jnp.concatenate([own_y, jnp.full((1,), shards_y, jnp.int32)])
+    vmem = pl.BlockSpec(memory_space=pltpu.VMEM)
+    return pl.pallas_call(
+        convolution_kernel,
+        in_specs=[pl.BlockSpec(memory_space=pltpu.SMEM)] + [vmem] * 6,
+        out_specs=vmem,
+        out_shape=jax.ShapeDtypeStruct(flow.shape, jnp.bfloat16),
+        scratch_shapes=[
+            pltpu.VMEM((cells_x + 2, cells_y + 2, cells_z, 3 * channels), jnp.bfloat16)
+        ],
+        compiler_params=pltpu.CompilerParams(vmem_limit_bytes=24 << 20),
+        cost_estimate=pl.CostEstimate(
+            flops=2 * 2 * flow.size * 27 * channels,
+            bytes_accessed=6 * flow.size,
+            transcendentals=0,
+        ),
+    )(scalars, flow, left, right, front, back, weight)
 
 
 def signed_modes(mode_count):
@@ -47,7 +387,7 @@
     )
 
 
-def spectral_part(flow_field, spectral_weight):
+def split_pair_spectral(flow_field, spectral_weight):
     highest = lax.Precision.HIGHEST
     cells_x, cells_y, cells_z, channels = flow_field.shape
     count_x = lax.axis_size("gx")
@@ -105,30 +445,79 @@
     return jnp.einsum("pxykc,pkz->xyzc", y_inverse, backward_z, preferred_element_type=jnp.float32)
 
 
-def convolve(flow_field, conv_weight):
-    cells_x, cells_y, cells_z, channels = flow_field.shape
-    padded = with_halo(flow_field, (("gx", 0), ("gy", 1)), 1)
-    padded = jnp.pad(padded, ((0, 0), (0, 0), (1, 1), (0, 0)))
-    stacked = jnp.concatenate(
-        [padded[:, :, 0:cells_z], padded[:, :, 1 : cells_z + 1], padded[:, :, 2 : cells_z + 2]],
-        axis=3,
-    )
-    kernel = conv_weight.reshape(3, 3, 3 * channels, channels)
-    accumulated = jnp.zeros((cells_x, cells_y, cells_z, channels), jnp.float32)
-    for shift_x in range(3):
-        for shift_y in range(3):
-            accumulated = accumulated + jnp.dot(
-                stacked[shift_x : shift_x + cells_x, shift_y : shift_y + cells_y],
-                kernel[shift_x, shift_y],
-                preferred_element_type=jnp.float32,
-            )
-    return accumulated
-
-
-def body(flow_field, spectral_weight, conv_weight, channel_bias):
-    convolved = convolve(flow_field, conv_weight)
-    spectral = spectral_part(flow_field, spectral_weight)
-    return jax.nn.gelu(spectral + convolved + channel_bias, approximate=True).astype(jnp.bfloat16)
+def edges(first, last, axis):
+    size = lax.axis_size(axis)
+    if size == 2:
+        facing = jnp.where(lax.axis_index(axis) == 0, last, first)
+        arrived = lax.ppermute(facing, axis, [(0, 1), (1, 0)])
+        return arrived, arrived
+    up = [(i, i + 1) for i in range(size - 1)]
+    down = [(i + 1, i) for i in range(size - 1)]
+    return lax.ppermute(last, axis, up), lax.ppermute(first, axis, down)
+
+
+def convolve(own_y, flow, weight):
+    shards_y = lax.axis_size("gy")
+    channels = flow.shape[3]
+    left, right = edges(flow[:1], flow[-1:], "gx")
+    rows = [jnp.concatenate([left[:, i], flow[:, i], right[:, i]])[:, None] for i in (0, -1)]
+    front, back = edges(rows[0], rows[1], "gy")
+    kernel = weight.reshape(3, 3, 3 * channels, channels)
+    return convolution(own_y, shards_y, flow, left, right, front, back, kernel)
+
+
+def shifted(size, step):
+    return [(i, (i + step) % size) for i in range(size)]
+
+
+def body(flow, spectral_weight, conv_weight, bias):
+    cells_x, cells_y, cells_z, channels = flow.shape
+    shards_x, shards_y = lax.axis_size("gx"), lax.axis_size("gy")
+    items = spectral_weight.shape[0]
+    pairs = items // 2
+    own_y = lax.axis_index("gy").astype(jnp.int32).reshape(1)
+    if items % 2:
+        spectral = split_pair_spectral(flow, spectral_weight)
+        convolved = convolve(own_y, flow, conv_weight).astype(jnp.float32)
+        return jax.nn.gelu(spectral + convolved + bias, approximate=True).astype(jnp.bfloat16)
+    sizes = (shards_x, shards_y, pairs, cells_y, cells_z)
+    full_x = cells_x * shards_x
+
+    table = jnp.asarray(forward_yz_table(*sizes))
+    columns = flow.reshape(cells_x, cells_y * cells_z, channels)
+    sent = [
+        lax.ppermute(
+            forward_yz(own_y, table, columns, step, shards_x), "gy", shifted(shards_y, step)
+        )
+        for step in range(1, shards_y)
+    ]
+    total = forward_yz(own_y, table, columns, 0, shards_x).astype(jnp.float32)
+    for part in sent:
+        total = total + part.astype(jnp.float32)
+    rows = lax.all_to_all(total.astype(jnp.bfloat16), "gx", 0, 0, tiled=True)
+
+    convolved = convolve(own_y, flow, conv_weight)
+
+    weight = spectral_weight.reshape(items, MX, channels, channels)
+    returned = mixing(
+        rows.reshape(full_x * 2 * pairs, channels),
+        jnp.asarray(forward_x_table(full_x, pairs)),
+        jnp.asarray(backward_x_table(full_x, pairs)),
+        weight,
+        pairs,
+    )
+    returned = returned.reshape(shards_x, cells_x, 2 * pairs, channels)
+    returned = lax.all_to_all(returned, "gx", 0, 0, tiled=True)
+    coefficients = [returned] + [
+        lax.ppermute(returned, "gy", shifted(shards_y, step)) for step in range(1, shards_y)
+    ]
+    return final(
+        own_y,
+        jnp.asarray(backward_yz_table(*sizes)),
+        coefficients,
+        convolved,
+        bias.reshape(1, channels),
+    )
 
 
 def solution(mesh):

time: 137 us -> 80.2 us (0.59)
  matrix products: 51.1 us -> 0 us
  Pallas kernels: 0 us -> 35.7 us
  local copies, waits for them, and re-layouts: 31.7 us -> 4.34 us
  blocking collectives: 9.67 us -> 0 us
  waiting for transfers between devices: 10.4 us -> 17.5 us
  starting transfers between devices: 26 us -> 20.1 us
  other arithmetic: 6.95 us -> 1.75 us
    dot_general x16 -> x0, matrix products: 51.1 us -> none  [the longest x9 33 us: convolve(): jnp.dot(stacked[shift_x:shift_x + cells_x, shift_y:shift_y + cells_y], ke...]
    pallas_call x0 -> x5, Pallas kernels: none -> 35.7 us  [the longest x1 20.3 us: mixing(): pl.pallas_call(mixing_kernel, grid=(pairs,), in_specs=[pl.BlockSpec(rows....]
    unnamed x38 -> x16, local copies, waits for them, and re-layouts: 14.9 us -> 2.85 us
    all_to_all x4 -> x2, starting transfers between devices: 20 us -> 9.66 us  [the longest x1 6.13 us: body(): rows = lax.all_to_all(total.astype(jnp.bfloat16), 'gx', 0, 0, tiled=True)]
    all_gather x1 -> x0, blocking collectives: 9.67 us -> none  [spectral_part(): lax.all_gather(summed.astype(jnp.bfloat16), 'gy', axis=2, tiled=True)]
    all_to_all x5 -> x0, local copies, waits for them, and re-layouts: 7.99 us -> none  [the longest x1 7.32 us: spectral_part(): lax.all_to_all(z_spectrum.astype(jnp.bfloat16), 'gy', split_axis=4, conca...]
    convert_element_type x5 -> x0, local copies, waits for them, and re-layouts: 7.81 us -> none  [the longest x1 6.43 us: spectral_part(): z_spectrum.astype(jnp.bfloat16)]
    ppermute x4 -> x5, waiting for transfers between devices: 0.01 us -> 5.85 us  [the longest x1 5.84 us: body(): lax.ppermute(forward_yz(own_y, table, columns, step, shards_x), 'gy', shi...]
  transfers between devices with their start and end apart: 8 -> 7, of which waited for: 3 -> 3; matrix products, arithmetic and copies ran while one was open for 32% -> 3% of each run, Pallas kernels for 0% -> 41%
where the time goes in v1:
time: 80.2 us; the launch traced here: 79.5 us
  Pallas kernels  35.7 us (45%)
  starting transfers between devices  20.1 us (25%)
  waiting for transfers between devices  17.5 us (22%)
  local copies, waits for them, and re-layouts  4.34 us (5%)
  other arithmetic  1.75 us (2%)
    pallas_call x1, Pallas kernels, mixing(): pl.pallas_call(mixing_kernel, grid=(pairs,), in_specs=[pl.BlockSpec(rows....  20.3 us
    pallas_call x1, Pallas kernels, convolution(): pl.pallas_call(convolution_kernel, in_specs=[pl.BlockSpec(memory_space=pl...  11.5 us
    all_to_all x1, waiting for transfers between devices, body(): returned = lax.all_to_all(returned, 'gx', 0, 0, tiled=True)  7.4 us
    all_to_all x1, starting transfers between devices, body(): rows = lax.all_to_all(total.astype(jnp.bfloat16), 'gx', 0, 0, tiled=True)  6.13 us
    ppermute x1, waiting for transfers between devices, body(): lax.ppermute(forward_yz(own_y, table, columns, step, shards_x), 'gy', shi...  5.84 us
    ppermute x2, starting transfers between devices, edges(): return (lax.ppermute(last, axis, up), lax.ppermute(first, axis, down))  4.33 us
    all_to_all x1, waiting for transfers between devices, body(): rows = lax.all_to_all(total.astype(jnp.bfloat16), 'gx', 0, 0, tiled=True)  4.22 us
    all_to_all x1, starting transfers between devices, body(): returned = lax.all_to_all(returned, 'gx', 0, 0, tiled=True)  3.53 us
  transfers between devices with their start and end apart: 7, of which 3 were waited for; matrix products, arithmetic and copies ran while one was open for 3% of the time, Pallas kernels for 41%

profile of v1, /device:TPU:0, one launch (start us, length us, event | category | flops | bytes accessed | tf_op | source)
XLA Modules:
  0.0 79.5 jit_solution(6219644446461117059)
XLA Ops:
  0.0 0.0 copy-start
  0.0 1.6 %copy-done = bf16[2,2,256,1024]{3,2,1,0:T(8,128)(2,1)S(1)} copy-done((bf16[2,2,256,1024]{3,2,1,0:T(8,128)(2,1)S(1)}, bf16[2,2,256,1024]{3,2,1,0:T(8,128)(2,1)}, u32[]{:S(2)}) %copy-start) | copy-done | bytes 2097176
  1.6 0.0 copy-start.1
  1.6 1.2 %copy-done.1 = bf16[4,16,64,128]{3,2,1,0:T(8,128)(2,1)S(1)} copy-done((bf16[4,16,64,128]{3,2,1,0:T(8,128)(2,1)S(1)}, bf16[4,16,64,128]{3,2,1,0:T(8,128)(2,1)}, u32[]{:S(2)}) %copy-start.1) | copy-done | bytes 1048600
  2.8 0.4 shard_map.83
  3.3 0.0 copy-start.2
  3.3 3.0 %collective-permute-start = (bf16[16,4,16,128]{3,2,1,0:T(8,128)(2,1)S(1)}, bf16[16,4,16,128]{3,2,1,0:T(8,128)(2,1)S(1)}, u32[]{:S(2)}, u32[]{:S(2)}) collective-permute-start(bf16[16,4,16,128]{3,2,1,0:T(8,128)(2,1)S(1)} %shard_map.83), channel_id=1, source_target_pairs={{0,1},{1,0},{2,3},{3,2},{4,5},{5,4},{6,7},{7,6},{8,9},{9,8},{10,11... | collective-permute-start | bytes 786440 | tf_op jit(solution)/shard_map/ppermute | solution.py:489
  6.3 0.4 shard_map.82
  6.7 0.0 copy-start.4
  6.8 0.0 copy-start.5
  6.8 5.8 %collective-permute-done = bf16[16,4,16,128]{3,2,1,0:T(8,128)(2,1)S(1)} collective-permute-done((bf16[16,4,16,128]{3,2,1,0:T(8,128)(2,1)S(1)}, bf16[16,4,16,128]{3,2,1,0:T(8,128)(2,1)S(1)}, u32[]{:S(2)}, u32[]{:S(2)}) %collective-permute-start) | collective-permute-done | bytes 262176 | tf_op jit(solution)/shard_map/ppermute | solution.py:489
  12.6 0.8 add_convert_fusion
  13.4 6.1 %all-to-all-start = ((bf16[16,4,16,128]{3,2,1,0:T(8,128)(2,1)}), bf16[16,4,16,128]{3,2,1,0:T(8,128)(2,1)S(1)}, u32[]{:S(2)}, u32[]{:S(2)}) async-start(bf16[16,4,16,128]{3,2,1,0:T(8,128)(2,1)} %add_convert_fusion), calls=%async_computation | async-start | bytes 524288 | tf_op jit(solution)/shard_map/all_to_all | solution.py:497
  19.5 0.0 copy-done.2
  19.5 0.8 %fusion.1 = (bf16[1,16,64,128]{3,2,1,0:T(8,128)(2,1)}, bf16[1,16,64,128]{3,2,1,0:T(8,128)(2,1)}) fusion(bf16[4,16,64,128]{3,2,1,0:T(8,128)(2,1)S(1)} %copy-done.2), kind=kLoop, calls=%fused_computation.4 | loop fusion | bytes 1048576 | tf_op jit(solution)/shard_map/slice | solution.py:462
  20.4 1.3 %collective-permute-start.3 = (bf16[1,16,64,128]{3,2,1,0:T(8,128)(2,1)}, bf16[1,16,64,128]{3,2,1,0:T(8,128)(2,1)S(1)}, u32[]{:S(2)}, u32[]{:S(2)}) collective-permute-start(bf16[1,16,64,128]{3,2,1,0:T(8,128)(2,1)} %get-tuple-element.7), channel_id=1, source_target_pairs={{2,0},{4,2},{6,4},{8,6},{10,8},{12,10},{14,12},{16,14},{18,16},{20... | collective-permute-start | bytes 786440 | tf_op jit(solution)/shard_map/ppermute | solution.py:456
  21.7 3.0 %collective-permute-start.2 = (bf16[1,16,64,128]{3,2,1,0:T(8,128)(2,1)}, bf16[1,16,64,128]{3,2,1,0:T(8,128)(2,1)S(1)}, u32[]{:S(2)}, u32[]{:S(2)}) collective-permute-start(bf16[1,16,64,128]{3,2,1,0:T(8,128)(2,1)} %get-tuple-element.8), channel_id=1, source_target_pairs={{0,2},{2,4},{4,6},{6,8},{8,10},{10,12},{12,14},{14,16},{16,18},{18... | collective-permute-start | bytes 786440 | tf_op jit(solution)/shard_map/ppermute | solution.py:456
  24.7 0.7 fusion
  25.4 4.2 %all-to-all-done = bf16[16,4,16,128]{3,2,1,0:T(8,128)(2,1)S(1)} async-done(((bf16[16,4,16,128]{3,2,1,0:T(8,128)(2,1)}), bf16[16,4,16,128]{3,2,1,0:T(8,128)(2,1)S(1)}, u32[]{:S(2)}, u32[]{:S(2)}) %all-to-all-start) | async-done | bytes 262176 | tf_op jit(solution)/shard_map/all_to_all | solution.py:497
  29.6 0.0 copy-done.4
  29.6 0.0 copy-done.5
  29.6 0.0 copy-start.7
  29.6 20.3 %shard_map.84 = bf16[64,16,128]{2,1,0:T(8,128)(2,1)} custom-call(bf16[1024,128]{1,0:T(8,128)(2,1)S(1)} %bitcast.9, bf16[256,1024]{1,0:T(8,128)(2,1)S(1)} %copy-done.4, bf16[1024,128]{1,0:T(8,128)(2,1)S(1)} %copy-done.5, bf16[16,64,128,128]{3,2,1,0:T(8,128)(2,1)} %bitcast.12), custom_call_target="tpu_custom_call" | custom-call | flops 134217728 | bytes 33554432 | tf_op jit(solution)/shard_map/pallas_call | solution.py:210
  49.9 3.5 %all-to-all-start.1 = ((bf16[16,4,16,128]{3,2,1,0:T(8,128)(2,1)}), bf16[16,4,16,128]{3,2,1,0:T(8,128)(2,1)S(1)}, u32[]{:S(2)}, u32[]{:S(2)}) async-start(bf16[16,4,16,128]{3,2,1,0:T(8,128)(2,1)} %bitcast.4), calls=%async_computation.1 | async-start | bytes 524288 | tf_op jit(solution)/shard_map/all_to_all | solution.py:510
  53.5 0.0 collective-permute-done.3.right_ref
  53.5 0.0 collective-permute-done.2.left_ref
  53.5 0.9 %maximum_select_fusion = bf16[6,1,64,128]{3,2,1,0:T(8,128)(2,1)S(1)} fusion(bf16[1,1,64,128]{3,2,1,0:T(8,128)(2,1)S(1)} %get-tuple-element.12, bf16[4,1,64,128]{3,2,1,0:T(8,128)(2,1)} %get-tuple-element.6, bf16[1,1,64,128]{3,2,1,0:T(8,128)(2,1)S(1)} %get-tuple-element.10, bf16[1,1,64,128]{3,2,1,0:T(8,128)(2,1)S(1)} %get-tuple-element.11, ...), kind=kLoop, calls=%fused_computation.1 | loop fusion | flops 245760 | bytes 294913 | tf_op jit(solution)/shard_map/jit(_where)/select_n | solution.py:451
  54.4 1.6 %collective-permute-start.4 = (bf16[6,1,64,128]{3,2,1,0:T(8,128)(2,1)S(1)}, bf16[6,1,64,128]{3,2,1,0:T(8,128)(2,1)S(1)}, u32[]{:S(2)}, u32[]{:S(2)}) collective-permute-start(bf16[6,1,64,128]{3,2,1,0:T(8,128)(2,1)S(1)} %maximum_select_fusion), channel_id=1, source_target_pairs={{0,1},{1,0},{2,3},{3,2},{4,5},{5,4},{6,7},{7,6},{8,9},{9,8},{10,11... | collective-permute-start | bytes 294920 | tf_op jit(solution)/shard_map/ppermute | solution.py:452
  56.0 0.1 pad_add_fusion.own_ref
  56.1 7.4 %all-to-all-done.1.refs_0_ = bf16[16,4,16,128]{3,2,1,0:T(8,128)(2,1)S(1)} async-done(((bf16[16,4,16,128]{3,2,1,0:T(8,128)(2,1)}), bf16[16,4,16,128]{3,2,1,0:T(8,128)(2,1)S(1)}, u32[]{:S(2)}, u32[]{:S(2)}) %all-to-all-start.1) | async-done | bytes 262176 | tf_op jit(solution)/shard_map/all_to_all | solution.py:510
  63.5 1.5 %collective-permute-start.1 = (bf16[16,4,16,128]{3,2,1,0:T(8,128)(2,1)S(1)}, bf16[16,4,16,128]{3,2,1,0:T(8,128)(2,1)S(1)}, u32[]{:S(2)}, u32[]{:S(2)}) collective-permute-start(bf16[16,4,16,128]{3,2,1,0:T(8,128)(2,1)S(1)} %all-to-all-done.1.refs_0_), channel_id=1, source_target_pairs={{0,1},{1,0},{2,3},{3,2},{4,5},{5,4},{6,7},{7,6},{8,9},{9,8},{10,11... | collective-permute-start | bytes 786440 | tf_op jit(solution)/shard_map/ppermute | solution.py:512
  65.0 0.0 collective-permute-done.4.front_ref.back_ref
  65.0 0.0 copy-done.7
  65.0 0.0 copy-start.3
  65.0 0.0 copy-start.6
  65.0 11.5 %shard_map.85.refs_2_ = bf16[4,16,64,128]{3,2,1,0:T(8,128)(2,1)S(1)} custom-call(s32[2]{0:T(128)S(1)} %pad_add_fusion.own_ref, bf16[4,16,64,128]{3,2,1,0:T(8,128)(2,1)S(1)} %copy-done.2, bf16[1,16,64,128]{3,2,1,0:T(8,128)(2,1)S(1)} %collective-permute-done.2.left_ref, bf16[1,16,64,128]{3,2,1,0:T(8,128)(2,1)S(1)} %collective-permute-done.3.right_ref, ...), custom_call_target="tpu_custom_call" | custom-call | flops 7247757312 | bytes 3145728 | tf_op jit(solution)/shard_map/pallas_call | solution.py:349
  76.6 0.0 collective-permute-done.1.refs_1_
  76.6 0.0 copy-done.3
  76.6 0.0 copy-done.6
  76.6 2.9 %shard_map.86 = bf16[4,16,64,128]{3,2,1,0:T(8,128)(2,1)} custom-call(s32[1]{0:T(128)} %bitcast.own_ref, bf16[2,2,1024,256]{3,2,1,0:T(8,128)(2,1)S(1)} %copy-done.3, bf16[16,4,16,128]{3,2,1,0:T(8,128)(2,1)S(1)} %all-to-all-done.1.refs_0_, bf16[16,4,16,128]{3,2,1,0:T(8,128)(2,1)S(1)} %collective-permute-done.1.refs_1_, ...), custom_call_target="tpu_custom_call" | custom-call | flops 536870912 | bytes 3145728 | tf_op jit(solution)/shard_map/pallas_call | solution.py:258
  (2 shorter events, 0.0 us)
Async XLA Ops:
  0.0 1.6 %copy-start = (bf16[2,2,256,1024]{3,2,1,0:T(8,128)(2,1)S(1)}, bf16[2,2,256,1024]{3,2,1,0:T(8,128)(2,1)}, u32[]{:S(2)}) copy-start(bf16[2,2,256,1024]{3,2,1,0:T(8,128)(2,1)} %constant.16.clone.table_ref) | copy-start | bytes 6291460
  1.6 1.2 %copy-start.1 = (bf16[4,16,64,128]{3,2,1,0:T(8,128)(2,1)S(1)}, bf16[4,16,64,128]{3,2,1,0:T(8,128)(2,1)}, u32[]{:S(2)}) copy-start(bf16[4,16,64,128]{3,2,1,0:T(8,128)(2,1)} %flow_ref.1) | copy-start | bytes 3145732
  3.3 16.3 %copy-start.2 = (bf16[4,16,64,128]{3,2,1,0:T(8,128)(2,1)S(1)}, bf16[4,16,64,128]{3,2,1,0:T(8,128)(2,1)}, u32[]{:S(2)}) copy-start(bf16[4,16,64,128]{3,2,1,0:T(8,128)(2,1)} %flow_ref.1) | copy-start | bytes 3145732
  3.3 9.3 %collective-permute-start = (bf16[16,4,16,128]{3,2,1,0:T(8,128)(2,1)S(1)}, bf16[16,4,16,128]{3,2,1,0:T(8,128)(2,1)S(1)}, u32[]{:S(2)}, u32[]{:S(2)}) collective-permute-start(bf16[16,4,16,128]{3,2,1,0:T(8,128)(2,1)S(1)} %shard_map.83), channel_id=1, source_target_pairs={{0,1},{1,0},{2,3},{3,2},{4,5},{5,4},{6,7},{7,6},{8,9},{9,8},{10,11... | collective-permute-start | bytes 786440 | tf_op jit(solution)/shard_map/ppermute | solution.py:489
  6.7 22.8 %copy-start.4 = (bf16[256,1024]{1,0:T(8,128)(2,1)S(1)}, bf16[256,1024]{1,0:T(8,128)(2,1)}, u32[]{:S(2)}) copy-start(bf16[256,1024]{1,0:T(8,128)(2,1)} %constant.17.clone.forward_ref) | copy-start | bytes 1572868
  6.8 22.8 %copy-start.5 = (bf16[1024,128]{1,0:T(8,128)(2,1)S(1)}, bf16[1024,128]{1,0:T(8,128)(2,1)}, u32[]{:S(2)}) copy-start(bf16[1024,128]{1,0:T(8,128)(2,1)} %constant.18.clone.backward_ref) | copy-start | bytes 786436
  13.4 16.2 %all-to-all-start = ((bf16[16,4,16,128]{3,2,1,0:T(8,128)(2,1)}), bf16[16,4,16,128]{3,2,1,0:T(8,128)(2,1)S(1)}, u32[]{:S(2)}, u32[]{:S(2)}) async-start(bf16[16,4,16,128]{3,2,1,0:T(8,128)(2,1)} %add_convert_fusion), calls=%async_computation | async-start | bytes 524288 | tf_op jit(solution)/shard_map/all_to_all | solution.py:497
  20.4 33.1 %collective-permute-start.3 = (bf16[1,16,64,128]{3,2,1,0:T(8,128)(2,1)}, bf16[1,16,64,128]{3,2,1,0:T(8,128)(2,1)S(1)}, u32[]{:S(2)}, u32[]{:S(2)}) collective-permute-start(bf16[1,16,64,128]{3,2,1,0:T(8,128)(2,1)} %get-tuple-element.7), channel_id=1, source_target_pairs={{2,0},{4,2},{6,4},{8,6},{10,8},{12,10},{14,12},{16,14},{18,16},{20... | collective-permute-start | bytes 786440 | tf_op jit(solution)/shard_map/ppermute | solution.py:456
  21.7 31.8 %collective-permute-start.2 = (bf16[1,16,64,128]{3,2,1,0:T(8,128)(2,1)}, bf16[1,16,64,128]{3,2,1,0:T(8,128)(2,1)S(1)}, u32[]{:S(2)}, u32[]{:S(2)}) collective-permute-start(bf16[1,16,64,128]{3,2,1,0:T(8,128)(2,1)} %get-tuple-element.8), channel_id=1, source_target_pairs={{0,2},{2,4},{4,6},{6,8},{8,10},{10,12},{12,14},{14,16},{16,18},{18... | collective-permute-start | bytes 786440 | tf_op jit(solution)/shard_map/ppermute | solution.py:456
  29.6 35.4 %copy-start.7 = (bf16[3,3,3,128,128]{4,3,2,1,0:T(8,128)(2,1)S(1)}, bf16[3,3,3,128,128]{4,3,2,1,0:T(8,128)(2,1)}, u32[]{:S(2)}) copy-start(bf16[3,3,3,128,128]{4,3,2,1,0:T(8,128)(2,1)} %param.10) | copy-start | bytes 2654212
  49.9 13.5 %all-to-all-start.1 = ((bf16[16,4,16,128]{3,2,1,0:T(8,128)(2,1)}), bf16[16,4,16,128]{3,2,1,0:T(8,128)(2,1)S(1)}, u32[]{:S(2)}, u32[]{:S(2)}) async-start(bf16[16,4,16,128]{3,2,1,0:T(8,128)(2,1)} %bitcast.4), calls=%async_computation.1 | async-start | bytes 524288 | tf_op jit(solution)/shard_map/all_to_all | solution.py:510
  54.4 10.6 %collective-permute-start.4 = (bf16[6,1,64,128]{3,2,1,0:T(8,128)(2,1)S(1)}, bf16[6,1,64,128]{3,2,1,0:T(8,128)(2,1)S(1)}, u32[]{:S(2)}, u32[]{:S(2)}) collective-permute-start(bf16[6,1,64,128]{3,2,1,0:T(8,128)(2,1)S(1)} %maximum_select_fusion), channel_id=1, source_target_pairs={{0,1},{1,0},{2,3},{3,2},{4,5},{5,4},{6,7},{7,6},{8,9},{9,8},{10,11... | collective-permute-start | bytes 294920 | tf_op jit(solution)/shard_map/ppermute | solution.py:452
  63.5 13.1 %collective-permute-start.1 = (bf16[16,4,16,128]{3,2,1,0:T(8,128)(2,1)S(1)}, bf16[16,4,16,128]{3,2,1,0:T(8,128)(2,1)S(1)}, u32[]{:S(2)}, u32[]{:S(2)}) collective-permute-start(bf16[16,4,16,128]{3,2,1,0:T(8,128)(2,1)S(1)} %all-to-all-done.1.refs_0_), channel_id=1, source_target_pairs={{0,1},{1,0},{2,3},{3,2},{4,5},{5,4},{6,7},{7,6},{8,9},{9,8},{10,11... | collective-permute-start | bytes 786440 | tf_op jit(solution)/shard_map/ppermute | solution.py:512
  65.0 11.6 %copy-start.3 = (bf16[2,2,1024,256]{3,2,1,0:T(8,128)(2,1)S(1)}, bf16[2,2,1024,256]{3,2,1,0:T(8,128)(2,1)}, u32[]{:S(2)}) copy-start(bf16[2,2,1024,256]{3,2,1,0:T(8,128)(2,1)} %constant.19.clone.table_ref) | copy-start | bytes 6291460
  65.0 11.6 %copy-start.6 = (f32[128]{0:T(128)S(1)}, f32[128]{0:T(128)}, u32[]{:S(2)}) copy-start(f32[128]{0:T(128)} %param.11) | copy-start | bytes 1540

commit v2 on v1

--- a/solution.py
+++ b/solution.py
@@ -77,151 +77,178 @@
     ).astype(jnp.bfloat16)
 
 
-def forward_x_table(full_x, pairs):
+def forward_x_table(full_x):
     turn = np.conj(wave(frequencies(MX), np.arange(full_x), full_x, full_x**-0.5))
-    parts = np.empty((2, MX, 2, full_x, pairs, 2), np.float32)
-    cosine, sine = turn.real[:, :, None], turn.imag[:, :, None]
-    parts[0, :, 0, :, :, 0], parts[0, :, 0, :, :, 1] = cosine, -sine
-    parts[0, :, 1, :, :, 0], parts[0, :, 1, :, :, 1] = sine, cosine
+    parts = np.empty((2, MX, 2, 2, full_x), np.float32)
+    parts[0, :, 0, 0], parts[0, :, 0, 1] = turn.real, -turn.imag
+    parts[0, :, 1, 0], parts[0, :, 1, 1] = turn.imag, turn.real
     parts[1, :, 0] = -parts[0, :, 1]
     parts[1, :, 1] = parts[0, :, 0]
-    return parts.reshape(2 * MX * 2, full_x * pairs * 2).astype(jnp.bfloat16)
-
-
-def backward_x_table(full_x, pairs):
+    return parts.reshape(2 * MX * 2, 2 * full_x).astype(jnp.bfloat16)
+
+
+def backward_x_table(full_x):
     turn = wave(frequencies(MX), np.arange(full_x), full_x, MX**-0.5).T
-    parts = np.empty((full_x, pairs, 2, MX, 2), np.float32)
-    cosine, sine = turn.real[:, None, :], turn.imag[:, None, :]
-    parts[:, :, 0, :, 0], parts[:, :, 0, :, 1] = cosine, -sine
-    parts[:, :, 1, :, 0], parts[:, :, 1, :, 1] = sine, cosine
-    return parts.reshape(full_x * pairs * 2, MX * 2).astype(jnp.bfloat16)
+    parts = np.empty((2, full_x, MX, 2), np.float32)
+    parts[0, :, :, 0], parts[0, :, :, 1] = turn.real, -turn.imag
+    parts[1, :, :, 0], parts[1, :, :, 1] = turn.imag, turn.real
+    return parts.reshape(2 * full_x, MX * 2).astype(jnp.bfloat16)
 
 
 def dot(left, right):
     return jnp.dot(left, right, preferred_element_type=jnp.float32)
 
 
-def forward_kernel(own_ref, table_ref, flow_ref, out_ref):
+def forward_parts(table_ref, flow_ref, shape):
     cells_x = flow_ref.shape[0]
-    shards_x, _, rows, channels = out_ref.shape
+    shards_x, _, rows, channels = shape
     width = 2 if cells_x % 2 == 0 else 1
     for x in range(0, cells_x, width):
         columns = [flow_ref[x + i] for i in range(width)]
         result = dot(table_ref[0, 0], jnp.concatenate(columns, axis=1))
         for i in range(width):
             part = result[:, i * channels : (i + 1) * channels]
-            out_ref[:, x + i] = part.astype(out_ref.dtype).reshape(shards_x, rows, channels)
-
-
-def forward_yz(own_y, table, flow, step, shards_x):
+            yield x + i, part.reshape(shards_x, rows, channels)
+
+
+def send_kernel(own_ref, table_ref, flow_ref, out_ref, *edge_refs):
+    for x, part in forward_parts(table_ref, flow_ref, out_ref.shape):
+        out_ref[:, x] = part.astype(out_ref.dtype)
+    for ref, x in zip(edge_refs, (0, flow_ref.shape[0] - 1)):
+        ref[...] = flow_ref[x]
+
+
+def keep_kernel(own_ref, table_ref, flow_ref, *refs):
+    *arrived_refs, out_ref = refs
+    for x, part in forward_parts(table_ref, flow_ref, out_ref.shape):
+        for ref in arrived_refs:
+            part = part + ref[:, x].astype(jnp.float32)
+        out_ref[:, x] = part.astype(out_ref.dtype)
+
+
+def forward_yz(own_y, table, flow, step, shards_x, arrived=(), edges=False):
     cells_x, positions, channels = flow.shape
     rows = table.shape[2]
+    shape = (shards_x, cells_x, rows // shards_x, channels)
+    shapes = [jax.ShapeDtypeStruct(shape, jnp.bfloat16)]
+    if edges:
+        shapes += [jax.ShapeDtypeStruct((positions, channels), flow.dtype)] * 2
+    whole = lambda dims: pl.BlockSpec(dims, lambda i, own: (0,) * len(dims))
+    limit = {} if edges else {"vmem_limit_bytes": 24 << 20}
     return pl.pallas_call(
-        forward_kernel,
+        keep_kernel if arrived else send_kernel,
         grid_spec=pltpu.PrefetchScalarGridSpec(
             num_scalar_prefetch=1,
             grid=(1,),
             in_specs=[
                 pl.BlockSpec((1, 1, rows, positions), lambda i, own: (own[0], step, 0, 0)),
-                pl.BlockSpec((cells_x, positions, channels), lambda i, own: (0, 0, 0)),
+                whole(flow.shape),
+                *(whole(part.shape) for part in arrived),
             ],
-            out_specs=pl.BlockSpec(
-                (shards_x, cells_x, rows // shards_x, channels), lambda i, own: (0, 0, 0, 0)
-            ),
+            out_specs=[whole(one.shape) for one in shapes],
         ),
-        out_shape=jax.ShapeDtypeStruct(
-            (shards_x, cells_x, rows // shards_x, channels), jnp.bfloat16
-        ),
-        compiler_params=pltpu.CompilerParams(vmem_limit_bytes=24 << 20),
+        out_shape=shapes,
+        compiler_params=pltpu.CompilerParams(**limit),
         cost_estimate=pl.CostEstimate(
             flops=4 * rows * positions * cells_x * channels,
             bytes_accessed=2 * positions * (rows + cells_x * channels),
             transcendentals=0,
         ),
-    )(own_y, table, flow)
-
-
-def mixing_kernel(rows_ref, forward_ref, backward_ref, weight_ref, out_ref, left, mixed, total):
-    pair = pl.program_id(0)
-    pairs = pl.num_programs(0)
-    spectrum_rows = mixed.shape[0]
-    channels = rows_ref.shape[1]
+    )(own_y, table, flow, *arrived)
+
+
+def mixing_kernel(
+    rows_ref, forward_ref, backward_ref, weight_ref, out_ref, held, sems, wide, left, mixed
+):
+    slots, _, modes, _, channels = held.shape
+    pairs = weight_ref.shape[0] // 2
+    full_x = rows_ref.shape[0] // (2 * pairs)
     half = channels // 2
-
-    def owned(shape, axis):
-        index = lax.broadcasted_iota(jnp.int32, shape, axis)
-        return lax.rem(lax.div(index, 2), out_ref.shape[1] // 2) == pair
-
-    table = forward_ref[...]
-    table = jnp.where(owned(table.shape, 1), table, jnp.zeros_like(table))
-    both = dot(table, rows_ref[...])
-    value, turned = both[:spectrum_rows], both[spectrum_rows:]
-    low = lax.broadcasted_iota(jnp.int32, value.shape, 1) < half
-    first = jnp.where(low, value, pltpu.roll(turned, half, axis=1))
-    second = jnp.where(low, pltpu.roll(value, half, axis=1), turned)
-    left[:, :channels] = first.astype(left.dtype)
-    left[:, channels:] = second.astype(left.dtype)
+    parts = MX // modes
+    chunks = pairs * parts
+    span = 2 * MX
+
+    def copy(chunk):
+        slot = lax.rem(chunk, slots)
+        pair, part = lax.div(chunk, parts), lax.rem(chunk, parts)
+        return pltpu.make_async_copy(
+            weight_ref.at[pl.ds(2 * pair, 2), pl.ds(part * modes, modes)],
+            held.at[slot],
+            sems.at[slot],
+        )
+
+    for chunk in range(min(slots, chunks)):
+        copy(chunk).start()
+
+    wide[...] = rows_ref[...].astype(jnp.float32)
+    low = lax.broadcasted_iota(jnp.int32, (span, channels), 1) < half
+    for pair in range(pairs):
+        columns = [wide[pl.ds(2 * pair + p, full_x, stride=2 * pairs), :] for p in range(2)]
+        columns = jnp.concatenate(columns, axis=0).astype(jnp.bfloat16)
+        both = dot(forward_ref[...], columns)
+        value, turned = both[:span], both[span:]
+        first = jnp.where(low, value, pltpu.roll(turned, half, axis=1))
+        second = jnp.where(low, pltpu.roll(value, half, axis=1), turned)
+        left[pl.ds(pair * span, span), :channels] = first.astype(left.dtype)
+        left[pl.ds(pair * span, span), channels:] = second.astype(left.dtype)
 
     group = 16
     row = lax.broadcasted_iota(jnp.int32, (group, channels), 0) // 2
 
-    def mix(step, carry):
-        start = pl.multiple_of(step * group, group)
-        lhs = left[pl.ds(start, group), :]
-        gathered = jnp.zeros((group, channels), jnp.float32)
-        for i in range(0, group // 2, 2):
-            mode = step * (group // 2) + i
-            tiles = [
-                jnp.concatenate([weight_ref[0, mode + k], weight_ref[1, mode + k]], axis=0)
-                for k in range(2)
+    def mix(chunk, carry):
+        slot = lax.rem(chunk, slots)
+        copy(chunk).wait()
+        for step in range(2 * modes // group):
+            start = pl.multiple_of(chunk * 2 * modes + step * group, group)
+            lhs = left[pl.ds(start, group), :]
+            gathered = jnp.zeros((group, channels), jnp.float32)
+            for i in range(0, group // 2, 2):
+                mode = step * (group // 2) + i
+                tiles = [
+                    jnp.concatenate([held[slot, 0, mode + k], held[slot, 1, mode + k]], axis=0)
+                    for k in range(2)
+                ]
+                product = dot(lhs, jnp.concatenate(tiles, axis=1))
+                for k in range(2):
+                    gathered = jnp.where(
+                        row == i + k, product[:, k * channels : (k + 1) * channels], gathered
+                    )
+            mixed[pl.ds(start, group), :] = gathered.astype(mixed.dtype)
+
+        @pl.when(chunk + slots < chunks)
+        def _():
+            copy(chunk + slots).start()
+
+        return carry
+
+    lax.fori_loop(0, chunks, mix, 0)
+
+    for pair in range(pairs):
+        result = dot(backward_ref[...], mixed[pl.ds(pair * span, span), :])
+        for p in range(2):
+            wide[pl.ds(2 * pair + p, full_x, stride=2 * pairs), :] = result[
+                p * full_x : (p + 1) * full_x
             ]
-            product = dot(lhs, jnp.concatenate(tiles, axis=1))
-            for k in range(2):
-                gathered = jnp.where(
-                    row == i + k, product[:, k * channels : (k + 1) * channels], gathered
-                )
-        mixed[pl.ds(start, group), :] = gathered.astype(mixed.dtype)
-        return carry
-
-    lax.fori_loop(0, spectrum_rows // group, mix, 0)
-
-    table = backward_ref[...]
-    table = jnp.where(owned(table.shape, 0), table, jnp.zeros_like(table))
-    added = dot(table, mixed[...])
-
-    @pl.when(pair == 0)
-    def _():
-        total[...] = added
-
-    @pl.when(pair > 0)
-    def _():
-        total[...] += added
-
-    @pl.when(pair == pairs - 1)
-    def _():
-        out_ref[...] = total[...].reshape(out_ref.shape).astype(out_ref.dtype)
-
-
-def mixing(rows, forward_x, backward_x, weight, pairs):
+    out_ref[...] = wide[...].astype(out_ref.dtype)
+
+
+def mixing(rows, forward_x, backward_x, weight):
     row_count, channels = rows.shape
-    full_x = row_count // (2 * pairs)
     depth = weight.shape[2]
-    whole = lambda i: (0, 0)
+    pairs = weight.shape[0] // 2
+    slots, modes = 4, MX // 2
+    vmem = pl.BlockSpec(memory_space=pltpu.VMEM)
     return pl.pallas_call(
         mixing_kernel,
-        grid=(pairs,),
-        in_specs=[
-            pl.BlockSpec(rows.shape, whole),
-            pl.BlockSpec(forward_x.shape, whole),
-            pl.BlockSpec(backward_x.shape, whole),
-            pl.BlockSpec((2, MX, depth, channels), lambda i: (i, 0, 0, 0)),
-        ],
-        out_specs=pl.BlockSpec((full_x, 2 * pairs, channels), lambda i: (0, 0, 0)),
-        out_shape=jax.ShapeDtypeStruct((full_x, 2 * pairs, channels), jnp.bfloat16),
+        in_specs=[vmem, vmem, vmem, pl.BlockSpec(memory_space=pl.ANY)],
+        out_specs=vmem,
+        out_shape=jax.ShapeDtypeStruct(rows.shape, jnp.bfloat16),
         scratch_shapes=[
-            pltpu.VMEM((2 * MX, 2 * channels), jnp.bfloat16),
-            pltpu.VMEM((2 * MX, channels), jnp.bfloat16),
+            pltpu.VMEM((slots, 2, modes, depth, channels), jnp.bfloat16),
+            pltpu.SemaphoreType.DMA((slots,)),
             pltpu.VMEM((row_count, channels), jnp.float32),
+            pltpu.VMEM((pairs * 2 * MX, 2 * channels), jnp.bfloat16),
+            pltpu.VMEM((pairs * 2 * MX, channels), jnp.bfloat16),
         ],
         compiler_params=pltpu.CompilerParams(vmem_limit_bytes=40 << 20),
         cost_estimate=pl.CostEstimate(
@@ -284,22 +311,25 @@
     cells_x, cells_y, cells_z, channels = flow_ref.shape
     shards_y = own_ref[1]
     own_y = own_ref[0]
-    z = lax.broadcasted_iota(jnp.int32, (cells_z, channels), 0)
 
     def place(x, y, cells):
         wide = cells.astype(jnp.float32)
-        before = jnp.where(z == 0, 0.0, pltpu.roll(wide, 1, axis=0))
-        after = jnp.where(z == cells_z - 1, 0.0, pltpu.roll(wide, cells_z - 1, axis=0))
-        stacked[x, y, :, :channels] = before.astype(stacked.dtype)
-        stacked[x, y, :, channels : 2 * channels] = cells
-        stacked[x, y, :, 2 * channels :] = after.astype(stacked.dtype)
+        count = cells.shape[0]
+        z = lax.broadcasted_iota(jnp.int32, wide.shape, 1)
+        before = jnp.where(z == 0, 0.0, pltpu.roll(wide, 1, axis=1))
+        after = jnp.where(z == cells_z - 1, 0.0, pltpu.roll(wide, cells_z - 1, axis=1))
+        stacked[x, pl.ds(y, count), :, :channels] = before.astype(stacked.dtype)
+        stacked[x, pl.ds(y, count), :, channels : 2 * channels] = cells
+        stacked[x, pl.ds(y, count), :, 2 * channels :] = after.astype(stacked.dtype)
+
+    rows = 4 if cells_y % 4 == 0 else 1
 
     def inner(x, read):
-        def one(y, carry):
-            place(x, y + 1, read(y))
+        def one(step, carry):
+            place(x, step * rows + 1, read(pl.ds(step * rows, rows)))
             return carry
 
-        lax.fori_loop(0, cells_y, one, 0, unroll=2)
+        lax.fori_loop(0, cells_y // rows, one, 0)
 
     inner(0, lambda y: left_ref[0, y])
     inner(cells_x + 1, lambda y: right_ref[0, y])
@@ -311,7 +341,7 @@
     @pl.when(own_y > 0)
     def _():
         for x in range(cells_x + 2):
-            place(x, 0, front_ref[x, 0])
+            place(x, 0, front_ref[x])
 
     @pl.when(own_y == 0)
     def _():
@@ -320,26 +350,41 @@
     @pl.when(own_y < shards_y - 1)
     def _():
         for x in range(cells_x + 2):
-            place(x, cells_y + 1, back_ref[x, 0])
+            place(x, cells_y + 1, back_ref[x])
 
     @pl.when(own_y == shards_y - 1)
     def _():
         stacked[:, cells_y + 1] = blank
 
-    rows = 4 if cells_y % 4 == 0 else 1
+    width = 2 if cells_x % 2 == 0 else 1
+    taps = [(a, b) for a in range(width + 2) for b in range(3)]
+    none = jnp.zeros(weight_ref.shape[2:], weight_ref.dtype)
+
+    def kernel_of(a, b):
+        return jnp.concatenate(
+            [weight_ref[a - i, b] if 0 <= a - i < 3 else none for i in range(width)], axis=1
+        )
 
     def chunk(index, carry):
-        x = index // (cells_y // rows)
-        y = index % (cells_y // rows) * rows
-        total = jnp.zeros((rows * cells_z, channels), jnp.float32)
-        for a in range(3):
-            for b in range(3):
-                block = stacked[x + a, pl.ds(y + b, rows)]
-                total = total + dot(block.reshape(rows * cells_z, 3 * channels), weight_ref[a, b])
-        out_ref[x, pl.ds(y, rows)] = total.reshape(rows, cells_z, channels).astype(out_ref.dtype)
+        x = lax.div(index, cells_y // rows) * width
+        y = lax.rem(index, cells_y // rows) * rows
+        total = jnp.zeros((rows * cells_z, width * channels), jnp.float32)
+        for i in range(0, len(taps), width):
+            group = taps[i : i + width]
+            blocks = [
+                stacked[x + a, pl.ds(y + b, rows)].reshape(rows * cells_z, 3 * channels)
+                for a, b in group
+            ]
+            weights = [kernel_of(a, b) for a, b in group]
+            total = total + dot(
+                jnp.concatenate(blocks, axis=1), jnp.concatenate(weights, axis=0)
+            )
+        for i in range(width):
+            part = total[:, i * channels : (i + 1) * channels].reshape(rows, cells_z, channels)
+            out_ref[x + i, pl.ds(y, rows)] = part.astype(out_ref.dtype)
         return carry
 
-    lax.fori_loop(0, cells_x * (cells_y // rows), chunk, 0)
+    lax.fori_loop(0, cells_x // width * (cells_y // rows), chunk, 0)
 
 
 def convolution(own_y, shards_y, flow, left, right, front, back, weight):
@@ -456,10 +501,9 @@
     return lax.ppermute(last, axis, up), lax.ppermute(first, axis, down)
 
 
-def convolve(own_y, flow, weight):
+def convolve(own_y, flow, left, right, weight):
     shards_y = lax.axis_size("gy")
     channels = flow.shape[3]
-    left, right = edges(flow[:1], flow[-1:], "gx")
     rows = [jnp.concatenate([left[:, i], flow[:, i], right[:, i]])[:, None] for i in (0, -1)]
     front, back = edges(rows[0], rows[1], "gy")
     kernel = weight.reshape(3, 3, 3 * channels, channels)
@@ -478,33 +522,34 @@
     own_y = lax.axis_index("gy").astype(jnp.int32).reshape(1)
     if items % 2:
         spectral = split_pair_spectral(flow, spectral_weight)
-        convolved = convolve(own_y, flow, conv_weight).astype(jnp.float32)
+        left, right = edges(flow[:1], flow[-1:], "gx")
+        convolved = convolve(own_y, flow, left, right, conv_weight).astype(jnp.float32)
         return jax.nn.gelu(spectral + convolved + bias, approximate=True).astype(jnp.bfloat16)
     sizes = (shards_x, shards_y, pairs, cells_y, cells_z)
     full_x = cells_x * shards_x
 
     table = jnp.asarray(forward_yz_table(*sizes))
     columns = flow.reshape(cells_x, cells_y * cells_z, channels)
-    sent = [
-        lax.ppermute(
-            forward_yz(own_y, table, columns, step, shards_x), "gy", shifted(shards_y, step)
-        )
-        for step in range(1, shards_y)
-    ]
-    total = forward_yz(own_y, table, columns, 0, shards_x).astype(jnp.float32)
-    for part in sent:
-        total = total + part.astype(jnp.float32)
-    rows = lax.all_to_all(total.astype(jnp.bfloat16), "gx", 0, 0, tiled=True)
-
-    convolved = convolve(own_y, flow, conv_weight)
-
-    weight = spectral_weight.reshape(items, MX, channels, channels)
+    arrived = []
+    first = last = None
+    for step in range(1, shards_y):
+        sent, *layers = forward_yz(own_y, table, columns, step, shards_x, edges=step == 1)
+        arrived.append(lax.ppermute(sent, "gy", shifted(shards_y, step)))
+        if layers:
+            first, last = (layer.reshape(1, cells_y, cells_z, channels) for layer in layers)
+    left, right = edges(first, last, "gx")
+    arrived, left, right = lax.optimization_barrier((arrived, left, right))
+    (total,) = forward_yz(own_y, table, columns, 0, shards_x, arrived)
+    rows = lax.all_to_all(total, "gx", 0, 0, tiled=True)
+
+    convolved = convolve(own_y, flow, left, right, conv_weight)
+    rows, convolved = lax.optimization_barrier((rows, convolved))
+
     returned = mixing(
         rows.reshape(full_x * 2 * pairs, channels),
-        jnp.asarray(forward_x_table(full_x, pairs)),
-        jnp.asarray(backward_x_table(full_x, pairs)),
-        weight,
-        pairs,
+        jnp.asarray(forward_x_table(full_x)),
+        jnp.asarray(backward_x_table(full_x)),
+        spectral_weight.reshape(items, MX, channels, channels),
     )
     returned = returned.reshape(shards_x, cells_x, 2 * pairs, channels)
     returned = lax.all_to_all(returned, "gx", 0, 0, tiled=True)

time: 80.2 us -> 74.6 us (0.930)
  blocking collectives: 0 us -> 15.3 us
  Pallas kernels: 35.7 us -> 27.4 us
  waiting for transfers between devices: 17.5 us -> 12.6 us
  starting transfers between devices: 20.1 us -> 15.9 us
  local copies, waits for them, and re-layouts: 4.34 us -> 1.97 us
  other arithmetic: 1.75 us -> 0.74 us
    all_to_all x0 -> x1, blocking collectives: none -> 15.3 us  [body(): returned = lax.all_to_all(returned, 'gx', 0, 0, tiled=True)]
    all_to_all x2 -> x1, waiting for transfers between devices: 11.6 us -> 0.55 us  [body(): rows = lax.all_to_all(total, 'gx', 0, 0, tiled=True)]
    ppermute x1, waiting for transfers between devices: 0.01 us -> 6.55 us  [body(): lax.ppermute(returned, 'gy', shifted(shards_y, step))]
    pallas_call x3, Pallas kernels: 21.2 us -> 16.2 us  [the longest x1 12.2 us: mixing(): pl.pallas_call(mixing_kernel, in_specs=[vmem, vmem, vmem, pl.BlockSpec(me...]
    all_to_all x2 -> x1, starting transfers between devices: 9.66 us -> 5.32 us  [body(): rows = lax.all_to_all(total, 'gx', 0, 0, tiled=True)]
    pallas_call x1, Pallas kernels: 11.5 us -> 8.31 us  [convolution(): pl.pallas_call(convolution_kernel, in_specs=[pl.BlockSpec(memory_space=pl...]
    unnamed x16 -> x14, local copies, waits for them, and re-layouts: 2.85 us -> 1.18 us
    slice x2 -> x0, local copies, waits for them, and re-layouts: 0.83 us -> none  [the longest x1 0.83 us: convolve(): left, right = edges(flow[:1], flow[-1:], 'gx')]
  transfers between devices with their start and end apart: 7 -> 6, of which waited for: 3 -> 3; matrix products, arithmetic and copies ran while one was open for 3% -> 0% of each run, Pallas kernels for 41% -> 13%
where the time goes in v2:
time: 74.6 us; the launch traced here: 74.1 us
  Pallas kernels  27.4 us (37%)
  starting transfers between devices  15.9 us (21%)
  blocking collectives  15.3 us (21%)
  waiting for transfers between devices  12.6 us (17%)
  local copies, waits for them, and re-layouts  1.97 us (3%)
    all_to_all x1, blocking collectives, body(): returned = lax.all_to_all(returned, 'gx', 0, 0, tiled=True)  15.3 us
    pallas_call x1, Pallas kernels, mixing(): pl.pallas_call(mixing_kernel, in_specs=[vmem, vmem, vmem, pl.BlockSpec(me...  12.2 us
    pallas_call x1, Pallas kernels, convolution(): pl.pallas_call(convolution_kernel, in_specs=[pl.BlockSpec(memory_space=pl...  8.31 us
    ppermute x1, waiting for transfers between devices, body(): lax.ppermute(returned, 'gy', shifted(shards_y, step))  6.55 us
    ppermute x1, waiting for transfers between devices, body(): arrived.append(lax.ppermute(sent, 'gy', shifted(shards_y, step)))  5.51 us
    all_to_all x1, starting transfers between devices, body(): rows = lax.all_to_all(total, 'gx', 0, 0, tiled=True)  5.32 us
    ppermute x2, starting transfers between devices, edges(): return (lax.ppermute(last, axis, up), lax.ppermute(first, axis, down))  4.33 us
    pallas_call x2, Pallas kernels, forward_yz(): pl.pallas_call(keep_kernel if arrived else send_kernel, grid_spec=pltpu.P...  3.93 us
  transfers between devices with their start and end apart: 6, of which 3 were waited for; matrix products, arithmetic and copies ran while one was open for 0% of the time, Pallas kernels for 13%

profile of v2, /device:TPU:0, one launch (start us, length us, event | category | flops | bytes accessed | tf_op | source)
XLA Modules:
  0.0 74.1 jit_solution(15022957986964809579)
XLA Ops:
  0.0 0.0 copy-start
  0.0 0.0 copy-start.1
  0.0 2.8 %shard_map.82 = (bf16[16,4,16,128]{3,2,1,0:T(8,128)(2,1)}, bf16[1024,128]{1,0:T(8,128)(2,1)}, bf16[1024,128]{1,0:T(8,128)(2,1)}) custom-call(s32[1]{0:T(128)} %bitcast.own_ref, bf16[2,2,256,1024]{3,2,1,0:T(8,128)(2,1)} %constant.16.clone.table_ref, bf16[4,1024,128]{2,1,0:T(8,128)(2,1)} %bitcast.9), custom_call_target="tpu_custom_call" | custom-call | flops 536870912 | bytes 1572864 | tf_op jit(solution)/shard_map/pallas_call | solution.py:138
  2.8 3.0 %collective-permute-start.1 = (bf16[1,16,64,128]{3,2,1,0:T(8,128)(2,1)}, bf16[1,16,64,128]{3,2,1,0:T(8,128)(2,1)}, u32[]{:S(2)}, u32[]{:S(2)}) collective-permute-start(bf16[1,16,64,128]{3,2,1,0:T(8,128)(2,1)} %bitcast.17), channel_id=1, source_target_pairs={{0,2},{2,4},{4,6},{6,8},{8,10},{10,12},{12,14},{14,16},{16,18},{18... | collective-permute-start | bytes 786440 | tf_op jit(solution)/shard_map/ppermute | solution.py:501
  5.8 2.4 %collective-permute-start = (bf16[16,4,16,128]{3,2,1,0:T(8,128)(2,1)}, bf16[16,4,16,128]{3,2,1,0:T(8,128)(2,1)S(1)}, u32[]{:S(2)}, u32[]{:S(2)}) collective-permute-start(bf16[16,4,16,128]{3,2,1,0:T(8,128)(2,1)} %get-tuple-element.13), channel_id=1, source_target_pairs={{0,1},{1,0},{2,3},{3,2},{4,5},{5,4},{6,7},{7,6},{8,9},{9,8},{10,11... | collective-permute-start | bytes 786440 | tf_op jit(solution)/shard_map/ppermute | solution.py:537
  8.2 1.3 %collective-permute-start.2 = (bf16[1,16,64,128]{3,2,1,0:T(8,128)(2,1)}, bf16[1,16,64,128]{3,2,1,0:T(8,128)(2,1)}, u32[]{:S(2)}, u32[]{:S(2)}) collective-permute-start(bf16[1,16,64,128]{3,2,1,0:T(8,128)(2,1)} %bitcast.16), channel_id=1, source_target_pairs={{2,0},{4,2},{6,4},{8,6},{10,8},{12,10},{14,12},{16,14},{18,16},{20... | collective-permute-start | bytes 786440 | tf_op jit(solution)/shard_map/ppermute | solution.py:501
  9.5 0.0 copy-done.1
  9.5 0.0 collective-permute-done.1.left_ref
  9.5 5.5 %collective-permute-done.refs_0_ = bf16[16,4,16,128]{3,2,1,0:T(8,128)(2,1)S(1)} collective-permute-done((bf16[16,4,16,128]{3,2,1,0:T(8,128)(2,1)}, bf16[16,4,16,128]{3,2,1,0:T(8,128)(2,1)S(1)}, u32[]{:S(2)}, u32[]{:S(2)}) %collective-permute-start) | collective-permute-done | bytes 262176 | tf_op jit(solution)/shard_map/ppermute | solution.py:537
  15.0 0.0 collective-permute-done.2.right_ref
  15.0 0.8 %fusion.1 = (bf16[1,1,64,128]{3,2,1,0:T(8,128)(2,1)S(1)}, bf16[1,1,64,128]{3,2,1,0:T(8,128)(2,1)S(1)}, bf16[1,1,64,128]{3,2,1,0:T(8,128)(2,1)S(1)}, bf16[1,1,64,128]{3,2,1,0:T(8,128)(2,1)S(1)}) fusion(bf16[1,16,64,128]{3,2,1,0:T(8,128)(2,1)} %collective-permute-done.1.left_ref, bf16[1,16,64,128]{3,2,1,0:T(8,128)(2,1)} %collective-permute-done.2.right_ref), kind=kLoop, calls=%fused_computation.3 | loop fusion | bytes 131072 | tf_op jit(solution)/shard_map/slice | solution.py:507
  15.8 0.7 maximum_select_fusion
  16.5 2.4 %collective-permute-start.3 = (bf16[6,1,64,128]{3,2,1,0:T(8,128)(2,1)}, bf16[6,1,64,128]{3,2,1,0:T(8,128)(2,1)S(1)}, u32[]{:S(2)}, u32[]{:S(2)}) collective-permute-start(bf16[6,1,64,128]{3,2,1,0:T(8,128)(2,1)} %maximum_select_fusion), channel_id=1, source_target_pairs={{0,1},{1,0},{2,3},{3,2},{4,5},{5,4},{6,7},{7,6},{8,9},{9,8},{10,11... | collective-permute-start | bytes 294920 | tf_op jit(solution)/shard_map/ppermute | solution.py:497
  18.9 0.1 pad_add_fusion.own_ref
  18.9 0.0 copy-done
  18.9 1.1 %shard_map.83 = bf16[16,4,16,128]{3,2,1,0:T(8,128)(2,1)} custom-call(s32[1]{0:T(128)} %bitcast.own_ref, bf16[2,2,256,1024]{3,2,1,0:T(8,128)(2,1)S(1)} %copy-done, bf16[4,1024,128]{2,1,0:T(8,128)(2,1)S(1)} %bitcast.10, bf16[16,4,16,128]{3,2,1,0:T(8,128)(2,1)S(1)} %collective-permute-done.refs_0_), custom_call_target="tpu_custom_call" | custom-call | flops 536870912 | bytes 1572864 | tf_op jit(solution)/shard_map/pallas_call | solution.py:138
  20.1 5.3 %all-to-all-start = ((bf16[16,4,16,128]{3,2,1,0:T(8,128)(2,1)}), bf16[16,4,16,128]{3,2,1,0:T(8,128)(2,1)S(1)}, u32[]{:S(2)}, u32[]{:S(2)}) async-start(bf16[16,4,16,128]{3,2,1,0:T(8,128)(2,1)} %shard_map.83), calls=%async_computation | async-start | bytes 524288 | tf_op jit(solution)/shard_map/all_to_all | solution.py:543
  25.4 0.0 collective-permute-done.3.front_ref.back_ref
  25.4 0.0 copy-start.6
  25.4 1.2 %copy-done.6 = bf16[3,3,3,128,128]{4,3,2,1,0:T(8,128)(2,1)S(1)} copy-done((bf16[3,3,3,128,128]{4,3,2,1,0:T(8,128)(2,1)S(1)}, bf16[3,3,3,128,128]{4,3,2,1,0:T(8,128)(2,1)}, u32[]{:S(2)}) %copy-start.6) | copy-done | bytes 884760
  26.6 0.0 copy-start.3
  26.6 0.0 copy-start.4
  26.6 8.3 %shard_map.84.refs_2_ = bf16[4,16,64,128]{3,2,1,0:T(8,128)(2,1)S(1)} custom-call(s32[2]{0:T(128)S(1)} %pad_add_fusion.own_ref, bf16[4,16,64,128]{3,2,1,0:T(8,128)(2,1)S(1)} %copy-done.1, bf16[1,16,64,128]{3,2,1,0:T(8,128)(2,1)} %collective-permute-done.1.left_ref, bf16[1,16,64,128]{3,2,1,0:T(8,128)(2,1)} %collective-permute-done.2.right_ref, ...), custom_call_target="tpu_custom_call" | custom-call | flops 7247757312 | bytes 3145728 | tf_op jit(solution)/shard_map/pallas_call | solution.py:394
  34.9 0.5 all-to-all-done
  35.5 0.0 copy-done.3
  35.5 0.0 copy-done.4
  35.5 0.0 copy-start.2
  35.5 0.0 copy-start.5
  35.5 12.2 %shard_map.85 = bf16[1024,128]{1,0:T(8,128)(2,1)S(1)} custom-call(bf16[1024,128]{1,0:T(8,128)(2,1)S(1)} %bitcast.11, bf16[256,128]{1,0:T(8,128)(2,1)S(1)} %copy-done.3, bf16[128,128]{1,0:T(8,128)(2,1)S(1)} %copy-done.4, bf16[16,64,128,128]{3,2,1,0:T(8,128)(2,1)} %bitcast.15), custom_call_target="tpu_custom_call" | custom-call | flops 134217728 | bytes 33554432 | tf_op jit(solution)/shard_map/pallas_call | solution.py:241
  47.7 15.3 %all_to_all.10.refs_0_ = bf16[16,4,16,128]{3,2,1,0:T(8,128)(2,1)S(1)} all-to-all(bf16[16,4,16,128]{3,2,1,0:T(8,128)(2,1)S(1)} %bitcast.12), channel_id=1, replica_groups=mesh['gx'=16,'gy'=2] {'gx'}, dimensions={0} | all-to-all | bytes 524288 | tf_op jit(solution)/shard_map/all_to_all | solution.py:555
  63.1 1.5 %collective-permute-start.4 = (bf16[16,4,16,128]{3,2,1,0:T(8,128)(2,1)S(1)}, bf16[16,4,16,128]{3,2,1,0:T(8,128)(2,1)S(1)}, u32[]{:S(2)}, u32[]{:S(2)}) collective-permute-start(bf16[16,4,16,128]{3,2,1,0:T(8,128)(2,1)S(1)} %all_to_all.10.refs_0_), channel_id=1, source_target_pairs={{0,1},{1,0},{2,3},{3,2},{4,5},{5,4},{6,7},{7,6},{8,9},{9,8},{10,11... | collective-permute-start | bytes 786440 | tf_op jit(solution)/shard_map/ppermute | solution.py:557
  64.6 6.5 %collective-permute-done.4.refs_1_ = bf16[16,4,16,128]{3,2,1,0:T(8,128)(2,1)S(1)} collective-permute-done((bf16[16,4,16,128]{3,2,1,0:T(8,128)(2,1)S(1)}, bf16[16,4,16,128]{3,2,1,0:T(8,128)(2,1)S(1)}, u32[]{:S(2)}, u32[]{:S(2)}) %collective-permute-start.4) | collective-permute-done | bytes 262176 | tf_op jit(solution)/shard_map/ppermute | solution.py:557
  71.1 0.0 copy-done.2
  71.1 0.0 copy-done.5
  71.1 2.9 %shard_map.86 = bf16[4,16,64,128]{3,2,1,0:T(8,128)(2,1)} custom-call(s32[1]{0:T(128)} %bitcast.own_ref, bf16[2,2,1024,256]{3,2,1,0:T(8,128)(2,1)S(1)} %copy-done.2, bf16[16,4,16,128]{3,2,1,0:T(8,128)(2,1)S(1)} %all_to_all.10.refs_0_, bf16[16,4,16,128]{3,2,1,0:T(8,128)(2,1)S(1)} %collective-permute-done.4.refs_1_, ...), custom_call_target="tpu_custom_call" | custom-call | flops 536870912 | bytes 3145728 | tf_op jit(solution)/shard_map/pallas_call | solution.py:285
  (1 shorter events, 0.0 us)
Async XLA Ops:
  0.0 18.9 %copy-start = (bf16[2,2,256,1024]{3,2,1,0:T(8,128)(2,1)S(1)}, bf16[2,2,256,1024]{3,2,1,0:T(8,128)(2,1)}, u32[]{:S(2)}) copy-start(bf16[2,2,256,1024]{3,2,1,0:T(8,128)(2,1)} %constant.16.clone.table_ref) | copy-start | bytes 6291460
  0.0 9.5 %copy-start.1 = (bf16[4,16,64,128]{3,2,1,0:T(8,128)(2,1)S(1)}, bf16[4,16,64,128]{3,2,1,0:T(8,128)(2,1)}, u32[]{:S(2)}) copy-start(bf16[4,16,64,128]{3,2,1,0:T(8,128)(2,1)} %flow_ref.1) | copy-start | bytes 3145732
  2.8 6.7 %collective-permute-start.1 = (bf16[1,16,64,128]{3,2,1,0:T(8,128)(2,1)}, bf16[1,16,64,128]{3,2,1,0:T(8,128)(2,1)}, u32[]{:S(2)}, u32[]{:S(2)}) collective-permute-start(bf16[1,16,64,128]{3,2,1,0:T(8,128)(2,1)} %bitcast.17), channel_id=1, source_target_pairs={{0,2},{2,4},{4,6},{6,8},{8,10},{10,12},{12,14},{14,16},{16,18},{18... | collective-permute-start | bytes 786440 | tf_op jit(solution)/shard_map/ppermute | solution.py:501
  5.8 9.2 %collective-permute-start = (bf16[16,4,16,128]{3,2,1,0:T(8,128)(2,1)}, bf16[16,4,16,128]{3,2,1,0:T(8,128)(2,1)S(1)}, u32[]{:S(2)}, u32[]{:S(2)}) collective-permute-start(bf16[16,4,16,128]{3,2,1,0:T(8,128)(2,1)} %get-tuple-element.13), channel_id=1, source_target_pairs={{0,1},{1,0},{2,3},{3,2},{4,5},{5,4},{6,7},{7,6},{8,9},{9,8},{10,11... | collective-permute-start | bytes 786440 | tf_op jit(solution)/shard_map/ppermute | solution.py:537
  8.2 6.8 %collective-permute-start.2 = (bf16[1,16,64,128]{3,2,1,0:T(8,128)(2,1)}, bf16[1,16,64,128]{3,2,1,0:T(8,128)(2,1)}, u32[]{:S(2)}, u32[]{:S(2)}) collective-permute-start(bf16[1,16,64,128]{3,2,1,0:T(8,128)(2,1)} %bitcast.16), channel_id=1, source_target_pairs={{2,0},{4,2},{6,4},{8,6},{10,8},{12,10},{14,12},{16,14},{18,16},{20... | collective-permute-start | bytes 786440 | tf_op jit(solution)/shard_map/ppermute | solution.py:501
  16.5 8.9 %collective-permute-start.3 = (bf16[6,1,64,128]{3,2,1,0:T(8,128)(2,1)}, bf16[6,1,64,128]{3,2,1,0:T(8,128)(2,1)S(1)}, u32[]{:S(2)}, u32[]{:S(2)}) collective-permute-start(bf16[6,1,64,128]{3,2,1,0:T(8,128)(2,1)} %maximum_select_fusion), channel_id=1, source_target_pairs={{0,1},{1,0},{2,3},{3,2},{4,5},{5,4},{6,7},{7,6},{8,9},{9,8},{10,11... | collective-permute-start | bytes 294920 | tf_op jit(solution)/shard_map/ppermute | solution.py:497
  20.1 15.4 %all-to-all-start = ((bf16[16,4,16,128]{3,2,1,0:T(8,128)(2,1)}), bf16[16,4,16,128]{3,2,1,0:T(8,128)(2,1)S(1)}, u32[]{:S(2)}, u32[]{:S(2)}) async-start(bf16[16,4,16,128]{3,2,1,0:T(8,128)(2,1)} %shard_map.83), calls=%async_computation | async-start | bytes 524288 | tf_op jit(solution)/shard_map/all_to_all | solution.py:543
  25.4 1.2 %copy-start.6 = (bf16[3,3,3,128,128]{4,3,2,1,0:T(8,128)(2,1)S(1)}, bf16[3,3,3,128,128]{4,3,2,1,0:T(8,128)(2,1)}, u32[]{:S(2)}) copy-start(bf16[3,3,3,128,128]{4,3,2,1,0:T(8,128)(2,1)} %param.10) | copy-start | bytes 2654212
  26.6 8.9 %copy-start.3 = (bf16[256,128]{1,0:T(8,128)(2,1)S(1)}, bf16[256,128]{1,0:T(8,128)(2,1)}, u32[]{:S(2)}) copy-start(bf16[256,128]{1,0:T(8,128)(2,1)} %constant.17.clone.forward_ref) | copy-start | bytes 196612
  26.6 8.9 %copy-start.4 = (bf16[128,128]{1,0:T(8,128)(2,1)S(1)}, bf16[128,128]{1,0:T(8,128)(2,1)}, u32[]{:S(2)}) copy-start(bf16[128,128]{1,0:T(8,128)(2,1)} %constant.18.clone.backward_ref) | copy-start | bytes 98308
  35.5 35.7 %copy-start.2 = (bf16[2,2,1024,256]{3,2,1,0:T(8,128)(2,1)S(1)}, bf16[2,2,1024,256]{3,2,1,0:T(8,128)(2,1)}, u32[]{:S(2)}) copy-start(bf16[2,2,1024,256]{3,2,1,0:T(8,128)(2,1)} %constant.19.clone.table_ref) | copy-start | bytes 6291460
  35.5 35.7 %copy-start.5 = (f32[128]{0:T(128)S(1)}, f32[128]{0:T(128)}, u32[]{:S(2)}) copy-start(f32[128]{0:T(128)} %param.11) | copy-start | bytes 1540
  63.1 8.1 %collective-permute-start.4 = (bf16[16,4,16,128]{3,2,1,0:T(8,128)(2,1)S(1)}, bf16[16,4,16,128]{3,2,1,0:T(8,128)(2,1)S(1)}, u32[]{:S(2)}, u32[]{:S(2)}) collective-permute-start(bf16[16,4,16,128]{3,2,1,0:T(8,128)(2,1)S(1)} %all_to_all.10.refs_0_), channel_id=1, source_target_pairs={{0,1},{1,0},{2,3},{3,2},{4,5},{5,4},{6,7},{7,6},{8,9},{9,8},{10,11... | collective-permute-start | bytes 786440 | tf_op jit(solution)/shard_map/ppermute | solution.py:557

commit v3 on v2

--- a/solution.py
+++ b/solution.py
@@ -40,19 +40,13 @@
     turn_z = rounded(turn_z.real) - 1j * rounded(turn_z.imag)
     turn_y = np.conj(wave(frequencies(MY), np.arange(full_y), full_y, full_y**-0.5))
     mode_y, mode_z = item_modes(shards_x, shards_y, pairs)
-    table = np.empty(
-        (shards_y, shards_y, shards_x, pairs, 2, cells_y, cells_z), np.float32
-    )
+    table = np.empty((shards_y, shards_y, shards_x, pairs, 2, cells_y, cells_z), np.float32)
     for own in range(shards_y):
         rows = turn_y[:, own * cells_y : (own + 1) * cells_y]
-        for step in range(shards_y):
-            owner = (own + step) % shards_y
-            product = rows[mode_y[owner]][..., :, None] * turn_z[mode_z[owner]][..., None, :]
-            table[own, step, :, :, 0] = product.real
-            table[own, step, :, :, 1] = product.imag
-    return table.reshape(
-        shards_y, shards_y, shards_x * pairs * 2, cells_y * cells_z
-    ).astype(jnp.bfloat16)
+        product = rows[mode_y][..., :, None] * turn_z[mode_z][..., None, :]
+        table[own, :, :, :, 0] = product.real
+        table[own, :, :, :, 1] = product.imag
+    return table.reshape(shards_y, -1, cells_y * cells_z).astype(jnp.bfloat16)
 
 
 def backward_yz_table(shards_x, shards_y, pairs, cells_y, cells_z):
@@ -61,20 +55,14 @@
     turn_z = rounded(turn_z.real) + 1j * rounded(turn_z.imag)
     turn_y = wave(frequencies(MY), np.arange(full_y), full_y, MY**-0.5)
     mode_y, mode_z = item_modes(shards_x, shards_y, pairs)
-    table = np.empty(
-        (shards_y, shards_y, cells_y, cells_z, shards_x, pairs, 2), np.float32
-    )
+    table = np.empty((shards_y, cells_y, cells_z, shards_y, shards_x, pairs, 2), np.float32)
     for own in range(shards_y):
         rows = turn_y[:, own * cells_y : (own + 1) * cells_y]
-        for step in range(shards_y):
-            owner = (own - step) % shards_y
-            product = rows[mode_y[owner]][..., :, None] * turn_z[mode_z[owner]][..., None, :]
-            product = np.moveaxis(product, (2, 3), (0, 1))
-            table[own, step, ..., 0] = product.real
-            table[own, step, ..., 1] = -product.imag
-    return table.reshape(
-        shards_y, shards_y, cells_y * cells_z, shards_x * pairs * 2
-    ).astype(jnp.bfloat16)
+        product = rows[mode_y][..., :, None] * turn_z[mode_z][..., None, :]
+        product = np.moveaxis(product, (3, 4), (0, 1))
+        table[own, ..., 0] = product.real
+        table[own, ..., 1] = -product.imag
+    return table.reshape(shards_y, cells_y * cells_z, -1).astype(jnp.bfloat16)
 
 
 def forward_x_table(full_x):
@@ -99,62 +87,41 @@
     return jnp.dot(left, right, preferred_element_type=jnp.float32)
 
 
-def forward_parts(table_ref, flow_ref, shape):
+def forward_kernel(own_ref, table_ref, flow_ref, out_ref):
     cells_x = flow_ref.shape[0]
-    shards_x, _, rows, channels = shape
+    _, shards_x, _, rows, channels = out_ref.shape
     width = 2 if cells_x % 2 == 0 else 1
     for x in range(0, cells_x, width):
         columns = [flow_ref[x + i] for i in range(width)]
-        result = dot(table_ref[0, 0], jnp.concatenate(columns, axis=1))
+        result = dot(table_ref[0], jnp.concatenate(columns, axis=1))
         for i in range(width):
-            part = result[:, i * channels : (i + 1) * channels]
-            yield x + i, part.reshape(shards_x, rows, channels)
-
-
-def send_kernel(own_ref, table_ref, flow_ref, out_ref, *edge_refs):
-    for x, part in forward_parts(table_ref, flow_ref, out_ref.shape):
-        out_ref[:, x] = part.astype(out_ref.dtype)
-    for ref, x in zip(edge_refs, (0, flow_ref.shape[0] - 1)):
-        ref[...] = flow_ref[x]
-
-
-def keep_kernel(own_ref, table_ref, flow_ref, *refs):
-    *arrived_refs, out_ref = refs
-    for x, part in forward_parts(table_ref, flow_ref, out_ref.shape):
-        for ref in arrived_refs:
-            part = part + ref[:, x].astype(jnp.float32)
-        out_ref[:, x] = part.astype(out_ref.dtype)
-
-
-def forward_yz(own_y, table, flow, step, shards_x, arrived=(), edges=False):
+            part = result[:, i * channels : (i + 1) * channels].astype(out_ref.dtype)
+            out_ref[0, :, x + i] = part.reshape(shards_x, rows, channels)
+
+
+def forward_yz(own_y, table, flow, shards_x):
     cells_x, positions, channels = flow.shape
-    rows = table.shape[2]
-    shape = (shards_x, cells_x, rows // shards_x, channels)
-    shapes = [jax.ShapeDtypeStruct(shape, jnp.bfloat16)]
-    if edges:
-        shapes += [jax.ShapeDtypeStruct((positions, channels), flow.dtype)] * 2
-    whole = lambda dims: pl.BlockSpec(dims, lambda i, own: (0,) * len(dims))
-    limit = {} if edges else {"vmem_limit_bytes": 24 << 20}
+    shards_y, rows, _ = table.shape
+    rows = rows // shards_y
+    shape = (shards_y, shards_x, cells_x, rows // shards_x, channels)
     return pl.pallas_call(
-        keep_kernel if arrived else send_kernel,
+        forward_kernel,
         grid_spec=pltpu.PrefetchScalarGridSpec(
             num_scalar_prefetch=1,
-            grid=(1,),
+            grid=(shards_y,),
             in_specs=[
-                pl.BlockSpec((1, 1, rows, positions), lambda i, own: (own[0], step, 0, 0)),
-                whole(flow.shape),
-                *(whole(part.shape) for part in arrived),
+                pl.BlockSpec((1, rows, positions), lambda i, own: (own[0], i, 0)),
+                pl.BlockSpec(flow.shape, lambda i, own: (0, 0, 0)),
             ],
-            out_specs=[whole(one.shape) for one in shapes],
-        ),
-        out_shape=shapes,
-        compiler_params=pltpu.CompilerParams(**limit),
+            out_specs=pl.BlockSpec((1, *shape[1:]), lambda i, own: (i, 0, 0, 0, 0)),
+        ),
+        out_shape=jax.ShapeDtypeStruct(shape, jnp.bfloat16),
         cost_estimate=pl.CostEstimate(
-            flops=4 * rows * positions * cells_x * channels,
-            bytes_accessed=2 * positions * (rows + cells_x * channels),
+            flops=2 * shards_y * rows * positions * cells_x * channels,
+            bytes_accessed=2 * positions * (shards_y * rows + cells_x * channels),
             transcendentals=0,
         ),
-    )(own_y, table, flow, *arrived)
+    )(own_y, table, flow)
 
 
 def mixing_kernel(
@@ -162,7 +129,7 @@
 ):
     slots, _, modes, _, channels = held.shape
     pairs = weight_ref.shape[0] // 2
-    full_x = rows_ref.shape[0] // (2 * pairs)
+    full_x = rows_ref.shape[1] // (2 * pairs)
     half = channels // 2
     parts = MX // modes
     chunks = pairs * parts
@@ -180,7 +147,7 @@
     for chunk in range(min(slots, chunks)):
         copy(chunk).start()
 
-    wide[...] = rows_ref[...].astype(jnp.float32)
+    wide[...] = sum(rows_ref[i].astype(jnp.float32) for i in range(rows_ref.shape[0]))
     low = lax.broadcasted_iota(jnp.int32, (span, channels), 1) < half
     for pair in range(pairs):
         columns = [wide[pl.ds(2 * pair + p, full_x, stride=2 * pairs), :] for p in range(2)]
@@ -229,11 +196,12 @@
             wide[pl.ds(2 * pair + p, full_x, stride=2 * pairs), :] = result[
                 p * full_x : (p + 1) * full_x
             ]
-    out_ref[...] = wide[...].astype(out_ref.dtype)
+    for i in range(out_ref.shape[0]):
+        out_ref[i] = wide[...].astype(out_ref.dtype)
 
 
 def mixing(rows, forward_x, backward_x, weight):
-    row_count, channels = rows.shape
+    _, row_count, channels = rows.shape
     depth = weight.shape[2]
     pairs = weight.shape[0] // 2
     slots, modes = 4, MX // 2
@@ -257,18 +225,14 @@
     )(rows, forward_x, backward_x, weight)
 
 
-def final_kernel(own_ref, table_ref, *refs):
-    *coefficient_refs, convolved_ref, bias_ref, out_ref = refs
+def final_kernel(own_ref, table_ref, coefficient_ref, convolved_ref, bias_ref, out_ref):
     cells_x, cells_y, cells_z, channels = out_ref.shape
+    depth = table_ref.shape[2]
     width = 2 if cells_x % 2 == 0 else 1
     bias = bias_ref[...]
     for x in range(0, cells_x, width):
-        total = None
-        for step, ref in enumerate(coefficient_refs):
-            depth = ref.shape[0] * ref.shape[2]
-            columns = [ref[:, x + i].reshape(depth, channels) for i in range(width)]
-            product = dot(table_ref[0, step], jnp.concatenate(columns, axis=1))
-            total = product if total is None else total + product
+        columns = [coefficient_ref[:, x + i].reshape(depth, channels) for i in range(width)]
+        total = dot(table_ref[0], jnp.concatenate(columns, axis=1))
         for i in range(width):
             spectral = total[:, i * channels : (i + 1) * channels]
             spectral = spectral.reshape(cells_y, cells_z, channels)
@@ -281,15 +245,15 @@
     parts = 4 if cells_y % 4 == 0 else 1
     rows = cells_y // parts * cells_z
     block = (cells_x, cells_y // parts, cells_z, channels)
-    depth = table.shape[3]
+    depth = table.shape[2]
     return pl.pallas_call(
         final_kernel,
         grid_spec=pltpu.PrefetchScalarGridSpec(
             num_scalar_prefetch=1,
             grid=(parts,),
             in_specs=[
-                pl.BlockSpec((1, table.shape[1], rows, depth), lambda i, own: (own[0], 0, i, 0)),
-                *(pl.BlockSpec(c.shape, lambda i, own: (0, 0, 0, 0)) for c in coefficients),
+                pl.BlockSpec((1, rows, depth), lambda i, own: (own[0], i, 0)),
+                pl.BlockSpec(coefficients.shape, lambda i, own: (0, 0, 0, 0)),
                 pl.BlockSpec(block, lambda i, own: (0, i, 0, 0)),
                 pl.BlockSpec((1, channels), lambda i, own: (0, 0)),
             ],
@@ -298,114 +262,159 @@
         out_shape=jax.ShapeDtypeStruct(convolved.shape, jnp.bfloat16),
         compiler_params=pltpu.CompilerParams(vmem_limit_bytes=24 << 20),
         cost_estimate=pl.CostEstimate(
-            flops=2 * table.shape[1] * table.shape[2] * depth * cells_x * channels,
+            flops=2 * table.shape[1] * depth * cells_x * channels,
             bytes_accessed=6 * convolved.size,
             transcendentals=convolved.size,
         ),
-    )(own_y, table, *coefficients, convolved, bias)
-
-
-def convolution_kernel(
-    own_ref, flow_ref, left_ref, right_ref, front_ref, back_ref, weight_ref, out_ref, stacked
+    )(own_y, table, coefficients, convolved, bias)
+
+
+def stack(stacked, at, cells):
+    count, cells_z, channels = cells.shape
+    wide = cells.astype(jnp.float32)
+    z = lax.broadcasted_iota(jnp.int32, wide.shape, 1)
+    before = jnp.where(z == 0, 0.0, pltpu.roll(wide, 1, axis=1))
+    after = jnp.where(z == cells_z - 1, 0.0, pltpu.roll(wide, cells_z - 1, axis=1))
+    x, y = at
+    stacked[x, pl.ds(y, count), :, :channels] = before.astype(stacked.dtype)
+    stacked[x, pl.ds(y, count), :, channels : 2 * channels] = cells
+    stacked[x, pl.ds(y, count), :, 2 * channels :] = after.astype(stacked.dtype)
+
+
+def stack_planes(stacked, count, cells_y, read):
+    rows = 4 if cells_y % 4 == 0 else 1
+    for x in range(count):
+
+        def one(step, carry, x=x):
+            stack(stacked, (x, step * rows + 1), read(x, pl.ds(step * rows, rows)))
+            return carry
+
+        lax.fori_loop(0, cells_y // rows, one, 0)
+
+
+def own_planes_kernel(
+    flags_ref, flow_ref, front_ref, back_ref, weight_ref, out_ref, stacked
 ):
     cells_x, cells_y, cells_z, channels = flow_ref.shape
-    shards_y = own_ref[1]
-    own_y = own_ref[0]
-
-    def place(x, y, cells):
-        wide = cells.astype(jnp.float32)
-        count = cells.shape[0]
-        z = lax.broadcasted_iota(jnp.int32, wide.shape, 1)
-        before = jnp.where(z == 0, 0.0, pltpu.roll(wide, 1, axis=1))
-        after = jnp.where(z == cells_z - 1, 0.0, pltpu.roll(wide, cells_z - 1, axis=1))
-        stacked[x, pl.ds(y, count), :, :channels] = before.astype(stacked.dtype)
-        stacked[x, pl.ds(y, count), :, channels : 2 * channels] = cells
-        stacked[x, pl.ds(y, count), :, 2 * channels :] = after.astype(stacked.dtype)
+    stack_planes(stacked, cells_x, cells_y, lambda x, y: flow_ref[x, y])
+    blank = jnp.zeros((cells_x, cells_z, 3 * channels), stacked.dtype)
+    for flag, ref, y in ((0, front_ref, 0), (1, back_ref, cells_y + 1)):
+
+        @pl.when(flags_ref[flag] > 0)
+        def _(ref=ref, y=y):
+            for x in range(cells_x):
+                stack(stacked, (x, y), ref[x])
+
+        @pl.when(flags_ref[flag] == 0)
+        def _(y=y):
+            stacked[:, y] = blank
 
     rows = 4 if cells_y % 4 == 0 else 1
-
-    def inner(x, read):
-        def one(step, carry):
-            place(x, step * rows + 1, read(pl.ds(step * rows, rows)))
+    width = 2 if cells_x % 2 == 0 else 1
+    none = jnp.zeros(weight_ref.shape[2:], weight_ref.dtype)
+
+    for x in range(0, cells_x, width):
+        planes = [p for p in range(x - 1, x + width + 1) if 0 <= p < cells_x]
+        taps = [(p, b) for p in planes for b in range(3)]
+
+        def chunk(index, carry, x=x, taps=taps):
+            y = index * rows
+            total = jnp.zeros((rows * cells_z, width * channels), jnp.float32)
+            for i in range(0, len(taps), 3):
+                blocks, kernels = [], []
+                for p, b in taps[i : i + 3]:
+                    block = stacked[p, pl.ds(y + b, rows)]
+                    blocks.append(block.reshape(rows * cells_z, 3 * channels))
+                    offsets = [p - (x + k) + 1 for k in range(width)]
+                    kernels.append(
+                        jnp.concatenate(
+                            [weight_ref[a, b] if 0 <= a < 3 else none for a in offsets], axis=1
+                        )
+                    )
+                total = total + dot(
+                    jnp.concatenate(blocks, axis=1), jnp.concatenate(kernels, axis=0)
+                )
+            for k in range(width):
+                part = total[:, k * channels : (k + 1) * channels]
+                out_ref[x + k, pl.ds(y, rows)] = part.reshape(rows, cells_z, channels)
             return carry
 
+        lax.fori_loop(0, cells_y // rows, chunk, 0)
+
+
+def beside_planes_kernel(left_ref, right_ref, weight_ref, partial_ref, out_ref, stacked):
+    cells_x, cells_y, cells_z, channels = out_ref.shape
+    refs = (left_ref, right_ref)
+    for x in range(2):
+        stack(stacked, (x, 0), refs[x][pl.ds(0, 1)])
+        stack(stacked, (x, cells_y + 1), refs[x][pl.ds(cells_y + 1, 1)])
+
+    rows = 4 if cells_y % 4 == 0 else 1
+    for x in range(2):
+
+        def one(step, carry, x=x):
+            stack(stacked, (x, step * rows + 1), refs[x][pl.ds(step * rows + 1, rows)])
+            return carry
+
         lax.fori_loop(0, cells_y // rows, one, 0)
 
-    inner(0, lambda y: left_ref[0, y])
-    inner(cells_x + 1, lambda y: right_ref[0, y])
+    added = {0: [(0, 0)]}
+    added.setdefault(cells_x - 1, []).append((1, 2))
     for x in range(cells_x):
-        inner(x + 1, lambda y, x=x: flow_ref[x, y])
-
-    blank = jnp.zeros((cells_x + 2, cells_z, 3 * channels), stacked.dtype)
-
-    @pl.when(own_y > 0)
-    def _():
-        for x in range(cells_x + 2):
-            place(x, 0, front_ref[x])
-
-    @pl.when(own_y == 0)
-    def _():
-        stacked[:, 0] = blank
-
-    @pl.when(own_y < shards_y - 1)
-    def _():
-        for x in range(cells_x + 2):
-            place(x, cells_y + 1, back_ref[x])
-
-    @pl.when(own_y == shards_y - 1)
-    def _():
-        stacked[:, cells_y + 1] = blank
-
-    width = 2 if cells_x % 2 == 0 else 1
-    taps = [(a, b) for a in range(width + 2) for b in range(3)]
-    none = jnp.zeros(weight_ref.shape[2:], weight_ref.dtype)
-
-    def kernel_of(a, b):
-        return jnp.concatenate(
-            [weight_ref[a - i, b] if 0 <= a - i < 3 else none for i in range(width)], axis=1
-        )
-
-    def chunk(index, carry):
-        x = lax.div(index, cells_y // rows) * width
-        y = lax.rem(index, cells_y // rows) * rows
-        total = jnp.zeros((rows * cells_z, width * channels), jnp.float32)
-        for i in range(0, len(taps), width):
-            group = taps[i : i + width]
-            blocks = [
-                stacked[x + a, pl.ds(y + b, rows)].reshape(rows * cells_z, 3 * channels)
-                for a, b in group
-            ]
-            weights = [kernel_of(a, b) for a, b in group]
-            total = total + dot(
-                jnp.concatenate(blocks, axis=1), jnp.concatenate(weights, axis=0)
-            )
-        for i in range(width):
-            part = total[:, i * channels : (i + 1) * channels].reshape(rows, cells_z, channels)
-            out_ref[x + i, pl.ds(y, rows)] = part.astype(out_ref.dtype)
-        return carry
-
-    lax.fori_loop(0, cells_x // width * (cells_y // rows), chunk, 0)
-
-
-def convolution(own_y, shards_y, flow, left, right, front, back, weight):
+
+        def chunk(index, carry, x=x):
+            y = index * rows
+            total = partial_ref[x, pl.ds(y, rows)].reshape(rows * cells_z, channels)
+            for plane, a in added.get(x, ()):
+                blocks = [
+                    stacked[plane, pl.ds(y + b, rows)].reshape(rows * cells_z, 3 * channels)
+                    for b in range(3)
+                ]
+                kernels = [weight_ref[a, b] for b in range(3)]
+                total = total + dot(
+                    jnp.concatenate(blocks, axis=1), jnp.concatenate(kernels, axis=0)
+                )
+            part = total.reshape(rows, cells_z, channels)
+            out_ref[x, pl.ds(y, rows)] = part.astype(out_ref.dtype)
+            return carry
+
+        lax.fori_loop(0, cells_y // rows, chunk, 0)
+
+
+def own_planes(flags, flow, front, back, weight):
     cells_x, cells_y, cells_z, channels = flow.shape
-    scalars = jnp.concatenate([own_y, jnp.full((1,), shards_y, jnp.int32)])
     vmem = pl.BlockSpec(memory_space=pltpu.VMEM)
     return pl.pallas_call(
-        convolution_kernel,
-        in_specs=[pl.BlockSpec(memory_space=pltpu.SMEM)] + [vmem] * 6,
+        own_planes_kernel,
+        in_specs=[pl.BlockSpec(memory_space=pltpu.SMEM)] + [vmem] * 4,
         out_specs=vmem,
-        out_shape=jax.ShapeDtypeStruct(flow.shape, jnp.bfloat16),
-        scratch_shapes=[
-            pltpu.VMEM((cells_x + 2, cells_y + 2, cells_z, 3 * channels), jnp.bfloat16)
-        ],
+        out_shape=jax.ShapeDtypeStruct(flow.shape, jnp.float32),
+        scratch_shapes=[pltpu.VMEM((cells_x, cells_y + 2, cells_z, 3 * channels), flow.dtype)],
         compiler_params=pltpu.CompilerParams(vmem_limit_bytes=24 << 20),
         cost_estimate=pl.CostEstimate(
             flops=2 * 2 * flow.size * 27 * channels,
             bytes_accessed=6 * flow.size,
             transcendentals=0,
         ),
-    )(scalars, flow, left, right, front, back, weight)
+    )(flags, flow, front, back, weight)
+
+
+def beside_planes(left, right, weight, partial):
+    cells_x, cells_y, cells_z, channels = partial.shape
+    vmem = pl.BlockSpec(memory_space=pltpu.VMEM)
+    return pl.pallas_call(
+        beside_planes_kernel,
+        in_specs=[vmem] * 4,
+        out_specs=vmem,
+        out_shape=jax.ShapeDtypeStruct(partial.shape, jnp.bfloat16),
+        scratch_shapes=[pltpu.VMEM((2, cells_y + 2, cells_z, 3 * channels), jnp.bfloat16)],
+        compiler_params=pltpu.CompilerParams(vmem_limit_bytes=24 << 20),
+        cost_estimate=pl.CostEstimate(
+            flops=2 * partial.size * 27 * channels,
+            bytes_accessed=6 * partial.size,
+            transcendentals=0,
+        ),
+    )(left, right, weight, partial)
 
 
 def signed_modes(mode_count):
@@ -501,17 +510,10 @@
     return lax.ppermute(last, axis, up), lax.ppermute(first, axis, down)
 
 
-def convolve(own_y, flow, left, right, weight):
-    shards_y = lax.axis_size("gy")
-    channels = flow.shape[3]
-    rows = [jnp.concatenate([left[:, i], flow[:, i], right[:, i]])[:, None] for i in (0, -1)]
-    front, back = edges(rows[0], rows[1], "gy")
-    kernel = weight.reshape(3, 3, 3 * channels, channels)
-    return convolution(own_y, shards_y, flow, left, right, front, back, kernel)
-
-
-def shifted(size, step):
-    return [(i, (i + step) % size) for i in range(size)]
+def with_rows(flags, front, plane, back):
+    front = jnp.where(flags[0] > 0, front, jnp.zeros_like(front))
+    back = jnp.where(flags[1] > 0, back, jnp.zeros_like(back))
+    return jnp.concatenate([front, plane, back], axis=1)
 
 
 def body(flow, spectral_weight, conv_weight, bias):
@@ -520,46 +522,49 @@
     items = spectral_weight.shape[0]
     pairs = items // 2
     own_y = lax.axis_index("gy").astype(jnp.int32).reshape(1)
-    if items % 2:
+    flags = jnp.concatenate([own_y > 0, own_y < shards_y - 1]).astype(jnp.int32)
+    kernel = conv_weight.reshape(3, 3, 3 * channels, channels)
+    fits = items % 2 == 0
+    axes = ("gy", "gx")
+    if fits:
+        sizes = (shards_x, shards_y, pairs, cells_y, cells_z)
+        columns = flow.reshape(cells_x, cells_y * cells_z, channels)
+        sent = forward_yz(own_y, jnp.asarray(forward_yz_table(*sizes)), columns, shards_x)
+        sent = sent.reshape(-1, *sent.shape[2:])
+
+    ends = (flow[:, :1], flow[:, -1:])
+    if fits:
+        sent, ends = lax.optimization_barrier((sent, ends))
+        rows = lax.all_to_all(sent, axes, 0, 0, tiled=True)
+    front, back = edges(*ends, "gy")
+    partial = own_planes(flags, flow, front, back, kernel)
+    first, last = (
+        with_rows(flags, front[x], flow[x], back[x]) for x in (slice(0, 1), slice(-1, None))
+    )
+    partial, first, last = lax.optimization_barrier((partial, first, last))
+    left, right = edges(first, last, "gx")
+
+    if not fits:
         spectral = split_pair_spectral(flow, spectral_weight)
-        left, right = edges(flow[:1], flow[-1:], "gx")
-        convolved = convolve(own_y, flow, left, right, conv_weight).astype(jnp.float32)
+        convolved = beside_planes(left[0], right[0], kernel, partial).astype(jnp.float32)
         return jax.nn.gelu(spectral + convolved + bias, approximate=True).astype(jnp.bfloat16)
-    sizes = (shards_x, shards_y, pairs, cells_y, cells_z)
+
+    rows, partial = lax.optimization_barrier((rows, partial))
     full_x = cells_x * shards_x
-
-    table = jnp.asarray(forward_yz_table(*sizes))
-    columns = flow.reshape(cells_x, cells_y * cells_z, channels)
-    arrived = []
-    first = last = None
-    for step in range(1, shards_y):
-        sent, *layers = forward_yz(own_y, table, columns, step, shards_x, edges=step == 1)
-        arrived.append(lax.ppermute(sent, "gy", shifted(shards_y, step)))
-        if layers:
-            first, last = (layer.reshape(1, cells_y, cells_z, channels) for layer in layers)
-    left, right = edges(first, last, "gx")
-    arrived, left, right = lax.optimization_barrier((arrived, left, right))
-    (total,) = forward_yz(own_y, table, columns, 0, shards_x, arrived)
-    rows = lax.all_to_all(total, "gx", 0, 0, tiled=True)
-
-    convolved = convolve(own_y, flow, left, right, conv_weight)
-    rows, convolved = lax.optimization_barrier((rows, convolved))
-
     returned = mixing(
-        rows.reshape(full_x * 2 * pairs, channels),
+        rows.reshape(shards_y, full_x * 2 * pairs, channels),
         jnp.asarray(forward_x_table(full_x)),
         jnp.asarray(backward_x_table(full_x)),
         spectral_weight.reshape(items, MX, channels, channels),
     )
-    returned = returned.reshape(shards_x, cells_x, 2 * pairs, channels)
-    returned = lax.all_to_all(returned, "gx", 0, 0, tiled=True)
-    coefficients = [returned] + [
-        lax.ppermute(returned, "gy", shifted(shards_y, step)) for step in range(1, shards_y)
-    ]
+    returned, left, right = lax.optimization_barrier((returned, left, right))
+    convolved = beside_planes(left[0], right[0], kernel, partial)
+    returned = returned.reshape(shards_y * shards_x, cells_x, 2 * pairs, channels)
+    returned = lax.all_to_all(returned, axes, 0, 0, tiled=True)
     return final(
         own_y,
         jnp.asarray(backward_yz_table(*sizes)),
-        coefficients,
+        returned,
         convolved,
         bias.reshape(1, channels),
     )

time: 74.6 us -> 71.5 us (0.958)
  blocking collectives: 15.3 us -> 0 us
  local copies, waits for them, and re-layouts: 1.97 us -> 8.63 us
  starting transfers between devices: 15.9 us -> 21.1 us
  between operations: 0.1 us -> 1.6 us
  waiting for transfers between devices: 12.6 us -> 11.2 us
  Pallas kernels: 27.4 us -> 28.2 us
    all_to_all x1 -> x0, blocking collectives: 15.3 us -> none  [body(): returned = lax.all_to_all(returned, 'gx', 0, 0, tiled=True)]
    ppermute x2 -> x0, waiting for transfers between devices: 12.1 us -> none  [the longest x1 6.55 us: body(): lax.ppermute(returned, 'gy', shifted(shards_y, step))]
    all_to_all x1 -> x2, starting transfers between devices: 5.32 us -> 16.7 us  [the longest x1 9.39 us: body(): returned = lax.all_to_all(returned, axes, 0, 0, tiled=True)]
    all_to_all x1 -> x2, waiting for transfers between devices: 0.55 us -> 8.43 us  [the longest x1 8.43 us: body(): returned = lax.all_to_all(returned, axes, 0, 0, tiled=True)]
    unnamed x14 -> x28, local copies, waits for them, and re-layouts: 1.18 us -> 7.07 us
    ppermute x2 -> x0, starting transfers between devices: 3.87 us -> none  [the longest x1 2.35 us: body(): arrived.append(lax.ppermute(sent, 'gy', shifted(shards_y, step)))]
    ppermute x1, waiting for transfers between devices: 0.01 us -> 2.81 us  [edges(): arrived = lax.ppermute(facing, axis, [(0, 1), (1, 0)])]
    ppermute x2, starting transfers between devices: 4.33 us -> 2.59 us  [edges(): return (lax.ppermute(last, axis, up), lax.ppermute(first, axis, down))]
  transfers between devices with their start and end apart: 6 -> 5, of which waited for: 3 -> 2; matrix products, arithmetic and copies ran while one was open for 0% -> 1% of each run, Pallas kernels for 13% -> 31%
where the time goes in v3:
time: 71.5 us; the launch traced here: 71 us
  Pallas kernels  28.2 us (39%)
  starting transfers between devices  21.1 us (30%)
  waiting for transfers between devices  11.2 us (16%)
  local copies, waits for them, and re-layouts  8.63 us (12%)
  between operations  1.6 us (2%)
    pallas_call x1, Pallas kernels, mixing(): pl.pallas_call(mixing_kernel, in_specs=[vmem, vmem, vmem, pl.BlockSpec(me...  12.7 us
    all_to_all x1, starting transfers between devices, body(): returned = lax.all_to_all(returned, axes, 0, 0, tiled=True)  9.39 us
    all_to_all x1, waiting for transfers between devices, body(): returned = lax.all_to_all(returned, axes, 0, 0, tiled=True)  8.43 us
    all_to_all x1, starting transfers between devices, body(): rows = lax.all_to_all(sent, axes, 0, 0, tiled=True)  7.3 us
    unnamed x28, local copies, waits for them, and re-layouts  7.07 us
    pallas_call x1, Pallas kernels, own_planes(): pl.pallas_call(own_planes_kernel, in_specs=[pl.BlockSpec(memory_space=plt...  6.61 us
    pallas_call x1, Pallas kernels, forward_yz(): pl.pallas_call(forward_kernel, grid_spec=pltpu.PrefetchScalarGridSpec(num...  3.09 us
    pallas_call x1, Pallas kernels, beside_planes(): pl.pallas_call(beside_planes_kernel, in_specs=[vmem] * 4, out_specs=vmem,...  2.96 us
  transfers between devices with their start and end apart: 5, of which 2 were waited for; matrix products, arithmetic and copies ran while one was open for 1% of the time, Pallas kernels for 31%

profile of v3, /device:TPU:0, one launch (start us, length us, event | category | flops | bytes accessed | tf_op | source)
XLA Modules:
  0.0 71.0 jit_solution(11140621362325232078)
XLA Ops:
  0.0 0.9 %fusion.1 = (bf16[4,1,64,128]{3,2,1,0:T(8,128)(2,1)S(1)}, bf16[4,1,64,128]{3,2,1,0:T(8,128)(2,1)S(1)}) fusion(bf16[4,16,64,128]{3,2,1,0:T(8,128)(2,1)} %flow_ref.1), kind=kLoop, calls=%fused_computation.9 | loop fusion | bytes 262144 | tf_op jit(solution)/shard_map/slice | solution.py:535
  0.9 0.0 copy-start
  0.9 3.1 %shard_map.82 = bf16[2,16,4,16,128]{4,3,2,1,0:T(8,128)(2,1)} custom-call(s32[1]{0:T(128)} %bitcast.own_ref, bf16[2,512,1024]{2,1,0:T(8,128)(2,1)} %constant.22.clone.table_ref, bf16[4,1024,128]{2,1,0:T(8,128)(2,1)} %bitcast.12), custom_call_target="tpu_custom_call" | custom-call | flops 536870912 | bytes 2097152 | tf_op jit(solution)/shard_map/pallas_call | solution.py:107
  4.0 0.0 copy-start.7
  4.0 7.3 %all-to-all-start = ((bf16[32,4,16,128]{3,2,1,0:T(8,128)(2,1)}), bf16[32,4,16,128]{3,2,1,0:T(8,128)(2,1)S(1)}, u32[]{:S(2)}, u32[]{:S(2)}) async-start(bf16[32,4,16,128]{3,2,1,0:T(8,128)(2,1)} %bitcast.20), calls=%async_computation | async-start | bytes 1048576 | tf_op jit(solution)/shard_map/all_to_all | solution.py:538
  11.3 1.8 %collective-permute-start = (bf16[4,1,64,128]{3,2,1,0:T(8,128)(2,1)S(1)}, bf16[4,1,64,128]{3,2,1,0:T(8,128)(2,1)S(1)}, u32[]{:S(2)}, u32[]{:S(2)}) collective-permute-start(bf16[4,1,64,128]{3,2,1,0:T(8,128)(2,1)S(1)} %broadcast_select_fusion), channel_id=1, source_target_pairs={{0,1},{1,0},{2,3},{3,2},{4,5},{5,4},{6,7},{7,6},{8,9},{9,8},{10,11... | collective-permute-start | bytes 196616 | tf_op jit(solution)/shard_map/ppermute | solution.py:506
  13.2 0.0 copy-done
  13.2 0.1 add_convert_fusion.flags_ref
  13.3 0.6 fusion.2
  15.3 2.8 %collective-permute-done.front_ref.back_ref = bf16[4,1,64,128]{3,2,1,0:T(8,128)(2,1)S(1)} collective-permute-done((bf16[4,1,64,128]{3,2,1,0:T(8,128)(2,1)S(1)}, bf16[4,1,64,128]{3,2,1,0:T(8,128)(2,1)S(1)}, u32[]{:S(2)}, u32[]{:S(2)}) %collective-permute-start) | collective-permute-done | bytes 65568 | tf_op jit(solution)/shard_map/ppermute | solution.py:506
  18.1 0.1 pad_maximum_fusion
  18.2 0.0 copy-done.7
  18.2 0.0 copy-start.4
  18.2 0.0 copy-start.5
  18.2 6.6 %shard_map.83.partial_ref = f32[4,16,64,128]{3,2,1,0:T(8,128)S(1)} custom-call(s32[2]{0:T(128)S(1)} %add_convert_fusion.flags_ref, bf16[4,16,64,128]{3,2,1,0:T(8,128)(2,1)S(1)} %copy-done, bf16[4,1,64,128]{3,2,1,0:T(8,128)(2,1)S(1)} %collective-permute-done.front_ref.back_ref, bf16[4,1,64,128]{3,2,1,0:T(8,128)(2,1)S(1)} %collective-permute-done.front_ref.back_ref, ...), custom_call_target="tpu_custom_call" | custom-call | flops 7247757312 | bytes 3145728 | tf_op jit(solution)/shard_map/pallas_call | solution.py:387
  24.9 0.0 copy-start.12
  24.9 1.3 %copy-done.12 = f32[4,16,64,128]{3,2,1,0:T(8,128)} copy-done((f32[4,16,64,128]{3,2,1,0:T(8,128)}, f32[4,16,64,128]{3,2,1,0:T(8,128)S(1)}, u32[]{:S(2)}) %copy-start.12) | copy-done | bytes 2097176
  26.2 1.3 %collective-permute-start.1 = (bf16[1,18,64,128]{3,2,1,0:T(8,128)(2,1)S(1)}, bf16[1,18,64,128]{3,2,1,0:T(8,128)(2,1)S(1)}, u32[]{:S(2)}, u32[]{:S(2)}) collective-permute-start(bf16[1,18,64,128]{3,2,1,0:T(8,128)(2,1)S(1)} %get-tuple-element.21), channel_id=1, source_target_pairs={{0,2},{2,4},{4,6},{6,8},{8,10},{10,12},{12,14},{14,16},{16,18},{18... | collective-permute-start | bytes 884744 | tf_op jit(solution)/shard_map/ppermute | solution.py:510
  27.5 1.3 %collective-permute-start.2 = (bf16[1,18,64,128]{3,2,1,0:T(8,128)(2,1)S(1)}, bf16[1,18,64,128]{3,2,1,0:T(8,128)(2,1)S(1)}, u32[]{:S(2)}, u32[]{:S(2)}) collective-permute-start(bf16[1,18,64,128]{3,2,1,0:T(8,128)(2,1)S(1)} %get-tuple-element.22), channel_id=1, source_target_pairs={{2,0},{4,2},{6,4},{8,6},{10,8},{12,10},{14,12},{16,14},{18,16},{20... | collective-permute-start | bytes 884744 | tf_op jit(solution)/shard_map/ppermute | solution.py:510
  28.8 0.0 all-to-all-done
  28.8 0.0 copy-done.4
  28.8 0.0 copy-done.5
  28.8 12.7 %shard_map.84 = bf16[2,1024,128]{2,1,0:T(8,128)(2,1)} custom-call(bf16[2,1024,128]{2,1,0:T(8,128)(2,1)S(1)} %bitcast.13, bf16[256,128]{1,0:T(8,128)(2,1)S(1)} %copy-done.4, bf16[128,128]{1,0:T(8,128)(2,1)S(1)} %copy-done.5, bf16[16,64,128,128]{3,2,1,0:T(8,128)(2,1)} %bitcast.19), custom_call_target="tpu_custom_call" | custom-call | flops 134217728 | bytes 33554432 | tf_op jit(solution)/shard_map/pallas_call | solution.py:209
  41.5 0.0 collective-permute-done.1
  41.5 0.0 copy-start.8
  41.5 0.0 collective-permute-done.2
  41.6 0.0 copy-start.10
  41.6 9.4 %all-to-all-start.1 = ((bf16[32,4,16,128]{3,2,1,0:T(8,128)(2,1)}), bf16[32,4,16,128]{3,2,1,0:T(8,128)(2,1)S(1)}, u32[]{:S(2)}, u32[]{:S(2)}) async-start(bf16[32,4,16,128]{3,2,1,0:T(8,128)(2,1)} %bitcast.8), calls=%async_computation.1 | async-start | bytes 1048576 | tf_op jit(solution)/shard_map/all_to_all | solution.py:563
  51.0 0.0 copy-done.8
  51.0 0.0 copy-done.10
  51.0 0.0 copy-start.9
  51.0 1.0 %copy-done.9 = bf16[1,18,64,128]{3,2,1,0:T(8,128)(2,1)S(1)} copy-done((bf16[1,18,64,128]{3,2,1,0:T(8,128)(2,1)S(1)}, bf16[1,18,64,128]{3,2,1,0:T(8,128)(2,1)}, u32[]{:S(2)}) %copy-start.9) | copy-done | bytes 294936
  51.9 0.0 copy-start.11
  52.0 1.0 %copy-done.11 = bf16[1,18,64,128]{3,2,1,0:T(8,128)(2,1)S(1)} copy-done((bf16[1,18,64,128]{3,2,1,0:T(8,128)(2,1)S(1)}, bf16[1,18,64,128]{3,2,1,0:T(8,128)(2,1)}, u32[]{:S(2)}) %copy-start.11) | copy-done | bytes 294936
  52.9 0.0 copy-start.13
  52.9 1.6 %copy-done.13 = f32[4,16,64,128]{3,2,1,0:T(8,128)S(1)} copy-done((f32[4,16,64,128]{3,2,1,0:T(8,128)S(1)}, f32[4,16,64,128]{3,2,1,0:T(8,128)}, u32[]{:S(2)}) %copy-start.13) | copy-done | bytes 2097176
  54.5 0.0 copy-start.1
  54.5 0.0 copy-start.6
  54.5 3.0 %shard_map.85.convolved_ref = bf16[4,16,64,128]{3,2,1,0:T(8,128)(2,1)S(1)} custom-call(bf16[18,64,128]{2,1,0:T(8,128)(2,1)S(1)} %bitcast.17, bf16[18,64,128]{2,1,0:T(8,128)(2,1)S(1)} %bitcast.18, bf16[3,3,384,128]{3,2,1,0:T(8,128)(2,1)S(1)} %bitcast.16, f32[4,16,64,128]{3,2,1,0:T(8,128)S(1)} %copy-done.13), custom_call_target="tpu_custom_call" | custom-call | flops 3623878656 | bytes 3145728 | tf_op jit(solution)/shard_map/pallas_call | solution.py:405
  57.5 0.0 copy-start.2
  57.5 1.0 %copy-done.2 = bf16[4,16,64,128]{3,2,1,0:T(8,128)(2,1)} copy-done((bf16[4,16,64,128]{3,2,1,0:T(8,128)(2,1)}, bf16[4,16,64,128]{3,2,1,0:T(8,128)(2,1)S(1)}, u32[]{:S(2)}) %copy-start.2) | copy-done | bytes 1048600
  58.4 8.4 %all-to-all-done.1.coefficient_ref = bf16[32,4,16,128]{3,2,1,0:T(8,128)(2,1)S(1)} async-done(((bf16[32,4,16,128]{3,2,1,0:T(8,128)(2,1)}), bf16[32,4,16,128]{3,2,1,0:T(8,128)(2,1)S(1)}, u32[]{:S(2)}, u32[]{:S(2)}) %all-to-all-start.1) | async-done | bytes 524320 | tf_op jit(solution)/shard_map/all_to_all | solution.py:563
  66.9 0.0 copy-done.1
  66.9 0.0 copy-done.6
  66.9 0.0 copy-start.3
  66.9 1.2 %copy-done.3 = bf16[4,16,64,128]{3,2,1,0:T(8,128)(2,1)S(1)} copy-done((bf16[4,16,64,128]{3,2,1,0:T(8,128)(2,1)S(1)}, bf16[4,16,64,128]{3,2,1,0:T(8,128)(2,1)}, u32[]{:S(2)}) %copy-start.3) | copy-done | bytes 1048600
  68.1 2.9 %shard_map.86 = bf16[4,16,64,128]{3,2,1,0:T(8,128)(2,1)} custom-call(s32[1]{0:T(128)} %bitcast.own_ref, bf16[2,1024,512]{2,1,0:T(8,128)(2,1)S(1)} %copy-done.1, bf16[32,4,16,128]{3,2,1,0:T(8,128)(2,1)S(1)} %all-to-all-done.1.coefficient_ref, bf16[4,16,64,128]{3,2,1,0:T(8,128)(2,1)S(1)} %copy-done.3, f32[1,128]{1,0:T(1,128)S(1)} %bitcast.14), custom_call_target="tpu_custom_call" | custom-call | flops 536870912 | bytes 3145728 | tf_op jit(solution)/shard_map/pallas_call | solution.py:249
  (3 shorter events, 0.1 us)
Async XLA Ops:
  0.9 12.3 %copy-start = (bf16[4,16,64,128]{3,2,1,0:T(8,128)(2,1)S(1)}, bf16[4,16,64,128]{3,2,1,0:T(8,128)(2,1)}, u32[]{:S(2)}) copy-start(bf16[4,16,64,128]{3,2,1,0:T(8,128)(2,1)} %flow_ref.1) | copy-start | bytes 3145732
  4.0 14.2 %copy-start.7 = (bf16[3,3,3,128,128]{4,3,2,1,0:T(8,128)(2,1)S(1)}, bf16[3,3,3,128,128]{4,3,2,1,0:T(8,128)(2,1)}, u32[]{:S(2)}) copy-start(bf16[3,3,3,128,128]{4,3,2,1,0:T(8,128)(2,1)} %param.10) | copy-start | bytes 2654212
  4.0 24.8 %all-to-all-start = ((bf16[32,4,16,128]{3,2,1,0:T(8,128)(2,1)}), bf16[32,4,16,128]{3,2,1,0:T(8,128)(2,1)S(1)}, u32[]{:S(2)}, u32[]{:S(2)}) async-start(bf16[32,4,16,128]{3,2,1,0:T(8,128)(2,1)} %bitcast.20), calls=%async_computation | async-start | bytes 1048576 | tf_op jit(solution)/shard_map/all_to_all | solution.py:538
  11.3 6.8 %collective-permute-start = (bf16[4,1,64,128]{3,2,1,0:T(8,128)(2,1)S(1)}, bf16[4,1,64,128]{3,2,1,0:T(8,128)(2,1)S(1)}, u32[]{:S(2)}, u32[]{:S(2)}) collective-permute-start(bf16[4,1,64,128]{3,2,1,0:T(8,128)(2,1)S(1)} %broadcast_select_fusion), channel_id=1, source_target_pairs={{0,1},{1,0},{2,3},{3,2},{4,5},{5,4},{6,7},{7,6},{8,9},{9,8},{10,11... | collective-permute-start | bytes 196616 | tf_op jit(solution)/shard_map/ppermute | solution.py:506
  18.2 10.6 %copy-start.4 = (bf16[256,128]{1,0:T(8,128)(2,1)S(1)}, bf16[256,128]{1,0:T(8,128)(2,1)}, u32[]{:S(2)}) copy-start(bf16[256,128]{1,0:T(8,128)(2,1)} %constant.23.clone.forward_ref) | copy-start | bytes 196612
  18.2 10.6 %copy-start.5 = (bf16[128,128]{1,0:T(8,128)(2,1)S(1)}, bf16[128,128]{1,0:T(8,128)(2,1)}, u32[]{:S(2)}) copy-start(bf16[128,128]{1,0:T(8,128)(2,1)} %constant.24.clone.backward_ref) | copy-start | bytes 98308
  24.9 1.3 %copy-start.12 = (f32[4,16,64,128]{3,2,1,0:T(8,128)}, f32[4,16,64,128]{3,2,1,0:T(8,128)S(1)}, u32[]{:S(2)}) copy-start(f32[4,16,64,128]{3,2,1,0:T(8,128)S(1)} %shard_map.83.partial_ref) | copy-start | bytes 6291460
  26.2 15.3 %collective-permute-start.1 = (bf16[1,18,64,128]{3,2,1,0:T(8,128)(2,1)S(1)}, bf16[1,18,64,128]{3,2,1,0:T(8,128)(2,1)S(1)}, u32[]{:S(2)}, u32[]{:S(2)}) collective-permute-start(bf16[1,18,64,128]{3,2,1,0:T(8,128)(2,1)S(1)} %get-tuple-element.21), channel_id=1, source_target_pairs={{0,2},{2,4},{4,6},{6,8},{8,10},{10,12},{12,14},{14,16},{16,18},{18... | collective-permute-start | bytes 884744 | tf_op jit(solution)/shard_map/ppermute | solution.py:510
  27.5 14.0 %collective-permute-start.2 = (bf16[1,18,64,128]{3,2,1,0:T(8,128)(2,1)S(1)}, bf16[1,18,64,128]{3,2,1,0:T(8,128)(2,1)S(1)}, u32[]{:S(2)}, u32[]{:S(2)}) collective-permute-start(bf16[1,18,64,128]{3,2,1,0:T(8,128)(2,1)S(1)} %get-tuple-element.22), channel_id=1, source_target_pairs={{2,0},{4,2},{6,4},{8,6},{10,8},{12,10},{14,12},{16,14},{18,16},{20... | collective-permute-start | bytes 884744 | tf_op jit(solution)/shard_map/ppermute | solution.py:510
  41.5 9.4 %copy-start.8 = (bf16[1,18,64,128]{3,2,1,0:T(8,128)(2,1)}, bf16[1,18,64,128]{3,2,1,0:T(8,128)(2,1)S(1)}, u32[]{:S(2)}) copy-start(bf16[1,18,64,128]{3,2,1,0:T(8,128)(2,1)S(1)} %collective-permute-done.1) | copy-start | bytes 884740
  41.6 9.4 %copy-start.10 = (bf16[1,18,64,128]{3,2,1,0:T(8,128)(2,1)}, bf16[1,18,64,128]{3,2,1,0:T(8,128)(2,1)S(1)}, u32[]{:S(2)}) copy-start(bf16[1,18,64,128]{3,2,1,0:T(8,128)(2,1)S(1)} %collective-permute-done.2) | copy-start | bytes 884740
  41.6 25.3 %all-to-all-start.1 = ((bf16[32,4,16,128]{3,2,1,0:T(8,128)(2,1)}), bf16[32,4,16,128]{3,2,1,0:T(8,128)(2,1)S(1)}, u32[]{:S(2)}, u32[]{:S(2)}) async-start(bf16[32,4,16,128]{3,2,1,0:T(8,128)(2,1)} %bitcast.8), calls=%async_computation.1 | async-start | bytes 1048576 | tf_op jit(solution)/shard_map/all_to_all | solution.py:563
  51.0 1.0 %copy-start.9 = (bf16[1,18,64,128]{3,2,1,0:T(8,128)(2,1)S(1)}, bf16[1,18,64,128]{3,2,1,0:T(8,128)(2,1)}, u32[]{:S(2)}) copy-start(bf16[1,18,64,128]{3,2,1,0:T(8,128)(2,1)} %copy-done.8) | copy-start | bytes 884740
  51.9 1.0 %copy-start.11 = (bf16[1,18,64,128]{3,2,1,0:T(8,128)(2,1)S(1)}, bf16[1,18,64,128]{3,2,1,0:T(8,128)(2,1)}, u32[]{:S(2)}) copy-start(bf16[1,18,64,128]{3,2,1,0:T(8,128)(2,1)} %copy-done.10) | copy-start | bytes 884740
  52.9 1.6 %copy-start.13 = (f32[4,16,64,128]{3,2,1,0:T(8,128)S(1)}, f32[4,16,64,128]{3,2,1,0:T(8,128)}, u32[]{:S(2)}) copy-start(f32[4,16,64,128]{3,2,1,0:T(8,128)} %copy-done.12) | copy-start | bytes 6291460
  54.5 12.4 %copy-start.1 = (bf16[2,1024,512]{2,1,0:T(8,128)(2,1)S(1)}, bf16[2,1024,512]{2,1,0:T(8,128)(2,1)}, u32[]{:S(2)}) copy-start(bf16[2,1024,512]{2,1,0:T(8,128)(2,1)} %constant.25.clone.table_ref) | copy-start | bytes 6291460
  54.5 12.4 %copy-start.6 = (f32[128]{0:T(128)S(1)}, f32[128]{0:T(128)}, u32[]{:S(2)}) copy-start(f32[128]{0:T(128)} %param.11) | copy-start | bytes 1540
  57.5 1.0 %copy-start.2 = (bf16[4,16,64,128]{3,2,1,0:T(8,128)(2,1)}, bf16[4,16,64,128]{3,2,1,0:T(8,128)(2,1)S(1)}, u32[]{:S(2)}) copy-start(bf16[4,16,64,128]{3,2,1,0:T(8,128)(2,1)S(1)} %shard_map.85.convolved_ref) | copy-start | bytes 3145732
  66.9 1.2 %copy-start.3 = (bf16[4,16,64,128]{3,2,1,0:T(8,128)(2,1)S(1)}, bf16[4,16,64,128]{3,2,1,0:T(8,128)(2,1)}, u32[]{:S(2)}) copy-start(bf16[4,16,64,128]{3,2,1,0:T(8,128)(2,1)} %copy-done.2) | copy-start | bytes 3145732

commit v4 on v0

--- a/solution.py
+++ b/solution.py
@@ -1,13 +1,541 @@
+import functools
 import math
 
 import jax
 import jax.numpy as jnp
+import numpy as np
 from jax import lax
+from jax.experimental import pallas as pl
+from jax.experimental.pallas import tpu as pltpu
 from jax.sharding import PartitionSpec as P
 
 MX = 64
 MY = 16
 MZ = 16
+
+
+def frequencies(mode_count):
+    position = np.arange(mode_count)
+    return np.where(position < mode_count // 2, position, position - mode_count)
+
+
+def wave(first, second, length, factor):
+    turns = (np.asarray(first)[:, None] * np.asarray(second)[None, :]) % length
+    angles = turns * (2.0 * math.pi / length)
+    return (np.cos(angles) + 1j * np.sin(angles)) * factor
+
+
+def rounded(values):
+    return values.astype(np.float32).astype(jnp.bfloat16).astype(np.float64)
+
+
+def item_modes(shards_x, shards_y, pairs):
+    index = np.arange(shards_y * shards_x * pairs).reshape(shards_y, shards_x, pairs)
+    return index // MZ, index % MZ
+
+
+def forward_yz_table(shards_x, shards_y, pairs, cells_y, cells_z):
+    full_y = shards_y * cells_y
+    turn_z = wave(np.arange(MZ), np.arange(cells_z), cells_z, cells_z**-0.5)
+    turn_z = rounded(turn_z.real) - 1j * rounded(turn_z.imag)
+    turn_y = np.conj(wave(frequencies(MY), np.arange(full_y), full_y, full_y**-0.5))
+    mode_y, mode_z = item_modes(shards_x, shards_y, pairs)
+    table = np.empty((shards_y, shards_y, shards_x, pairs, 2, cells_y, cells_z), np.float32)
+    for own in range(shards_y):
+        rows = turn_y[:, own * cells_y : (own + 1) * cells_y]
+        product = rows[mode_y][..., :, None] * turn_z[mode_z][..., None, :]
+        table[own, :, :, :, 0] = product.real
+        table[own, :, :, :, 1] = product.imag
+    return table.reshape(shards_y, -1, cells_y * cells_z).astype(jnp.bfloat16)
+
+
+def backward_yz_table(shards_x, shards_y, pairs, cells_y, cells_z):
+    full_y = shards_y * cells_y
+    turn_z = wave(np.arange(MZ), np.arange(cells_z), cells_z, MZ**-0.5)
+    turn_z = rounded(turn_z.real) + 1j * rounded(turn_z.imag)
+    turn_y = wave(frequencies(MY), np.arange(full_y), full_y, MY**-0.5)
+    mode_y, mode_z = item_modes(shards_x, shards_y, pairs)
+    table = np.empty((shards_y, cells_y, cells_z, shards_y, shards_x, pairs, 2), np.float32)
+    for own in range(shards_y):
+        rows = turn_y[:, own * cells_y : (own + 1) * cells_y]
+        product = rows[mode_y][..., :, None] * turn_z[mode_z][..., None, :]
+        product = np.moveaxis(product, (3, 4), (0, 1))
+        table[own, ..., 0] = product.real
+        table[own, ..., 1] = -product.imag
+    return table.reshape(shards_y, cells_y * cells_z, -1).astype(jnp.bfloat16)
+
+
+def forward_x_table(full_x):
+    turn = np.conj(wave(frequencies(MX), np.arange(full_x), full_x, full_x**-0.5))
+    parts = np.empty((2, MX, 2, 2, full_x), np.float32)
+    parts[0, :, 0, 0], parts[0, :, 0, 1] = turn.real, -turn.imag
+    parts[0, :, 1, 0], parts[0, :, 1, 1] = turn.imag, turn.real
+    parts[1, :, 0] = -parts[0, :, 1]
+    parts[1, :, 1] = parts[0, :, 0]
+    return parts.reshape(2 * MX * 2, 2 * full_x).astype(jnp.bfloat16)
+
+
+def backward_x_table(full_x):
+    turn = wave(frequencies(MX), np.arange(full_x), full_x, MX**-0.5).T
+    parts = np.empty((2, full_x, MX, 2), np.float32)
+    parts[0, :, :, 0], parts[0, :, :, 1] = turn.real, -turn.imag
+    parts[1, :, :, 0], parts[1, :, :, 1] = turn.imag, turn.real
+    return parts.reshape(2 * full_x, MX * 2).astype(jnp.bfloat16)
+
+
+def dot(left, right):
+    return jnp.dot(left, right, preferred_element_type=jnp.float32)
+
+
+def peer(index, step, count):
+    if count & (count - 1) == 0:
+        return index ^ step
+    return lax.rem(index + step, count)
+
+
+def origin(index, step, count):
+    if count & (count - 1) == 0:
+        return index ^ step
+    return lax.rem(index + (count - step), count)
+
+
+def place(me, shards):
+    outer, inner = shards
+    across = lax.rem(me, outer * inner)
+    return lax.div(me, outer * inner), lax.div(across, inner), lax.rem(across, inner)
+
+
+def in_vmem(count):
+    return [pl.BlockSpec(memory_space=pltpu.VMEM)] * count
+
+
+IN_SMEM = pl.BlockSpec(memory_space=pltpu.SMEM)
+
+
+def forward_kernel(shards, pieces, edges, me_ref, table_ref, flow_ref, *refs):
+    cells_x = flow_ref.shape[0]
+    outer, inner = shards
+    rows, channels = refs[0].shape[-2:]
+    _, own, _ = place(me_ref[0], shards)
+    steps = [step for piece in pieces for step in piece]
+    block = inner * rows
+    table = [
+        table_ref[0, pl.ds(pl.multiple_of(peer(own, step, outer) * block, block), block), :]
+        for step in steps
+    ]
+    table = jnp.concatenate(table, axis=0)
+    width = 2 if cells_x % 2 == 0 else 1
+    for x in range(0, cells_x, width):
+        columns = [flow_ref[x + i] for i in range(width)]
+        result = dot(table, jnp.concatenate(columns, axis=1))
+        for i in range(width):
+            part = result[:, i * channels : (i + 1) * channels]
+            at = 0
+            for ref, piece in zip(refs, pieces):
+                for slot in range(len(piece)):
+                    value = part[at : at + block].reshape(inner, rows, channels)
+                    ref[slot, :, x + i] = value.astype(ref.dtype)
+                    at += block
+    if edges:
+        refs[-2][...] = flow_ref[0]
+        refs[-1][...] = flow_ref[cells_x - 1]
+
+
+def forward_yz(me, table, flow, step, shards, shards_y, pieces, dtype, edges=False):
+    cells_x, positions, channels = flow.shape
+    outer, inner = shards
+    rows = table.shape[1] // shards_y
+    unit = (inner, cells_x, rows // (outer * inner), channels)
+    shapes = [jax.ShapeDtypeStruct((len(piece), *unit), dtype) for piece in pieces]
+    if edges:
+        shapes += [jax.ShapeDtypeStruct((positions, channels), flow.dtype)] * 2
+    whole = lambda dims: pl.BlockSpec(dims, lambda i, me: (0,) * len(dims))
+
+    def owner(i, me):
+        own = lax.div(me[0], outer * inner)
+        return own, lax.rem(own + step, shards_y), 0
+
+    limit = {"vmem_limit_bytes": 24 << 20} if step == 0 else {}
+    return pl.pallas_call(
+        functools.partial(forward_kernel, shards, pieces, edges),
+        grid_spec=pltpu.PrefetchScalarGridSpec(
+            num_scalar_prefetch=1,
+            grid=(1,),
+            in_specs=[pl.BlockSpec((1, rows, positions), owner), whole(flow.shape)],
+            out_specs=[whole(one.shape) for one in shapes],
+        ),
+        out_shape=shapes,
+        compiler_params=pltpu.CompilerParams(**limit),
+        cost_estimate=pl.CostEstimate(
+            flops=2 * rows * positions * cells_x * channels,
+            bytes_accessed=2 * positions * (rows + cells_x * channels),
+            transcendentals=0,
+        ),
+    )(me, table, flow)
+
+
+def add_kernel(count, *refs):
+    out_refs = refs[count:]
+    for slot, out_ref in enumerate(out_refs):
+        total = refs[0][slot]
+        for ref in refs[1:count]:
+            total = total + ref[slot].astype(jnp.float32)
+        out_ref[...] = total.astype(out_ref.dtype)
+
+
+def add_pieces(own, arrived):
+    slots, *unit = own.shape
+    return pl.pallas_call(
+        functools.partial(add_kernel, 1 + len(arrived)),
+        in_specs=in_vmem(1 + len(arrived)),
+        out_specs=in_vmem(slots),
+        out_shape=[jax.ShapeDtypeStruct(unit, jnp.bfloat16)] * slots,
+        cost_estimate=pl.CostEstimate(flops=own.size, bytes_accessed=0, transcendentals=0),
+        compiler_params=pltpu.CompilerParams(vmem_limit_bytes=16 << 20),
+    )(own, *arrived)
+
+
+def regroup_kernel(shards, chosen, me_ref, *refs):
+    _, _, own = place(me_ref[0], shards)
+    count = refs[0].shape[0]
+    in_refs, out_refs = refs[:-count], refs[-count:]
+    for step, out_ref in enumerate(out_refs):
+        at = peer(own, step, count) if chosen else step
+        for slot, in_ref in enumerate(in_refs):
+            out_ref[slot] = in_ref[at]
+
+
+def regroup(me, arrays, shards, chosen):
+    count, *unit = arrays[0].shape
+    return pl.pallas_call(
+        functools.partial(regroup_kernel, shards, chosen),
+        in_specs=[IN_SMEM] + in_vmem(len(arrays)),
+        out_specs=in_vmem(count),
+        out_shape=[jax.ShapeDtypeStruct((len(arrays), *unit), arrays[0].dtype)] * count,
+        cost_estimate=pl.CostEstimate(
+            flops=arrays[0].size, bytes_accessed=0, transcendentals=0
+        ),
+        compiler_params=pltpu.CompilerParams(vmem_limit_bytes=16 << 20),
+    )(me, *arrays)
+
+
+def edge_kernel(me_ref, left_ref, flow_ref, right_ref, out_ref):
+    out_ref[0] = left_ref[0]
+    out_ref[1 : 1 + flow_ref.shape[0]] = flow_ref[...]
+    out_ref[1 + flow_ref.shape[0]] = right_ref[0]
+
+
+def y_edge(me, left, flow, right, per_y, row):
+    cells_x, cells_y, cells_z, channels = flow.shape
+    at = lambda i, me: (0, row(lax.div(me[0], per_y)), 0, 0)
+    shape = (cells_x + 2, 1, cells_z, channels)
+    return pl.pallas_call(
+        edge_kernel,
+        grid_spec=pltpu.PrefetchScalarGridSpec(
+            num_scalar_prefetch=1,
+            grid=(1,),
+            in_specs=[
+                pl.BlockSpec((1, 1, cells_z, channels), at),
+                pl.BlockSpec((cells_x, 1, cells_z, channels), at),
+                pl.BlockSpec((1, 1, cells_z, channels), at),
+            ],
+            out_specs=pl.BlockSpec(shape, lambda i, me: (0, 0, 0, 0)),
+        ),
+        out_shape=jax.ShapeDtypeStruct(shape, flow.dtype),
+    )(me, left, flow, right)
+
+
+def mixing_kernel(shards, shards_y, me_ref, *refs):
+    outer, inner = shards
+    row_refs, refs = refs[:inner], refs[inner:]
+    forward_ref, backward_ref, weight_ref, flow_ref, left_ref, right_ref, *refs = refs
+    front_ref, back_ref, kernel_ref, *refs = refs
+    out_refs, refs = refs[:inner], refs[inner:]
+    convolved_ref, held, sems, wide, left, mixed, stacked = refs
+
+    slots, _, modes, _, channels = held.shape
+    _, cells_x, item_rows, _ = row_refs[0].shape
+    cells_y, cells_z = flow_ref.shape[1:3]
+    pairs = item_rows // 2
+    full_x = outer * inner * cells_x
+    half = channels // 2
+    span = 2 * MX
+    block = cells_x * item_rows
+    own_y, own_outer, own_inner = place(me_ref[0], shards)
+
+    def copy(pair):
+        slot = lax.rem(pair, slots)
+        return pltpu.make_async_copy(
+            weight_ref.at[pl.ds(2 * pair, 2)], held.at[slot], sems.at[slot]
+        )
+
+    for pair in range(min(slots - 1, pairs)):
+        copy(pair).start()
+
+    def rows_of(outer_index, inner_index):
+        start = pl.multiple_of((outer_index * inner + inner_index) * block, block)
+        return pl.ds(start, block)
+
+    for step in range(inner):
+        source = origin(own_inner, step, inner)
+        for slot in range(outer):
+            value = row_refs[step][slot].reshape(block, channels)
+            at = rows_of(origin(own_outer, slot, outer), source)
+            wide[at, :] = value.astype(jnp.float32)
+    low = lax.broadcasted_iota(jnp.int32, (span, channels), 1) < half
+    for pair in range(pairs):
+        columns = [wide[pl.ds(2 * pair + p, full_x, stride=item_rows), :] for p in range(2)]
+        columns = jnp.concatenate(columns, axis=0).astype(jnp.bfloat16)
+        both = dot(forward_ref[...], columns)
+        value, turned = both[:span], both[span:]
+        first = jnp.where(low, value, pltpu.roll(turned, half, axis=1))
+        second = jnp.where(low, pltpu.roll(value, half, axis=1), turned)
+        left[pl.ds(pair * span, span), :channels] = first.astype(left.dtype)
+        left[pl.ds(pair * span, span), channels:] = second.astype(left.dtype)
+
+    group = 16
+    row = lax.broadcasted_iota(jnp.int32, (group, channels), 0) // 2
+
+    def mix(pair, slot):
+        for step in range(span // group):
+            start = pl.multiple_of(pair * span + step * group, group)
+            lhs = left[pl.ds(start, group), :]
+            gathered = jnp.zeros((group, channels), jnp.float32)
+            for i in range(0, group // 2, 2):
+                mode = step * (group // 2) + i
+                tiles = [
+                    jnp.concatenate([held[slot, 0, mode + k], held[slot, 1, mode + k]], axis=0)
+                    for k in range(2)
+                ]
+                product = dot(lhs, jnp.concatenate(tiles, axis=1))
+                for k in range(2):
+                    gathered = jnp.where(
+                        row == i + k, product[:, k * channels : (k + 1) * channels], gathered
+                    )
+            mixed[pl.ds(start, group), :] = gathered.astype(mixed.dtype)
+
+    width = 2 if cells_x % 2 == 0 else 1
+    rows = stacked.shape[1] - 2
+    y_units = cells_y // rows
+    units = cells_x // width * y_units
+
+    def stack(plane, at, cells):
+        deep = cells.astype(jnp.float32)
+        z = lax.broadcasted_iota(jnp.int32, deep.shape, 1)
+        before = jnp.where(z == 0, 0.0, pltpu.roll(deep, 1, axis=1))
+        after = jnp.where(z == cells_z - 1, 0.0, pltpu.roll(deep, cells_z - 1, axis=1))
+        at = pl.ds(at, cells.shape[0])
+        stacked[plane, at, :, :channels] = before.astype(stacked.dtype)
+        stacked[plane, at, :, channels : 2 * channels] = cells
+        stacked[plane, at, :, 2 * channels :] = after.astype(stacked.dtype)
+
+    def stack_unit(unit):
+        x, y = lax.div(unit, y_units) * width, lax.rem(unit, y_units) * rows
+        for plane in range(width + 2):
+            source = x + plane - 1
+
+            def fill(inside, low_edge, high_edge, plane=plane):
+                stack(plane, 1, inside(pl.ds(y, rows)))
+
+                @pl.when(y > 0)
+                def _():
+                    stack(plane, 0, inside(pl.ds(y - 1, 1)))
+
+                @pl.when(y == 0)
+                def _():
+                    edge = low_edge()
+                    stack(plane, 0, jnp.where(own_y > 0, edge, jnp.zeros_like(edge)))
+
+                @pl.when(y + rows < cells_y)
+                def _():
+                    stack(plane, rows + 1, inside(pl.ds(y + rows, 1)))
+
+                @pl.when(y + rows == cells_y)
+                def _():
+                    edge = high_edge()
+                    last = own_y == shards_y - 1
+                    stack(plane, rows + 1, jnp.where(last, jnp.zeros_like(edge), edge))
+
+            edges = (lambda: front_ref[source + 1], lambda: back_ref[source + 1])
+            if plane == 0:
+
+                @pl.when(source < 0)
+                def _():
+                    fill(lambda at: left_ref[0, at], *edges)
+
+            if plane == width + 1:
+
+                @pl.when(source == cells_x)
+                def _():
+                    fill(lambda at: right_ref[0, at], *edges)
+
+            @pl.when(jnp.logical_and(source >= 0, source < cells_x))
+            def _():
+                inside = jnp.clip(source, 0, cells_x - 1)
+                fill(lambda at: flow_ref[inside, at], *edges)
+
+    none = jnp.zeros(kernel_ref.shape[2:], kernel_ref.dtype)
+    taps = [(a, b) for a in range(width + 2) for b in range(3)]
+
+    def convolve_unit(unit):
+        x, y = lax.div(unit, y_units) * width, lax.rem(unit, y_units) * rows
+        total = jnp.zeros((rows * cells_z, width * channels), jnp.float32)
+        for i in range(0, len(taps), 2):
+            blocks, kernels = [], []
+            for a, b in taps[i : i + 2]:
+                part = stacked[a, pl.ds(b, rows)]
+                blocks.append(part.reshape(rows * cells_z, 3 * channels))
+                parts = [kernel_ref[a - k, b] if 0 <= a - k < 3 else none for k in range(width)]
+                kernels.append(jnp.concatenate(parts, axis=1))
+            total = total + dot(jnp.concatenate(blocks, axis=1), jnp.concatenate(kernels, axis=0))
+        for k in range(width):
+            part = total[:, k * channels : (k + 1) * channels].reshape(rows, cells_z, channels)
+            convolved_ref[x + k, pl.ds(y, rows)] = part.astype(convolved_ref.dtype)
+
+    def both(pair, carry):
+        stack_unit(pair)
+
+        @pl.when(pair + slots - 1 < pairs)
+        def _():
+            copy(pair + slots - 1).start()
+
+        copy(pair).wait()
+        convolve_unit(pair)
+        mix(pair, lax.rem(pair, slots))
+        return carry
+
+    shared = min(units, pairs)
+    lax.fori_loop(0, shared, both, 0)
+
+    def only_mix(pair, carry):
+        @pl.when(pair + slots - 1 < pairs)
+        def _():
+            copy(pair + slots - 1).start()
+
+        copy(pair).wait()
+        mix(pair, lax.rem(pair, slots))
+        return carry
+
+    def only_convolve(unit, carry):
+        stack_unit(unit)
+        convolve_unit(unit)
+        return carry
+
+    if shared < pairs:
+        lax.fori_loop(shared, pairs, only_mix, 0)
+    if shared < units:
+        lax.fori_loop(shared, units, only_convolve, 0)
+
+    for pair in range(pairs):
+        result = dot(backward_ref[...], mixed[pl.ds(pair * span, span), :])
+        for p in range(2):
+            wide[pl.ds(2 * pair + p, full_x, stride=item_rows), :] = result[
+                p * full_x : (p + 1) * full_x
+            ]
+    for step in range(inner):
+        target = peer(own_inner, step, inner)
+        for slot in range(outer):
+            value = wide[rows_of(peer(own_outer, slot, outer), target), :]
+            value = value.reshape(cells_x, item_rows, channels)
+            out_refs[step][slot] = value.astype(out_refs[step].dtype)
+
+
+def mixing(me, rows, forward_x, backward_x, weight, halos, kernel, shards, shards_y):
+    outer, inner = shards
+    _, cells_x, item_rows, channels = rows[0].shape
+    depth = weight.shape[2]
+    flow = halos[0]
+    _, cells_y, cells_z, _ = flow.shape
+    pairs = item_rows // 2
+    row_count = outer * inner * cells_x * item_rows
+    slots = 3
+    y_rows = 4 if cells_y % 4 == 0 else 1
+    width = 2 if cells_x % 2 == 0 else 1
+    return pl.pallas_call(
+        functools.partial(mixing_kernel, shards, shards_y),
+        in_specs=[IN_SMEM]
+        + in_vmem(inner + 2)
+        + [pl.BlockSpec(memory_space=pl.ANY)]
+        + in_vmem(len(halos) + 1),
+        out_specs=in_vmem(inner + 1),
+        out_shape=[jax.ShapeDtypeStruct(rows[0].shape, jnp.bfloat16)] * inner
+        + [jax.ShapeDtypeStruct(flow.shape, jnp.bfloat16)],
+        scratch_shapes=[
+            pltpu.VMEM((slots, 2, MX, depth, channels), jnp.bfloat16),
+            pltpu.SemaphoreType.DMA((slots,)),
+            pltpu.VMEM((row_count, channels), jnp.float32),
+            pltpu.VMEM((pairs * 2 * MX, 2 * channels), jnp.bfloat16),
+            pltpu.VMEM((pairs * 2 * MX, channels), jnp.bfloat16),
+            pltpu.VMEM((width + 2, y_rows + 2, cells_z, 3 * channels), jnp.bfloat16),
+        ],
+        compiler_params=pltpu.CompilerParams(vmem_limit_bytes=44 << 20),
+        cost_estimate=pl.CostEstimate(
+            flops=8 * weight.size, bytes_accessed=2 * weight.size, transcendentals=0
+        ),
+    )(me, *rows, forward_x, backward_x, weight, *halos, kernel)
+
+
+def final_kernel(shards, shards_y, me_ref, table_ref, *refs):
+    outer, inner = shards
+    *piece_refs, convolved_ref, bias_ref, out_ref, held = refs
+    cells_x, cells_y, cells_z, channels = out_ref.shape
+    own_y, own_outer, own_inner = place(me_ref[0], shards)
+    rows = piece_refs[0].shape[2]
+
+    @pl.when(pl.program_id(0) == 0)
+    def _():
+        for number, ref in enumerate(piece_refs):
+            step, slot = divmod(number, outer)
+            source_y = lax.rem(own_y + (shards_y - step), shards_y)
+            source = source_y * outer + origin(own_outer, slot, outer)
+            for part in range(inner):
+                at = (source * inner + origin(own_inner, part, inner)) * rows
+                for x in range(cells_x):
+                    held[x, pl.ds(pl.multiple_of(at, rows), rows), :] = ref[part, x]
+
+    width = 2 if cells_x % 2 == 0 else 1
+    bias = bias_ref[...]
+    for x in range(0, cells_x, width):
+        columns = [held[x + i] for i in range(width)]
+        total = dot(table_ref[0], jnp.concatenate(columns, axis=1))
+        for i in range(width):
+            spectral = total[:, i * channels : (i + 1) * channels]
+            spectral = spectral.reshape(cells_y, cells_z, channels)
+            value = spectral + convolved_ref[x + i].astype(jnp.float32) + bias
+            out_ref[x + i] = jax.nn.gelu(value, approximate=True).astype(out_ref.dtype)
+
+
+def final(me, table, pieces, convolved, bias, shards, shards_y):
+    cells_x, cells_y, cells_z, channels = convolved.shape
+    parts = 4 if cells_y % 4 == 0 else 1
+    rows = cells_y // parts * cells_z
+    block = (cells_x, cells_y // parts, cells_z, channels)
+    depth = table.shape[2]
+    outer, inner = shards
+    return pl.pallas_call(
+        functools.partial(final_kernel, shards, shards_y),
+        grid_spec=pltpu.PrefetchScalarGridSpec(
+            num_scalar_prefetch=1,
+            grid=(parts,),
+            in_specs=[
+                pl.BlockSpec(
+                    (1, rows, depth), lambda i, me: (lax.div(me[0], outer * inner), i, 0)
+                ),
+                *in_vmem(len(pieces)),
+                pl.BlockSpec(block, lambda i, me: (0, i, 0, 0)),
+                pl.BlockSpec((1, channels), lambda i, me: (0, 0)),
+            ],
+            out_specs=pl.BlockSpec(block, lambda i, me: (0, i, 0, 0)),
+            scratch_shapes=[pltpu.VMEM((cells_x, depth, channels), jnp.bfloat16)],
+        ),
+        out_shape=jax.ShapeDtypeStruct(convolved.shape, jnp.bfloat16),
+        compiler_params=pltpu.CompilerParams(vmem_limit_bytes=24 << 20),
+        cost_estimate=pl.CostEstimate(
+            flops=2 * table.shape[1] * depth * cells_x * channels,
+            bytes_accessed=6 * convolved.size,
+            transcendentals=convolved.size,
+        ),
+    )(me, table, *pieces, convolved, bias)
 
 
 def with_halo(array, sides, width):
@@ -47,7 +575,7 @@
     )
 
 
-def spectral_part(flow_field, spectral_weight):
+def split_pair_spectral(flow_field, spectral_weight):
     highest = lax.Precision.HIGHEST
     cells_x, cells_y, cells_z, channels = flow_field.shape
     count_x = lax.axis_size("gx")
@@ -105,7 +633,7 @@
     return jnp.einsum("pxykc,pkz->xyzc", y_inverse, backward_z, preferred_element_type=jnp.float32)
 
 
-def convolve(flow_field, conv_weight):
+def split_pair_convolve(flow_field, conv_weight):
     cells_x, cells_y, cells_z, channels = flow_field.shape
     padded = with_halo(flow_field, (("gx", 0), ("gy", 1)), 1)
     padded = jnp.pad(padded, ((0, 0), (0, 0), (1, 1), (0, 0)))
@@ -125,10 +653,107 @@
     return accumulated
 
 
-def body(flow_field, spectral_weight, conv_weight, channel_bias):
-    convolved = convolve(flow_field, conv_weight)
-    spectral = spectral_part(flow_field, spectral_weight)
-    return jax.nn.gelu(spectral + convolved + channel_bias, approximate=True).astype(jnp.bfloat16)
+def neighbours(first, last, axis):
+    size = lax.axis_size(axis)
+    up = [(i, i + 1) for i in range(size - 1)]
+    down = [(i + 1, i) for i in range(size - 1)]
+    return lax.ppermute(last, axis, up), lax.ppermute(first, axis, down)
+
+
+def exchange(array, step, shards, along_outer):
+    outer, inner = shards
+    pairs = []
+    for i in range(outer * inner):
+        a, b = divmod(i, inner)
+        count, own = (outer, a) if along_outer else (inner, b)
+        to = own ^ step if count & (count - 1) == 0 else (own + step) % count
+        pairs.append((i, to * inner + b if along_outer else a * inner + to))
+    return lax.ppermute(array, "gx", pairs)
+
+
+def over_y(array, step, shards_y):
+    return lax.ppermute(array, "gy", [(i, (i + step) % shards_y) for i in range(shards_y)])
+
+
+def body(flow, spectral_weight, conv_weight, bias):
+    cells_x, cells_y, cells_z, channels = flow.shape
+    shards_x, shards_y = lax.axis_size("gx"), lax.axis_size("gy")
+    items = spectral_weight.shape[0]
+    pairs = items // 2
+    if items % 2 or shards_y < 2:
+        spectral = split_pair_spectral(flow, spectral_weight)
+        convolved = split_pair_convolve(flow, conv_weight)
+        return jax.nn.gelu(spectral + convolved + bias, approximate=True).astype(jnp.bfloat16)
+
+    inner = max(d for d in range(1, shards_x + 1) if shards_x % d == 0 and d * d <= shards_x)
+    shards = (shards_x // inner, inner)
+    outer = shards[0]
+    me = lax.axis_index(("gy", "gx")).astype(jnp.int32).reshape(1)
+    sizes = (shards_x, shards_y, pairs, cells_y, cells_z)
+    full_x = cells_x * shards_x
+    kernel = conv_weight.reshape(3, 3, 3 * channels, channels)
+
+    table = jnp.asarray(forward_yz_table(*sizes))
+    columns = flow.reshape(cells_x, cells_y * cells_z, channels)
+    order = list(range(outer - 1, -1, -1))
+    cut = (outer + 1) // 2
+    pieces = [piece for piece in (order[:cut], order[cut:]) if piece]
+    arrived = [[] for _ in pieces]
+    for step in range(1, shards_y):
+        sent = forward_yz(me, table, columns, step, shards, shards_y, pieces, jnp.bfloat16)
+        for into, piece in zip(arrived, sent):
+            into.append(over_y(piece, step, shards_y))
+    *kept, first, last = forward_yz(
+        me, table, columns, 0, shards, shards_y, pieces, jnp.float32, edges=True
+    )
+    first, last = (x.reshape(1, cells_y, cells_z, channels) for x in (first, last))
+
+    left, right = neighbours(first, last, "gx")
+    if shards_y == 2:
+        facing = lambda own: jnp.where(own == 0, cells_y - 1, 0)
+        edge = y_edge(me, left, flow, right, shards_x, facing)
+        front = back = over_y(edge, 1, shards_y)
+    else:
+        low = y_edge(me, left, flow, right, shards_x, lambda own: 0)
+        high = y_edge(me, left, flow, right, shards_x, lambda own: cells_y - 1)
+        front, back = neighbours(low, high, "gy")
+
+    by_outer = [None] * outer
+    for piece, own, parts in zip(pieces, kept, arrived):
+        for step, total in zip(piece, add_pieces(own, parts)):
+            by_outer[step] = exchange(total, step, shards, True) if step else total
+    by_inner = regroup(me, by_outer, shards, True)
+    rows = [by_inner[0]] + [exchange(by_inner[s], s, shards, False) for s in range(1, inner)]
+
+    *returned, convolved = mixing(
+        me,
+        rows,
+        jnp.asarray(forward_x_table(full_x)),
+        jnp.asarray(backward_x_table(full_x)),
+        spectral_weight.reshape(items, MX, channels, channels),
+        (flow, left, right, front, back),
+        kernel,
+        shards,
+        shards_y,
+    )
+
+    returned = [returned[0]] + [
+        exchange(returned[s], s, shards, False) for s in range(1, inner)
+    ]
+    returned = regroup(me, returned, shards, False)
+    returned = [returned[0]] + [exchange(returned[s], s, shards, True) for s in range(1, outer)]
+    coefficients = list(returned)
+    for step in range(1, shards_y):
+        coefficients += [over_y(part, step, shards_y) for part in returned]
+    return final(
+        me,
+        jnp.asarray(backward_yz_table(*sizes)),
+        coefficients,
+        convolved,
+        bias.reshape(1, channels),
+        shards,
+        shards_y,
+    )
 
 
 def solution(mesh):

time: 137 us -> 76.4 us (0.56)
  matrix products: 51.1 us -> 0 us
  local copies, waits for them, and re-layouts: 31.7 us -> 6.12 us
  Pallas kernels: 0 us -> 23.5 us
  blocking collectives: 9.67 us -> 0 us
  other arithmetic: 6.95 us -> 0 us
  waiting for transfers between devices: 10.4 us -> 17.2 us
  starting transfers between devices: 26 us -> 29.1 us
    dot_general x16 -> x0, matrix products: 51.1 us -> none  [the longest x9 33 us: convolve(): jnp.dot(stacked[shift_x:shift_x + cells_x, shift_y:shift_y + cells_y], ke...]
    pallas_call x0 -> x9, Pallas kernels: none -> 23.5 us  [the longest x1 15.4 us: mixing(): pl.pallas_call(functools.partial(mixing_kernel, shards, shards_y), in_spe...]
    ppermute x4 -> x21, starting transfers between devices: 5.96 us -> 29.1 us  [the longest x12 17.3 us: exchange(): return lax.ppermute(array, 'gx', pairs)]
    all_to_all x4 -> x0, starting transfers between devices: 20 us -> none  [the longest x1 7.89 us: spectral_part(): lax.all_to_all(owned_modes.astype(jnp.bfloat16), 'gx', split_axis=2, conc...]
    ppermute x4 -> x21, waiting for transfers between devices: 0.01 us -> 17.2 us  [the longest x12 11.1 us: exchange(): return lax.ppermute(array, 'gx', pairs)]
    all_to_all x4 -> x0, waiting for transfers between devices: 10.4 us -> none  [the longest x1 3.73 us: spectral_part(): lax.all_to_all(z_spectrum.astype(jnp.bfloat16), 'gy', split_axis=4, conca...]
    all_gather x1 -> x0, blocking collectives: 9.67 us -> none  [spectral_part(): lax.all_gather(summed.astype(jnp.bfloat16), 'gy', axis=2, tiled=True)]
    unnamed x38 -> x24, local copies, waits for them, and re-layouts: 14.9 us -> 6.12 us
  transfers between devices with their start and end apart: 8 -> 21, of which waited for: 3 -> 10; matrix products, arithmetic and copies ran while one was open for 32% -> 0% of each run, Pallas kernels for 0% -> 5%
where the time goes in v4:
time: 76.4 us; the launch traced here: 76.1 us
  starting transfers between devices  29.1 us (38%)
  Pallas kernels  23.5 us (31%)
  waiting for transfers between devices  17.2 us (23%)
  local copies, waits for them, and re-layouts  6.12 us (8%)
    ppermute x12, starting transfers between devices, exchange(): return lax.ppermute(array, 'gx', pairs)  17.3 us
    pallas_call x1, Pallas kernels, mixing(): pl.pallas_call(functools.partial(mixing_kernel, shards, shards_y), in_spe...  15.4 us
    ppermute x12, waiting for transfers between devices, exchange(): return lax.ppermute(array, 'gx', pairs)  11.1 us
    ppermute x7, starting transfers between devices, over_y(): lax.ppermute(array, 'gy', [(i, (i + step) % shards_y) for i in range(shar...  8.14 us
    unnamed x24, local copies, waits for them, and re-layouts  6.12 us
    ppermute x7, waiting for transfers between devices, over_y(): lax.ppermute(array, 'gy', [(i, (i + step) % shards_y) for i in range(shar...  6.1 us
    ppermute x2, starting transfers between devices, neighbours(): return (lax.ppermute(last, axis, up), lax.ppermute(first, axis, down))  3.65 us
    pallas_call x2, Pallas kernels, forward_yz(): pl.pallas_call(functools.partial(forward_kernel, shards, pieces, edges),...  3.53 us
  transfers between devices with their start and end apart: 21, of which 10 were waited for; matrix products, arithmetic and copies ran while one was open for 0% of the time, Pallas kernels for 5%

profile of v4, /device:TPU:0, one launch (start us, length us, event | category | flops | bytes accessed | tf_op | source)
XLA Modules:
  0.0 76.1 jit_solution(3383922399572795397)
XLA Ops:
  0.0 1.2 %copy-done = bf16[4,16,64,128]{3,2,1,0:T(8,128)(2,1)S(1)} copy-done((bf16[4,16,64,128]{3,2,1,0:T(8,128)(2,1)S(1)}, bf16[4,16,64,128]{3,2,1,0:T(8,128)(2,1)}, u32[]{:S(2)}) %copy-start) | copy-done | bytes 1048600
  1.2 1.6 %copy-done.2 = bf16[2,512,1024]{2,1,0:T(8,128)(2,1)S(1)} copy-done((bf16[2,512,1024]{2,1,0:T(8,128)(2,1)S(1)}, bf16[2,512,1024]{2,1,0:T(8,128)(2,1)}, u32[]{:S(2)}) %copy-start.2) | copy-done | bytes 2097176
  2.8 1.0 %shard_map.82 = (f32[2,4,4,16,128]{4,3,2,1,0:T(8,128)S(1)}, f32[2,4,4,16,128]{4,3,2,1,0:T(8,128)S(1)}, bf16[1024,128]{1,0:T(8,128)(2,1)S(1)}, bf16[1024,128]{1,0:T(8,128)(2,1)}) custom-call(s32[1]{0:T(128)} %bitcast.me_ref, bf16[2,512,1024]{2,1,0:T(8,128)(2,1)S(1)} %copy-done.2, bf16[4,1024,128]{2,1,0:T(8,128)(2,1)S(1)} %bitcast.8), custom_call_target="tpu_custom_call" | custom-call | flops 268435456 | bytes 1572864 | tf_op jit(solution)/shard_map/pallas_call | solution.py:159
  3.8 2.4 %collective-permute-start.8 = (bf16[1,16,64,128]{3,2,1,0:T(8,128)(2,1)}, bf16[1,16,64,128]{3,2,1,0:T(8,128)(2,1)S(1)}, u32[]{:S(2)}, u32[]{:S(2)}) collective-permute-start(bf16[1,16,64,128]{3,2,1,0:T(8,128)(2,1)} %bitcast.3), channel_id=1, source_target_pairs={{0,2},{2,4},{4,6},{6,8},{8,10},{10,12},{12,14},{14,16},{16,18},{18... | collective-permute-start | bytes 786440 | tf_op jit(solution)/shard_map/ppermute | solution.py:660
  6.2 1.3 %collective-permute-start.9 = (bf16[1,16,64,128]{3,2,1,0:T(8,128)(2,1)S(1)}, bf16[1,16,64,128]{3,2,1,0:T(8,128)(2,1)S(1)}, u32[]{:S(2)}, u32[]{:S(2)}) collective-permute-start(bf16[1,16,64,128]{3,2,1,0:T(8,128)(2,1)S(1)} %bitcast.11), channel_id=1, source_target_pairs={{2,0},{4,2},{6,4},{8,6},{10,8},{12,10},{14,12},{16,14},{18,16},{20... | collective-permute-start | bytes 786440 | tf_op jit(solution)/shard_map/ppermute | solution.py:660
  7.5 2.5 %shard_map.83 = (bf16[2,4,4,16,128]{4,3,2,1,0:T(8,128)(2,1)}, bf16[2,4,4,16,128]{4,3,2,1,0:T(8,128)(2,1)}) custom-call(s32[1]{0:T(128)} %bitcast.me_ref, bf16[2,512,1024]{2,1,0:T(8,128)(2,1)} %constant.18.clone.table_ref, bf16[4,1024,128]{2,1,0:T(8,128)(2,1)} %bitcast.7), custom_call_target="tpu_custom_call" | custom-call | flops 268435456 | bytes 1572864 | tf_op jit(solution)/shard_map/pallas_call | solution.py:159
  10.0 2.4 %collective-permute-start.2 = (bf16[2,4,4,16,128]{4,3,2,1,0:T(8,128)(2,1)}, bf16[2,4,4,16,128]{4,3,2,1,0:T(8,128)(2,1)S(1)}, u32[]{:S(2)}, u32[]{:S(2)}) collective-permute-start(bf16[2,4,4,16,128]{4,3,2,1,0:T(8,128)(2,1)} %get-tuple-element.33), channel_id=1, source_target_pairs={{0,1},{1,0},{2,3},{3,2},{4,5},{5,4},{6,7},{7,6},{8,9},{9,8},{10,11... | collective-permute-start | bytes 393224 | tf_op jit(solution)/shard_map/ppermute | solution.py:675
  12.4 0.1 collective-permute-start
  12.5 3.1 %collective-permute-done.2.refs_1_ = bf16[2,4,4,16,128]{4,3,2,1,0:T(8,128)(2,1)S(1)} collective-permute-done((bf16[2,4,4,16,128]{4,3,2,1,0:T(8,128)(2,1)}, bf16[2,4,4,16,128]{4,3,2,1,0:T(8,128)(2,1)S(1)}, u32[]{:S(2)}, u32[]{:S(2)}) %collective-permute-start.2) | collective-permute-done | bytes 131104 | tf_op jit(solution)/shard_map/ppermute | solution.py:675
  15.6 7.4 %collective-permute-start.3 = (bf16[4,4,16,128]{3,2,1,0:T(8,128)(2,1)S(1)}, bf16[4,4,16,128]{3,2,1,0:T(8,128)(2,1)S(1)}, u32[]{:S(2)}, u32[]{:S(2)}) collective-permute-start(bf16[4,4,16,128]{3,2,1,0:T(8,128)(2,1)S(1)} %get-tuple-element.34), channel_id=1, source_target_pairs={{0,16},{2,18},{4,20},{6,22},{8,24},{10,26},{12,28},{14,30},{16,0},... | collective-permute-start | bytes 196616 | tf_op jit(solution)/shard_map/ppermute | solution.py:671
  23.0 1.3 %collective-permute-start.4 = (bf16[4,4,16,128]{3,2,1,0:T(8,128)(2,1)S(1)}, bf16[4,4,16,128]{3,2,1,0:T(8,128)(2,1)S(1)}, u32[]{:S(2)}, u32[]{:S(2)}) collective-permute-start(bf16[4,4,16,128]{3,2,1,0:T(8,128)(2,1)S(1)} %get-tuple-element.35), channel_id=1, source_target_pairs={{0,24},{2,26},{4,28},{6,30},{8,16},{10,18},{12,20},{14,22},{16,8},... | collective-permute-start | bytes 196616 | tf_op jit(solution)/shard_map/ppermute | solution.py:671
  24.4 0.0 collective-permute-done.refs_1_
  24.4 0.3 collective-permute-start.1
  24.7 0.0 collective-permute-done.8.left_ref.refs_8_
  24.7 0.0 collective-permute-done.9.right_ref.refs_9_
  24.7 0.7 copy-done.4
  25.4 0.7 copy-done.6
  26.1 1.5 %shard_map.87 = bf16[6,1,64,128]{3,2,1,0:T(8,128)(2,1)} custom-call(s32[1]{0:T(128)} %bitcast.me_ref, bf16[1,16,64,128]{3,2,1,0:T(8,128)(2,1)} %copy-done.4, bf16[4,16,64,128]{3,2,1,0:T(8,128)(2,1)} %refs_7_.1, bf16[1,16,64,128]{3,2,1,0:T(8,128)(2,1)} %copy-done.6), custom_call_target="tpu_custom_call" | custom-call | tf_op jit(solution)/shard_map/pallas_call | solution.py:232
  27.6 1.5 %collective-permute-start.10 = (bf16[6,1,64,128]{3,2,1,0:T(8,128)(2,1)}, bf16[6,1,64,128]{3,2,1,0:T(8,128)(2,1)S(1)}, u32[]{:S(2)}, u32[]{:S(2)}) collective-permute-start(bf16[6,1,64,128]{3,2,1,0:T(8,128)(2,1)} %shard_map.87), channel_id=1, source_target_pairs={{0,1},{1,0},{2,3},{3,2},{4,5},{5,4},{6,7},{7,6},{8,9},{9,8},{10,11... | collective-permute-start | bytes 294920 | tf_op jit(solution)/shard_map/ppermute | solution.py:675
  29.1 0.1 collective-permute-done.4.refs_3_
  29.2 0.2 collective-permute-done.1.refs_1_
  29.5 0.1 collective-permute-start.5
  29.5 1.3 %collective-permute-start.6 = (bf16[4,4,16,128]{3,2,1,0:T(8,128)(2,1)S(1)}, bf16[4,4,16,128]{3,2,1,0:T(8,128)(2,1)S(1)}, u32[]{:S(2)}, u32[]{:S(2)}) collective-permute-start(bf16[4,4,16,128]{3,2,1,0:T(8,128)(2,1)S(1)} %get-tuple-element.38), channel_id=1, source_target_pairs={{0,4},{2,6},{4,0},{6,2},{8,12},{10,14},{12,8},{14,10},{16,20},{18,... | collective-permute-start | bytes 196616 | tf_op jit(solution)/shard_map/ppermute | solution.py:671
  30.8 0.6 collective-permute-start.7
  31.4 3.0 %collective-permute-done.6.refs_2_ = bf16[4,4,16,128]{3,2,1,0:T(8,128)(2,1)S(1)} collective-permute-done((bf16[4,4,16,128]{3,2,1,0:T(8,128)(2,1)S(1)}, bf16[4,4,16,128]{3,2,1,0:T(8,128)(2,1)S(1)}, u32[]{:S(2)}, u32[]{:S(2)}) %collective-permute-start.6) | collective-permute-done | bytes 65568 | tf_op jit(solution)/shard_map/ppermute | solution.py:671
  34.4 0.8 %collective-permute-done.7.refs_3_ = bf16[4,4,16,128]{3,2,1,0:T(8,128)(2,1)S(1)} collective-permute-done((bf16[4,4,16,128]{3,2,1,0:T(8,128)(2,1)S(1)}, bf16[4,4,16,128]{3,2,1,0:T(8,128)(2,1)S(1)}, u32[]{:S(2)}, u32[]{:S(2)}) %collective-permute-start.7) | collective-permute-done | bytes 65568 | tf_op jit(solution)/shard_map/ppermute | solution.py:671
  35.1 0.0 collective-permute-done.10.refs_10_.refs_11_
  35.2 0.0 copy-start.5
  35.2 0.9 %copy-done.5 = bf16[1,16,64,128]{3,2,1,0:T(8,128)(2,1)S(1)} copy-done((bf16[1,16,64,128]{3,2,1,0:T(8,128)(2,1)S(1)}, bf16[1,16,64,128]{3,2,1,0:T(8,128)(2,1)}, u32[]{:S(2)}) %copy-start.5) | copy-done | bytes 262168
  36.1 0.9 %copy-done.7 = bf16[1,16,64,128]{3,2,1,0:T(8,128)(2,1)S(1)} copy-done((bf16[1,16,64,128]{3,2,1,0:T(8,128)(2,1)S(1)}, bf16[1,16,64,128]{3,2,1,0:T(8,128)(2,1)}, u32[]{:S(2)}) %copy-start.7) | copy-done | bytes 262168
  37.1 15.4 %shard_map.88 = (bf16[4,4,16,128]{3,2,1,0:T(8,128)(2,1)S(1)}, bf16[4,4,16,128]{3,2,1,0:T(8,128)(2,1)S(1)}, bf16[4,4,16,128]{3,2,1,0:T(8,128)(2,1)S(1)}, bf16[4,4...) custom-call(s32[1]{0:T(128)} %bitcast.me_ref, bf16[4,4,16,128]{3,2,1,0:T(8,128)(2,1)S(1)} %get-tuple-element.36.refs_0_, ...), custom_call_target="tpu_custom_call" | custom-call | flops 134217728 | bytes 33554432 | tf_op jit(solution)/shard_map/pallas_call | solution.py:454
  52.5 0.2 collective-permute-start.11
  52.7 1.2 %collective-permute-start.12 = (bf16[4,4,16,128]{3,2,1,0:T(8,128)(2,1)S(1)}, bf16[4,4,16,128]{3,2,1,0:T(8,128)(2,1)S(1)}, u32[]{:S(2)}, u32[]{:S(2)}) collective-permute-start(bf16[4,4,16,128]{3,2,1,0:T(8,128)(2,1)S(1)} %get-tuple-element.44), channel_id=1, source_target_pairs={{0,4},{2,6},{4,0},{6,2},{8,12},{10,14},{12,8},{14,10},{16,20},{18,... | collective-permute-start | bytes 196616 | tf_op jit(solution)/shard_map/ppermute | solution.py:671
  53.9 0.5 collective-permute-start.13
  54.4 0.0 collective-permute-done.11.refs_1_
  54.4 2.9 %collective-permute-done.12.refs_2_ = bf16[4,4,16,128]{3,2,1,0:T(8,128)(2,1)S(1)} collective-permute-done((bf16[4,4,16,128]{3,2,1,0:T(8,128)(2,1)S(1)}, bf16[4,4,16,128]{3,2,1,0:T(8,128)(2,1)S(1)}, u32[]{:S(2)}, u32[]{:S(2)}) %collective-permute-start.12) | collective-permute-done | bytes 65568 | tf_op jit(solution)/shard_map/ppermute | solution.py:671
  57.3 0.9 %collective-permute-done.13.refs_3_ = bf16[4,4,16,128]{3,2,1,0:T(8,128)(2,1)S(1)} collective-permute-done((bf16[4,4,16,128]{3,2,1,0:T(8,128)(2,1)S(1)}, bf16[4,4,16,128]{3,2,1,0:T(8,128)(2,1)S(1)}, u32[]{:S(2)}, u32[]{:S(2)}) %collective-permute-start.13) | collective-permute-done | bytes 65568 | tf_op jit(solution)/shard_map/ppermute | solution.py:671
  58.2 1.6 %collective-permute-start.14 = (bf16[4,4,16,128]{3,2,1,0:T(8,128)(2,1)S(1)}, bf16[4,4,16,128]{3,2,1,0:T(8,128)(2,1)S(1)}, u32[]{:S(2)}, u32[]{:S(2)}) collective-permute-start(bf16[4,4,16,128]{3,2,1,0:T(8,128)(2,1)S(1)} %get-tuple-element.47), channel_id=1, source_target_pairs={{0,8},{2,10},{4,12},{6,14},{8,0},{10,2},{12,4},{14,6},{16,24},{18,... | collective-permute-start | bytes 196616 | tf_op jit(solution)/shard_map/ppermute | solution.py:671
  59.8 1.1 %collective-permute-start.15 = (bf16[4,4,16,128]{3,2,1,0:T(8,128)(2,1)S(1)}, bf16[4,4,16,128]{3,2,1,0:T(8,128)(2,1)S(1)}, u32[]{:S(2)}, u32[]{:S(2)}) collective-permute-start(bf16[4,4,16,128]{3,2,1,0:T(8,128)(2,1)S(1)} %get-tuple-element.48), channel_id=1, source_target_pairs={{0,16},{2,18},{4,20},{6,22},{8,24},{10,26},{12,28},{14,30},{16,0},... | collective-permute-start | bytes 196616 | tf_op jit(solution)/shard_map/ppermute | solution.py:671
  60.9 1.7 %collective-permute-start.16 = (bf16[4,4,16,128]{3,2,1,0:T(8,128)(2,1)S(1)}, bf16[4,4,16,128]{3,2,1,0:T(8,128)(2,1)S(1)}, u32[]{:S(2)}, u32[]{:S(2)}) collective-permute-start(bf16[4,4,16,128]{3,2,1,0:T(8,128)(2,1)S(1)} %get-tuple-element.49), channel_id=1, source_target_pairs={{0,24},{2,26},{4,28},{6,30},{8,16},{10,18},{12,20},{14,22},{16,8},... | collective-permute-start | bytes 196616 | tf_op jit(solution)/shard_map/ppermute | solution.py:671
  62.7 1.5 %collective-permute-start.17 = (bf16[4,4,16,128]{3,2,1,0:T(8,128)(2,1)S(1)}, bf16[4,4,16,128]{3,2,1,0:T(8,128)(2,1)S(1)}, u32[]{:S(2)}, u32[]{:S(2)}) collective-permute-start(bf16[4,4,16,128]{3,2,1,0:T(8,128)(2,1)S(1)} %get-tuple-element.46.refs_0_), channel_id=1, source_target_pairs={{0,1},{1,0},{2,3},{3,2},{4,5},{5,4},{6,7},{7,6},{8,9},{9,8},{10,11... | collective-permute-start | bytes 196616 | tf_op jit(solution)/shard_map/ppermute | solution.py:675
  64.2 0.6 collective-permute-start.18
  64.8 3.3 %collective-permute-done.15.refs_2_ = bf16[4,4,16,128]{3,2,1,0:T(8,128)(2,1)S(1)} collective-permute-done((bf16[4,4,16,128]{3,2,1,0:T(8,128)(2,1)S(1)}, bf16[4,4,16,128]{3,2,1,0:T(8,128)(2,1)S(1)}, u32[]{:S(2)}, u32[]{:S(2)}) %collective-permute-start.15) | collective-permute-done | bytes 65568 | tf_op jit(solution)/shard_map/ppermute | solution.py:671
  68.0 0.8 %collective-permute-start.19 = (bf16[4,4,16,128]{3,2,1,0:T(8,128)(2,1)S(1)}, bf16[4,4,16,128]{3,2,1,0:T(8,128)(2,1)S(1)}, u32[]{:S(2)}, u32[]{:S(2)}) collective-permute-start(bf16[4,4,16,128]{3,2,1,0:T(8,128)(2,1)S(1)} %collective-permute-done.15.refs_2_), channel_id=1, source_target_pairs={{0,1},{1,0},{2,3},{3,2},{4,5},{5,4},{6,7},{7,6},{8,9},{9,8},{10,11... | collective-permute-start | bytes 196616 | tf_op jit(solution)/shard_map/ppermute | solution.py:675
  68.8 1.2 %collective-permute-start.20 = (bf16[4,4,16,128]{3,2,1,0:T(8,128)(2,1)S(1)}, bf16[4,4,16,128]{3,2,1,0:T(8,128)(2,1)S(1)}, u32[]{:S(2)}, u32[]{:S(2)}) collective-permute-start(bf16[4,4,16,128]{3,2,1,0:T(8,128)(2,1)S(1)} %collective-permute-done.16.refs_3_), channel_id=1, source_target_pairs={{0,1},{1,0},{2,3},{3,2},{4,5},{5,4},{6,7},{7,6},{8,9},{9,8},{10,11... | collective-permute-start | bytes 196616 | tf_op jit(solution)/shard_map/ppermute | solution.py:675
  70.1 2.2 %collective-permute-done.19.refs_6_ = bf16[4,4,16,128]{3,2,1,0:T(8,128)(2,1)S(1)} collective-permute-done((bf16[4,4,16,128]{3,2,1,0:T(8,128)(2,1)S(1)}, bf16[4,4,16,128]{3,2,1,0:T(8,128)(2,1)S(1)}, u32[]{:S(2)}, u32[]{:S(2)}) %collective-permute-start.19) | collective-permute-done | bytes 65568 | tf_op jit(solution)/shard_map/ppermute | solution.py:675
  72.3 0.8 %collective-permute-done.20.refs_7_ = bf16[4,4,16,128]{3,2,1,0:T(8,128)(2,1)S(1)} collective-permute-done((bf16[4,4,16,128]{3,2,1,0:T(8,128)(2,1)S(1)}, bf16[4,4,16,128]{3,2,1,0:T(8,128)(2,1)S(1)}, u32[]{:S(2)}, u32[]{:S(2)}) %collective-permute-start.20) | collective-permute-done | bytes 65568 | tf_op jit(solution)/shard_map/ppermute | solution.py:675
  73.1 3.0 %shard_map.90 = bf16[4,16,64,128]{3,2,1,0:T(8,128)(2,1)} custom-call(s32[1]{0:T(128)} %bitcast.me_ref, bf16[2,1024,512]{2,1,0:T(8,128)(2,1)S(1)} %copy-done.3, bf16[4,4,16,128]{3,2,1,0:T(8,128)(2,1)S(1)} %get-tuple-element.46.refs_0_, bf16[4,4,16,128]{3,2,1,0:T(8,128)(2,1)S(1)} %collective-permute-done.14.refs_1_, ...), custom_call_target="tpu_custom_call" | custom-call | flops 536870912 | bytes 3145728 | tf_op jit(solution)/shard_map/pallas_call | solution.py:515
  (27 shorter events, 0.1 us)
Async XLA Ops:
  0.0 1.2 %copy-start = (bf16[4,16,64,128]{3,2,1,0:T(8,128)(2,1)S(1)}, bf16[4,16,64,128]{3,2,1,0:T(8,128)(2,1)}, u32[]{:S(2)}) copy-start(bf16[4,16,64,128]{3,2,1,0:T(8,128)(2,1)} %refs_7_.1) | copy-start | bytes 3145732
  1.2 1.6 %copy-start.2 = (bf16[2,512,1024]{2,1,0:T(8,128)(2,1)S(1)}, bf16[2,512,1024]{2,1,0:T(8,128)(2,1)}, u32[]{:S(2)}) copy-start(bf16[2,512,1024]{2,1,0:T(8,128)(2,1)} %constant.18.clone.table_ref) | copy-start | bytes 6291460
  3.8 20.9 %collective-permute-start.8 = (bf16[1,16,64,128]{3,2,1,0:T(8,128)(2,1)}, bf16[1,16,64,128]{3,2,1,0:T(8,128)(2,1)S(1)}, u32[]{:S(2)}, u32[]{:S(2)}) collective-permute-start(bf16[1,16,64,128]{3,2,1,0:T(8,128)(2,1)} %bitcast.3), channel_id=1, source_target_pairs={{0,2},{2,4},{4,6},{6,8},{8,10},{10,12},{12,14},{14,16},{16,18},{18... | collective-permute-start | bytes 786440 | tf_op jit(solution)/shard_map/ppermute | solution.py:660
  6.2 18.5 %collective-permute-start.9 = (bf16[1,16,64,128]{3,2,1,0:T(8,128)(2,1)S(1)}, bf16[1,16,64,128]{3,2,1,0:T(8,128)(2,1)S(1)}, u32[]{:S(2)}, u32[]{:S(2)}) collective-permute-start(bf16[1,16,64,128]{3,2,1,0:T(8,128)(2,1)S(1)} %bitcast.11), channel_id=1, source_target_pairs={{2,0},{4,2},{6,4},{8,6},{10,8},{12,10},{14,12},{16,14},{18,16},{20... | collective-permute-start | bytes 786440 | tf_op jit(solution)/shard_map/ppermute | solution.py:660
  10.0 25.1 %copy-start.1 = (bf16[4,16,64,128]{3,2,1,0:T(8,128)(2,1)S(1)}, bf16[4,16,64,128]{3,2,1,0:T(8,128)(2,1)}, u32[]{:S(2)}) copy-start(bf16[4,16,64,128]{3,2,1,0:T(8,128)(2,1)} %refs_7_.1) | copy-start | bytes 3145732
  10.0 25.1 %copy-start.8 = (bf16[3,3,3,128,128]{4,3,2,1,0:T(8,128)(2,1)S(1)}, bf16[3,3,3,128,128]{4,3,2,1,0:T(8,128)(2,1)}, u32[]{:S(2)}) copy-start(bf16[3,3,3,128,128]{4,3,2,1,0:T(8,128)(2,1)} %param.10) | copy-start | bytes 2654212
  10.0 25.1 %copy-start.9 = (bf16[256,128]{1,0:T(8,128)(2,1)S(1)}, bf16[256,128]{1,0:T(8,128)(2,1)}, u32[]{:S(2)}) copy-start(bf16[256,128]{1,0:T(8,128)(2,1)} %constant.19.clone.refs_4_) | copy-start | bytes 196612
  10.0 25.1 %copy-start.10 = (bf16[128,128]{1,0:T(8,128)(2,1)S(1)}, bf16[128,128]{1,0:T(8,128)(2,1)}, u32[]{:S(2)}) copy-start(bf16[128,128]{1,0:T(8,128)(2,1)} %constant.20.clone.refs_5_) | copy-start | bytes 98308
  10.0 5.6 %collective-permute-start.2 = (bf16[2,4,4,16,128]{4,3,2,1,0:T(8,128)(2,1)}, bf16[2,4,4,16,128]{4,3,2,1,0:T(8,128)(2,1)S(1)}, u32[]{:S(2)}, u32[]{:S(2)}) collective-permute-start(bf16[2,4,4,16,128]{4,3,2,1,0:T(8,128)(2,1)} %get-tuple-element.33), channel_id=1, source_target_pairs={{0,1},{1,0},{2,3},{3,2},{4,5},{5,4},{6,7},{7,6},{8,9},{9,8},{10,11... | collective-permute-start | bytes 393224 | tf_op jit(solution)/shard_map/ppermute | solution.py:675
  12.4 11.9 %collective-permute-start = (bf16[2,4,4,16,128]{4,3,2,1,0:T(8,128)(2,1)}, bf16[2,4,4,16,128]{4,3,2,1,0:T(8,128)(2,1)S(1)}, u32[]{:S(2)}, u32[]{:S(2)}) collective-permute-start(bf16[2,4,4,16,128]{4,3,2,1,0:T(8,128)(2,1)} %get-tuple-element.29), channel_id=1, source_target_pairs={{0,1},{1,0},{2,3},{3,2},{4,5},{5,4},{6,7},{7,6},{8,9},{9,8},{10,11... | collective-permute-start | bytes 393224 | tf_op jit(solution)/shard_map/ppermute | solution.py:675
  15.6 13.5 %collective-permute-start.3 = (bf16[4,4,16,128]{3,2,1,0:T(8,128)(2,1)S(1)}, bf16[4,4,16,128]{3,2,1,0:T(8,128)(2,1)S(1)}, u32[]{:S(2)}, u32[]{:S(2)}) collective-permute-start(bf16[4,4,16,128]{3,2,1,0:T(8,128)(2,1)S(1)} %get-tuple-element.34), channel_id=1, source_target_pairs={{0,16},{2,18},{4,20},{6,22},{8,24},{10,26},{12,28},{14,30},{16,0},... | collective-permute-start | bytes 196616 | tf_op jit(solution)/shard_map/ppermute | solution.py:671
  23.0 6.2 %collective-permute-start.4 = (bf16[4,4,16,128]{3,2,1,0:T(8,128)(2,1)S(1)}, bf16[4,4,16,128]{3,2,1,0:T(8,128)(2,1)S(1)}, u32[]{:S(2)}, u32[]{:S(2)}) collective-permute-start(bf16[4,4,16,128]{3,2,1,0:T(8,128)(2,1)S(1)} %get-tuple-element.35), channel_id=1, source_target_pairs={{0,24},{2,26},{4,28},{6,30},{8,16},{10,18},{12,20},{14,22},{16,8},... | collective-permute-start | bytes 196616 | tf_op jit(solution)/shard_map/ppermute | solution.py:671
  24.4 5.0 %collective-permute-start.1 = (bf16[4,4,16,128]{3,2,1,0:T(8,128)(2,1)S(1)}, bf16[4,4,16,128]{3,2,1,0:T(8,128)(2,1)S(1)}, u32[]{:S(2)}, u32[]{:S(2)}) collective-permute-start(bf16[4,4,16,128]{3,2,1,0:T(8,128)(2,1)S(1)} %get-tuple-element.31), channel_id=1, source_target_pairs={{0,8},{2,10},{4,12},{6,14},{8,0},{10,2},{12,4},{14,6},{16,24},{18,... | collective-permute-start | bytes 196616 | tf_op jit(solution)/shard_map/ppermute | solution.py:671
  24.7 0.7 copy-start.4
  25.4 0.7 copy-start.6
  27.6 7.5 %collective-permute-start.10 = (bf16[6,1,64,128]{3,2,1,0:T(8,128)(2,1)}, bf16[6,1,64,128]{3,2,1,0:T(8,128)(2,1)S(1)}, u32[]{:S(2)}, u32[]{:S(2)}) collective-permute-start(bf16[6,1,64,128]{3,2,1,0:T(8,128)(2,1)} %shard_map.87), channel_id=1, source_target_pairs={{0,1},{1,0},{2,3},{3,2},{4,5},{5,4},{6,7},{7,6},{8,9},{9,8},{10,11... | collective-permute-start | bytes 294920 | tf_op jit(solution)/shard_map/ppermute | solution.py:675
  29.5 1.9 %collective-permute-start.5 = (bf16[4,4,16,128]{3,2,1,0:T(8,128)(2,1)S(1)}, bf16[4,4,16,128]{3,2,1,0:T(8,128)(2,1)S(1)}, u32[]{:S(2)}, u32[]{:S(2)}) collective-permute-start(bf16[4,4,16,128]{3,2,1,0:T(8,128)(2,1)S(1)} %get-tuple-element.37), channel_id=1, source_target_pairs={{0,2},{2,0},{4,6},{6,4},{8,10},{10,8},{12,14},{14,12},{16,18},{18,... | collective-permute-start | bytes 196616 | tf_op jit(solution)/shard_map/ppermute | solution.py:671
  29.5 4.8 %collective-permute-start.6 = (bf16[4,4,16,128]{3,2,1,0:T(8,128)(2,1)S(1)}, bf16[4,4,16,128]{3,2,1,0:T(8,128)(2,1)S(1)}, u32[]{:S(2)}, u32[]{:S(2)}) collective-permute-start(bf16[4,4,16,128]{3,2,1,0:T(8,128)(2,1)S(1)} %get-tuple-element.38), channel_id=1, source_target_pairs={{0,4},{2,6},{4,0},{6,2},{8,12},{10,14},{12,8},{14,10},{16,20},{18,... | collective-permute-start | bytes 196616 | tf_op jit(solution)/shard_map/ppermute | solution.py:671
  30.8 4.3 %collective-permute-start.7 = (bf16[4,4,16,128]{3,2,1,0:T(8,128)(2,1)S(1)}, bf16[4,4,16,128]{3,2,1,0:T(8,128)(2,1)S(1)}, u32[]{:S(2)}, u32[]{:S(2)}) collective-permute-start(bf16[4,4,16,128]{3,2,1,0:T(8,128)(2,1)S(1)} %get-tuple-element.39), channel_id=1, source_target_pairs={{0,6},{2,4},{4,2},{6,0},{8,14},{10,12},{12,10},{14,8},{16,22},{18,... | collective-permute-start | bytes 196616 | tf_op jit(solution)/shard_map/ppermute | solution.py:671
  35.2 1.0 %copy-start.5 = (bf16[1,16,64,128]{3,2,1,0:T(8,128)(2,1)S(1)}, bf16[1,16,64,128]{3,2,1,0:T(8,128)(2,1)}, u32[]{:S(2)}) copy-start(bf16[1,16,64,128]{3,2,1,0:T(8,128)(2,1)} %copy-done.4) | copy-start | bytes 786436
  36.1 0.9 %copy-start.7 = (bf16[1,16,64,128]{3,2,1,0:T(8,128)(2,1)S(1)}, bf16[1,16,64,128]{3,2,1,0:T(8,128)(2,1)}, u32[]{:S(2)}) copy-start(bf16[1,16,64,128]{3,2,1,0:T(8,128)(2,1)} %copy-done.6) | copy-start | bytes 786436
  37.1 36.0 %copy-start.3 = (bf16[2,1024,512]{2,1,0:T(8,128)(2,1)S(1)}, bf16[2,1024,512]{2,1,0:T(8,128)(2,1)}, u32[]{:S(2)}) copy-start(bf16[2,1024,512]{2,1,0:T(8,128)(2,1)} %constant.21.clone.table_ref) | copy-start | bytes 6291460
  37.1 36.0 %copy-start.11 = (f32[128]{0:T(128)S(1)}, f32[128]{0:T(128)}, u32[]{:S(2)}) copy-start(f32[128]{0:T(128)} %param.11) | copy-start | bytes 1540
  52.5 1.9 %collective-permute-start.11 = (bf16[4,4,16,128]{3,2,1,0:T(8,128)(2,1)S(1)}, bf16[4,4,16,128]{3,2,1,0:T(8,128)(2,1)S(1)}, u32[]{:S(2)}, u32[]{:S(2)}) collective-permute-start(bf16[4,4,16,128]{3,2,1,0:T(8,128)(2,1)S(1)} %get-tuple-element.43), channel_id=1, source_target_pairs={{0,2},{2,0},{4,6},{6,4},{8,10},{10,8},{12,14},{14,12},{16,18},{18,... | collective-permute-start | bytes 196616 | tf_op jit(solution)/shard_map/ppermute | solution.py:671
  52.7 4.6 %collective-permute-start.12 = (bf16[4,4,16,128]{3,2,1,0:T(8,128)(2,1)S(1)}, bf16[4,4,16,128]{3,2,1,0:T(8,128)(2,1)S(1)}, u32[]{:S(2)}, u32[]{:S(2)}) collective-permute-start(bf16[4,4,16,128]{3,2,1,0:T(8,128)(2,1)S(1)} %get-tuple-element.44), channel_id=1, source_target_pairs={{0,4},{2,6},{4,0},{6,2},{8,12},{10,14},{12,8},{14,10},{16,20},{18,... | collective-permute-start | bytes 196616 | tf_op jit(solution)/shard_map/ppermute | solution.py:671
  53.9 4.3 %collective-permute-start.13 = (bf16[4,4,16,128]{3,2,1,0:T(8,128)(2,1)S(1)}, bf16[4,4,16,128]{3,2,1,0:T(8,128)(2,1)S(1)}, u32[]{:S(2)}, u32[]{:S(2)}) collective-permute-start(bf16[4,4,16,128]{3,2,1,0:T(8,128)(2,1)S(1)} %get-tuple-element.45), channel_id=1, source_target_pairs={{0,6},{2,4},{4,2},{6,0},{8,14},{10,12},{12,10},{14,8},{16,22},{18,... | collective-permute-start | bytes 196616 | tf_op jit(solution)/shard_map/ppermute | solution.py:671
  58.2 6.0 %collective-permute-start.14 = (bf16[4,4,16,128]{3,2,1,0:T(8,128)(2,1)S(1)}, bf16[4,4,16,128]{3,2,1,0:T(8,128)(2,1)S(1)}, u32[]{:S(2)}, u32[]{:S(2)}) collective-permute-start(bf16[4,4,16,128]{3,2,1,0:T(8,128)(2,1)S(1)} %get-tuple-element.47), channel_id=1, source_target_pairs={{0,8},{2,10},{4,12},{6,14},{8,0},{10,2},{12,4},{14,6},{16,24},{18,... | collective-permute-start | bytes 196616 | tf_op jit(solution)/shard_map/ppermute | solution.py:671
  59.8 8.2 %collective-permute-start.15 = (bf16[4,4,16,128]{3,2,1,0:T(8,128)(2,1)S(1)}, bf16[4,4,16,128]{3,2,1,0:T(8,128)(2,1)S(1)}, u32[]{:S(2)}, u32[]{:S(2)}) collective-permute-start(bf16[4,4,16,128]{3,2,1,0:T(8,128)(2,1)S(1)} %get-tuple-element.48), channel_id=1, source_target_pairs={{0,16},{2,18},{4,20},{6,22},{8,24},{10,26},{12,28},{14,30},{16,0},... | collective-permute-start | bytes 196616 | tf_op jit(solution)/shard_map/ppermute | solution.py:671
  60.9 7.9 %collective-permute-start.16 = (bf16[4,4,16,128]{3,2,1,0:T(8,128)(2,1)S(1)}, bf16[4,4,16,128]{3,2,1,0:T(8,128)(2,1)S(1)}, u32[]{:S(2)}, u32[]{:S(2)}) collective-permute-start(bf16[4,4,16,128]{3,2,1,0:T(8,128)(2,1)S(1)} %get-tuple-element.49), channel_id=1, source_target_pairs={{0,24},{2,26},{4,28},{6,30},{8,16},{10,18},{12,20},{14,22},{16,8},... | collective-permute-start | bytes 196616 | tf_op jit(solution)/shard_map/ppermute | solution.py:671
  62.7 7.4 %collective-permute-start.17 = (bf16[4,4,16,128]{3,2,1,0:T(8,128)(2,1)S(1)}, bf16[4,4,16,128]{3,2,1,0:T(8,128)(2,1)S(1)}, u32[]{:S(2)}, u32[]{:S(2)}) collective-permute-start(bf16[4,4,16,128]{3,2,1,0:T(8,128)(2,1)S(1)} %get-tuple-element.46.refs_0_), channel_id=1, source_target_pairs={{0,1},{1,0},{2,3},{3,2},{4,5},{5,4},{6,7},{7,6},{8,9},{9,8},{10,11... | collective-permute-start | bytes 196616 | tf_op jit(solution)/shard_map/ppermute | solution.py:675
  64.2 5.9 %collective-permute-start.18 = (bf16[4,4,16,128]{3,2,1,0:T(8,128)(2,1)S(1)}, bf16[4,4,16,128]{3,2,1,0:T(8,128)(2,1)S(1)}, u32[]{:S(2)}, u32[]{:S(2)}) collective-permute-start(bf16[4,4,16,128]{3,2,1,0:T(8,128)(2,1)S(1)} %collective-permute-done.14.refs_1_), channel_id=1, source_target_pairs={{0,1},{1,0},{2,3},{3,2},{4,5},{5,4},{6,7},{7,6},{8,9},{9,8},{10,11... | collective-permute-start | bytes 196616 | tf_op jit(solution)/shard_map/ppermute | solution.py:675
  68.0 4.3 %collective-permute-start.19 = (bf16[4,4,16,128]{3,2,1,0:T(8,128)(2,1)S(1)}, bf16[4,4,16,128]{3,2,1,0:T(8,128)(2,1)S(1)}, u32[]{:S(2)}, u32[]{:S(2)}) collective-permute-start(bf16[4,4,16,128]{3,2,1,0:T(8,128)(2,1)S(1)} %collective-permute-done.15.refs_2_), channel_id=1, source_target_pairs={{0,1},{1,0},{2,3},{3,2},{4,5},{5,4},{6,7},{7,6},{8,9},{9,8},{10,11... | collective-permute-start | bytes 196616 | tf_op jit(solution)/shard_map/ppermute | solution.py:675
  68.8 4.3 %collective-permute-start.20 = (bf16[4,4,16,128]{3,2,1,0:T(8,128)(2,1)S(1)}, bf16[4,4,16,128]{3,2,1,0:T(8,128)(2,1)S(1)}, u32[]{:S(2)}, u32[]{:S(2)}) collective-permute-start(bf16[4,4,16,128]{3,2,1,0:T(8,128)(2,1)S(1)} %collective-permute-done.16.refs_3_), channel_id=1, source_target_pairs={{0,1},{1,0},{2,3},{3,2},{4,5},{5,4},{6,7},{7,6},{8,9},{9,8},{10,11... | collective-permute-start | bytes 196616 | tf_op jit(solution)/shard_map/ppermute | solution.py:675

commit v5 on v4

--- a/solution.py
+++ b/solution.py
@@ -137,11 +137,15 @@
                     ref[slot, :, x + i] = value.astype(ref.dtype)
                     at += block
     if edges:
-        refs[-2][...] = flow_ref[0]
-        refs[-1][...] = flow_ref[cells_x - 1]
-
-
-def forward_yz(me, table, flow, step, shards, shards_y, pieces, dtype, edges=False):
+        first, last, low, high = refs[-4:]
+        first[...] = flow_ref[0]
+        last[...] = flow_ref[cells_x - 1]
+        cells_z = low.shape[1]
+        low[...] = flow_ref[:, :cells_z]
+        high[...] = flow_ref[:, flow_ref.shape[1] - cells_z :]
+
+
+def forward_yz(me, table, flow, step, shards, shards_y, pieces, dtype, edges=0):
     cells_x, positions, channels = flow.shape
     outer, inner = shards
     rows = table.shape[1] // shards_y
@@ -149,13 +153,14 @@
     shapes = [jax.ShapeDtypeStruct((len(piece), *unit), dtype) for piece in pieces]
     if edges:
         shapes += [jax.ShapeDtypeStruct((positions, channels), flow.dtype)] * 2
+        shapes += [jax.ShapeDtypeStruct((cells_x, edges, channels), flow.dtype)] * 2
     whole = lambda dims: pl.BlockSpec(dims, lambda i, me: (0,) * len(dims))
 
     def owner(i, me):
         own = lax.div(me[0], outer * inner)
         return own, lax.rem(own + step, shards_y), 0
 
-    limit = {"vmem_limit_bytes": 24 << 20} if step == 0 else {}
+    limit = {} if step else {"vmem_limit_bytes": 10 << 20}
     return pl.pallas_call(
         functools.partial(forward_kernel, shards, pieces, edges),
         grid_spec=pltpu.PrefetchScalarGridSpec(
@@ -191,7 +196,7 @@
         out_specs=in_vmem(slots),
         out_shape=[jax.ShapeDtypeStruct(unit, jnp.bfloat16)] * slots,
         cost_estimate=pl.CostEstimate(flops=own.size, bytes_accessed=0, transcendentals=0),
-        compiler_params=pltpu.CompilerParams(vmem_limit_bytes=16 << 20),
+        compiler_params=pltpu.CompilerParams(vmem_limit_bytes=10 << 20),
     )(own, *arrived)
 
 
@@ -215,61 +220,84 @@
         cost_estimate=pl.CostEstimate(
             flops=arrays[0].size, bytes_accessed=0, transcendentals=0
         ),
-        compiler_params=pltpu.CompilerParams(vmem_limit_bytes=16 << 20),
+        compiler_params=pltpu.CompilerParams(vmem_limit_bytes=10 << 20),
     )(me, *arrays)
 
 
-def edge_kernel(me_ref, left_ref, flow_ref, right_ref, out_ref):
-    out_ref[0] = left_ref[0]
-    out_ref[1 : 1 + flow_ref.shape[0]] = flow_ref[...]
-    out_ref[1 + flow_ref.shape[0]] = right_ref[0]
-
-
-def y_edge(me, left, flow, right, per_y, row):
-    cells_x, cells_y, cells_z, channels = flow.shape
-    at = lambda i, me: (0, row(lax.div(me[0], per_y)), 0, 0)
-    shape = (cells_x + 2, 1, cells_z, channels)
+def edge_kernel(choose, per_y, me_ref, left_ref, low_ref, high_ref, right_ref, out_ref):
+    cells_x, cells_y = low_ref.shape[0], left_ref.shape[1]
+
+    def fill(row, rows_ref):
+        out_ref[0, 0] = left_ref[0, row]
+        out_ref[1 : 1 + cells_x, 0] = rows_ref[...]
+        out_ref[1 + cells_x, 0] = right_ref[0, row]
+
+    is_low = choose(lax.div(me_ref[0], per_y))
+
+    @pl.when(is_low)
+    def _():
+        fill(0, low_ref)
+
+    @pl.when(jnp.logical_not(is_low))
+    def _():
+        fill(cells_y - 1, high_ref)
+
+
+def y_edge(me, left, low, high, right, per_y, choose):
+    cells_x, cells_z, channels = low.shape
     return pl.pallas_call(
-        edge_kernel,
-        grid_spec=pltpu.PrefetchScalarGridSpec(
-            num_scalar_prefetch=1,
-            grid=(1,),
-            in_specs=[
-                pl.BlockSpec((1, 1, cells_z, channels), at),
-                pl.BlockSpec((cells_x, 1, cells_z, channels), at),
-                pl.BlockSpec((1, 1, cells_z, channels), at),
-            ],
-            out_specs=pl.BlockSpec(shape, lambda i, me: (0, 0, 0, 0)),
+        functools.partial(edge_kernel, choose, per_y),
+        in_specs=[IN_SMEM] + in_vmem(4),
+        out_specs=in_vmem(1)[0],
+        out_shape=jax.ShapeDtypeStruct((cells_x + 2, 1, cells_z, channels), low.dtype),
+        compiler_params=pltpu.CompilerParams(vmem_limit_bytes=4 << 20),
+    )(me, left, low, high, right)
+
+
+def preload_kernel(pair, weight_ref, out_ref, sem):
+    copy = pltpu.make_async_copy(weight_ref.at[pl.ds(2 * pair, 2)], out_ref, sem)
+    copy.start()
+    copy.wait()
+
+
+def preload(weight, pair):
+    shape = (2, *weight.shape[1:])
+    return pl.pallas_call(
+        functools.partial(preload_kernel, pair),
+        in_specs=[pl.BlockSpec(memory_space=pltpu.HBM)],
+        out_specs=in_vmem(1)[0],
+        out_shape=jax.ShapeDtypeStruct(shape, weight.dtype),
+        scratch_shapes=[pltpu.SemaphoreType.DMA],
+        compiler_params=pltpu.CompilerParams(vmem_limit_bytes=36 << 20),
+        cost_estimate=pl.CostEstimate(
+            flops=0, bytes_accessed=2 * math.prod(shape), transcendentals=0
         ),
-        out_shape=jax.ShapeDtypeStruct(shape, flow.dtype),
-    )(me, left, flow, right)
-
-
-def mixing_kernel(shards, shards_y, me_ref, *refs):
+    )(weight)
+
+
+def mixing_kernel(shards, loaded, me_ref, *refs):
     outer, inner = shards
     row_refs, refs = refs[:inner], refs[inner:]
-    forward_ref, backward_ref, weight_ref, flow_ref, left_ref, right_ref, *refs = refs
-    front_ref, back_ref, kernel_ref, *refs = refs
-    out_refs, refs = refs[:inner], refs[inner:]
-    convolved_ref, held, sems, wide, left, mixed, stacked = refs
-
-    slots, _, modes, _, channels = held.shape
+    forward_ref, backward_ref, weight_ref, *refs = refs
+    loaded_refs, refs = refs[:loaded], refs[loaded:]
+    out_refs, (held, sems, wide, left, mixed) = refs[:inner], refs[inner:]
+
+    channels = wide.shape[1]
     _, cells_x, item_rows, _ = row_refs[0].shape
-    cells_y, cells_z = flow_ref.shape[1:3]
     pairs = item_rows // 2
     full_x = outer * inner * cells_x
     half = channels // 2
     span = 2 * MX
     block = cells_x * item_rows
-    own_y, own_outer, own_inner = place(me_ref[0], shards)
+    _, own_outer, own_inner = place(me_ref[0], shards)
 
     def copy(pair):
-        slot = lax.rem(pair, slots)
+        slot = pair - loaded
         return pltpu.make_async_copy(
             weight_ref.at[pl.ds(2 * pair, 2)], held.at[slot], sems.at[slot]
         )
 
-    for pair in range(min(slots - 1, pairs)):
+    for pair in range(loaded, pairs):
         copy(pair).start()
 
     def rows_of(outer_index, inner_index):
@@ -296,7 +324,7 @@
     group = 16
     row = lax.broadcasted_iota(jnp.int32, (group, channels), 0) // 2
 
-    def mix(pair, slot):
+    def mix(pair, tile_of):
         for step in range(span // group):
             start = pl.multiple_of(pair * span + step * group, group)
             lhs = left[pl.ds(start, group), :]
@@ -304,7 +332,7 @@
             for i in range(0, group // 2, 2):
                 mode = step * (group // 2) + i
                 tiles = [
-                    jnp.concatenate([held[slot, 0, mode + k], held[slot, 1, mode + k]], axis=0)
+                    jnp.concatenate([tile_of(h, mode + k) for h in range(2)], axis=0)
                     for k in range(2)
                 ]
                 product = dot(lhs, jnp.concatenate(tiles, axis=1))
@@ -314,117 +342,15 @@
                     )
             mixed[pl.ds(start, group), :] = gathered.astype(mixed.dtype)
 
-    width = 2 if cells_x % 2 == 0 else 1
-    rows = stacked.shape[1] - 2
-    y_units = cells_y // rows
-    units = cells_x // width * y_units
-
-    def stack(plane, at, cells):
-        deep = cells.astype(jnp.float32)
-        z = lax.broadcasted_iota(jnp.int32, deep.shape, 1)
-        before = jnp.where(z == 0, 0.0, pltpu.roll(deep, 1, axis=1))
-        after = jnp.where(z == cells_z - 1, 0.0, pltpu.roll(deep, cells_z - 1, axis=1))
-        at = pl.ds(at, cells.shape[0])
-        stacked[plane, at, :, :channels] = before.astype(stacked.dtype)
-        stacked[plane, at, :, channels : 2 * channels] = cells
-        stacked[plane, at, :, 2 * channels :] = after.astype(stacked.dtype)
-
-    def stack_unit(unit):
-        x, y = lax.div(unit, y_units) * width, lax.rem(unit, y_units) * rows
-        for plane in range(width + 2):
-            source = x + plane - 1
-
-            def fill(inside, low_edge, high_edge, plane=plane):
-                stack(plane, 1, inside(pl.ds(y, rows)))
-
-                @pl.when(y > 0)
-                def _():
-                    stack(plane, 0, inside(pl.ds(y - 1, 1)))
-
-                @pl.when(y == 0)
-                def _():
-                    edge = low_edge()
-                    stack(plane, 0, jnp.where(own_y > 0, edge, jnp.zeros_like(edge)))
-
-                @pl.when(y + rows < cells_y)
-                def _():
-                    stack(plane, rows + 1, inside(pl.ds(y + rows, 1)))
-
-                @pl.when(y + rows == cells_y)
-                def _():
-                    edge = high_edge()
-                    last = own_y == shards_y - 1
-                    stack(plane, rows + 1, jnp.where(last, jnp.zeros_like(edge), edge))
-
-            edges = (lambda: front_ref[source + 1], lambda: back_ref[source + 1])
-            if plane == 0:
-
-                @pl.when(source < 0)
-                def _():
-                    fill(lambda at: left_ref[0, at], *edges)
-
-            if plane == width + 1:
-
-                @pl.when(source == cells_x)
-                def _():
-                    fill(lambda at: right_ref[0, at], *edges)
-
-            @pl.when(jnp.logical_and(source >= 0, source < cells_x))
-            def _():
-                inside = jnp.clip(source, 0, cells_x - 1)
-                fill(lambda at: flow_ref[inside, at], *edges)
-
-    none = jnp.zeros(kernel_ref.shape[2:], kernel_ref.dtype)
-    taps = [(a, b) for a in range(width + 2) for b in range(3)]
-
-    def convolve_unit(unit):
-        x, y = lax.div(unit, y_units) * width, lax.rem(unit, y_units) * rows
-        total = jnp.zeros((rows * cells_z, width * channels), jnp.float32)
-        for i in range(0, len(taps), 2):
-            blocks, kernels = [], []
-            for a, b in taps[i : i + 2]:
-                part = stacked[a, pl.ds(b, rows)]
-                blocks.append(part.reshape(rows * cells_z, 3 * channels))
-                parts = [kernel_ref[a - k, b] if 0 <= a - k < 3 else none for k in range(width)]
-                kernels.append(jnp.concatenate(parts, axis=1))
-            total = total + dot(jnp.concatenate(blocks, axis=1), jnp.concatenate(kernels, axis=0))
-        for k in range(width):
-            part = total[:, k * channels : (k + 1) * channels].reshape(rows, cells_z, channels)
-            convolved_ref[x + k, pl.ds(y, rows)] = part.astype(convolved_ref.dtype)
-
-    def both(pair, carry):
-        stack_unit(pair)
-
-        @pl.when(pair + slots - 1 < pairs)
-        def _():
-            copy(pair + slots - 1).start()
-
+    for pair, ref in enumerate(loaded_refs):
+        mix(pair, lambda h, mode, ref=ref: ref[h, mode])
+
+    def streamed(pair, carry):
         copy(pair).wait()
-        convolve_unit(pair)
-        mix(pair, lax.rem(pair, slots))
+        mix(pair, lambda h, mode: held[pair - loaded, h, mode])
         return carry
 
-    shared = min(units, pairs)
-    lax.fori_loop(0, shared, both, 0)
-
-    def only_mix(pair, carry):
-        @pl.when(pair + slots - 1 < pairs)
-        def _():
-            copy(pair + slots - 1).start()
-
-        copy(pair).wait()
-        mix(pair, lax.rem(pair, slots))
-        return carry
-
-    def only_convolve(unit, carry):
-        stack_unit(unit)
-        convolve_unit(unit)
-        return carry
-
-    if shared < pairs:
-        lax.fori_loop(shared, pairs, only_mix, 0)
-    if shared < units:
-        lax.fori_loop(shared, units, only_convolve, 0)
+    lax.fori_loop(loaded, pairs, streamed, 0)
 
     for pair in range(pairs):
         result = dot(backward_ref[...], mixed[pl.ds(pair * span, span), :])
@@ -440,45 +366,111 @@
             out_refs[step][slot] = value.astype(out_refs[step].dtype)
 
 
-def mixing(me, rows, forward_x, backward_x, weight, halos, kernel, shards, shards_y):
+def mixing(me, rows, forward_x, backward_x, weight, loaded, shards):
     outer, inner = shards
     _, cells_x, item_rows, channels = rows[0].shape
-    depth = weight.shape[2]
-    flow = halos[0]
-    _, cells_y, cells_z, _ = flow.shape
     pairs = item_rows // 2
     row_count = outer * inner * cells_x * item_rows
-    slots = 3
-    y_rows = 4 if cells_y % 4 == 0 else 1
-    width = 2 if cells_x % 2 == 0 else 1
     return pl.pallas_call(
-        functools.partial(mixing_kernel, shards, shards_y),
+        functools.partial(mixing_kernel, shards, len(loaded)),
         in_specs=[IN_SMEM]
         + in_vmem(inner + 2)
-        + [pl.BlockSpec(memory_space=pl.ANY)]
-        + in_vmem(len(halos) + 1),
-        out_specs=in_vmem(inner + 1),
-        out_shape=[jax.ShapeDtypeStruct(rows[0].shape, jnp.bfloat16)] * inner
-        + [jax.ShapeDtypeStruct(flow.shape, jnp.bfloat16)],
+        + [pl.BlockSpec(memory_space=pltpu.HBM)]
+        + in_vmem(len(loaded)),
+        out_specs=in_vmem(inner),
+        out_shape=[jax.ShapeDtypeStruct(rows[0].shape, jnp.bfloat16)] * inner,
         scratch_shapes=[
-            pltpu.VMEM((slots, 2, MX, depth, channels), jnp.bfloat16),
-            pltpu.SemaphoreType.DMA((slots,)),
+            pltpu.VMEM((pairs - len(loaded), 2, *weight.shape[1:]), weight.dtype),
+            pltpu.SemaphoreType.DMA((pairs - len(loaded),)),
             pltpu.VMEM((row_count, channels), jnp.float32),
             pltpu.VMEM((pairs * 2 * MX, 2 * channels), jnp.bfloat16),
             pltpu.VMEM((pairs * 2 * MX, channels), jnp.bfloat16),
-            pltpu.VMEM((width + 2, y_rows + 2, cells_z, 3 * channels), jnp.bfloat16),
         ],
-        compiler_params=pltpu.CompilerParams(vmem_limit_bytes=44 << 20),
+        compiler_params=pltpu.CompilerParams(vmem_limit_bytes=36 << 20),
         cost_estimate=pl.CostEstimate(
             flops=8 * weight.size, bytes_accessed=2 * weight.size, transcendentals=0
         ),
-    )(me, *rows, forward_x, backward_x, weight, *halos, kernel)
+    )(me, *rows, forward_x, backward_x, weight, *loaded)
+
+
+def convolution_kernel(x, shards_y, per_y, me_ref, *refs):
+    *plane_refs, front_ref, back_ref, kernel_ref, out_ref, stacked = refs
+    cells_y, cells_z, channels = out_ref.shape
+    own_y = lax.div(me_ref[0], per_y)
+
+    def stack(plane, at, cells):
+        deep = cells.astype(jnp.float32)
+        z = lax.broadcasted_iota(jnp.int32, deep.shape, 1)
+        before = jnp.where(z == 0, 0.0, pltpu.roll(deep, 1, axis=1))
+        after = jnp.where(z == cells_z - 1, 0.0, pltpu.roll(deep, cells_z - 1, axis=1))
+        at = pl.ds(at, cells.shape[0])
+        stacked[plane, at, :, :channels] = before.astype(stacked.dtype)
+        stacked[plane, at, :, channels : 2 * channels] = cells
+        stacked[plane, at, :, 2 * channels :] = after.astype(stacked.dtype)
+
+    rows = 4 if cells_y % 4 == 0 else 1
+    for plane, ref in enumerate(plane_refs):
+
+        def one(step, carry, plane=plane, ref=ref):
+            stack(plane, step * rows + 1, ref[0, pl.ds(step * rows, rows)])
+            return carry
+
+        lax.fori_loop(0, cells_y // rows, one, 0)
+        edge = front_ref[x + plane]
+        stack(plane, 0, jnp.where(own_y > 0, edge, jnp.zeros_like(edge)))
+        edge = back_ref[x + plane]
+        stack(plane, cells_y + 1, jnp.where(own_y < shards_y - 1, edge, jnp.zeros_like(edge)))
+
+    taps = [(a, b) for a in range(3) for b in range(3)]
+
+    def chunk(index, carry):
+        y = index * rows
+        total = jnp.zeros((rows * cells_z, channels), jnp.float32)
+        for a in range(3):
+            blocks, kernels = [], []
+            for b in range(3):
+                part = stacked[a, pl.ds(y + b, rows)]
+                blocks.append(part.reshape(rows * cells_z, 3 * channels))
+                kernels.append(kernel_ref[a, b])
+            total = total + dot(jnp.concatenate(blocks, axis=1), jnp.concatenate(kernels, axis=0))
+        out_ref[pl.ds(y, rows)] = total.reshape(rows, cells_z, channels).astype(out_ref.dtype)
+        return carry
+
+    lax.fori_loop(0, cells_y // rows, chunk, 0)
+
+
+def convolution(me, x, flow, left, right, front, back, kernel, shards_y, per_y):
+    cells_x, cells_y, cells_z, channels = flow.shape
+    specs, planes = [], []
+    for p in (x - 1, x, x + 1):
+        inside = 0 <= p < cells_x
+        planes.append(flow if inside else (left if p < 0 else right))
+        at = p if inside else 0
+        specs.append(
+            pl.BlockSpec((1, cells_y, cells_z, channels), lambda i, at=at: (at, 0, 0, 0))
+        )
+    whole = lambda array: pl.BlockSpec(array.shape, lambda i: (0,) * array.ndim)
+    return pl.pallas_call(
+        functools.partial(convolution_kernel, x, shards_y, per_y),
+        grid=(1,),
+        in_specs=[IN_SMEM] + specs + [whole(front), whole(back), whole(kernel)],
+        out_specs=pl.BlockSpec((cells_y, cells_z, channels), lambda i: (0, 0, 0)),
+        out_shape=jax.ShapeDtypeStruct((cells_y, cells_z, channels), jnp.bfloat16),
+        scratch_shapes=[pltpu.VMEM((3, cells_y + 2, cells_z, 3 * channels), flow.dtype)],
+        compiler_params=pltpu.CompilerParams(vmem_limit_bytes=10 << 20),
+        cost_estimate=pl.CostEstimate(
+            flops=2 * 27 * cells_y * cells_z * channels * channels,
+            bytes_accessed=10 * cells_y * cells_z * channels,
+            transcendentals=0,
+        ),
+    )(me, *planes, front, back, kernel)
 
 
 def final_kernel(shards, shards_y, me_ref, table_ref, *refs):
     outer, inner = shards
-    *piece_refs, convolved_ref, bias_ref, out_ref, held = refs
+    *piece_refs, bias_ref, out_ref, held = refs
     cells_x, cells_y, cells_z, channels = out_ref.shape
+    piece_refs, convolved_refs = piece_refs[:-cells_x], piece_refs[-cells_x:]
     own_y, own_outer, own_inner = place(me_ref[0], shards)
     rows = piece_refs[0].shape[2]
 
@@ -495,47 +487,45 @@
 
     width = 2 if cells_x % 2 == 0 else 1
     bias = bias_ref[...]
+    part = pl.program_id(0)
+    count = cells_y * cells_z
+    table = table_ref[own_y, pl.ds(pl.multiple_of(part * count, count), count), :]
     for x in range(0, cells_x, width):
         columns = [held[x + i] for i in range(width)]
-        total = dot(table_ref[0], jnp.concatenate(columns, axis=1))
+        total = dot(table, jnp.concatenate(columns, axis=1))
         for i in range(width):
             spectral = total[:, i * channels : (i + 1) * channels]
             spectral = spectral.reshape(cells_y, cells_z, channels)
-            value = spectral + convolved_ref[x + i].astype(jnp.float32) + bias
+            convolved = convolved_refs[x + i][pl.ds(part * cells_y, cells_y)]
+            value = spectral + convolved.astype(jnp.float32) + bias
             out_ref[x + i] = jax.nn.gelu(value, approximate=True).astype(out_ref.dtype)
 
 
 def final(me, table, pieces, convolved, bias, shards, shards_y):
-    cells_x, cells_y, cells_z, channels = convolved.shape
+    cells_x = len(convolved)
+    cells_y, cells_z, channels = convolved[0].shape
     parts = 4 if cells_y % 4 == 0 else 1
-    rows = cells_y // parts * cells_z
     block = (cells_x, cells_y // parts, cells_z, channels)
     depth = table.shape[2]
-    outer, inner = shards
     return pl.pallas_call(
         functools.partial(final_kernel, shards, shards_y),
         grid_spec=pltpu.PrefetchScalarGridSpec(
             num_scalar_prefetch=1,
             grid=(parts,),
             in_specs=[
-                pl.BlockSpec(
-                    (1, rows, depth), lambda i, me: (lax.div(me[0], outer * inner), i, 0)
-                ),
-                *in_vmem(len(pieces)),
-                pl.BlockSpec(block, lambda i, me: (0, i, 0, 0)),
-                pl.BlockSpec((1, channels), lambda i, me: (0, 0)),
+                *in_vmem(2 + len(pieces) + cells_x),
             ],
             out_specs=pl.BlockSpec(block, lambda i, me: (0, i, 0, 0)),
             scratch_shapes=[pltpu.VMEM((cells_x, depth, channels), jnp.bfloat16)],
         ),
-        out_shape=jax.ShapeDtypeStruct(convolved.shape, jnp.bfloat16),
-        compiler_params=pltpu.CompilerParams(vmem_limit_bytes=24 << 20),
+        out_shape=jax.ShapeDtypeStruct((cells_x, *convolved[0].shape), jnp.bfloat16),
+        compiler_params=pltpu.CompilerParams(vmem_limit_bytes=10 << 20),
         cost_estimate=pl.CostEstimate(
             flops=2 * table.shape[1] * depth * cells_x * channels,
-            bytes_accessed=6 * convolved.size,
-            transcendentals=convolved.size,
+            bytes_accessed=6 * cells_x * convolved[0].size,
+            transcendentals=cells_x * convolved[0].size,
         ),
-    )(me, table, *pieces, convolved, bias)
+    )(me, table, *pieces, *convolved, bias)
 
 
 def with_halo(array, sides, width):
@@ -693,6 +683,8 @@
     full_x = cells_x * shards_x
     kernel = conv_weight.reshape(3, 3, 3 * channels, channels)
 
+    weight = spectral_weight.reshape(items, MX, channels, channels)
+
     table = jnp.asarray(forward_yz_table(*sizes))
     columns = flow.reshape(cells_x, cells_y * cells_z, channels)
     order = list(range(outer - 1, -1, -1))
@@ -701,41 +693,51 @@
     arrived = [[] for _ in pieces]
     for step in range(1, shards_y):
         sent = forward_yz(me, table, columns, step, shards, shards_y, pieces, jnp.bfloat16)
+        sent, columns, weight = lax.optimization_barrier((sent, columns, weight))
         for into, piece in zip(arrived, sent):
             into.append(over_y(piece, step, shards_y))
-    *kept, first, last = forward_yz(
-        me, table, columns, 0, shards, shards_y, pieces, jnp.float32, edges=True
+    *kept, first, last, low, high = forward_yz(
+        me, table, columns, 0, shards, shards_y, pieces, jnp.float32, edges=cells_z
     )
     first, last = (x.reshape(1, cells_y, cells_z, channels) for x in (first, last))
 
     left, right = neighbours(first, last, "gx")
-    if shards_y == 2:
-        facing = lambda own: jnp.where(own == 0, cells_y - 1, 0)
-        edge = y_edge(me, left, flow, right, shards_x, facing)
-        front = back = over_y(edge, 1, shards_y)
-    else:
-        low = y_edge(me, left, flow, right, shards_x, lambda own: 0)
-        high = y_edge(me, left, flow, right, shards_x, lambda own: cells_y - 1)
-        front, back = neighbours(low, high, "gy")
 
     by_outer = [None] * outer
     for piece, own, parts in zip(pieces, kept, arrived):
         for step, total in zip(piece, add_pieces(own, parts)):
             by_outer[step] = exchange(total, step, shards, True) if step else total
     by_inner = regroup(me, by_outer, shards, True)
+    early = 1 if pairs > 2 else 0
+    loaded = [preload(weight, pair) for pair in range(early)]
+    by_inner, weight = lax.optimization_barrier((by_inner, weight))
     rows = [by_inner[0]] + [exchange(by_inner[s], s, shards, False) for s in range(1, inner)]
-
-    *returned, convolved = mixing(
+    loaded += [preload(weight, pair) for pair in range(early, min(early + 2, pairs - 1))]
+
+
+    returned = mixing(
         me,
         rows,
         jnp.asarray(forward_x_table(full_x)),
         jnp.asarray(backward_x_table(full_x)),
-        spectral_weight.reshape(items, MX, channels, channels),
-        (flow, left, right, front, back),
-        kernel,
+        weight,
+        loaded,
         shards,
-        shards_y,
-    )
+    )
+    returned, left, right = lax.optimization_barrier((returned, left, right))
+    if shards_y == 2:
+        edge = y_edge(me, left, low, high, right, shards_x, lambda own: own > 0)
+        front = back = over_y(edge, 1, shards_y)
+    else:
+        ends = [
+            y_edge(me, left, low, high, right, shards_x, lambda own, use=use: own >= use)
+            for use in (0, shards_y)
+        ]
+        front, back = neighbours(*ends, "gy")
+    planes = (flow, left, right, front, back, kernel)
+    convolved = [
+        convolution(me, x, *planes, shards_y, shards_x) for x in range(cells_x)
+    ]
 
     returned = [returned[0]] + [
         exchange(returned[s], s, shards, False) for s in range(1, inner)

time: 76.4 us -> 73.9 us (0.967)
  Pallas kernels: 23.5 us -> 33.7 us
  waiting for transfers between devices: 17.2 us -> 12.1 us
  local copies, waits for them, and re-layouts: 6.12 us -> 1.27 us
  starting transfers between devices: 29.1 us -> 26.2 us
    pallas_call x2 -> x9, Pallas kernels: 16.9 us -> 27.6 us  [the longest x4 12.4 us: convolution(): pl.pallas_call(functools.partial(convolution_kernel, x, shards_y, per_y),...]
    unnamed x24 -> x16, local copies, waits for them, and re-layouts: 6.12 us -> 1.27 us
    ppermute x7, waiting for transfers between devices: 6.1 us -> 2.04 us  [over_y(): lax.ppermute(array, 'gy', [(i, (i + step) % shards_y) for i in range(shar...]
    ppermute x12, starting transfers between devices: 17.3 us -> 14.7 us  [exchange(): return lax.ppermute(array, 'gx', pairs)]
    ppermute x12, waiting for transfers between devices: 11.1 us -> 10.1 us  [exchange(): return lax.ppermute(array, 'gx', pairs)]
    ppermute x2, starting transfers between devices: 3.65 us -> 2.77 us  [neighbours(): return (lax.ppermute(last, axis, up), lax.ppermute(first, axis, down))]
  transfers between devices with their start and end apart: 21 -> 21, of which waited for: 10 -> 5; matrix products, arithmetic and copies ran while one was open for 0% -> 0% of each run, Pallas kernels for 5% -> 38%
where the time goes in v5:
time: 73.9 us; the launch traced here: 73.6 us
  Pallas kernels  33.7 us (46%)
  starting transfers between devices  26.2 us (35%)
  waiting for transfers between devices  12.1 us (16%)
  local copies, waits for them, and re-layouts  1.27 us (2%)
    ppermute x12, starting transfers between devices, exchange(): return lax.ppermute(array, 'gx', pairs)  14.7 us
    pallas_call x4, Pallas kernels, convolution(): pl.pallas_call(functools.partial(convolution_kernel, x, shards_y, per_y),...  12.4 us
    ppermute x12, waiting for transfers between devices, exchange(): return lax.ppermute(array, 'gx', pairs)  10.1 us
    ppermute x7, starting transfers between devices, over_y(): lax.ppermute(array, 'gy', [(i, (i + step) % shards_y) for i in range(shar...  8.71 us
    pallas_call x1, Pallas kernels, mixing(): pl.pallas_call(functools.partial(mixing_kernel, shards, len(loaded)), in_...  8.57 us
    pallas_call x3, Pallas kernels, preload(): pl.pallas_call(functools.partial(preload_kernel, pair), in_specs=[pl.Bloc...  6.62 us
    pallas_call x2, Pallas kernels, forward_yz(): pl.pallas_call(functools.partial(forward_kernel, shards, pieces, edges),...  3.06 us
    pallas_call x1, Pallas kernels, final(): pl.pallas_call(functools.partial(final_kernel, shards, shards_y), grid_sp...  2.95 us
  transfers between devices with their start and end apart: 21, of which 5 were waited for; matrix products, arithmetic and copies ran while one was open for 0% of the time, Pallas kernels for 38%

profile of v5, /device:TPU:0, one launch (start us, length us, event | category | flops | bytes accessed | tf_op | source)
XLA Modules:
  0.0 73.6 jit_solution(272399545206077436)
XLA Ops:
  0.0 2.6 %shard_map.82 = (bf16[2,4,4,16,128]{4,3,2,1,0:T(8,128)(2,1)}, bf16[2,4,4,16,128]{4,3,2,1,0:T(8,128)(2,1)}) custom-call(s32[1]{0:T(128)} %bitcast.me_ref, bf16[2,512,1024]{2,1,0:T(8,128)(2,1)} %constant.18.clone.table_ref, bf16[4,1024,128]{2,1,0:T(8,128)(2,1)} %bitcast.7), custom_call_target="tpu_custom_call" | custom-call | flops 268435456 | bytes 1572864 | tf_op jit(solution)/shard_map/pallas_call | solution.py:164
  2.6 3.0 %collective-permute-start = (bf16[2,4,4,16,128]{4,3,2,1,0:T(8,128)(2,1)}, bf16[2,4,4,16,128]{4,3,2,1,0:T(8,128)(2,1)S(1)}, u32[]{:S(2)}, u32[]{:S(2)}) collective-permute-start(bf16[2,4,4,16,128]{4,3,2,1,0:T(8,128)(2,1)} %get-tuple-element.48), channel_id=1, source_target_pairs={{0,1},{1,0},{2,3},{3,2},{4,5},{5,4},{6,7},{7,6},{8,9},{9,8},{10,11... | collective-permute-start | bytes 393224 | tf_op jit(solution)/shard_map/ppermute | solution.py:665
  5.6 0.0 collective-permute-start.2
  5.6 1.2 %copy-done = bf16[4,16,64,128]{3,2,1,0:T(8,128)(2,1)S(1)} copy-done((bf16[4,16,64,128]{3,2,1,0:T(8,128)(2,1)S(1)}, bf16[4,16,64,128]{3,2,1,0:T(8,128)(2,1)}, u32[]{:S(2)}) %copy-start) | copy-done | bytes 1048600
  6.9 0.4 shard_map.83
  7.3 1.5 %collective-permute-start.8 = (bf16[1,16,64,128]{3,2,1,0:T(8,128)(2,1)S(1)}, bf16[1,16,64,128]{3,2,1,0:T(8,128)(2,1)S(1)}, u32[]{:S(2)}, u32[]{:S(2)}) collective-permute-start(bf16[1,16,64,128]{3,2,1,0:T(8,128)(2,1)S(1)} %bitcast.15), channel_id=1, source_target_pairs={{0,2},{2,4},{4,6},{6,8},{8,10},{10,12},{12,14},{14,16},{16,18},{18... | collective-permute-start | bytes 786440 | tf_op jit(solution)/shard_map/ppermute | solution.py:650
  8.8 1.3 %collective-permute-start.9 = (bf16[1,16,64,128]{3,2,1,0:T(8,128)(2,1)S(1)}, bf16[1,16,64,128]{3,2,1,0:T(8,128)(2,1)S(1)}, u32[]{:S(2)}, u32[]{:S(2)}) collective-permute-start(bf16[1,16,64,128]{3,2,1,0:T(8,128)(2,1)S(1)} %bitcast.14), channel_id=1, source_target_pairs={{2,0},{4,2},{6,4},{8,6},{10,8},{12,10},{14,12},{16,14},{18,16},{20... | collective-permute-start | bytes 786440 | tf_op jit(solution)/shard_map/ppermute | solution.py:650
  10.1 2.0 %collective-permute-done.2.refs_1_ = bf16[2,4,4,16,128]{4,3,2,1,0:T(8,128)(2,1)S(1)} collective-permute-done((bf16[2,4,4,16,128]{4,3,2,1,0:T(8,128)(2,1)}, bf16[2,4,4,16,128]{4,3,2,1,0:T(8,128)(2,1)S(1)}, u32[]{:S(2)}, u32[]{:S(2)}) %collective-permute-start.2) | collective-permute-done | bytes 131104 | tf_op jit(solution)/shard_map/ppermute | solution.py:665
  12.1 4.8 %collective-permute-start.3 = (bf16[4,4,16,128]{3,2,1,0:T(8,128)(2,1)S(1)}, bf16[4,4,16,128]{3,2,1,0:T(8,128)(2,1)S(1)}, u32[]{:S(2)}, u32[]{:S(2)}) collective-permute-start(bf16[4,4,16,128]{3,2,1,0:T(8,128)(2,1)S(1)} %get-tuple-element.53), channel_id=1, source_target_pairs={{0,16},{2,18},{4,20},{6,22},{8,24},{10,26},{12,28},{14,30},{16,0},... | collective-permute-start | bytes 196616 | tf_op jit(solution)/shard_map/ppermute | solution.py:661
  17.0 1.3 %collective-permute-start.4 = (bf16[4,4,16,128]{3,2,1,0:T(8,128)(2,1)S(1)}, bf16[4,4,16,128]{3,2,1,0:T(8,128)(2,1)S(1)}, u32[]{:S(2)}, u32[]{:S(2)}) collective-permute-start(bf16[4,4,16,128]{3,2,1,0:T(8,128)(2,1)S(1)} %get-tuple-element.54), channel_id=1, source_target_pairs={{0,24},{2,26},{4,28},{6,30},{8,16},{10,18},{12,20},{14,22},{16,8},... | collective-permute-start | bytes 196616 | tf_op jit(solution)/shard_map/ppermute | solution.py:661
  18.3 0.3 collective-permute-start.1
  18.6 4.8 %collective-permute-done.3.refs_2_ = bf16[4,4,16,128]{3,2,1,0:T(8,128)(2,1)S(1)} collective-permute-done((bf16[4,4,16,128]{3,2,1,0:T(8,128)(2,1)S(1)}, bf16[4,4,16,128]{3,2,1,0:T(8,128)(2,1)S(1)}, u32[]{:S(2)}, u32[]{:S(2)}) %collective-permute-start.3) | collective-permute-done | bytes 65568 | tf_op jit(solution)/shard_map/ppermute | solution.py:661
  23.5 1.6 %collective-permute-done.4.refs_3_ = bf16[4,4,16,128]{3,2,1,0:T(8,128)(2,1)S(1)} collective-permute-done((bf16[4,4,16,128]{3,2,1,0:T(8,128)(2,1)S(1)}, bf16[4,4,16,128]{3,2,1,0:T(8,128)(2,1)S(1)}, u32[]{:S(2)}, u32[]{:S(2)}) %collective-permute-start.4) | collective-permute-done | bytes 65568 | tf_op jit(solution)/shard_map/ppermute | solution.py:661
  25.1 0.0 collective-permute-done.1.refs_1_
  25.1 0.1 collective-permute-start.5
  25.2 0.1 collective-permute-start.6
  25.3 1.8 %collective-permute-start.7 = (bf16[4,4,16,128]{3,2,1,0:T(8,128)(2,1)S(1)}, bf16[4,4,16,128]{3,2,1,0:T(8,128)(2,1)S(1)}, u32[]{:S(2)}, u32[]{:S(2)}) collective-permute-start(bf16[4,4,16,128]{3,2,1,0:T(8,128)(2,1)S(1)} %get-tuple-element.63), channel_id=1, source_target_pairs={{0,6},{2,4},{4,2},{6,0},{8,14},{10,12},{12,10},{14,8},{16,22},{18,... | collective-permute-start | bytes 196616 | tf_op jit(solution)/shard_map/ppermute | solution.py:661
  27.1 2.2 %shard_map.87.refs_7_ = bf16[2,64,128,128]{3,2,1,0:T(8,128)(2,1)S(1)} custom-call(bf16[16,64,128,128]{3,2,1,0:T(8,128)(2,1)} %bitcast.16), custom_call_target="tpu_custom_call" | custom-call | bytes 4194304 | tf_op jit(solution)/shard_map/pallas_call | solution.py:265
  29.3 2.2 %shard_map.89.refs_9_ = bf16[2,64,128,128]{3,2,1,0:T(8,128)(2,1)S(1)} custom-call(bf16[16,64,128,128]{3,2,1,0:T(8,128)(2,1)} %bitcast.17), custom_call_target="tpu_custom_call" | custom-call | bytes 4194304 | tf_op jit(solution)/shard_map/pallas_call | solution.py:265
  31.5 0.0 copy-start.5
  31.5 0.0 copy-start.6
  31.5 2.2 %shard_map.88.refs_8_ = bf16[2,64,128,128]{3,2,1,0:T(8,128)(2,1)S(1)} custom-call(bf16[16,64,128,128]{3,2,1,0:T(8,128)(2,1)} %bitcast.18), custom_call_target="tpu_custom_call" | custom-call | bytes 4194304 | tf_op jit(solution)/shard_map/pallas_call | solution.py:265
  33.7 0.0 copy-start.1
  33.7 0.0 copy-start.2
  33.8 0.0 collective-permute-done.6.refs_2_
  33.8 0.0 collective-permute-done.7.refs_3_
  33.8 8.6 %shard_map.90 = (bf16[4,4,16,128]{3,2,1,0:T(8,128)(2,1)S(1)}, bf16[4,4,16,128]{3,2,1,0:T(8,128)(2,1)S(1)}, bf16[4,4,16,128]{3,2,1,0:T(8,128)(2,1)S(1)}, bf16[4,4,16,128]{3,2,1,0:T(8,128)(2,1)S(1)}) custom-call(s32[1]{0:T(128)} %bitcast.me_ref, bf16[4,4,16,128]{3,2,1,0:T(8,128)(2,1)S(1)} %get-tuple-element.60.refs_0_, ...), custom_call_target="tpu_custom_call" | custom-call | flops 134217728 | bytes 33554432 | tf_op jit(solution)/shard_map/pallas_call | solution.py:374
  42.4 0.0 collective-permute-done.8.left_ref.refs_0_
  42.4 1.6 %collective-permute-start.20 = (bf16[6,1,64,128]{3,2,1,0:T(8,128)(2,1)S(1)}, bf16[6,1,64,128]{3,2,1,0:T(8,128)(2,1)S(1)}, u32[]{:S(2)}, u32[]{:S(2)}) collective-permute-start(bf16[6,1,64,128]{3,2,1,0:T(8,128)(2,1)S(1)} %shard_map.92), channel_id=1, source_target_pairs={{0,1},{1,0},{2,3},{3,2},{4,5},{5,4},{6,7},{7,6},{8,9},{9,8},{10,11... | collective-permute-start | bytes 294920 | tf_op jit(solution)/shard_map/ppermute | solution.py:665
  44.0 0.1 collective-permute-start.10
  44.1 0.2 collective-permute-start.11
  44.3 1.6 %collective-permute-start.12 = (bf16[4,4,16,128]{3,2,1,0:T(8,128)(2,1)S(1)}, bf16[4,4,16,128]{3,2,1,0:T(8,128)(2,1)S(1)}, u32[]{:S(2)}, u32[]{:S(2)}) collective-permute-start(bf16[4,4,16,128]{3,2,1,0:T(8,128)(2,1)S(1)} %get-tuple-element.74), channel_id=1, source_target_pairs={{0,6},{2,4},{4,2},{6,0},{8,14},{10,12},{12,10},{14,8},{16,22},{18,... | collective-permute-start | bytes 196616 | tf_op jit(solution)/shard_map/ppermute | solution.py:661
  45.9 3.1 %collective-permute-done.11.refs_2_ = bf16[4,4,16,128]{3,2,1,0:T(8,128)(2,1)S(1)} collective-permute-done((bf16[4,4,16,128]{3,2,1,0:T(8,128)(2,1)S(1)}, bf16[4,4,16,128]{3,2,1,0:T(8,128)(2,1)S(1)}, u32[]{:S(2)}, u32[]{:S(2)}) %collective-permute-start.11) | collective-permute-done | bytes 65568 | tf_op jit(solution)/shard_map/ppermute | solution.py:661
  49.0 0.5 collective-permute-done.12.refs_3_
  49.5 1.1 %collective-permute-start.13 = (bf16[4,4,16,128]{3,2,1,0:T(8,128)(2,1)S(1)}, bf16[4,4,16,128]{3,2,1,0:T(8,128)(2,1)S(1)}, u32[]{:S(2)}, u32[]{:S(2)}) collective-permute-start(bf16[4,4,16,128]{3,2,1,0:T(8,128)(2,1)S(1)} %get-tuple-element.76), channel_id=1, source_target_pairs={{0,8},{2,10},{4,12},{6,14},{8,0},{10,2},{12,4},{14,6},{16,24},{18,... | collective-permute-start | bytes 196616 | tf_op jit(solution)/shard_map/ppermute | solution.py:661
  50.6 0.2 collective-permute-start.14
  50.8 3.1 %collective-permute-start.15 = (bf16[4,4,16,128]{3,2,1,0:T(8,128)(2,1)S(1)}, bf16[4,4,16,128]{3,2,1,0:T(8,128)(2,1)S(1)}, u32[]{:S(2)}, u32[]{:S(2)}) collective-permute-start(bf16[4,4,16,128]{3,2,1,0:T(8,128)(2,1)S(1)} %get-tuple-element.78), channel_id=1, source_target_pairs={{0,24},{2,26},{4,28},{6,30},{8,16},{10,18},{12,20},{14,22},{16,8},... | collective-permute-start | bytes 196616 | tf_op jit(solution)/shard_map/ppermute | solution.py:661
  54.0 0.5 collective-permute-start.16
  54.5 3.1 %shard_map.96.refs_11_ = bf16[16,64,128]{2,1,0:T(8,128)(2,1)S(1)} custom-call(s32[1]{0:T(128)} %bitcast.me_ref, bf16[4,16,64,128]{3,2,1,0:T(8,128)(2,1)S(1)} %copy-done.1, bf16[4,16,64,128]{3,2,1,0:T(8,128)(2,1)S(1)} %copy-done.1, bf16[1,16,64,128]{3,2,1,0:T(8,128)(2,1)S(1)} %collective-permute-done.9.right_ref.refs_2_, ...), custom_call_target="tpu_custom_call" | custom-call | flops 905969664 | bytes 1310720 | tf_op jit(solution)/shard_map/pallas_call | solution.py:453
  57.6 3.1 %shard_map.93.refs_8_ = bf16[16,64,128]{2,1,0:T(8,128)(2,1)S(1)} custom-call(s32[1]{0:T(128)} %bitcast.me_ref, bf16[1,16,64,128]{3,2,1,0:T(8,128)(2,1)S(1)} %collective-permute-done.8.left_ref.refs_0_, bf16[4,16,64,128]{3,2,1,0:T(8,128)(2,1)S(1)} %copy-done.1, bf16[4,16,64,128]{3,2,1,0:T(8,128)(2,1)S(1)} %copy-done.1, ...), custom_call_target="tpu_custom_call" | custom-call | flops 905969664 | bytes 1310720 | tf_op jit(solution)/shard_map/pallas_call | solution.py:453
  60.7 0.0 copy-start.4
  60.7 0.0 copy-start.7
  60.7 3.1 %shard_map.95.refs_10_ = bf16[16,64,128]{2,1,0:T(8,128)(2,1)S(1)} custom-call(s32[1]{0:T(128)} %bitcast.me_ref, bf16[4,16,64,128]{3,2,1,0:T(8,128)(2,1)S(1)} %copy-done.1, bf16[4,16,64,128]{3,2,1,0:T(8,128)(2,1)S(1)} %copy-done.1, bf16[4,16,64,128]{3,2,1,0:T(8,128)(2,1)S(1)} %copy-done.1, ...), custom_call_target="tpu_custom_call" | custom-call | flops 905969664 | bytes 1310720 | tf_op jit(solution)/shard_map/pallas_call | solution.py:453
  63.8 1.6 %collective-permute-start.17 = (bf16[4,4,16,128]{3,2,1,0:T(8,128)(2,1)S(1)}, bf16[4,4,16,128]{3,2,1,0:T(8,128)(2,1)S(1)}, u32[]{:S(2)}, u32[]{:S(2)}) collective-permute-start(bf16[4,4,16,128]{3,2,1,0:T(8,128)(2,1)S(1)} %collective-permute-done.13.refs_1_), channel_id=1, source_target_pairs={{0,1},{1,0},{2,3},{3,2},{4,5},{5,4},{6,7},{7,6},{8,9},{9,8},{10,11... | collective-permute-start | bytes 196616 | tf_op jit(solution)/shard_map/ppermute | solution.py:665
  65.4 0.5 collective-permute-start.18
  65.9 1.5 %collective-permute-start.19 = (bf16[4,4,16,128]{3,2,1,0:T(8,128)(2,1)S(1)}, bf16[4,4,16,128]{3,2,1,0:T(8,128)(2,1)S(1)}, u32[]{:S(2)}, u32[]{:S(2)}) collective-permute-start(bf16[4,4,16,128]{3,2,1,0:T(8,128)(2,1)S(1)} %collective-permute-done.15.refs_3_), channel_id=1, source_target_pairs={{0,1},{1,0},{2,3},{3,2},{4,5},{5,4},{6,7},{7,6},{8,9},{9,8},{10,11... | collective-permute-start | bytes 196616 | tf_op jit(solution)/shard_map/ppermute | solution.py:665
  67.5 3.1 %shard_map.94.refs_9_ = bf16[16,64,128]{2,1,0:T(8,128)(2,1)S(1)} custom-call(s32[1]{0:T(128)} %bitcast.me_ref, bf16[4,16,64,128]{3,2,1,0:T(8,128)(2,1)S(1)} %copy-done.1, bf16[4,16,64,128]{3,2,1,0:T(8,128)(2,1)S(1)} %copy-done.1, bf16[4,16,64,128]{3,2,1,0:T(8,128)(2,1)S(1)} %copy-done.1, bf16[6,1,64,128]{3,2,1,0:T(8,128)(2,1)S(1)} %collective-permute-done.20.refs_3_.refs_4_, ...), custom_call_target="tpu_custom_call" | custom-call | flops 905969664 | bytes 1310720 | tf_op jit(solution)/shard_map/pallas_call | solution.py:453
  70.6 2.9 %shard_map.97 = bf16[4,16,64,128]{3,2,1,0:T(8,128)(2,1)} custom-call(s32[1]{0:T(128)} %bitcast.me_ref, bf16[2,1024,512]{2,1,0:T(8,128)(2,1)S(1)} %copy-done.4, bf16[4,4,16,128]{3,2,1,0:T(8,128)(2,1)S(1)} %get-tuple-element.75.refs_0_, bf16[4,4,16,128]{3,2,1,0:T(8,128)(2,1)S(1)} %collective-permute-done.13.refs_1_, ...), custom_call_target="tpu_custom_call" | custom-call | flops 536870912 | bytes 3145728 | tf_op jit(solution)/shard_map/pallas_call | solution.py:510
  (26 shorter events, 0.2 us)
Async XLA Ops:
  0.0 5.6 %copy-start.3 = (bf16[2,512,1024]{2,1,0:T(8,128)(2,1)S(1)}, bf16[2,512,1024]{2,1,0:T(8,128)(2,1)}, u32[]{:S(2)}) copy-start(bf16[2,512,1024]{2,1,0:T(8,128)(2,1)} %constant.18.clone.table_ref) | copy-start | bytes 6291460
  2.6 15.7 %collective-permute-start = (bf16[2,4,4,16,128]{4,3,2,1,0:T(8,128)(2,1)}, bf16[2,4,4,16,128]{4,3,2,1,0:T(8,128)(2,1)S(1)}, u32[]{:S(2)}, u32[]{:S(2)}) collective-permute-start(bf16[2,4,4,16,128]{4,3,2,1,0:T(8,128)(2,1)} %get-tuple-element.48), channel_id=1, source_target_pairs={{0,1},{1,0},{2,3},{3,2},{4,5},{5,4},{6,7},{7,6},{8,9},{9,8},{10,11... | collective-permute-start | bytes 393224 | tf_op jit(solution)/shard_map/ppermute | solution.py:665
  5.6 6.5 %collective-permute-start.2 = (bf16[2,4,4,16,128]{4,3,2,1,0:T(8,128)(2,1)}, bf16[2,4,4,16,128]{4,3,2,1,0:T(8,128)(2,1)S(1)}, u32[]{:S(2)}, u32[]{:S(2)}) collective-permute-start(bf16[2,4,4,16,128]{4,3,2,1,0:T(8,128)(2,1)} %get-tuple-element.52), channel_id=1, source_target_pairs={{0,1},{1,0},{2,3},{3,2},{4,5},{5,4},{6,7},{7,6},{8,9},{9,8},{10,11... | collective-permute-start | bytes 393224 | tf_op jit(solution)/shard_map/ppermute | solution.py:665
  5.6 1.2 %copy-start = (bf16[4,16,64,128]{3,2,1,0:T(8,128)(2,1)S(1)}, bf16[4,16,64,128]{3,2,1,0:T(8,128)(2,1)}, u32[]{:S(2)}) copy-start(bf16[4,16,64,128]{3,2,1,0:T(8,128)(2,1)} %refs_1_.7) | copy-start | bytes 3145732
  7.3 35.1 %collective-permute-start.8 = (bf16[1,16,64,128]{3,2,1,0:T(8,128)(2,1)S(1)}, bf16[1,16,64,128]{3,2,1,0:T(8,128)(2,1)S(1)}, u32[]{:S(2)}, u32[]{:S(2)}) collective-permute-start(bf16[1,16,64,128]{3,2,1,0:T(8,128)(2,1)S(1)} %bitcast.15), channel_id=1, source_target_pairs={{0,2},{2,4},{4,6},{6,8},{8,10},{10,12},{12,14},{14,16},{16,18},{18... | collective-permute-start | bytes 786440 | tf_op jit(solution)/shard_map/ppermute | solution.py:650
  8.8 33.6 %collective-permute-start.9 = (bf16[1,16,64,128]{3,2,1,0:T(8,128)(2,1)S(1)}, bf16[1,16,64,128]{3,2,1,0:T(8,128)(2,1)S(1)}, u32[]{:S(2)}, u32[]{:S(2)}) collective-permute-start(bf16[1,16,64,128]{3,2,1,0:T(8,128)(2,1)S(1)} %bitcast.14), channel_id=1, source_target_pairs={{2,0},{4,2},{6,4},{8,6},{10,8},{12,10},{14,12},{16,14},{18,16},{20... | collective-permute-start | bytes 786440 | tf_op jit(solution)/shard_map/ppermute | solution.py:650
  12.1 11.3 %collective-permute-start.3 = (bf16[4,4,16,128]{3,2,1,0:T(8,128)(2,1)S(1)}, bf16[4,4,16,128]{3,2,1,0:T(8,128)(2,1)S(1)}, u32[]{:S(2)}, u32[]{:S(2)}) collective-permute-start(bf16[4,4,16,128]{3,2,1,0:T(8,128)(2,1)S(1)} %get-tuple-element.53), channel_id=1, source_target_pairs={{0,16},{2,18},{4,20},{6,22},{8,24},{10,26},{12,28},{14,30},{16,0},... | collective-permute-start | bytes 196616 | tf_op jit(solution)/shard_map/ppermute | solution.py:661
  17.0 8.1 %collective-permute-start.4 = (bf16[4,4,16,128]{3,2,1,0:T(8,128)(2,1)S(1)}, bf16[4,4,16,128]{3,2,1,0:T(8,128)(2,1)S(1)}, u32[]{:S(2)}, u32[]{:S(2)}) collective-permute-start(bf16[4,4,16,128]{3,2,1,0:T(8,128)(2,1)S(1)} %get-tuple-element.54), channel_id=1, source_target_pairs={{0,24},{2,26},{4,28},{6,30},{8,16},{10,18},{12,20},{14,22},{16,8},... | collective-permute-start | bytes 196616 | tf_op jit(solution)/shard_map/ppermute | solution.py:661
  18.3 6.8 %collective-permute-start.1 = (bf16[4,4,16,128]{3,2,1,0:T(8,128)(2,1)S(1)}, bf16[4,4,16,128]{3,2,1,0:T(8,128)(2,1)S(1)}, u32[]{:S(2)}, u32[]{:S(2)}) collective-permute-start(bf16[4,4,16,128]{3,2,1,0:T(8,128)(2,1)S(1)} %get-tuple-element.50), channel_id=1, source_target_pairs={{0,8},{2,10},{4,12},{6,14},{8,0},{10,2},{12,4},{14,6},{16,24},{18,... | collective-permute-start | bytes 196616 | tf_op jit(solution)/shard_map/ppermute | solution.py:661
  25.1 8.6 %collective-permute-start.5 = (bf16[4,4,16,128]{3,2,1,0:T(8,128)(2,1)S(1)}, bf16[4,4,16,128]{3,2,1,0:T(8,128)(2,1)S(1)}, u32[]{:S(2)}, u32[]{:S(2)}) collective-permute-start(bf16[4,4,16,128]{3,2,1,0:T(8,128)(2,1)S(1)} %get-tuple-element.61), channel_id=1, source_target_pairs={{0,2},{2,0},{4,6},{6,4},{8,10},{10,8},{12,14},{14,12},{16,18},{18,... | collective-permute-start | bytes 196616 | tf_op jit(solution)/shard_map/ppermute | solution.py:661
  25.2 8.6 %collective-permute-start.6 = (bf16[4,4,16,128]{3,2,1,0:T(8,128)(2,1)S(1)}, bf16[4,4,16,128]{3,2,1,0:T(8,128)(2,1)S(1)}, u32[]{:S(2)}, u32[]{:S(2)}) collective-permute-start(bf16[4,4,16,128]{3,2,1,0:T(8,128)(2,1)S(1)} %get-tuple-element.62), channel_id=1, source_target_pairs={{0,4},{2,6},{4,0},{6,2},{8,12},{10,14},{12,8},{14,10},{16,20},{18,... | collective-permute-start | bytes 196616 | tf_op jit(solution)/shard_map/ppermute | solution.py:661
  25.3 8.5 %collective-permute-start.7 = (bf16[4,4,16,128]{3,2,1,0:T(8,128)(2,1)S(1)}, bf16[4,4,16,128]{3,2,1,0:T(8,128)(2,1)S(1)}, u32[]{:S(2)}, u32[]{:S(2)}) collective-permute-start(bf16[4,4,16,128]{3,2,1,0:T(8,128)(2,1)S(1)} %get-tuple-element.63), channel_id=1, source_target_pairs={{0,6},{2,4},{4,2},{6,0},{8,14},{10,12},{12,10},{14,8},{16,22},{18,... | collective-permute-start | bytes 196616 | tf_op jit(solution)/shard_map/ppermute | solution.py:661
  31.5 2.3 %copy-start.5 = (bf16[256,128]{1,0:T(8,128)(2,1)S(1)}, bf16[256,128]{1,0:T(8,128)(2,1)}, u32[]{:S(2)}) copy-start(bf16[256,128]{1,0:T(8,128)(2,1)} %constant.19.clone.refs_4_) | copy-start | bytes 196612
  31.5 2.3 %copy-start.6 = (bf16[128,128]{1,0:T(8,128)(2,1)S(1)}, bf16[128,128]{1,0:T(8,128)(2,1)}, u32[]{:S(2)}) copy-start(bf16[128,128]{1,0:T(8,128)(2,1)} %constant.20.clone.refs_5_) | copy-start | bytes 98308
  33.7 20.7 %copy-start.1 = (bf16[4,16,64,128]{3,2,1,0:T(8,128)(2,1)S(1)}, bf16[4,16,64,128]{3,2,1,0:T(8,128)(2,1)}, u32[]{:S(2)}) copy-start(bf16[4,16,64,128]{3,2,1,0:T(8,128)(2,1)} %refs_1_.7) | copy-start | bytes 3145732
  33.7 20.7 %copy-start.2 = (bf16[3,3,3,128,128]{4,3,2,1,0:T(8,128)(2,1)S(1)}, bf16[3,3,3,128,128]{4,3,2,1,0:T(8,128)(2,1)}, u32[]{:S(2)}) copy-start(bf16[3,3,3,128,128]{4,3,2,1,0:T(8,128)(2,1)} %param.10) | copy-start | bytes 2654212
  42.4 12.0 %collective-permute-start.20 = (bf16[6,1,64,128]{3,2,1,0:T(8,128)(2,1)S(1)}, bf16[6,1,64,128]{3,2,1,0:T(8,128)(2,1)S(1)}, u32[]{:S(2)}, u32[]{:S(2)}) collective-permute-start(bf16[6,1,64,128]{3,2,1,0:T(8,128)(2,1)S(1)} %shard_map.92), channel_id=1, source_target_pairs={{0,1},{1,0},{2,3},{3,2},{4,5},{5,4},{6,7},{7,6},{8,9},{9,8},{10,11... | collective-permute-start | bytes 294920 | tf_op jit(solution)/shard_map/ppermute | solution.py:665
  44.0 1.9 %collective-permute-start.10 = (bf16[4,4,16,128]{3,2,1,0:T(8,128)(2,1)S(1)}, bf16[4,4,16,128]{3,2,1,0:T(8,128)(2,1)S(1)}, u32[]{:S(2)}, u32[]{:S(2)}) collective-permute-start(bf16[4,4,16,128]{3,2,1,0:T(8,128)(2,1)S(1)} %get-tuple-element.72), channel_id=1, source_target_pairs={{0,2},{2,0},{4,6},{6,4},{8,10},{10,8},{12,14},{14,12},{16,18},{18,... | collective-permute-start | bytes 196616 | tf_op jit(solution)/shard_map/ppermute | solution.py:661
  44.1 4.9 %collective-permute-start.11 = (bf16[4,4,16,128]{3,2,1,0:T(8,128)(2,1)S(1)}, bf16[4,4,16,128]{3,2,1,0:T(8,128)(2,1)S(1)}, u32[]{:S(2)}, u32[]{:S(2)}) collective-permute-start(bf16[4,4,16,128]{3,2,1,0:T(8,128)(2,1)S(1)} %get-tuple-element.73), channel_id=1, source_target_pairs={{0,4},{2,6},{4,0},{6,2},{8,12},{10,14},{12,8},{14,10},{16,20},{18,... | collective-permute-start | bytes 196616 | tf_op jit(solution)/shard_map/ppermute | solution.py:661
  44.3 5.2 %collective-permute-start.12 = (bf16[4,4,16,128]{3,2,1,0:T(8,128)(2,1)S(1)}, bf16[4,4,16,128]{3,2,1,0:T(8,128)(2,1)S(1)}, u32[]{:S(2)}, u32[]{:S(2)}) collective-permute-start(bf16[4,4,16,128]{3,2,1,0:T(8,128)(2,1)S(1)} %get-tuple-element.74), channel_id=1, source_target_pairs={{0,6},{2,4},{4,2},{6,0},{8,14},{10,12},{12,10},{14,8},{16,22},{18,... | collective-permute-start | bytes 196616 | tf_op jit(solution)/shard_map/ppermute | solution.py:661
  49.5 14.3 %collective-permute-start.13 = (bf16[4,4,16,128]{3,2,1,0:T(8,128)(2,1)S(1)}, bf16[4,4,16,128]{3,2,1,0:T(8,128)(2,1)S(1)}, u32[]{:S(2)}, u32[]{:S(2)}) collective-permute-start(bf16[4,4,16,128]{3,2,1,0:T(8,128)(2,1)S(1)} %get-tuple-element.76), channel_id=1, source_target_pairs={{0,8},{2,10},{4,12},{6,14},{8,0},{10,2},{12,4},{14,6},{16,24},{18,... | collective-permute-start | bytes 196616 | tf_op jit(solution)/shard_map/ppermute | solution.py:661
  50.6 14.8 %collective-permute-start.14 = (bf16[4,4,16,128]{3,2,1,0:T(8,128)(2,1)S(1)}, bf16[4,4,16,128]{3,2,1,0:T(8,128)(2,1)S(1)}, u32[]{:S(2)}, u32[]{:S(2)}) collective-permute-start(bf16[4,4,16,128]{3,2,1,0:T(8,128)(2,1)S(1)} %get-tuple-element.77), channel_id=1, source_target_pairs={{0,16},{2,18},{4,20},{6,22},{8,24},{10,26},{12,28},{14,30},{16,0},... | collective-permute-start | bytes 196616 | tf_op jit(solution)/shard_map/ppermute | solution.py:661
  50.8 15.1 %collective-permute-start.15 = (bf16[4,4,16,128]{3,2,1,0:T(8,128)(2,1)S(1)}, bf16[4,4,16,128]{3,2,1,0:T(8,128)(2,1)S(1)}, u32[]{:S(2)}, u32[]{:S(2)}) collective-permute-start(bf16[4,4,16,128]{3,2,1,0:T(8,128)(2,1)S(1)} %get-tuple-element.78), channel_id=1, source_target_pairs={{0,24},{2,26},{4,28},{6,30},{8,16},{10,18},{12,20},{14,22},{16,8},... | collective-permute-start | bytes 196616 | tf_op jit(solution)/shard_map/ppermute | solution.py:661
  54.0 16.6 %collective-permute-start.16 = (bf16[4,4,16,128]{3,2,1,0:T(8,128)(2,1)S(1)}, bf16[4,4,16,128]{3,2,1,0:T(8,128)(2,1)S(1)}, u32[]{:S(2)}, u32[]{:S(2)}) collective-permute-start(bf16[4,4,16,128]{3,2,1,0:T(8,128)(2,1)S(1)} %get-tuple-element.75.refs_0_), channel_id=1, source_target_pairs={{0,1},{1,0},{2,3},{3,2},{4,5},{5,4},{6,7},{7,6},{8,9},{9,8},{10,11... | collective-permute-start | bytes 196616 | tf_op jit(solution)/shard_map/ppermute | solution.py:665
  60.7 9.9 %copy-start.4 = (bf16[2,1024,512]{2,1,0:T(8,128)(2,1)S(1)}, bf16[2,1024,512]{2,1,0:T(8,128)(2,1)}, u32[]{:S(2)}) copy-start(bf16[2,1024,512]{2,1,0:T(8,128)(2,1)} %constant.21.clone.table_ref) | copy-start | bytes 6291460
  60.7 9.9 %copy-start.7 = (f32[128]{0:T(128)S(1)}, f32[128]{0:T(128)}, u32[]{:S(2)}) copy-start(f32[128]{0:T(128)} %param.11) | copy-start | bytes 1540
  63.8 6.7 %collective-permute-start.17 = (bf16[4,4,16,128]{3,2,1,0:T(8,128)(2,1)S(1)}, bf16[4,4,16,128]{3,2,1,0:T(8,128)(2,1)S(1)}, u32[]{:S(2)}, u32[]{:S(2)}) collective-permute-start(bf16[4,4,16,128]{3,2,1,0:T(8,128)(2,1)S(1)} %collective-permute-done.13.refs_1_), channel_id=1, source_target_pairs={{0,1},{1,0},{2,3},{3,2},{4,5},{5,4},{6,7},{7,6},{8,9},{9,8},{10,11... | collective-permute-start | bytes 196616 | tf_op jit(solution)/shard_map/ppermute | solution.py:665
  65.4 5.2 %collective-permute-start.18 = (bf16[4,4,16,128]{3,2,1,0:T(8,128)(2,1)S(1)}, bf16[4,4,16,128]{3,2,1,0:T(8,128)(2,1)S(1)}, u32[]{:S(2)}, u32[]{:S(2)}) collective-permute-start(bf16[4,4,16,128]{3,2,1,0:T(8,128)(2,1)S(1)} %collective-permute-done.14.refs_2_), channel_id=1, source_target_pairs={{0,1},{1,0},{2,3},{3,2},{4,5},{5,4},{6,7},{7,6},{8,9},{9,8},{10,11... | collective-permute-start | bytes 196616 | tf_op jit(solution)/shard_map/ppermute | solution.py:665
  65.9 4.7 %collective-permute-start.19 = (bf16[4,4,16,128]{3,2,1,0:T(8,128)(2,1)S(1)}, bf16[4,4,16,128]{3,2,1,0:T(8,128)(2,1)S(1)}, u32[]{:S(2)}, u32[]{:S(2)}) collective-permute-start(bf16[4,4,16,128]{3,2,1,0:T(8,128)(2,1)S(1)} %collective-permute-done.15.refs_3_), channel_id=1, source_target_pairs={{0,1},{1,0},{2,3},{3,2},{4,5},{5,4},{6,7},{7,6},{8,9},{9,8},{10,11... | collective-permute-start | bytes 196616 | tf_op jit(solution)/shard_map/ppermute | solution.py:665

commit v6 on v5

--- a/solution.py
+++ b/solution.py
@@ -112,22 +112,36 @@
 IN_SMEM = pl.BlockSpec(memory_space=pltpu.SMEM)
 
 
-def forward_kernel(shards, pieces, edges, me_ref, table_ref, flow_ref, *refs):
-    cells_x = flow_ref.shape[0]
+def forward_kernel(shards, shards_y, pieces, step, me_ref, table_ref, flow_ref, *refs):
+    *refs, table, flow, table_sems, flow_sems = refs
+    cells_x = flow.shape[0]
     outer, inner = shards
     rows, channels = refs[0].shape[-2:]
-    _, own, _ = place(me_ref[0], shards)
+    own_y, own, _ = place(me_ref[0], shards)
+    owner = lax.rem(own_y + step, shards_y)
     steps = [step for piece in pieces for step in piece]
     block = inner * rows
-    table = [
-        table_ref[0, pl.ds(pl.multiple_of(peer(own, step, outer) * block, block), block), :]
-        for step in steps
+    copies = []
+    for i, other in enumerate(steps):
+        start = (owner * outer + peer(own, other, outer)) * block
+        source = table_ref.at[own_y, pl.ds(pl.multiple_of(start, block), block)]
+        copies.append(
+            pltpu.make_async_copy(source, table.at[pl.ds(i * block, block)], table_sems.at[i])
+        )
+    loads = [
+        pltpu.make_async_copy(flow_ref.at[x], flow.at[x], flow_sems.at[x])
+        for x in range(cells_x)
     ]
-    table = jnp.concatenate(table, axis=0)
+    for copy in copies + loads:
+        copy.start()
+    for copy in copies:
+        copy.wait()
     width = 2 if cells_x % 2 == 0 else 1
     for x in range(0, cells_x, width):
-        columns = [flow_ref[x + i] for i in range(width)]
-        result = dot(table, jnp.concatenate(columns, axis=1))
+        for i in range(width):
+            loads[x + i].wait()
+        columns = [flow[x + i] for i in range(width)]
+        result = dot(table[...], jnp.concatenate(columns, axis=1))
         for i in range(width):
             part = result[:, i * channels : (i + 1) * channels]
             at = 0
@@ -136,13 +150,13 @@
                     value = part[at : at + block].reshape(inner, rows, channels)
                     ref[slot, :, x + i] = value.astype(ref.dtype)
                     at += block
-    if edges:
+    if len(refs) > len(pieces):
         first, last, low, high = refs[-4:]
-        first[...] = flow_ref[0]
-        last[...] = flow_ref[cells_x - 1]
+        first[...] = flow[0]
+        last[...] = flow[cells_x - 1]
         cells_z = low.shape[1]
-        low[...] = flow_ref[:, :cells_z]
-        high[...] = flow_ref[:, flow_ref.shape[1] - cells_z :]
+        low[...] = flow[:, :cells_z]
+        high[...] = flow[:, flow.shape[1] - cells_z :]
 
 
 def forward_yz(me, table, flow, step, shards, shards_y, pieces, dtype, edges=0):
@@ -154,23 +168,18 @@
     if edges:
         shapes += [jax.ShapeDtypeStruct((positions, channels), flow.dtype)] * 2
         shapes += [jax.ShapeDtypeStruct((cells_x, edges, channels), flow.dtype)] * 2
-    whole = lambda dims: pl.BlockSpec(dims, lambda i, me: (0,) * len(dims))
-
-    def owner(i, me):
-        own = lax.div(me[0], outer * inner)
-        return own, lax.rem(own + step, shards_y), 0
-
-    limit = {} if step else {"vmem_limit_bytes": 10 << 20}
     return pl.pallas_call(
-        functools.partial(forward_kernel, shards, pieces, edges),
-        grid_spec=pltpu.PrefetchScalarGridSpec(
-            num_scalar_prefetch=1,
-            grid=(1,),
-            in_specs=[pl.BlockSpec((1, rows, positions), owner), whole(flow.shape)],
-            out_specs=[whole(one.shape) for one in shapes],
-        ),
+        functools.partial(forward_kernel, shards, shards_y, pieces, step),
+        in_specs=[IN_SMEM] + [pl.BlockSpec(memory_space=pltpu.HBM)] * 2,
+        out_specs=in_vmem(len(shapes)),
         out_shape=shapes,
-        compiler_params=pltpu.CompilerParams(**limit),
+        scratch_shapes=[
+            pltpu.VMEM((rows, positions), table.dtype),
+            pltpu.VMEM(flow.shape, flow.dtype),
+            pltpu.SemaphoreType.DMA((outer,)),
+            pltpu.SemaphoreType.DMA((cells_x,)),
+        ],
+        compiler_params=pltpu.CompilerParams(vmem_limit_bytes=(60 if step else 10) << 20),
         cost_estimate=pl.CostEstimate(
             flops=2 * rows * positions * cells_x * channels,
             bytes_accessed=2 * positions * (rows + cells_x * channels),
@@ -254,20 +263,32 @@
     )(me, left, low, high, right)
 
 
-def preload_kernel(pair, weight_ref, out_ref, sem):
-    copy = pltpu.make_async_copy(weight_ref.at[pl.ds(2 * pair, 2)], out_ref, sem)
-    copy.start()
-    copy.wait()
-
-
-def preload(weight, pair):
-    shape = (2, *weight.shape[1:])
+def preload_kernel(first, weight_ref, out_ref, sems):
+    count = out_ref.shape[0]
+    pieces = sems.shape[0] // count
+    modes = out_ref.shape[1] // pieces
+    copies = []
+    for i in range(count * pieces):
+        item, at = i // pieces, pl.ds(i % pieces * modes, modes)
+        copies.append(
+            pltpu.make_async_copy(
+                weight_ref.at[first + item, at], out_ref.at[item, at], sems.at[i]
+            )
+        )
+    for copy in copies:
+        copy.start()
+    for copy in copies:
+        copy.wait()
+
+
+def preload(weight, pair, count):
+    shape = (2 * count, *weight.shape[1:])
     return pl.pallas_call(
-        functools.partial(preload_kernel, pair),
+        functools.partial(preload_kernel, 2 * pair),
         in_specs=[pl.BlockSpec(memory_space=pltpu.HBM)],
         out_specs=in_vmem(1)[0],
         out_shape=jax.ShapeDtypeStruct(shape, weight.dtype),
-        scratch_shapes=[pltpu.SemaphoreType.DMA],
+        scratch_shapes=[pltpu.SemaphoreType.DMA((2 * 2 * count,))],
         compiler_params=pltpu.CompilerParams(vmem_limit_bytes=36 << 20),
         cost_estimate=pl.CostEstimate(
             flops=0, bytes_accessed=2 * math.prod(shape), transcendentals=0
@@ -280,6 +301,7 @@
     row_refs, refs = refs[:inner], refs[inner:]
     forward_ref, backward_ref, weight_ref, *refs = refs
     loaded_refs, refs = refs[:loaded], refs[loaded:]
+    loaded = sum(ref.shape[0] // 2 for ref in loaded_refs)
     out_refs, (held, sems, wide, left, mixed) = refs[:inner], refs[inner:]
 
     channels = wide.shape[1]
@@ -342,8 +364,16 @@
                     )
             mixed[pl.ds(start, group), :] = gathered.astype(mixed.dtype)
 
-    for pair, ref in enumerate(loaded_refs):
-        mix(pair, lambda h, mode, ref=ref: ref[h, mode])
+    pair = 0
+    for ref in loaded_refs:
+        count = ref.shape[0] // 2
+
+        def ready(i, carry, ref=ref, pair=pair):
+            mix(pair + i, lambda h, mode: ref[2 * i + h, mode])
+            return carry
+
+        lax.fori_loop(0, count, ready, 0)
+        pair += count
 
     def streamed(pair, carry):
         copy(pair).wait()
@@ -371,6 +401,7 @@
     _, cells_x, item_rows, channels = rows[0].shape
     pairs = item_rows // 2
     row_count = outer * inner * cells_x * item_rows
+    streamed = pairs - sum(part.shape[0] // 2 for part in loaded)
     return pl.pallas_call(
         functools.partial(mixing_kernel, shards, len(loaded)),
         in_specs=[IN_SMEM]
@@ -380,69 +411,70 @@
         out_specs=in_vmem(inner),
         out_shape=[jax.ShapeDtypeStruct(rows[0].shape, jnp.bfloat16)] * inner,
         scratch_shapes=[
-            pltpu.VMEM((pairs - len(loaded), 2, *weight.shape[1:]), weight.dtype),
-            pltpu.SemaphoreType.DMA((pairs - len(loaded),)),
+            pltpu.VMEM((streamed, 2, *weight.shape[1:]), weight.dtype),
+            pltpu.SemaphoreType.DMA((streamed,)),
             pltpu.VMEM((row_count, channels), jnp.float32),
             pltpu.VMEM((pairs * 2 * MX, 2 * channels), jnp.bfloat16),
             pltpu.VMEM((pairs * 2 * MX, channels), jnp.bfloat16),
         ],
-        compiler_params=pltpu.CompilerParams(vmem_limit_bytes=36 << 20),
+        compiler_params=pltpu.CompilerParams(vmem_limit_bytes=20 << 20),
         cost_estimate=pl.CostEstimate(
             flops=8 * weight.size, bytes_accessed=2 * weight.size, transcendentals=0
         ),
     )(me, *rows, forward_x, backward_x, weight, *loaded)
 
 
-def convolution_kernel(x, shards_y, per_y, me_ref, *refs):
-    *plane_refs, front_ref, back_ref, kernel_ref, out_ref, stacked = refs
-    cells_y, cells_z, channels = out_ref.shape
+def convolution_kernel(x, width, shards_y, per_y, me_ref, *refs):
+    *plane_refs, front_ref, back_ref, kernel_ref, out_ref, padded = refs
+    _, cells_y, cells_z, channels = out_ref.shape
     own_y = lax.div(me_ref[0], per_y)
-
-    def stack(plane, at, cells):
-        deep = cells.astype(jnp.float32)
-        z = lax.broadcasted_iota(jnp.int32, deep.shape, 1)
-        before = jnp.where(z == 0, 0.0, pltpu.roll(deep, 1, axis=1))
-        after = jnp.where(z == cells_z - 1, 0.0, pltpu.roll(deep, cells_z - 1, axis=1))
-        at = pl.ds(at, cells.shape[0])
-        stacked[plane, at, :, :channels] = before.astype(stacked.dtype)
-        stacked[plane, at, :, channels : 2 * channels] = cells
-        stacked[plane, at, :, 2 * channels :] = after.astype(stacked.dtype)
+    for plane, ref in enumerate(plane_refs):
+        padded[plane, 1 : cells_y + 1] = ref[0]
+        edge = front_ref[x + plane, 0]
+        padded[plane, 0] = jnp.where(own_y > 0, edge, jnp.zeros_like(edge))
+        edge = back_ref[x + plane, 0]
+        padded[plane, cells_y + 1] = jnp.where(own_y < shards_y - 1, edge, jnp.zeros_like(edge))
 
     rows = 4 if cells_y % 4 == 0 else 1
-    for plane, ref in enumerate(plane_refs):
-
-        def one(step, carry, plane=plane, ref=ref):
-            stack(plane, step * rows + 1, ref[0, pl.ds(step * rows, rows)])
-            return carry
-
-        lax.fori_loop(0, cells_y // rows, one, 0)
-        edge = front_ref[x + plane]
-        stack(plane, 0, jnp.where(own_y > 0, edge, jnp.zeros_like(edge)))
-        edge = back_ref[x + plane]
-        stack(plane, cells_y + 1, jnp.where(own_y < shards_y - 1, edge, jnp.zeros_like(edge)))
-
-    taps = [(a, b) for a in range(3) for b in range(3)]
+    columns = [(k, d) for k in range(width) for d in range(3)]
+    columns = [columns[i : i + 2] for i in range(0, len(columns), 2)]
+    none = jnp.zeros((channels, channels), kernel_ref.dtype)
 
     def chunk(index, carry):
         y = index * rows
-        total = jnp.zeros((rows * cells_z, channels), jnp.float32)
-        for a in range(3):
+        products = {}
+        for group in columns:
             blocks, kernels = [], []
-            for b in range(3):
-                part = stacked[a, pl.ds(y + b, rows)]
-                blocks.append(part.reshape(rows * cells_z, 3 * channels))
-                kernels.append(kernel_ref[a, b])
-            total = total + dot(jnp.concatenate(blocks, axis=1), jnp.concatenate(kernels, axis=0))
-        out_ref[pl.ds(y, rows)] = total.reshape(rows, cells_z, channels).astype(out_ref.dtype)
+            for p in range(width + 2):
+                if not any(0 <= p - k < 3 for k, _ in group):
+                    continue
+                for b in range(3):
+                    part = padded[p, pl.ds(y + b, rows)]
+                    blocks.append(part.reshape(rows * cells_z, channels))
+                    parts = [
+                        kernel_ref[p - k, b, d] if 0 <= p - k < 3 else none for k, d in group
+                    ]
+                    kernels.append(jnp.concatenate(parts, axis=1))
+            product = dot(jnp.concatenate(blocks, axis=1), jnp.concatenate(kernels, axis=0))
+            for i, column in enumerate(group):
+                part = product[:, i * channels : (i + 1) * channels]
+                products[column] = part.reshape(rows, cells_z, channels)
+        z = lax.broadcasted_iota(jnp.int32, (rows, cells_z, channels), 1)
+        for k in range(width):
+            before = jnp.where(z == 0, 0.0, pltpu.roll(products[k, 0], 1, axis=1))
+            after = pltpu.roll(products[k, 2], cells_z - 1, axis=1)
+            after = jnp.where(z == cells_z - 1, 0.0, after)
+            total = before + products[k, 1] + after
+            out_ref[k, pl.ds(y, rows)] = total.astype(out_ref.dtype)
         return carry
 
     lax.fori_loop(0, cells_y // rows, chunk, 0)
 
 
-def convolution(me, x, flow, left, right, front, back, kernel, shards_y, per_y):
+def convolution(me, x, width, flow, left, right, front, back, kernel, shards_y, per_y):
     cells_x, cells_y, cells_z, channels = flow.shape
     specs, planes = [], []
-    for p in (x - 1, x, x + 1):
+    for p in range(x - 1, x + width + 1):
         inside = 0 <= p < cells_x
         planes.append(flow if inside else (left if p < 0 else right))
         at = p if inside else 0
@@ -450,16 +482,17 @@
             pl.BlockSpec((1, cells_y, cells_z, channels), lambda i, at=at: (at, 0, 0, 0))
         )
     whole = lambda array: pl.BlockSpec(array.shape, lambda i: (0,) * array.ndim)
+    shape = (width, cells_y, cells_z, channels)
     return pl.pallas_call(
-        functools.partial(convolution_kernel, x, shards_y, per_y),
+        functools.partial(convolution_kernel, x, width, shards_y, per_y),
         grid=(1,),
         in_specs=[IN_SMEM] + specs + [whole(front), whole(back), whole(kernel)],
-        out_specs=pl.BlockSpec((cells_y, cells_z, channels), lambda i: (0, 0, 0)),
-        out_shape=jax.ShapeDtypeStruct((cells_y, cells_z, channels), jnp.bfloat16),
-        scratch_shapes=[pltpu.VMEM((3, cells_y + 2, cells_z, 3 * channels), flow.dtype)],
-        compiler_params=pltpu.CompilerParams(vmem_limit_bytes=10 << 20),
+        out_specs=pl.BlockSpec(shape, lambda i: (0, 0, 0, 0)),
+        out_shape=jax.ShapeDtypeStruct(shape, jnp.bfloat16),
+        scratch_shapes=[pltpu.VMEM((width + 2, cells_y + 2, cells_z, channels), flow.dtype)],
+        compiler_params=pltpu.CompilerParams(vmem_limit_bytes=14 << 20),
         cost_estimate=pl.CostEstimate(
-            flops=2 * 27 * cells_y * cells_z * channels * channels,
+            flops=3 * 27 * width * cells_y * cells_z * channels * channels,
             bytes_accessed=10 * cells_y * cells_z * channels,
             transcendentals=0,
         ),
@@ -470,7 +503,9 @@
     outer, inner = shards
     *piece_refs, bias_ref, out_ref, held = refs
     cells_x, cells_y, cells_z, channels = out_ref.shape
-    piece_refs, convolved_refs = piece_refs[:-cells_x], piece_refs[-cells_x:]
+    width = 2 if cells_x % 2 == 0 else 1
+    count = -(-cells_x // width)
+    piece_refs, convolved_refs = piece_refs[:-count], piece_refs[-count:]
     own_y, own_outer, own_inner = place(me_ref[0], shards)
     rows = piece_refs[0].shape[2]
 
@@ -485,7 +520,6 @@
                 for x in range(cells_x):
                     held[x, pl.ds(pl.multiple_of(at, rows), rows), :] = ref[part, x]
 
-    width = 2 if cells_x % 2 == 0 else 1
     bias = bias_ref[...]
     part = pl.program_id(0)
     count = cells_y * cells_z
@@ -496,14 +530,14 @@
         for i in range(width):
             spectral = total[:, i * channels : (i + 1) * channels]
             spectral = spectral.reshape(cells_y, cells_z, channels)
-            convolved = convolved_refs[x + i][pl.ds(part * cells_y, cells_y)]
+            convolved = convolved_refs[x // width][i, pl.ds(part * cells_y, cells_y)]
             value = spectral + convolved.astype(jnp.float32) + bias
             out_ref[x + i] = jax.nn.gelu(value, approximate=True).astype(out_ref.dtype)
 
 
 def final(me, table, pieces, convolved, bias, shards, shards_y):
-    cells_x = len(convolved)
-    cells_y, cells_z, channels = convolved[0].shape
+    width, cells_y, cells_z, channels = convolved[0].shape
+    cells_x = width * len(convolved)
     parts = 4 if cells_y % 4 == 0 else 1
     block = (cells_x, cells_y // parts, cells_z, channels)
     depth = table.shape[2]
@@ -513,17 +547,17 @@
             num_scalar_prefetch=1,
             grid=(parts,),
             in_specs=[
-                *in_vmem(2 + len(pieces) + cells_x),
+                *in_vmem(2 + len(pieces) + len(convolved)),
             ],
             out_specs=pl.BlockSpec(block, lambda i, me: (0, i, 0, 0)),
             scratch_shapes=[pltpu.VMEM((cells_x, depth, channels), jnp.bfloat16)],
         ),
-        out_shape=jax.ShapeDtypeStruct((cells_x, *convolved[0].shape), jnp.bfloat16),
+        out_shape=jax.ShapeDtypeStruct((cells_x, cells_y, cells_z, channels), jnp.bfloat16),
         compiler_params=pltpu.CompilerParams(vmem_limit_bytes=10 << 20),
         cost_estimate=pl.CostEstimate(
             flops=2 * table.shape[1] * depth * cells_x * channels,
-            bytes_accessed=6 * cells_x * convolved[0].size,
-            transcendentals=cells_x * convolved[0].size,
+            bytes_accessed=6 * len(convolved) * convolved[0].size,
+            transcendentals=len(convolved) * convolved[0].size,
         ),
     )(me, table, *pieces, *convolved, bias)
 
@@ -681,7 +715,6 @@
     me = lax.axis_index(("gy", "gx")).astype(jnp.int32).reshape(1)
     sizes = (shards_x, shards_y, pairs, cells_y, cells_z)
     full_x = cells_x * shards_x
-    kernel = conv_weight.reshape(3, 3, 3 * channels, channels)
 
     weight = spectral_weight.reshape(items, MX, channels, channels)
 
@@ -701,18 +734,23 @@
     )
     first, last = (x.reshape(1, cells_y, cells_z, channels) for x in (first, last))
 
-    left, right = neighbours(first, last, "gx")
-
+    early = pairs // 4
+    loaded = [preload(weight, 0, early)] if early else []
+    loaded, arrived = lax.optimization_barrier((loaded, arrived))
     by_outer = [None] * outer
     for piece, own, parts in zip(pieces, kept, arrived):
         for step, total in zip(piece, add_pieces(own, parts)):
             by_outer[step] = exchange(total, step, shards, True) if step else total
+    if early:
+        loaded.append(preload(weight, early, early))
+    by_outer, loaded = lax.optimization_barrier((by_outer, loaded))
     by_inner = regroup(me, by_outer, shards, True)
-    early = 1 if pairs > 2 else 0
-    loaded = [preload(weight, pair) for pair in range(early)]
     by_inner, weight = lax.optimization_barrier((by_inner, weight))
+    if early:
+        loaded.append(preload(weight, 2 * early, 1))
     rows = [by_inner[0]] + [exchange(by_inner[s], s, shards, False) for s in range(1, inner)]
-    loaded += [preload(weight, pair) for pair in range(early, min(early + 2, pairs - 1))]
+    rows, first, last = lax.optimization_barrier((rows, first, last))
+    left, right = neighbours(first, last, "gx")
 
 
     returned = mixing(
@@ -734,9 +772,10 @@
             for use in (0, shards_y)
         ]
         front, back = neighbours(*ends, "gy")
-    planes = (flow, left, right, front, back, kernel)
+    planes = (flow, left, right, front, back, conv_weight)
+    width = 2 if cells_x % 2 == 0 else 1
     convolved = [
-        convolution(me, x, *planes, shards_y, shards_x) for x in range(cells_x)
+        convolution(me, x, width, *planes, shards_y, shards_x) for x in range(0, cells_x, width)
     ]
 
     returned = [returned[0]] + [

time: 73.9 us -> 66.4 us (0.90)
  Pallas kernels: 33.7 us -> 28.9 us
  waiting for transfers between devices: 12.1 us -> 10.1 us
  local copies, waits for them, and re-layouts: 1.27 us -> 0.03 us
    pallas_call x1, Pallas kernels: 8.57 us -> 6.08 us  [mixing(): pl.pallas_call(functools.partial(mixing_kernel, shards, len(loaded)), in_...]
    pallas_call x9 -> x7, Pallas kernels: 22.1 us -> 19.8 us  [the longest x3 9.15 us: preload(): pl.pallas_call(functools.partial(preload_kernel, 2 * pair), in_specs=[pl....]
    unnamed x16 -> x14, local copies, waits for them, and re-layouts: 1.27 us -> 0.03 us
    ppermute x12, waiting for transfers between devices: 10.1 us -> 8.92 us  [exchange(): return lax.ppermute(array, 'gx', pairs)]
    ppermute x7, waiting for transfers between devices: 2.04 us -> 1.2 us  [over_y(): lax.ppermute(array, 'gy', [(i, (i + step) % shards_y) for i in range(shar...]
  transfers between devices with their start and end apart: 21 -> 21, of which waited for: 5 -> 7; matrix products, arithmetic and copies ran while one was open for 0% -> 0% of each run, Pallas kernels for 38% -> 35%
where the time goes in v6:
time: 66.4 us; the launch traced here: 66.2 us
  Pallas kernels  28.9 us (44%)
  starting transfers between devices  26.9 us (41%)
  waiting for transfers between devices  10.1 us (15%)
    ppermute x12, starting transfers between devices, exchange(): return lax.ppermute(array, 'gx', pairs)  14.6 us
    pallas_call x3, Pallas kernels, preload(): pl.pallas_call(functools.partial(preload_kernel, 2 * pair), in_specs=[pl....  9.15 us
    ppermute x12, waiting for transfers between devices, exchange(): return lax.ppermute(array, 'gx', pairs)  8.92 us
    ppermute x7, starting transfers between devices, over_y(): lax.ppermute(array, 'gy', [(i, (i + step) % shards_y) for i in range(shar...  8.81 us
    pallas_call x1, Pallas kernels, mixing(): pl.pallas_call(functools.partial(mixing_kernel, shards, len(loaded)), in_...  6.08 us
    pallas_call x2, Pallas kernels, convolution(): pl.pallas_call(functools.partial(convolution_kernel, x, width, shards_y,...  5.99 us
    pallas_call x2, Pallas kernels, forward_yz(): pl.pallas_call(functools.partial(forward_kernel, shards, shards_y, pieces...  4.62 us
    ppermute x2, starting transfers between devices, neighbours(): return (lax.ppermute(last, axis, up), lax.ppermute(first, axis, down))  3.5 us
  transfers between devices with their start and end apart: 21, of which 7 were waited for; matrix products, arithmetic and copies ran while one was open for 0% of the time, Pallas kernels for 35%

profile of v6, /device:TPU:0, one launch (start us, length us, event | category | flops | bytes accessed | tf_op | source)
XLA Modules:
  0.0 66.2 jit_solution(1735177711899655820)
XLA Ops:
  0.0 2.9 %shard_map.82 = (bf16[2,4,4,16,128]{4,3,2,1,0:T(8,128)(2,1)}, bf16[2,4,4,16,128]{4,3,2,1,0:T(8,128)(2,1)}) custom-call(s32[1]{0:T(128)} %bitcast.me_ref, bf16[2,512,1024]{2,1,0:T(8,128)(2,1)} %constant.18.clone.table_ref, bf16[4,1024,128]{2,1,0:T(8,128)(2,1)} %bitcast.6), custom_call_target="tpu_custom_call" | custom-call | flops 268435456 | bytes 1572864 | tf_op jit(solution)/shard_map/pallas_call | solution.py:171
  2.9 0.0 copy-start
  2.9 0.0 copy-start.1
  2.9 3.0 %collective-permute-start = (bf16[2,4,4,16,128]{4,3,2,1,0:T(8,128)(2,1)}, bf16[2,4,4,16,128]{4,3,2,1,0:T(8,128)(2,1)S(1)}, u32[]{:S(2)}, u32[]{:S(2)}) collective-permute-start(bf16[2,4,4,16,128]{4,3,2,1,0:T(8,128)(2,1)} %get-tuple-element.64), channel_id=1, source_target_pairs={{0,1},{1,0},{2,3},{3,2},{4,5},{5,4},{6,7},{7,6},{8,9},{9,8},{10,11... | collective-permute-start | bytes 393224 | tf_op jit(solution)/shard_map/ppermute | solution.py:699
  5.9 0.1 collective-permute-start.1
  6.0 3.5 %shard_map.84.refs_7_ = bf16[4,64,128,128]{3,2,1,0:T(8,128)(2,1)S(1)} custom-call(bf16[16,64,128,128]{3,2,1,0:T(8,128)(2,1)} %bitcast.11), custom_call_target="tpu_custom_call" | custom-call | bytes 8388608 | tf_op jit(solution)/shard_map/pallas_call | solution.py:286
  9.5 1.7 %shard_map.83 = (f32[2,4,4,16,128]{4,3,2,1,0:T(8,128)S(1)}, f32[2,4,4,16,128]{4,3,2,1,0:T(8,128)S(1)}, bf16[1024,128]{1,0:T(8,128)(2,1)S(1)}, bf16[1024,128]{1,0...) custom-call(s32[1]{0:T(128)} %bitcast.me_ref, bf16[2,512,1024]{2,1,0:T(8,128)(2,1)S(1)} %copy-done, ...), custom_call_target="tpu_custom_call" | custom-call | flops 268435456 | bytes 1572864 | tf_op jit(solution)/shard_map/pallas_call | solution.py:171
  11.3 0.0 collective-permute-done.refs_1_
  11.3 1.2 %collective-permute-done.1.refs_1_ = bf16[2,4,4,16,128]{4,3,2,1,0:T(8,128)(2,1)S(1)} collective-permute-done((bf16[2,4,4,16,128]{4,3,2,1,0:T(8,128)(2,1)}, bf16[2,4,4,16,128]{4,3,2,1,0:T(8,128)(2,1)S(1)}, u32[]{:S(2)}, u32[]{:S(2)}) %collective-permute-start.1) | collective-permute-done | bytes 131104 | tf_op jit(solution)/shard_map/ppermute | solution.py:699
  12.5 2.9 %collective-permute-start.3 = (bf16[4,4,16,128]{3,2,1,0:T(8,128)(2,1)S(1)}, bf16[4,4,16,128]{3,2,1,0:T(8,128)(2,1)S(1)}, u32[]{:S(2)}, u32[]{:S(2)}) collective-permute-start(bf16[4,4,16,128]{3,2,1,0:T(8,128)(2,1)S(1)} %get-tuple-element.71), channel_id=1, source_target_pairs={{0,16},{2,18},{4,20},{6,22},{8,24},{10,26},{12,28},{14,30},{16,0},... | collective-permute-start | bytes 196616 | tf_op jit(solution)/shard_map/ppermute | solution.py:695
  15.4 1.3 %collective-permute-start.4 = (bf16[4,4,16,128]{3,2,1,0:T(8,128)(2,1)S(1)}, bf16[4,4,16,128]{3,2,1,0:T(8,128)(2,1)S(1)}, u32[]{:S(2)}, u32[]{:S(2)}) collective-permute-start(bf16[4,4,16,128]{3,2,1,0:T(8,128)(2,1)S(1)} %get-tuple-element.72), channel_id=1, source_target_pairs={{0,24},{2,26},{4,28},{6,30},{8,16},{10,18},{12,20},{14,22},{16,8},... | collective-permute-start | bytes 196616 | tf_op jit(solution)/shard_map/ppermute | solution.py:695
  16.7 0.3 collective-permute-start.2
  17.0 3.5 %shard_map.87.refs_8_ = bf16[4,64,128,128]{3,2,1,0:T(8,128)(2,1)S(1)} custom-call(bf16[16,64,128,128]{3,2,1,0:T(8,128)(2,1)} %bitcast.12), custom_call_target="tpu_custom_call" | custom-call | bytes 8388608 | tf_op jit(solution)/shard_map/pallas_call | solution.py:286
  20.5 1.0 %collective-permute-done.4.refs_3_ = bf16[4,4,16,128]{3,2,1,0:T(8,128)(2,1)S(1)} collective-permute-done((bf16[4,4,16,128]{3,2,1,0:T(8,128)(2,1)S(1)}, bf16[4,4,16,128]{3,2,1,0:T(8,128)(2,1)S(1)}, u32[]{:S(2)}, u32[]{:S(2)}) %collective-permute-start.4) | collective-permute-done | bytes 65568 | tf_op jit(solution)/shard_map/ppermute | solution.py:695
  21.5 0.2 collective-permute-done.2.refs_1_
  21.8 0.1 collective-permute-start.5
  21.9 1.6 %collective-permute-start.6 = (bf16[4,4,16,128]{3,2,1,0:T(8,128)(2,1)S(1)}, bf16[4,4,16,128]{3,2,1,0:T(8,128)(2,1)S(1)}, u32[]{:S(2)}, u32[]{:S(2)}) collective-permute-start(bf16[4,4,16,128]{3,2,1,0:T(8,128)(2,1)S(1)} %get-tuple-element.84), channel_id=1, source_target_pairs={{0,4},{2,6},{4,0},{6,2},{8,12},{10,14},{12,8},{14,10},{16,20},{18,... | collective-permute-start | bytes 196616 | tf_op jit(solution)/shard_map/ppermute | solution.py:695
  23.4 0.3 collective-permute-start.7
  23.7 0.0 collective-permute-done.5.refs_1_
  23.7 2.6 %collective-permute-done.6.refs_2_ = bf16[4,4,16,128]{3,2,1,0:T(8,128)(2,1)S(1)} collective-permute-done((bf16[4,4,16,128]{3,2,1,0:T(8,128)(2,1)S(1)}, bf16[4,4,16,128]{3,2,1,0:T(8,128)(2,1)S(1)}, u32[]{:S(2)}, u32[]{:S(2)}) %collective-permute-start.6) | collective-permute-done | bytes 65568 | tf_op jit(solution)/shard_map/ppermute | solution.py:695
  26.4 1.1 %collective-permute-done.7.refs_3_ = bf16[4,4,16,128]{3,2,1,0:T(8,128)(2,1)S(1)} collective-permute-done((bf16[4,4,16,128]{3,2,1,0:T(8,128)(2,1)S(1)}, bf16[4,4,16,128]{3,2,1,0:T(8,128)(2,1)S(1)}, u32[]{:S(2)}, u32[]{:S(2)}) %collective-permute-start.7) | collective-permute-done | bytes 65568 | tf_op jit(solution)/shard_map/ppermute | solution.py:695
  27.5 2.2 %collective-permute-start.8 = (bf16[1,16,64,128]{3,2,1,0:T(8,128)(2,1)S(1)}, bf16[1,16,64,128]{3,2,1,0:T(8,128)(2,1)S(1)}, u32[]{:S(2)}, u32[]{:S(2)}) collective-permute-start(bf16[1,16,64,128]{3,2,1,0:T(8,128)(2,1)S(1)} %bitcast.10), channel_id=1, source_target_pairs={{0,2},{2,4},{4,6},{6,8},{8,10},{10,12},{12,14},{14,16},{16,18},{18... | collective-permute-start | bytes 786440 | tf_op jit(solution)/shard_map/ppermute | solution.py:684
  29.7 1.3 %collective-permute-start.9 = (bf16[1,16,64,128]{3,2,1,0:T(8,128)(2,1)S(1)}, bf16[1,16,64,128]{3,2,1,0:T(8,128)(2,1)S(1)}, u32[]{:S(2)}, u32[]{:S(2)}) collective-permute-start(bf16[1,16,64,128]{3,2,1,0:T(8,128)(2,1)S(1)} %bitcast.9), channel_id=1, source_target_pairs={{2,0},{4,2},{6,4},{8,6},{10,8},{12,10},{14,12},{16,14},{18,16},{20... | collective-permute-start | bytes 786440 | tf_op jit(solution)/shard_map/ppermute | solution.py:684
  31.0 2.2 %shard_map.89.refs_9_ = bf16[2,64,128,128]{3,2,1,0:T(8,128)(2,1)S(1)} custom-call(bf16[16,64,128,128]{3,2,1,0:T(8,128)(2,1)} %bitcast.13), custom_call_target="tpu_custom_call" | custom-call | bytes 4194304 | tf_op jit(solution)/shard_map/pallas_call | solution.py:286
  33.2 0.0 copy-start.6
  33.3 6.1 %shard_map.90 = (bf16[4,4,16,128]{3,2,1,0:T(8,128)(2,1)S(1)}, bf16[4,4,16,128]{3,2,1,0:T(8,128)(2,1)S(1)}, bf16[4,4,16,128]{3,2,1,0:T(8,128)(2,1)S(1)}, bf16[4,4,16,128]{3,2,1,0:T(8,128)(2,1)S(1)}) custom-call(s32[1]{0:T(128)} %bitcast.me_ref, bf16[4,4,16,128]{3,2,1,0:T(8,128)(2,1)S(1)} %get-tuple-element.88.refs_0_, ...), custom_call_target="tpu_custom_call" | custom-call | flops 134217728 | bytes 33554432 | tf_op jit(solution)/shard_map/pallas_call | solution.py:405
  39.3 0.0 collective-permute-done.9.right_ref.refs_3_
  39.4 1.6 %collective-permute-start.20 = (bf16[6,1,64,128]{3,2,1,0:T(8,128)(2,1)S(1)}, bf16[6,1,64,128]{3,2,1,0:T(8,128)(2,1)S(1)}, u32[]{:S(2)}, u32[]{:S(2)}) collective-permute-start(bf16[6,1,64,128]{3,2,1,0:T(8,128)(2,1)S(1)} %shard_map.92), channel_id=1, source_target_pairs={{0,1},{1,0},{2,3},{3,2},{4,5},{5,4},{6,7},{7,6},{8,9},{9,8},{10,11... | collective-permute-start | bytes 294920 | tf_op jit(solution)/shard_map/ppermute | solution.py:699
  41.0 1.6 %collective-permute-start.10 = (bf16[4,4,16,128]{3,2,1,0:T(8,128)(2,1)S(1)}, bf16[4,4,16,128]{3,2,1,0:T(8,128)(2,1)S(1)}, u32[]{:S(2)}, u32[]{:S(2)}) collective-permute-start(bf16[4,4,16,128]{3,2,1,0:T(8,128)(2,1)S(1)} %get-tuple-element.102), channel_id=1, source_target_pairs={{0,2},{2,0},{4,6},{6,4},{8,10},{10,8},{12,14},{14,12},{16,18},{18,... | collective-permute-start | bytes 196616 | tf_op jit(solution)/shard_map/ppermute | solution.py:695
  42.6 1.9 %collective-permute-start.11 = (bf16[4,4,16,128]{3,2,1,0:T(8,128)(2,1)S(1)}, bf16[4,4,16,128]{3,2,1,0:T(8,128)(2,1)S(1)}, u32[]{:S(2)}, u32[]{:S(2)}) collective-permute-start(bf16[4,4,16,128]{3,2,1,0:T(8,128)(2,1)S(1)} %get-tuple-element.103), channel_id=1, source_target_pairs={{0,4},{2,6},{4,0},{6,2},{8,12},{10,14},{12,8},{14,10},{16,20},{18,... | collective-permute-start | bytes 196616 | tf_op jit(solution)/shard_map/ppermute | solution.py:695
  44.5 0.1 collective-permute-start.12
  44.7 0.0 collective-permute-done.10.refs_1_
  44.7 2.6 %collective-permute-done.11.refs_2_ = bf16[4,4,16,128]{3,2,1,0:T(8,128)(2,1)S(1)} collective-permute-done((bf16[4,4,16,128]{3,2,1,0:T(8,128)(2,1)S(1)}, bf16[4,4,16,128]{3,2,1,0:T(8,128)(2,1)S(1)}, u32[]{:S(2)}, u32[]{:S(2)}) %collective-permute-start.11) | collective-permute-done | bytes 65568 | tf_op jit(solution)/shard_map/ppermute | solution.py:695
  47.3 1.3 %collective-permute-done.12.refs_3_ = bf16[4,4,16,128]{3,2,1,0:T(8,128)(2,1)S(1)} collective-permute-done((bf16[4,4,16,128]{3,2,1,0:T(8,128)(2,1)S(1)}, bf16[4,4,16,128]{3,2,1,0:T(8,128)(2,1)S(1)}, u32[]{:S(2)}, u32[]{:S(2)}) %collective-permute-start.12) | collective-permute-done | bytes 65568 | tf_op jit(solution)/shard_map/ppermute | solution.py:695
  48.6 1.7 %collective-permute-start.13 = (bf16[4,4,16,128]{3,2,1,0:T(8,128)(2,1)S(1)}, bf16[4,4,16,128]{3,2,1,0:T(8,128)(2,1)S(1)}, u32[]{:S(2)}, u32[]{:S(2)}) collective-permute-start(bf16[4,4,16,128]{3,2,1,0:T(8,128)(2,1)S(1)} %get-tuple-element.106), channel_id=1, source_target_pairs={{0,8},{2,10},{4,12},{6,14},{8,0},{10,2},{12,4},{14,6},{16,24},{18,... | collective-permute-start | bytes 196616 | tf_op jit(solution)/shard_map/ppermute | solution.py:695
  50.3 2.2 %collective-permute-start.14 = (bf16[4,4,16,128]{3,2,1,0:T(8,128)(2,1)S(1)}, bf16[4,4,16,128]{3,2,1,0:T(8,128)(2,1)S(1)}, u32[]{:S(2)}, u32[]{:S(2)}) collective-permute-start(bf16[4,4,16,128]{3,2,1,0:T(8,128)(2,1)S(1)} %get-tuple-element.107), channel_id=1, source_target_pairs={{0,16},{2,18},{4,20},{6,22},{8,24},{10,26},{12,28},{14,30},{16,0},... | collective-permute-start | bytes 196616 | tf_op jit(solution)/shard_map/ppermute | solution.py:695
  52.4 0.6 collective-permute-start.15
  53.1 0.5 collective-permute-start.16
  53.6 3.0 %shard_map.94.refs_9_ = bf16[2,16,64,128]{3,2,1,0:T(8,128)(2,1)S(1)} custom-call(s32[1]{0:T(128)} %bitcast.me_ref, bf16[4,16,64,128]{3,2,1,0:T(8,128)(2,1)S(1)} %copy-done.1, bf16[4,16,64,128]{3,2,1,0:T(8,128)(2,1)S(1)} %copy-done.1, bf16[4,16,64,128]{3,2,1,0:T(8,128)(2,1)S(1)} %copy-done.1, ...), custom_call_target="tpu_custom_call" | custom-call | flops 2717908992 | bytes 1310720 | tf_op jit(solution)/shard_map/pallas_call | solution.py:486
  56.6 1.6 %collective-permute-start.17 = (bf16[4,4,16,128]{3,2,1,0:T(8,128)(2,1)S(1)}, bf16[4,4,16,128]{3,2,1,0:T(8,128)(2,1)S(1)}, u32[]{:S(2)}, u32[]{:S(2)}) collective-permute-start(bf16[4,4,16,128]{3,2,1,0:T(8,128)(2,1)S(1)} %collective-permute-done.13.refs_1_), channel_id=1, source_target_pairs={{0,1},{1,0},{2,3},{3,2},{4,5},{5,4},{6,7},{7,6},{8,9},{9,8},{10,11... | collective-permute-start | bytes 196616 | tf_op jit(solution)/shard_map/ppermute | solution.py:699
  58.2 0.0 collective-permute-done.14.refs_2_
  58.2 0.5 collective-permute-start.18
  58.7 1.5 %collective-permute-start.19 = (bf16[4,4,16,128]{3,2,1,0:T(8,128)(2,1)S(1)}, bf16[4,4,16,128]{3,2,1,0:T(8,128)(2,1)S(1)}, u32[]{:S(2)}, u32[]{:S(2)}) collective-permute-start(bf16[4,4,16,128]{3,2,1,0:T(8,128)(2,1)S(1)} %collective-permute-done.15.refs_3_), channel_id=1, source_target_pairs={{0,1},{1,0},{2,3},{3,2},{4,5},{5,4},{6,7},{7,6},{8,9},{9,8},{10,11... | collective-permute-start | bytes 196616 | tf_op jit(solution)/shard_map/ppermute | solution.py:699
  60.2 3.0 %shard_map.93.refs_8_ = bf16[2,16,64,128]{3,2,1,0:T(8,128)(2,1)S(1)} custom-call(s32[1]{0:T(128)} %bitcast.me_ref, bf16[1,16,64,128]{3,2,1,0:T(8,128)(2,1)S(1)} %collective-permute-done.8.left_ref.refs_0_, bf16[4,16,64,128]{3,2,1,0:T(8,128)(2,1)S(1)} %copy-done.1, bf16[4,16,64,128]{3,2,1,0:T(8,128)(2,1)S(1)} %copy-done.1, ...), custom_call_target="tpu_custom_call" | custom-call | flops 2717908992 | bytes 1310720 | tf_op jit(solution)/shard_map/pallas_call | solution.py:486
  63.2 0.0 collective-permute-done.16.refs_4_
  63.2 0.0 collective-permute-done.17.refs_5_
  63.2 0.0 collective-permute-done.19.refs_7_
  63.3 2.9 %shard_map.95 = bf16[4,16,64,128]{3,2,1,0:T(8,128)(2,1)} custom-call(s32[1]{0:T(128)} %bitcast.me_ref, bf16[2,1024,512]{2,1,0:T(8,128)(2,1)S(1)} %copy-done.2, bf16[4,4,16,128]{3,2,1,0:T(8,128)(2,1)S(1)} %get-tuple-element.105.refs_0_, bf16[4,4,16,128]{3,2,1,0:T(8,128)(2,1)S(1)} %collective-permute-done.13.refs_1_, ...), custom_call_target="tpu_custom_call" | custom-call | flops 536870912 | bytes 3145728 | tf_op jit(solution)/shard_map/pallas_call | solution.py:544
  (22 shorter events, 0.1 us)
Async XLA Ops:
  2.9 6.6 %copy-start = (bf16[2,512,1024]{2,1,0:T(8,128)(2,1)S(1)}, bf16[2,512,1024]{2,1,0:T(8,128)(2,1)}, u32[]{:S(2)}) copy-start(bf16[2,512,1024]{2,1,0:T(8,128)(2,1)} %constant.18.clone.table_ref) | copy-start | bytes 6291460
  2.9 6.6 %copy-start.1 = (bf16[4,16,64,128]{3,2,1,0:T(8,128)(2,1)S(1)}, bf16[4,16,64,128]{3,2,1,0:T(8,128)(2,1)}, u32[]{:S(2)}) copy-start(bf16[4,16,64,128]{3,2,1,0:T(8,128)(2,1)} %refs_2_.3) | copy-start | bytes 3145732
  2.9 8.4 %collective-permute-start = (bf16[2,4,4,16,128]{4,3,2,1,0:T(8,128)(2,1)}, bf16[2,4,4,16,128]{4,3,2,1,0:T(8,128)(2,1)S(1)}, u32[]{:S(2)}, u32[]{:S(2)}) collective-permute-start(bf16[2,4,4,16,128]{4,3,2,1,0:T(8,128)(2,1)} %get-tuple-element.64), channel_id=1, source_target_pairs={{0,1},{1,0},{2,3},{3,2},{4,5},{5,4},{6,7},{7,6},{8,9},{9,8},{10,11... | collective-permute-start | bytes 393224 | tf_op jit(solution)/shard_map/ppermute | solution.py:699
  5.9 6.5 %collective-permute-start.1 = (bf16[2,4,4,16,128]{4,3,2,1,0:T(8,128)(2,1)}, bf16[2,4,4,16,128]{4,3,2,1,0:T(8,128)(2,1)S(1)}, u32[]{:S(2)}, u32[]{:S(2)}) collective-permute-start(bf16[2,4,4,16,128]{4,3,2,1,0:T(8,128)(2,1)} %get-tuple-element.65), channel_id=1, source_target_pairs={{0,1},{1,0},{2,3},{3,2},{4,5},{5,4},{6,7},{7,6},{8,9},{9,8},{10,11... | collective-permute-start | bytes 393224 | tf_op jit(solution)/shard_map/ppermute | solution.py:699
  12.5 8.0 %collective-permute-start.3 = (bf16[4,4,16,128]{3,2,1,0:T(8,128)(2,1)S(1)}, bf16[4,4,16,128]{3,2,1,0:T(8,128)(2,1)S(1)}, u32[]{:S(2)}, u32[]{:S(2)}) collective-permute-start(bf16[4,4,16,128]{3,2,1,0:T(8,128)(2,1)S(1)} %get-tuple-element.71), channel_id=1, source_target_pairs={{0,16},{2,18},{4,20},{6,22},{8,24},{10,26},{12,28},{14,30},{16,0},... | collective-permute-start | bytes 196616 | tf_op jit(solution)/shard_map/ppermute | solution.py:695
  15.4 6.2 %collective-permute-start.4 = (bf16[4,4,16,128]{3,2,1,0:T(8,128)(2,1)S(1)}, bf16[4,4,16,128]{3,2,1,0:T(8,128)(2,1)S(1)}, u32[]{:S(2)}, u32[]{:S(2)}) collective-permute-start(bf16[4,4,16,128]{3,2,1,0:T(8,128)(2,1)S(1)} %get-tuple-element.72), channel_id=1, source_target_pairs={{0,24},{2,26},{4,28},{6,30},{8,16},{10,18},{12,20},{14,22},{16,8},... | collective-permute-start | bytes 196616 | tf_op jit(solution)/shard_map/ppermute | solution.py:695
  16.7 5.0 %collective-permute-start.2 = (bf16[4,4,16,128]{3,2,1,0:T(8,128)(2,1)S(1)}, bf16[4,4,16,128]{3,2,1,0:T(8,128)(2,1)S(1)}, u32[]{:S(2)}, u32[]{:S(2)}) collective-permute-start(bf16[4,4,16,128]{3,2,1,0:T(8,128)(2,1)S(1)} %get-tuple-element.68), channel_id=1, source_target_pairs={{0,8},{2,10},{4,12},{6,14},{8,0},{10,2},{12,4},{14,6},{16,24},{18,... | collective-permute-start | bytes 196616 | tf_op jit(solution)/shard_map/ppermute | solution.py:695
  21.8 1.9 %collective-permute-start.5 = (bf16[4,4,16,128]{3,2,1,0:T(8,128)(2,1)S(1)}, bf16[4,4,16,128]{3,2,1,0:T(8,128)(2,1)S(1)}, u32[]{:S(2)}, u32[]{:S(2)}) collective-permute-start(bf16[4,4,16,128]{3,2,1,0:T(8,128)(2,1)S(1)} %get-tuple-element.83), channel_id=1, source_target_pairs={{0,2},{2,0},{4,6},{6,4},{8,10},{10,8},{12,14},{14,12},{16,18},{18,... | collective-permute-start | bytes 196616 | tf_op jit(solution)/shard_map/ppermute | solution.py:695
  21.9 4.5 %collective-permute-start.6 = (bf16[4,4,16,128]{3,2,1,0:T(8,128)(2,1)S(1)}, bf16[4,4,16,128]{3,2,1,0:T(8,128)(2,1)S(1)}, u32[]{:S(2)}, u32[]{:S(2)}) collective-permute-start(bf16[4,4,16,128]{3,2,1,0:T(8,128)(2,1)S(1)} %get-tuple-element.84), channel_id=1, source_target_pairs={{0,4},{2,6},{4,0},{6,2},{8,12},{10,14},{12,8},{14,10},{16,20},{18,... | collective-permute-start | bytes 196616 | tf_op jit(solution)/shard_map/ppermute | solution.py:695
  23.4 4.0 %collective-permute-start.7 = (bf16[4,4,16,128]{3,2,1,0:T(8,128)(2,1)S(1)}, bf16[4,4,16,128]{3,2,1,0:T(8,128)(2,1)S(1)}, u32[]{:S(2)}, u32[]{:S(2)}) collective-permute-start(bf16[4,4,16,128]{3,2,1,0:T(8,128)(2,1)S(1)} %get-tuple-element.85), channel_id=1, source_target_pairs={{0,6},{2,4},{4,2},{6,0},{8,14},{10,12},{12,10},{14,8},{16,22},{18,... | collective-permute-start | bytes 196616 | tf_op jit(solution)/shard_map/ppermute | solution.py:695
  27.5 5.7 %copy-start.3 = (bf16[256,128]{1,0:T(8,128)(2,1)S(1)}, bf16[256,128]{1,0:T(8,128)(2,1)}, u32[]{:S(2)}) copy-start(bf16[256,128]{1,0:T(8,128)(2,1)} %constant.19.clone.refs_4_) | copy-start | bytes 196612
  27.5 5.7 %copy-start.4 = (bf16[128,128]{1,0:T(8,128)(2,1)S(1)}, bf16[128,128]{1,0:T(8,128)(2,1)}, u32[]{:S(2)}) copy-start(bf16[128,128]{1,0:T(8,128)(2,1)} %constant.20.clone.refs_5_) | copy-start | bytes 98308
  27.5 11.9 %collective-permute-start.8 = (bf16[1,16,64,128]{3,2,1,0:T(8,128)(2,1)S(1)}, bf16[1,16,64,128]{3,2,1,0:T(8,128)(2,1)S(1)}, u32[]{:S(2)}, u32[]{:S(2)}) collective-permute-start(bf16[1,16,64,128]{3,2,1,0:T(8,128)(2,1)S(1)} %bitcast.10), channel_id=1, source_target_pairs={{0,2},{2,4},{4,6},{6,8},{8,10},{10,12},{12,14},{14,16},{16,18},{18... | collective-permute-start | bytes 786440 | tf_op jit(solution)/shard_map/ppermute | solution.py:684
  29.7 9.6 %collective-permute-start.9 = (bf16[1,16,64,128]{3,2,1,0:T(8,128)(2,1)S(1)}, bf16[1,16,64,128]{3,2,1,0:T(8,128)(2,1)S(1)}, u32[]{:S(2)}, u32[]{:S(2)}) collective-permute-start(bf16[1,16,64,128]{3,2,1,0:T(8,128)(2,1)S(1)} %bitcast.9), channel_id=1, source_target_pairs={{2,0},{4,2},{6,4},{8,6},{10,8},{12,10},{14,12},{16,14},{18,16},{20... | collective-permute-start | bytes 786440 | tf_op jit(solution)/shard_map/ppermute | solution.py:684
  33.2 20.3 %copy-start.6 = (bf16[3,3,3,128,128]{4,3,2,1,0:T(8,128)(2,1)S(1)}, bf16[3,3,3,128,128]{4,3,2,1,0:T(8,128)(2,1)}, u32[]{:S(2)}) copy-start(bf16[3,3,3,128,128]{4,3,2,1,0:T(8,128)(2,1)} %refs_6_.3) | copy-start | bytes 2654212
  39.4 14.2 %collective-permute-start.20 = (bf16[6,1,64,128]{3,2,1,0:T(8,128)(2,1)S(1)}, bf16[6,1,64,128]{3,2,1,0:T(8,128)(2,1)S(1)}, u32[]{:S(2)}, u32[]{:S(2)}) collective-permute-start(bf16[6,1,64,128]{3,2,1,0:T(8,128)(2,1)S(1)} %shard_map.92), channel_id=1, source_target_pairs={{0,1},{1,0},{2,3},{3,2},{4,5},{5,4},{6,7},{7,6},{8,9},{9,8},{10,11... | collective-permute-start | bytes 294920 | tf_op jit(solution)/shard_map/ppermute | solution.py:699
  41.0 3.7 %collective-permute-start.10 = (bf16[4,4,16,128]{3,2,1,0:T(8,128)(2,1)S(1)}, bf16[4,4,16,128]{3,2,1,0:T(8,128)(2,1)S(1)}, u32[]{:S(2)}, u32[]{:S(2)}) collective-permute-start(bf16[4,4,16,128]{3,2,1,0:T(8,128)(2,1)S(1)} %get-tuple-element.102), channel_id=1, source_target_pairs={{0,2},{2,0},{4,6},{6,4},{8,10},{10,8},{12,14},{14,12},{16,18},{18,... | collective-permute-start | bytes 196616 | tf_op jit(solution)/shard_map/ppermute | solution.py:695
  42.6 4.7 %collective-permute-start.11 = (bf16[4,4,16,128]{3,2,1,0:T(8,128)(2,1)S(1)}, bf16[4,4,16,128]{3,2,1,0:T(8,128)(2,1)S(1)}, u32[]{:S(2)}, u32[]{:S(2)}) collective-permute-start(bf16[4,4,16,128]{3,2,1,0:T(8,128)(2,1)S(1)} %get-tuple-element.103), channel_id=1, source_target_pairs={{0,4},{2,6},{4,0},{6,2},{8,12},{10,14},{12,8},{14,10},{16,20},{18,... | collective-permute-start | bytes 196616 | tf_op jit(solution)/shard_map/ppermute | solution.py:695
  44.5 4.1 %collective-permute-start.12 = (bf16[4,4,16,128]{3,2,1,0:T(8,128)(2,1)S(1)}, bf16[4,4,16,128]{3,2,1,0:T(8,128)(2,1)S(1)}, u32[]{:S(2)}, u32[]{:S(2)}) collective-permute-start(bf16[4,4,16,128]{3,2,1,0:T(8,128)(2,1)S(1)} %get-tuple-element.104), channel_id=1, source_target_pairs={{0,6},{2,4},{4,2},{6,0},{8,14},{10,12},{12,10},{14,8},{16,22},{18,... | collective-permute-start | bytes 196616 | tf_op jit(solution)/shard_map/ppermute | solution.py:695
  48.6 8.0 %collective-permute-start.13 = (bf16[4,4,16,128]{3,2,1,0:T(8,128)(2,1)S(1)}, bf16[4,4,16,128]{3,2,1,0:T(8,128)(2,1)S(1)}, u32[]{:S(2)}, u32[]{:S(2)}) collective-permute-start(bf16[4,4,16,128]{3,2,1,0:T(8,128)(2,1)S(1)} %get-tuple-element.106), channel_id=1, source_target_pairs={{0,8},{2,10},{4,12},{6,14},{8,0},{10,2},{12,4},{14,6},{16,24},{18,... | collective-permute-start | bytes 196616 | tf_op jit(solution)/shard_map/ppermute | solution.py:695
  50.3 7.9 %collective-permute-start.14 = (bf16[4,4,16,128]{3,2,1,0:T(8,128)(2,1)S(1)}, bf16[4,4,16,128]{3,2,1,0:T(8,128)(2,1)S(1)}, u32[]{:S(2)}, u32[]{:S(2)}) collective-permute-start(bf16[4,4,16,128]{3,2,1,0:T(8,128)(2,1)S(1)} %get-tuple-element.107), channel_id=1, source_target_pairs={{0,16},{2,18},{4,20},{6,22},{8,24},{10,26},{12,28},{14,30},{16,0},... | collective-permute-start | bytes 196616 | tf_op jit(solution)/shard_map/ppermute | solution.py:695
  52.4 6.3 %collective-permute-start.15 = (bf16[4,4,16,128]{3,2,1,0:T(8,128)(2,1)S(1)}, bf16[4,4,16,128]{3,2,1,0:T(8,128)(2,1)S(1)}, u32[]{:S(2)}, u32[]{:S(2)}) collective-permute-start(bf16[4,4,16,128]{3,2,1,0:T(8,128)(2,1)S(1)} %get-tuple-element.108), channel_id=1, source_target_pairs={{0,24},{2,26},{4,28},{6,30},{8,16},{10,18},{12,20},{14,22},{16,8},... | collective-permute-start | bytes 196616 | tf_op jit(solution)/shard_map/ppermute | solution.py:695
  53.1 10.2 %copy-start.2 = (bf16[2,1024,512]{2,1,0:T(8,128)(2,1)S(1)}, bf16[2,1024,512]{2,1,0:T(8,128)(2,1)}, u32[]{:S(2)}) copy-start(bf16[2,1024,512]{2,1,0:T(8,128)(2,1)} %constant.21.clone.table_ref) | copy-start | bytes 6291460
  53.1 10.2 %copy-start.5 = (f32[128]{0:T(128)S(1)}, f32[128]{0:T(128)}, u32[]{:S(2)}) copy-start(f32[128]{0:T(128)} %param.11) | copy-start | bytes 1540
  53.1 10.2 %collective-permute-start.16 = (bf16[4,4,16,128]{3,2,1,0:T(8,128)(2,1)S(1)}, bf16[4,4,16,128]{3,2,1,0:T(8,128)(2,1)S(1)}, u32[]{:S(2)}, u32[]{:S(2)}) collective-permute-start(bf16[4,4,16,128]{3,2,1,0:T(8,128)(2,1)S(1)} %get-tuple-element.105.refs_0_), channel_id=1, source_target_pairs={{0,1},{1,0},{2,3},{3,2},{4,5},{5,4},{6,7},{7,6},{8,9},{9,8},{10,11... | collective-permute-start | bytes 196616 | tf_op jit(solution)/shard_map/ppermute | solution.py:699
  56.6 6.6 %collective-permute-start.17 = (bf16[4,4,16,128]{3,2,1,0:T(8,128)(2,1)S(1)}, bf16[4,4,16,128]{3,2,1,0:T(8,128)(2,1)S(1)}, u32[]{:S(2)}, u32[]{:S(2)}) collective-permute-start(bf16[4,4,16,128]{3,2,1,0:T(8,128)(2,1)S(1)} %collective-permute-done.13.refs_1_), channel_id=1, source_target_pairs={{0,1},{1,0},{2,3},{3,2},{4,5},{5,4},{6,7},{7,6},{8,9},{9,8},{10,11... | collective-permute-start | bytes 196616 | tf_op jit(solution)/shard_map/ppermute | solution.py:699
  58.2 5.1 %collective-permute-start.18 = (bf16[4,4,16,128]{3,2,1,0:T(8,128)(2,1)S(1)}, bf16[4,4,16,128]{3,2,1,0:T(8,128)(2,1)S(1)}, u32[]{:S(2)}, u32[]{:S(2)}) collective-permute-start(bf16[4,4,16,128]{3,2,1,0:T(8,128)(2,1)S(1)} %collective-permute-done.14.refs_2_), channel_id=1, source_target_pairs={{0,1},{1,0},{2,3},{3,2},{4,5},{5,4},{6,7},{7,6},{8,9},{9,8},{10,11... | collective-permute-start | bytes 196616 | tf_op jit(solution)/shard_map/ppermute | solution.py:699
  58.7 4.6 %collective-permute-start.19 = (bf16[4,4,16,128]{3,2,1,0:T(8,128)(2,1)S(1)}, bf16[4,4,16,128]{3,2,1,0:T(8,128)(2,1)S(1)}, u32[]{:S(2)}, u32[]{:S(2)}) collective-permute-start(bf16[4,4,16,128]{3,2,1,0:T(8,128)(2,1)S(1)} %collective-permute-done.15.refs_3_), channel_id=1, source_target_pairs={{0,1},{1,0},{2,3},{3,2},{4,5},{5,4},{6,7},{7,6},{8,9},{9,8},{10,11... | collective-permute-start | bytes 196616 | tf_op jit(solution)/shard_map/ppermute | solution.py:699

commit v7 on v6

--- a/solution.py
+++ b/solution.py
@@ -99,6 +99,10 @@
     return lax.rem(index + (count - step), count)
 
 
+def far_first(count):
+    return list(range(count - 1, -1, -1))
+
+
 def place(me, shards):
     outer, inner = shards
     across = lax.rem(me, outer * inner)
@@ -112,17 +116,32 @@
 IN_SMEM = pl.BlockSpec(memory_space=pltpu.SMEM)
 
 
-def forward_kernel(shards, shards_y, pieces, step, me_ref, table_ref, flow_ref, *refs):
+def transform(table, flow_at, cells_x, refs, pieces):
+    inner, _, rows, channels = refs[0].shape[1:]
+    block = inner * rows
+    width = 2 if cells_x % 2 == 0 else 1
+    for x in range(0, cells_x, width):
+        columns = [flow_at(x + i) for i in range(width)]
+        result = dot(table, jnp.concatenate(columns, axis=1))
+        for i in range(width):
+            part = result[:, i * channels : (i + 1) * channels]
+            at = 0
+            for ref, piece in zip(refs, pieces):
+                for slot in range(len(piece)):
+                    value = part[at : at + block].reshape(inner, rows, channels)
+                    ref[slot, :, x + i] = value.astype(ref.dtype)
+                    at += block
+
+
+def send_kernel(shards, shards_y, pieces, step, me_ref, table_ref, flow_ref, *refs):
     *refs, table, flow, table_sems, flow_sems = refs
     cells_x = flow.shape[0]
-    outer, inner = shards
-    rows, channels = refs[0].shape[-2:]
+    outer, _ = shards
+    block = refs[0].shape[1] * refs[0].shape[3]
     own_y, own, _ = place(me_ref[0], shards)
     owner = lax.rem(own_y + step, shards_y)
-    steps = [step for piece in pieces for step in piece]
-    block = inner * rows
     copies = []
-    for i, other in enumerate(steps):
+    for i, other in enumerate(step for piece in pieces for step in piece):
         start = (owner * outer + peer(own, other, outer)) * block
         source = table_ref.at[own_y, pl.ds(pl.multiple_of(start, block), block)]
         copies.append(
@@ -136,50 +155,74 @@
         copy.start()
     for copy in copies:
         copy.wait()
-    width = 2 if cells_x % 2 == 0 else 1
-    for x in range(0, cells_x, width):
-        for i in range(width):
-            loads[x + i].wait()
-        columns = [flow[x + i] for i in range(width)]
-        result = dot(table[...], jnp.concatenate(columns, axis=1))
-        for i in range(width):
-            part = result[:, i * channels : (i + 1) * channels]
-            at = 0
-            for ref, piece in zip(refs, pieces):
-                for slot in range(len(piece)):
-                    value = part[at : at + block].reshape(inner, rows, channels)
-                    ref[slot, :, x + i] = value.astype(ref.dtype)
-                    at += block
-    if len(refs) > len(pieces):
-        first, last, low, high = refs[-4:]
-        first[...] = flow[0]
-        last[...] = flow[cells_x - 1]
-        cells_z = low.shape[1]
-        low[...] = flow[:, :cells_z]
-        high[...] = flow[:, flow.shape[1] - cells_z :]
-
-
-def forward_yz(me, table, flow, step, shards, shards_y, pieces, dtype, edges=0):
+
+    def flow_at(x):
+        loads[x].wait()
+        return flow[x]
+
+    transform(table[...], flow_at, cells_x, refs, pieces)
+
+
+def keep_kernel(shards, shards_y, pieces, me_ref, table_ref, flow_ref, *refs):
+    refs, (first, last, *rows) = refs[: len(pieces)], refs[len(pieces) :]
+    cells_x, positions, _ = flow_ref.shape
+    outer, _ = shards
+    block = refs[0].shape[1] * refs[0].shape[3]
+    own_y, own, _ = place(me_ref[0], shards)
+    tables = []
+    for other in (step for piece in pieces for step in piece):
+        start = (own_y * outer + peer(own, other, outer)) * block
+        tables.append(table_ref[own_y, pl.ds(pl.multiple_of(start, block), block), :])
+    transform(
+        jnp.concatenate(tables, axis=0), lambda x: flow_ref[x], cells_x, refs, pieces
+    )
+    first[...] = flow_ref[0]
+    last[...] = flow_ref[cells_x - 1]
+    cells_z = rows[0].shape[1]
+    low, high = pl.ds(0, cells_z), pl.ds(positions - cells_z, cells_z)
+    if len(rows) > 1:
+        rows[0][...] = flow_ref[:, low]
+        rows[1][...] = flow_ref[:, high]
+    else:
+
+        @pl.when(own_y > 0)
+        def _():
+            rows[0][...] = flow_ref[:, low]
+
+        @pl.when(own_y == 0)
+        def _():
+            rows[0][...] = flow_ref[:, high]
+
+
+def forward_yz(me, table, flow, step, shards, shards_y, pieces, cells_z=0):
     cells_x, positions, channels = flow.shape
     outer, inner = shards
     rows = table.shape[1] // shards_y
     unit = (inner, cells_x, rows // (outer * inner), channels)
+    dtype = jnp.bfloat16 if step else jnp.float32
     shapes = [jax.ShapeDtypeStruct((len(piece), *unit), dtype) for piece in pieces]
-    if edges:
-        shapes += [jax.ShapeDtypeStruct((positions, channels), flow.dtype)] * 2
-        shapes += [jax.ShapeDtypeStruct((cells_x, edges, channels), flow.dtype)] * 2
-    return pl.pallas_call(
-        functools.partial(forward_kernel, shards, shards_y, pieces, step),
-        in_specs=[IN_SMEM] + [pl.BlockSpec(memory_space=pltpu.HBM)] * 2,
-        out_specs=in_vmem(len(shapes)),
-        out_shape=shapes,
-        scratch_shapes=[
+    if step:
+        kernel = functools.partial(send_kernel, shards, shards_y, pieces, step)
+        specs = [pl.BlockSpec(memory_space=pltpu.HBM)] * 2
+        scratch = [
             pltpu.VMEM((rows, positions), table.dtype),
             pltpu.VMEM(flow.shape, flow.dtype),
             pltpu.SemaphoreType.DMA((outer,)),
             pltpu.SemaphoreType.DMA((cells_x,)),
-        ],
-        compiler_params=pltpu.CompilerParams(vmem_limit_bytes=(60 if step else 10) << 20),
+        ]
+    else:
+        kernel = functools.partial(keep_kernel, shards, shards_y, pieces)
+        specs, scratch = in_vmem(2), []
+        shapes += [jax.ShapeDtypeStruct((positions, channels), flow.dtype)] * 2
+        edge = jax.ShapeDtypeStruct((cells_x, cells_z, channels), flow.dtype)
+        shapes += [edge] * (1 if shards_y == 2 else 2)
+    return pl.pallas_call(
+        kernel,
+        in_specs=[IN_SMEM] + specs,
+        out_specs=in_vmem(len(shapes)),
+        out_shape=shapes,
+        scratch_shapes=scratch,
+        compiler_params=pltpu.CompilerParams(vmem_limit_bytes=(56 if step else 10) << 20),
         cost_estimate=pl.CostEstimate(
             flops=2 * rows * positions * cells_x * channels,
             bytes_accessed=2 * positions * (rows + cells_x * channels),
@@ -215,8 +258,8 @@
     in_refs, out_refs = refs[:-count], refs[-count:]
     for step, out_ref in enumerate(out_refs):
         at = peer(own, step, count) if chosen else step
-        for slot, in_ref in enumerate(in_refs):
-            out_ref[slot] = in_ref[at]
+        for number, in_ref in enumerate(in_refs):
+            out_ref[far_first(len(in_refs))[number]] = in_ref[at]
 
 
 def regroup(me, arrays, shards, chosen):
@@ -233,34 +276,41 @@
     )(me, *arrays)
 
 
-def edge_kernel(choose, per_y, me_ref, left_ref, low_ref, high_ref, right_ref, out_ref):
-    cells_x, cells_y = low_ref.shape[0], left_ref.shape[1]
-
-    def fill(row, rows_ref):
-        out_ref[0, 0] = left_ref[0, row]
-        out_ref[1 : 1 + cells_x, 0] = rows_ref[...]
-        out_ref[1 + cells_x, 0] = right_ref[0, row]
-
-    is_low = choose(lax.div(me_ref[0], per_y))
-
-    @pl.when(is_low)
+def halo_kernel(shards, shards_y, me_ref, first_ref, last_ref, front_ref, back_ref, *out_refs):
+    own_y, own_outer, own_inner = place(me_ref[0], shards)
+    even = lax.rem(own_outer * shards[1] + own_inner, 2) == 0
+    cells_x, cells_z, _ = front_ref.shape
+    cells_y = first_ref.shape[0] // cells_z
+
+    def fill(out_ref, x, plane_ref):
+        for y in range(cells_y):
+            out_ref[y + 1] = plane_ref[pl.ds(y * cells_z, cells_z), :]
+        row = front_ref[x]
+        out_ref[0] = jnp.where(own_y > 0, row, jnp.zeros_like(row))
+        row = back_ref[x]
+        out_ref[cells_y + 1] = jnp.where(own_y < shards_y - 1, row, jnp.zeros_like(row))
+
+    @pl.when(even)
     def _():
-        fill(0, low_ref)
-
-    @pl.when(jnp.logical_not(is_low))
+        fill(out_refs[0], cells_x - 1, last_ref)
+        fill(out_refs[1], 0, first_ref)
+
+    @pl.when(jnp.logical_not(even))
     def _():
-        fill(cells_y - 1, high_ref)
-
-
-def y_edge(me, left, low, high, right, per_y, choose):
-    cells_x, cells_z, channels = low.shape
+        fill(out_refs[0], 0, first_ref)
+        fill(out_refs[1], cells_x - 1, last_ref)
+
+
+def halo_planes(me, first, last, front, back, shards, shards_y):
+    cells_x, cells_z, channels = front.shape
+    shape = (first.shape[0] // cells_z + 2, cells_z, channels)
     return pl.pallas_call(
-        functools.partial(edge_kernel, choose, per_y),
+        functools.partial(halo_kernel, shards, shards_y),
         in_specs=[IN_SMEM] + in_vmem(4),
-        out_specs=in_vmem(1)[0],
-        out_shape=jax.ShapeDtypeStruct((cells_x + 2, 1, cells_z, channels), low.dtype),
-        compiler_params=pltpu.CompilerParams(vmem_limit_bytes=4 << 20),
-    )(me, left, low, high, right)
+        out_specs=in_vmem(2),
+        out_shape=[jax.ShapeDtypeStruct(shape, first.dtype)] * 2,
+        compiler_params=pltpu.CompilerParams(vmem_limit_bytes=10 << 20),
+    )(me, first, last, front, back)
 
 
 def preload_kernel(first, weight_ref, out_ref, sems):
@@ -326,10 +376,10 @@
         start = pl.multiple_of((outer_index * inner + inner_index) * block, block)
         return pl.ds(start, block)
 
-    for step in range(inner):
+    for number, step in enumerate(far_first(inner)):
         source = origin(own_inner, step, inner)
         for slot in range(outer):
-            value = row_refs[step][slot].reshape(block, channels)
+            value = row_refs[number][slot].reshape(block, channels)
             at = rows_of(origin(own_outer, slot, outer), source)
             wide[at, :] = value.astype(jnp.float32)
     low = lax.broadcasted_iota(jnp.int32, (span, channels), 1) < half
@@ -424,16 +474,30 @@
     )(me, *rows, forward_x, backward_x, weight, *loaded)
 
 
-def convolution_kernel(x, width, shards_y, per_y, me_ref, *refs):
-    *plane_refs, front_ref, back_ref, kernel_ref, out_ref, padded = refs
+def convolution_kernel(x, cells_x, width, shards, shards_y, me_ref, *refs):
+    flow_ref, paired_ref, other_ref, front_ref, back_ref, kernel_ref, out_ref, padded = refs
     _, cells_y, cells_z, channels = out_ref.shape
-    own_y = lax.div(me_ref[0], per_y)
-    for plane, ref in enumerate(plane_refs):
-        padded[plane, 1 : cells_y + 1] = ref[0]
-        edge = front_ref[x + plane, 0]
-        padded[plane, 0] = jnp.where(own_y > 0, edge, jnp.zeros_like(edge))
-        edge = back_ref[x + plane, 0]
-        padded[plane, cells_y + 1] = jnp.where(own_y < shards_y - 1, edge, jnp.zeros_like(edge))
+    own_y, own_outer, own_inner = place(me_ref[0], shards)
+    even = lax.rem(own_outer * shards[1] + own_inner, 2) == 0
+    for plane in range(width + 2):
+        p = x + plane - 1
+        if 0 <= p < cells_x:
+            padded[plane, 1 : cells_y + 1] = flow_ref[p]
+            row = front_ref[p]
+            padded[plane, 0] = jnp.where(own_y > 0, row, jnp.zeros_like(row))
+            row = back_ref[p]
+            last = own_y == shards_y - 1
+            padded[plane, cells_y + 1] = jnp.where(last, jnp.zeros_like(row), row)
+        else:
+            use_paired = jnp.logical_not(even) if p < 0 else even
+
+            @pl.when(use_paired)
+            def _(plane=plane):
+                padded[plane] = paired_ref[...]
+
+            @pl.when(jnp.logical_not(use_paired))
+            def _(plane=plane):
+                padded[plane] = other_ref[...]
 
     rows = 4 if cells_y % 4 == 0 else 1
     columns = [(k, d) for k in range(width) for d in range(3)]
@@ -471,23 +535,13 @@
     lax.fori_loop(0, cells_y // rows, chunk, 0)
 
 
-def convolution(me, x, width, flow, left, right, front, back, kernel, shards_y, per_y):
+def convolution(me, x, width, flow, halos, kernel, shards, shards_y):
     cells_x, cells_y, cells_z, channels = flow.shape
-    specs, planes = [], []
-    for p in range(x - 1, x + width + 1):
-        inside = 0 <= p < cells_x
-        planes.append(flow if inside else (left if p < 0 else right))
-        at = p if inside else 0
-        specs.append(
-            pl.BlockSpec((1, cells_y, cells_z, channels), lambda i, at=at: (at, 0, 0, 0))
-        )
-    whole = lambda array: pl.BlockSpec(array.shape, lambda i: (0,) * array.ndim)
     shape = (width, cells_y, cells_z, channels)
     return pl.pallas_call(
-        functools.partial(convolution_kernel, x, width, shards_y, per_y),
-        grid=(1,),
-        in_specs=[IN_SMEM] + specs + [whole(front), whole(back), whole(kernel)],
-        out_specs=pl.BlockSpec(shape, lambda i: (0, 0, 0, 0)),
+        functools.partial(convolution_kernel, x, cells_x, width, shards, shards_y),
+        in_specs=[IN_SMEM] + in_vmem(2 + len(halos)),
+        out_specs=in_vmem(1)[0],
         out_shape=jax.ShapeDtypeStruct(shape, jnp.bfloat16),
         scratch_shapes=[pltpu.VMEM((width + 2, cells_y + 2, cells_z, channels), flow.dtype)],
         compiler_params=pltpu.CompilerParams(vmem_limit_bytes=14 << 20),
@@ -496,7 +550,7 @@
             bytes_accessed=10 * cells_y * cells_z * channels,
             transcendentals=0,
         ),
-    )(me, *planes, front, back, kernel)
+    )(me, flow, *halos, kernel)
 
 
 def final_kernel(shards, shards_y, me_ref, table_ref, *refs):
@@ -513,6 +567,7 @@
     def _():
         for number, ref in enumerate(piece_refs):
             step, slot = divmod(number, outer)
+            slot = far_first(outer)[slot]
             source_y = lax.rem(own_y + (shards_y - step), shards_y)
             source = source_y * outer + origin(own_outer, slot, outer)
             for part in range(inner):
@@ -684,6 +739,12 @@
     return lax.ppermute(last, axis, up), lax.ppermute(first, axis, down)
 
 
+def with_neighbour(array, start, axis):
+    size = lax.axis_size(axis)
+    pairs = [(i, i + 1) for i in range(start, size - 1, 2)]
+    return lax.ppermute(array, axis, pairs + [(j, i) for i, j in pairs])
+
+
 def exchange(array, step, shards, along_outer):
     outer, inner = shards
     pairs = []
@@ -709,50 +770,55 @@
         convolved = split_pair_convolve(flow, conv_weight)
         return jax.nn.gelu(spectral + convolved + bias, approximate=True).astype(jnp.bfloat16)
 
+    barrier = lax.optimization_barrier
     inner = max(d for d in range(1, shards_x + 1) if shards_x % d == 0 and d * d <= shards_x)
-    shards = (shards_x // inner, inner)
-    outer = shards[0]
+    outer = shards_x // inner
+    shards = (outer, inner)
     me = lax.axis_index(("gy", "gx")).astype(jnp.int32).reshape(1)
     sizes = (shards_x, shards_y, pairs, cells_y, cells_z)
     full_x = cells_x * shards_x
-
     weight = spectral_weight.reshape(items, MX, channels, channels)
+    early = pairs // 4
 
     table = jnp.asarray(forward_yz_table(*sizes))
     columns = flow.reshape(cells_x, cells_y * cells_z, channels)
-    order = list(range(outer - 1, -1, -1))
+    order = far_first(outer)
     cut = (outer + 1) // 2
     pieces = [piece for piece in (order[:cut], order[cut:]) if piece]
     arrived = [[] for _ in pieces]
     for step in range(1, shards_y):
-        sent = forward_yz(me, table, columns, step, shards, shards_y, pieces, jnp.bfloat16)
-        sent, columns, weight = lax.optimization_barrier((sent, columns, weight))
+        sent = forward_yz(me, table, columns, step, shards, shards_y, pieces)
+        sent, columns, weight = barrier((sent, columns, weight))
         for into, piece in zip(arrived, sent):
             into.append(over_y(piece, step, shards_y))
-    *kept, first, last, low, high = forward_yz(
-        me, table, columns, 0, shards, shards_y, pieces, jnp.float32, edges=cells_z
-    )
-    first, last = (x.reshape(1, cells_y, cells_z, channels) for x in (first, last))
-
-    early = pairs // 4
+    kept = forward_yz(me, table, columns, 0, shards, shards_y, pieces, cells_z)
+    kept, (first, last, *ends) = kept[: len(pieces)], kept[len(pieces) :]
+    if shards_y == 2:
+        front = back = over_y(ends[0], 1, shards_y)
+    else:
+        front, back = neighbours(*ends, "gy")
     loaded = [preload(weight, 0, early)] if early else []
-    loaded, arrived = lax.optimization_barrier((loaded, arrived))
-    by_outer = [None] * outer
+    loaded, arrived[0] = barrier((loaded, arrived[0]))
+
+    by_outer = []
     for piece, own, parts in zip(pieces, kept, arrived):
         for step, total in zip(piece, add_pieces(own, parts)):
-            by_outer[step] = exchange(total, step, shards, True) if step else total
+            by_outer.append(exchange(total, step, shards, True) if step else total)
     if early:
         loaded.append(preload(weight, early, early))
-    by_outer, loaded = lax.optimization_barrier((by_outer, loaded))
+    by_outer, loaded, weight = barrier((by_outer, loaded, weight))
     by_inner = regroup(me, by_outer, shards, True)
-    by_inner, weight = lax.optimization_barrier((by_inner, weight))
+    by_inner, weight = barrier((by_inner, weight))
+    rows = [
+        exchange(by_inner[step], step, shards, False) if step else by_inner[0]
+        for step in far_first(inner)
+    ]
     if early:
         loaded.append(preload(weight, 2 * early, 1))
-    rows = [by_inner[0]] + [exchange(by_inner[s], s, shards, False) for s in range(1, inner)]
-    rows, first, last = lax.optimization_barrier((rows, first, last))
-    left, right = neighbours(first, last, "gx")
-
-
+
+    rows, loaded, first, last, front, back = barrier((rows, loaded, first, last, front, back))
+    planes = halo_planes(me, first, last, front, back, shards, shards_y)
+    planes = [with_neighbour(plane, start, "gx") for start, plane in enumerate(planes)]
     returned = mixing(
         me,
         rows,
@@ -762,27 +828,24 @@
         loaded,
         shards,
     )
-    returned, left, right = lax.optimization_barrier((returned, left, right))
-    if shards_y == 2:
-        edge = y_edge(me, left, low, high, right, shards_x, lambda own: own > 0)
-        front = back = over_y(edge, 1, shards_y)
-    else:
-        ends = [
-            y_edge(me, left, low, high, right, shards_x, lambda own, use=use: own >= use)
-            for use in (0, shards_y)
-        ]
-        front, back = neighbours(*ends, "gy")
-    planes = (flow, left, right, front, back, conv_weight)
+    returned, planes = barrier((list(returned), planes))
+    halos = (*planes, front, back)
     width = 2 if cells_x % 2 == 0 else 1
     convolved = [
-        convolution(me, x, width, *planes, shards_y, shards_x) for x in range(0, cells_x, width)
+        convolution(me, x, width, flow, halos, conv_weight, shards, shards_y)
+        for x in range(0, cells_x, width)
     ]
 
-    returned = [returned[0]] + [
-        exchange(returned[s], s, shards, False) for s in range(1, inner)
+    returned = [
+        exchange(returned[step], step, shards, False) if step else returned[0]
+        for step in far_first(inner)
     ]
+    returned, convolved[0] = barrier((returned, convolved[0]))
     returned = regroup(me, returned, shards, False)
-    returned = [returned[0]] + [exchange(returned[s], s, shards, True) for s in range(1, outer)]
+    returned = [
+        exchange(returned[step], step, shards, True) if step else returned[0]
+        for step in far_first(outer)
+    ]
     coefficients = list(returned)
     for step in range(1, shards_y):
         coefficients += [over_y(part, step, shards_y) for part in returned]

time: 66.4 us -> 62.1 us (0.935)
  waiting for transfers between devices: 10.1 us -> 5.9 us
  starting transfers between devices: 26.9 us -> 28.1 us
  Pallas kernels: 28.9 us -> 27.7 us
    ppermute x12, waiting for transfers between devices: 8.92 us -> 5.06 us  [exchange(): return lax.ppermute(array, 'gx', pairs)]
    ppermute x12, starting transfers between devices: 14.6 us -> 18.1 us  [exchange(): return lax.ppermute(array, 'gx', pairs)]
    ppermute x2, starting transfers between devices: 3.5 us -> 0.92 us  [with_neighbour(): return lax.ppermute(array, axis, pairs + [(j, i) for i, j in pairs])]
    pallas_call x5, Pallas kernels: 10.6 us -> 9.47 us  [the longest x2 5.99 us: convolution(): pl.pallas_call(functools.partial(convolution_kernel, x, cells_x, width, s...]
where the time goes in v7:
time: 62.1 us; the launch traced here: 62 us
  starting transfers between devices  28.1 us (45%)
  Pallas kernels  27.7 us (45%)
  waiting for transfers between devices  5.9 us (10%)
    ppermute x12, starting transfers between devices, exchange(): return lax.ppermute(array, 'gx', pairs)  18.1 us
    pallas_call x3, Pallas kernels, preload(): pl.pallas_call(functools.partial(preload_kernel, 2 * pair), in_specs=[pl....  9.15 us
    ppermute x7, starting transfers between devices, over_y(): lax.ppermute(array, 'gy', [(i, (i + step) % shards_y) for i in range(shar...  9.09 us
    pallas_call x1, Pallas kernels, mixing(): pl.pallas_call(functools.partial(mixing_kernel, shards, len(loaded)), in_...  6.08 us
    pallas_call x2, Pallas kernels, convolution(): pl.pallas_call(functools.partial(convolution_kernel, x, cells_x, width, s...  5.99 us
    ppermute x12, waiting for transfers between devices, exchange(): return lax.ppermute(array, 'gx', pairs)  5.06 us
    pallas_call x2, Pallas kernels, forward_yz(): pl.pallas_call(kernel, in_specs=[IN_SMEM] + specs, out_specs=in_vmem(len(...  3.42 us
    pallas_call x1, Pallas kernels, final(): pl.pallas_call(functools.partial(final_kernel, shards, shards_y), grid_sp...  2.89 us
  transfers between devices with their start and end apart: 21, of which 7 were waited for; matrix products, arithmetic and copies ran while one was open for 0% of the time, Pallas kernels for 35%

profile of v7, /device:TPU:0, one launch (start us, length us, event | category | flops | bytes accessed | tf_op | source)
XLA Modules:
  0.0 62.0 jit_solution(16277302034777976787)
XLA Ops:
  0.0 3.0 %shard_map.82 = (bf16[2,4,4,16,128]{4,3,2,1,0:T(8,128)(2,1)}, bf16[2,4,4,16,128]{4,3,2,1,0:T(8,128)(2,1)}) custom-call(s32[1]{0:T(128)} %bitcast.me_ref, bf16[2,512,1024]{2,1,0:T(8,128)(2,1)} %constant.18.clone.table_ref, bf16[4,1024,128]{2,1,0:T(8,128)(2,1)} %bitcast.4), custom_call_target="tpu_custom_call" | custom-call | flops 268435456 | bytes 1572864 | tf_op jit(solution)/shard_map/pallas_call | solution.py:219
  3.0 0.0 copy-start
  3.0 0.0 copy-start.1
  3.0 3.0 %collective-permute-start.3 = (bf16[2,4,4,16,128]{4,3,2,1,0:T(8,128)(2,1)}, bf16[2,4,4,16,128]{4,3,2,1,0:T(8,128)(2,1)S(1)}, u32[]{:S(2)}, u32[]{:S(2)}) collective-permute-start(bf16[2,4,4,16,128]{4,3,2,1,0:T(8,128)(2,1)} %get-tuple-element.80), channel_id=1, source_target_pairs={{0,1},{1,0},{2,3},{3,2},{4,5},{5,4},{6,7},{7,6},{8,9},{9,8},{10,11... | collective-permute-start | bytes 393224 | tf_op jit(solution)/shard_map/ppermute | solution.py:760
  6.0 0.1 collective-permute-start
  6.1 3.5 %shard_map.84.refs_7_ = bf16[4,64,128,128]{3,2,1,0:T(8,128)(2,1)S(1)} custom-call(bf16[16,64,128,128]{3,2,1,0:T(8,128)(2,1)} %bitcast.7), custom_call_target="tpu_custom_call" | custom-call | bytes 8388608 | tf_op jit(solution)/shard_map/pallas_call | solution.py:336
  9.6 0.4 shard_map.83
  10.1 0.5 collective-permute-done.3.refs_1_
  10.6 2.2 %collective-permute-start.4 = (bf16[4,4,16,128]{3,2,1,0:T(8,128)(2,1)S(1)}, bf16[4,4,16,128]{3,2,1,0:T(8,128)(2,1)S(1)}, u32[]{:S(2)}, u32[]{:S(2)}) collective-permute-start(bf16[4,4,16,128]{3,2,1,0:T(8,128)(2,1)S(1)} %get-tuple-element.81), channel_id=1, source_target_pairs={{0,8},{2,10},{4,12},{6,14},{8,0},{10,2},{12,4},{14,6},{16,24},{18,... | collective-permute-start | bytes 196616 | tf_op jit(solution)/shard_map/ppermute | solution.py:756
  12.8 0.0 collective-permute-done.refs_1_
  12.8 3.6 %collective-permute-start.1 = (bf16[4,4,16,128]{3,2,1,0:T(8,128)(2,1)S(1)}, bf16[4,4,16,128]{3,2,1,0:T(8,128)(2,1)S(1)}, u32[]{:S(2)}, u32[]{:S(2)}) collective-permute-start(bf16[4,4,16,128]{3,2,1,0:T(8,128)(2,1)S(1)} %get-tuple-element.77), channel_id=1, source_target_pairs={{0,24},{2,26},{4,28},{6,30},{8,16},{10,18},{12,20},{14,22},{16,8},... | collective-permute-start | bytes 196616 | tf_op jit(solution)/shard_map/ppermute | solution.py:756
  16.5 0.0 collective-permute-start.2
  16.5 1.5 %collective-permute-start.8 = (bf16[4,64,128]{2,1,0:T(8,128)(2,1)S(1)}, bf16[4,64,128]{2,1,0:T(8,128)(2,1)S(1)}, u32[]{:S(2)}, u32[]{:S(2)}) collective-permute-start(bf16[4,64,128]{2,1,0:T(8,128)(2,1)S(1)} %get-tuple-element.102), channel_id=1, source_target_pairs={{0,1},{1,0},{2,3},{3,2},{4,5},{5,4},{6,7},{7,6},{8,9},{9,8},{10,11... | collective-permute-start | bytes 196616 | tf_op jit(solution)/shard_map/ppermute | solution.py:760
  18.0 3.5 %shard_map.87.refs_8_ = bf16[4,64,128,128]{3,2,1,0:T(8,128)(2,1)S(1)} custom-call(bf16[16,64,128,128]{3,2,1,0:T(8,128)(2,1)} %bitcast.8), custom_call_target="tpu_custom_call" | custom-call | bytes 8388608 | tf_op jit(solution)/shard_map/pallas_call | solution.py:336
  21.5 0.0 collective-permute-done.1.refs_0_
  21.5 0.2 collective-permute-done.2.refs_1_
  21.7 0.0 copy-start.3
  21.7 0.0 copy-start.4
  21.7 0.3 collective-permute-start.5
  22.0 1.4 %collective-permute-start.6 = (bf16[4,4,16,128]{3,2,1,0:T(8,128)(2,1)S(1)}, bf16[4,4,16,128]{3,2,1,0:T(8,128)(2,1)S(1)}, u32[]{:S(2)}, u32[]{:S(2)}) collective-permute-start(bf16[4,4,16,128]{3,2,1,0:T(8,128)(2,1)S(1)} %get-tuple-element.94), channel_id=1, source_target_pairs={{0,4},{2,6},{4,0},{6,2},{8,12},{10,14},{12,8},{14,10},{16,20},{18,... | collective-permute-start | bytes 196616 | tf_op jit(solution)/shard_map/ppermute | solution.py:756
  23.3 0.3 collective-permute-start.7
  23.6 2.2 %shard_map.89.refs_9_ = bf16[2,64,128,128]{3,2,1,0:T(8,128)(2,1)S(1)} custom-call(bf16[16,64,128,128]{3,2,1,0:T(8,128)(2,1)} %bitcast.9), custom_call_target="tpu_custom_call" | custom-call | bytes 4194304 | tf_op jit(solution)/shard_map/pallas_call | solution.py:336
  25.9 0.3 collective-permute-done.5.refs_0_
  26.1 1.5 %collective-permute-done.6.refs_1_ = bf16[4,4,16,128]{3,2,1,0:T(8,128)(2,1)S(1)} collective-permute-done((bf16[4,4,16,128]{3,2,1,0:T(8,128)(2,1)S(1)}, bf16[4,4,16,128]{3,2,1,0:T(8,128)(2,1)S(1)}, u32[]{:S(2)}, u32[]{:S(2)}) %collective-permute-start.6) | collective-permute-done | bytes 65568 | tf_op jit(solution)/shard_map/ppermute | solution.py:756
  27.6 0.0 collective-permute-done.7.refs_2_
  27.6 0.1 shard_map.91
  27.6 0.1 collective-permute-start.9
  27.8 0.8 %collective-permute-start.10 = (bf16[18,64,128]{2,1,0:T(8,128)(2,1)S(1)}, bf16[18,64,128]{2,1,0:T(8,128)(2,1)S(1)}, u32[]{:S(2)}, u32[]{:S(2)}) collective-permute-start(bf16[18,64,128]{2,1,0:T(8,128)(2,1)S(1)} %get-tuple-element.119), channel_id=1, source_target_pairs={{2,4},{6,8},{10,12},{14,16},{18,20},{22,24},{26,28},{4,2},{8,6},{1... | collective-permute-start | bytes 884744 | tf_op jit(solution)/shard_map/ppermute | solution.py:745
  28.6 6.1 %shard_map.90 = (bf16[4,4,16,128]{3,2,1,0:T(8,128)(2,1)S(1)}, bf16[4,4,16,128]{3,2,1,0:T(8,128)(2,1)S(1)}, bf16[4,4,16,128]{3,2,1,0:T(8,128)(2,1)S(1)}, bf16[4,4,16,128]{3,2,1,0:T(8,128)(2,1)S(1)}) custom-call(s32[1]{0:T(128)} %bitcast.me_ref, bf16[4,4,16,128]{3,2,1,0:T(8,128)(2,1)S(1)} %collective-permute-done.5.refs_0_, ...), custom_call_target="tpu_custom_call" | custom-call | flops 134217728 | bytes 33554432 | tf_op jit(solution)/shard_map/pallas_call | solution.py:455
  34.7 0.0 copy-start.2
  34.7 0.0 copy-start.5
  34.7 3.1 %collective-permute-start.11 = (bf16[4,4,16,128]{3,2,1,0:T(8,128)(2,1)S(1)}, bf16[4,4,16,128]{3,2,1,0:T(8,128)(2,1)S(1)}, u32[]{:S(2)}, u32[]{:S(2)}) collective-permute-start(bf16[4,4,16,128]{3,2,1,0:T(8,128)(2,1)S(1)} %get-tuple-element.120), channel_id=1, source_target_pairs={{0,6},{2,4},{4,2},{6,0},{8,14},{10,12},{12,10},{14,8},{16,22},{18,... | collective-permute-start | bytes 196616 | tf_op jit(solution)/shard_map/ppermute | solution.py:756
  37.9 2.0 %collective-permute-start.12 = (bf16[4,4,16,128]{3,2,1,0:T(8,128)(2,1)S(1)}, bf16[4,4,16,128]{3,2,1,0:T(8,128)(2,1)S(1)}, u32[]{:S(2)}, u32[]{:S(2)}) collective-permute-start(bf16[4,4,16,128]{3,2,1,0:T(8,128)(2,1)S(1)} %get-tuple-element.121), channel_id=1, source_target_pairs={{0,4},{2,6},{4,0},{6,2},{8,12},{10,14},{12,8},{14,10},{16,20},{18,... | collective-permute-start | bytes 196616 | tf_op jit(solution)/shard_map/ppermute | solution.py:756
  39.9 0.1 collective-permute-start.13
  39.9 3.0 %shard_map.92.refs_8_ = bf16[2,16,64,128]{3,2,1,0:T(8,128)(2,1)S(1)} custom-call(s32[1]{0:T(128)} %bitcast.me_ref, bf16[4,16,64,128]{3,2,1,0:T(8,128)(2,1)S(1)} %copy-done.1, bf16[18,64,128]{2,1,0:T(8,128)(2,1)S(1)} %collective-permute-done.9.refs_1_, bf16[18,64,128]{2,1,0:T(8,128)(2,1)S(1)} %collective-permute-done.10.refs_2_, ...), custom_call_target="tpu_custom_call" | custom-call | flops 2717908992 | bytes 1310720 | tf_op jit(solution)/shard_map/pallas_call | solution.py:541
  43.0 0.0 collective-permute-done.12.refs_1_
  43.0 3.8 %collective-permute-start.14 = (bf16[4,4,16,128]{3,2,1,0:T(8,128)(2,1)S(1)}, bf16[4,4,16,128]{3,2,1,0:T(8,128)(2,1)S(1)}, u32[]{:S(2)}, u32[]{:S(2)}) collective-permute-start(bf16[4,4,16,128]{3,2,1,0:T(8,128)(2,1)S(1)} %get-tuple-element.130), channel_id=1, source_target_pairs={{0,24},{2,26},{4,28},{6,30},{8,16},{10,18},{12,20},{14,22},{16,8},... | collective-permute-start | bytes 196616 | tf_op jit(solution)/shard_map/ppermute | solution.py:756
  46.8 0.8 %collective-permute-start.15 = (bf16[4,4,16,128]{3,2,1,0:T(8,128)(2,1)S(1)}, bf16[4,4,16,128]{3,2,1,0:T(8,128)(2,1)S(1)}, u32[]{:S(2)}, u32[]{:S(2)}) collective-permute-start(bf16[4,4,16,128]{3,2,1,0:T(8,128)(2,1)S(1)} %get-tuple-element.131), channel_id=1, source_target_pairs={{0,16},{2,18},{4,20},{6,22},{8,24},{10,26},{12,28},{14,30},{16,0},... | collective-permute-start | bytes 196616 | tf_op jit(solution)/shard_map/ppermute | solution.py:756
  47.6 0.5 collective-permute-start.16
  48.1 0.9 %collective-permute-start.20 = (bf16[4,4,16,128]{3,2,1,0:T(8,128)(2,1)S(1)}, bf16[4,4,16,128]{3,2,1,0:T(8,128)(2,1)S(1)}, u32[]{:S(2)}, u32[]{:S(2)}) collective-permute-start(bf16[4,4,16,128]{3,2,1,0:T(8,128)(2,1)S(1)} %get-tuple-element.133.refs_3_), channel_id=1, source_target_pairs={{0,1},{1,0},{2,3},{3,2},{4,5},{5,4},{6,7},{7,6},{8,9},{9,8},{10,11... | collective-permute-start | bytes 196616 | tf_op jit(solution)/shard_map/ppermute | solution.py:760
  49.0 0.6 collective-permute-done.14.refs_0_
  49.6 1.5 %collective-permute-start.17 = (bf16[4,4,16,128]{3,2,1,0:T(8,128)(2,1)S(1)}, bf16[4,4,16,128]{3,2,1,0:T(8,128)(2,1)S(1)}, u32[]{:S(2)}, u32[]{:S(2)}) collective-permute-start(bf16[4,4,16,128]{3,2,1,0:T(8,128)(2,1)S(1)} %collective-permute-done.14.refs_0_), channel_id=1, source_target_pairs={{0,1},{1,0},{2,3},{3,2},{4,5},{5,4},{6,7},{7,6},{8,9},{9,8},{10,11... | collective-permute-start | bytes 196616 | tf_op jit(solution)/shard_map/ppermute | solution.py:760
  51.1 2.6 %collective-permute-done.15.refs_1_ = bf16[4,4,16,128]{3,2,1,0:T(8,128)(2,1)S(1)} collective-permute-done((bf16[4,4,16,128]{3,2,1,0:T(8,128)(2,1)S(1)}, bf16[4,4,16,128]{3,2,1,0:T(8,128)(2,1)S(1)}, u32[]{:S(2)}, u32[]{:S(2)}) %collective-permute-start.15) | collective-permute-done | bytes 65568 | tf_op jit(solution)/shard_map/ppermute | solution.py:756
  53.7 0.9 %collective-permute-start.18 = (bf16[4,4,16,128]{3,2,1,0:T(8,128)(2,1)S(1)}, bf16[4,4,16,128]{3,2,1,0:T(8,128)(2,1)S(1)}, u32[]{:S(2)}, u32[]{:S(2)}) collective-permute-start(bf16[4,4,16,128]{3,2,1,0:T(8,128)(2,1)S(1)} %collective-permute-done.15.refs_1_), channel_id=1, source_target_pairs={{0,1},{1,0},{2,3},{3,2},{4,5},{5,4},{6,7},{7,6},{8,9},{9,8},{10,11... | collective-permute-start | bytes 196616 | tf_op jit(solution)/shard_map/ppermute | solution.py:760
  54.6 1.1 %collective-permute-start.19 = (bf16[4,4,16,128]{3,2,1,0:T(8,128)(2,1)S(1)}, bf16[4,4,16,128]{3,2,1,0:T(8,128)(2,1)S(1)}, u32[]{:S(2)}, u32[]{:S(2)}) collective-permute-start(bf16[4,4,16,128]{3,2,1,0:T(8,128)(2,1)S(1)} %collective-permute-done.16.refs_2_), channel_id=1, source_target_pairs={{0,1},{1,0},{2,3},{3,2},{4,5},{5,4},{6,7},{7,6},{8,9},{9,8},{10,11... | collective-permute-start | bytes 196616 | tf_op jit(solution)/shard_map/ppermute | solution.py:760
  55.7 3.0 %shard_map.94.refs_9_ = bf16[2,16,64,128]{3,2,1,0:T(8,128)(2,1)S(1)} custom-call(s32[1]{0:T(128)} %bitcast.me_ref, bf16[4,16,64,128]{3,2,1,0:T(8,128)(2,1)S(1)} %copy-done.1, bf16[18,64,128]{2,1,0:T(8,128)(2,1)S(1)} %collective-permute-done.9.refs_1_, bf16[18,64,128]{2,1,0:T(8,128)(2,1)S(1)} %collective-permute-done.10.refs_2_, ...), custom_call_target="tpu_custom_call" | custom-call | flops 2717908992 | bytes 1310720 | tf_op jit(solution)/shard_map/pallas_call | solution.py:541
  58.7 0.3 collective-permute-done.19.refs_6_
  59.1 2.9 %shard_map.95 = bf16[4,16,64,128]{3,2,1,0:T(8,128)(2,1)} custom-call(s32[1]{0:T(128)} %bitcast.me_ref, bf16[2,1024,512]{2,1,0:T(8,128)(2,1)S(1)} %copy-done.2, bf16[4,4,16,128]{3,2,1,0:T(8,128)(2,1)S(1)} %collective-permute-done.14.refs_0_, bf16[4,4,16,128]{3,2,1,0:T(8,128)(2,1)S(1)} %collective-permute-done.15.refs_1_, ...), custom_call_target="tpu_custom_call" | custom-call | flops 536870912 | bytes 3145728 | tf_op jit(solution)/shard_map/pallas_call | solution.py:599
  (22 shorter events, 0.1 us)
Async XLA Ops:
  3.0 6.6 %copy-start = (bf16[2,512,1024]{2,1,0:T(8,128)(2,1)S(1)}, bf16[2,512,1024]{2,1,0:T(8,128)(2,1)}, u32[]{:S(2)}) copy-start(bf16[2,512,1024]{2,1,0:T(8,128)(2,1)} %constant.18.clone.table_ref) | copy-start | bytes 6291460
  3.0 6.6 %copy-start.1 = (bf16[4,16,64,128]{3,2,1,0:T(8,128)(2,1)S(1)}, bf16[4,16,64,128]{3,2,1,0:T(8,128)(2,1)}, u32[]{:S(2)}) copy-start(bf16[4,16,64,128]{3,2,1,0:T(8,128)(2,1)} %refs_0_.3) | copy-start | bytes 3145732
  3.0 7.6 %collective-permute-start.3 = (bf16[2,4,4,16,128]{4,3,2,1,0:T(8,128)(2,1)}, bf16[2,4,4,16,128]{4,3,2,1,0:T(8,128)(2,1)S(1)}, u32[]{:S(2)}, u32[]{:S(2)}) collective-permute-start(bf16[2,4,4,16,128]{4,3,2,1,0:T(8,128)(2,1)} %get-tuple-element.80), channel_id=1, source_target_pairs={{0,1},{1,0},{2,3},{3,2},{4,5},{5,4},{6,7},{7,6},{8,9},{9,8},{10,11... | collective-permute-start | bytes 393224 | tf_op jit(solution)/shard_map/ppermute | solution.py:760
  6.0 6.8 %collective-permute-start = (bf16[2,4,4,16,128]{4,3,2,1,0:T(8,128)(2,1)}, bf16[2,4,4,16,128]{4,3,2,1,0:T(8,128)(2,1)S(1)}, u32[]{:S(2)}, u32[]{:S(2)}) collective-permute-start(bf16[2,4,4,16,128]{4,3,2,1,0:T(8,128)(2,1)} %get-tuple-element.75), channel_id=1, source_target_pairs={{0,1},{1,0},{2,3},{3,2},{4,5},{5,4},{6,7},{7,6},{8,9},{9,8},{10,11... | collective-permute-start | bytes 393224 | tf_op jit(solution)/shard_map/ppermute | solution.py:760
  10.6 10.9 %collective-permute-start.4 = (bf16[4,4,16,128]{3,2,1,0:T(8,128)(2,1)S(1)}, bf16[4,4,16,128]{3,2,1,0:T(8,128)(2,1)S(1)}, u32[]{:S(2)}, u32[]{:S(2)}) collective-permute-start(bf16[4,4,16,128]{3,2,1,0:T(8,128)(2,1)S(1)} %get-tuple-element.81), channel_id=1, source_target_pairs={{0,8},{2,10},{4,12},{6,14},{8,0},{10,2},{12,4},{14,6},{16,24},{18,... | collective-permute-start | bytes 196616 | tf_op jit(solution)/shard_map/ppermute | solution.py:756
  12.8 8.7 %collective-permute-start.1 = (bf16[4,4,16,128]{3,2,1,0:T(8,128)(2,1)S(1)}, bf16[4,4,16,128]{3,2,1,0:T(8,128)(2,1)S(1)}, u32[]{:S(2)}, u32[]{:S(2)}) collective-permute-start(bf16[4,4,16,128]{3,2,1,0:T(8,128)(2,1)S(1)} %get-tuple-element.77), channel_id=1, source_target_pairs={{0,24},{2,26},{4,28},{6,30},{8,16},{10,18},{12,20},{14,22},{16,8},... | collective-permute-start | bytes 196616 | tf_op jit(solution)/shard_map/ppermute | solution.py:756
  16.5 5.2 %collective-permute-start.2 = (bf16[4,4,16,128]{3,2,1,0:T(8,128)(2,1)S(1)}, bf16[4,4,16,128]{3,2,1,0:T(8,128)(2,1)S(1)}, u32[]{:S(2)}, u32[]{:S(2)}) collective-permute-start(bf16[4,4,16,128]{3,2,1,0:T(8,128)(2,1)S(1)} %get-tuple-element.78), channel_id=1, source_target_pairs={{0,16},{2,18},{4,20},{6,22},{8,24},{10,26},{12,28},{14,30},{16,0},... | collective-permute-start | bytes 196616 | tf_op jit(solution)/shard_map/ppermute | solution.py:756
  16.5 9.4 %collective-permute-start.8 = (bf16[4,64,128]{2,1,0:T(8,128)(2,1)S(1)}, bf16[4,64,128]{2,1,0:T(8,128)(2,1)S(1)}, u32[]{:S(2)}, u32[]{:S(2)}) collective-permute-start(bf16[4,64,128]{2,1,0:T(8,128)(2,1)S(1)} %get-tuple-element.102), channel_id=1, source_target_pairs={{0,1},{1,0},{2,3},{3,2},{4,5},{5,4},{6,7},{7,6},{8,9},{9,8},{10,11... | collective-permute-start | bytes 196616 | tf_op jit(solution)/shard_map/ppermute | solution.py:760
  21.7 6.9 %copy-start.3 = (bf16[256,128]{1,0:T(8,128)(2,1)S(1)}, bf16[256,128]{1,0:T(8,128)(2,1)}, u32[]{:S(2)}) copy-start(bf16[256,128]{1,0:T(8,128)(2,1)} %constant.19.clone.refs_4_) | copy-start | bytes 196612
  21.7 6.9 %copy-start.4 = (bf16[128,128]{1,0:T(8,128)(2,1)S(1)}, bf16[128,128]{1,0:T(8,128)(2,1)}, u32[]{:S(2)}) copy-start(bf16[128,128]{1,0:T(8,128)(2,1)} %constant.20.clone.refs_5_) | copy-start | bytes 98308
  21.7 4.4 %collective-permute-start.5 = (bf16[4,4,16,128]{3,2,1,0:T(8,128)(2,1)S(1)}, bf16[4,4,16,128]{3,2,1,0:T(8,128)(2,1)S(1)}, u32[]{:S(2)}, u32[]{:S(2)}) collective-permute-start(bf16[4,4,16,128]{3,2,1,0:T(8,128)(2,1)S(1)} %get-tuple-element.93), channel_id=1, source_target_pairs={{0,6},{2,4},{4,2},{6,0},{8,14},{10,12},{12,10},{14,8},{16,22},{18,... | collective-permute-start | bytes 196616 | tf_op jit(solution)/shard_map/ppermute | solution.py:756
  22.0 5.6 %collective-permute-start.6 = (bf16[4,4,16,128]{3,2,1,0:T(8,128)(2,1)S(1)}, bf16[4,4,16,128]{3,2,1,0:T(8,128)(2,1)S(1)}, u32[]{:S(2)}, u32[]{:S(2)}) collective-permute-start(bf16[4,4,16,128]{3,2,1,0:T(8,128)(2,1)S(1)} %get-tuple-element.94), channel_id=1, source_target_pairs={{0,4},{2,6},{4,0},{6,2},{8,12},{10,14},{12,8},{14,10},{16,20},{18,... | collective-permute-start | bytes 196616 | tf_op jit(solution)/shard_map/ppermute | solution.py:756
  23.3 4.2 %collective-permute-start.7 = (bf16[4,4,16,128]{3,2,1,0:T(8,128)(2,1)S(1)}, bf16[4,4,16,128]{3,2,1,0:T(8,128)(2,1)S(1)}, u32[]{:S(2)}, u32[]{:S(2)}) collective-permute-start(bf16[4,4,16,128]{3,2,1,0:T(8,128)(2,1)S(1)} %get-tuple-element.95), channel_id=1, source_target_pairs={{0,2},{2,0},{4,6},{6,4},{8,10},{10,8},{12,14},{14,12},{16,18},{18,... | collective-permute-start | bytes 196616 | tf_op jit(solution)/shard_map/ppermute | solution.py:756
  27.6 7.0 %collective-permute-start.9 = (bf16[18,64,128]{2,1,0:T(8,128)(2,1)S(1)}, bf16[18,64,128]{2,1,0:T(8,128)(2,1)S(1)}, u32[]{:S(2)}, u32[]{:S(2)}) collective-permute-start(bf16[18,64,128]{2,1,0:T(8,128)(2,1)S(1)} %get-tuple-element.118), channel_id=1, source_target_pairs={{0,2},{4,6},{8,10},{12,14},{16,18},{20,22},{24,26},{28,30},{2,0},{... | collective-permute-start | bytes 884744 | tf_op jit(solution)/shard_map/ppermute | solution.py:745
  27.8 12.2 %copy-start.6 = (bf16[3,3,3,128,128]{4,3,2,1,0:T(8,128)(2,1)S(1)}, bf16[3,3,3,128,128]{4,3,2,1,0:T(8,128)(2,1)}, u32[]{:S(2)}) copy-start(bf16[3,3,3,128,128]{4,3,2,1,0:T(8,128)(2,1)} %refs_5_.4) | copy-start | bytes 2654212
  27.8 6.9 %collective-permute-start.10 = (bf16[18,64,128]{2,1,0:T(8,128)(2,1)S(1)}, bf16[18,64,128]{2,1,0:T(8,128)(2,1)S(1)}, u32[]{:S(2)}, u32[]{:S(2)}) collective-permute-start(bf16[18,64,128]{2,1,0:T(8,128)(2,1)S(1)} %get-tuple-element.119), channel_id=1, source_target_pairs={{2,4},{6,8},{10,12},{14,16},{18,20},{22,24},{26,28},{4,2},{8,6},{1... | collective-permute-start | bytes 884744 | tf_op jit(solution)/shard_map/ppermute | solution.py:745
  34.7 24.4 %copy-start.2 = (bf16[2,1024,512]{2,1,0:T(8,128)(2,1)S(1)}, bf16[2,1024,512]{2,1,0:T(8,128)(2,1)}, u32[]{:S(2)}) copy-start(bf16[2,1024,512]{2,1,0:T(8,128)(2,1)} %constant.21.clone.table_ref) | copy-start | bytes 6291460
  34.7 24.4 %copy-start.5 = (f32[128]{0:T(128)S(1)}, f32[128]{0:T(128)}, u32[]{:S(2)}) copy-start(f32[128]{0:T(128)} %param.11) | copy-start | bytes 1540
  34.7 8.2 %collective-permute-start.11 = (bf16[4,4,16,128]{3,2,1,0:T(8,128)(2,1)S(1)}, bf16[4,4,16,128]{3,2,1,0:T(8,128)(2,1)S(1)}, u32[]{:S(2)}, u32[]{:S(2)}) collective-permute-start(bf16[4,4,16,128]{3,2,1,0:T(8,128)(2,1)S(1)} %get-tuple-element.120), channel_id=1, source_target_pairs={{0,6},{2,4},{4,2},{6,0},{8,14},{10,12},{12,10},{14,8},{16,22},{18,... | collective-permute-start | bytes 196616 | tf_op jit(solution)/shard_map/ppermute | solution.py:756
  37.9 5.1 %collective-permute-start.12 = (bf16[4,4,16,128]{3,2,1,0:T(8,128)(2,1)S(1)}, bf16[4,4,16,128]{3,2,1,0:T(8,128)(2,1)S(1)}, u32[]{:S(2)}, u32[]{:S(2)}) collective-permute-start(bf16[4,4,16,128]{3,2,1,0:T(8,128)(2,1)S(1)} %get-tuple-element.121), channel_id=1, source_target_pairs={{0,4},{2,6},{4,0},{6,2},{8,12},{10,14},{12,8},{14,10},{16,20},{18,... | collective-permute-start | bytes 196616 | tf_op jit(solution)/shard_map/ppermute | solution.py:756
  39.9 3.1 %collective-permute-start.13 = (bf16[4,4,16,128]{3,2,1,0:T(8,128)(2,1)S(1)}, bf16[4,4,16,128]{3,2,1,0:T(8,128)(2,1)S(1)}, u32[]{:S(2)}, u32[]{:S(2)}) collective-permute-start(bf16[4,4,16,128]{3,2,1,0:T(8,128)(2,1)S(1)} %get-tuple-element.122), channel_id=1, source_target_pairs={{0,2},{2,0},{4,6},{6,4},{8,10},{10,8},{12,14},{14,12},{16,18},{18,... | collective-permute-start | bytes 196616 | tf_op jit(solution)/shard_map/ppermute | solution.py:756
  43.0 6.5 %collective-permute-start.14 = (bf16[4,4,16,128]{3,2,1,0:T(8,128)(2,1)S(1)}, bf16[4,4,16,128]{3,2,1,0:T(8,128)(2,1)S(1)}, u32[]{:S(2)}, u32[]{:S(2)}) collective-permute-start(bf16[4,4,16,128]{3,2,1,0:T(8,128)(2,1)S(1)} %get-tuple-element.130), channel_id=1, source_target_pairs={{0,24},{2,26},{4,28},{6,30},{8,16},{10,18},{12,20},{14,22},{16,8},... | collective-permute-start | bytes 196616 | tf_op jit(solution)/shard_map/ppermute | solution.py:756
  46.8 6.9 %collective-permute-start.15 = (bf16[4,4,16,128]{3,2,1,0:T(8,128)(2,1)S(1)}, bf16[4,4,16,128]{3,2,1,0:T(8,128)(2,1)S(1)}, u32[]{:S(2)}, u32[]{:S(2)}) collective-permute-start(bf16[4,4,16,128]{3,2,1,0:T(8,128)(2,1)S(1)} %get-tuple-element.131), channel_id=1, source_target_pairs={{0,16},{2,18},{4,20},{6,22},{8,24},{10,26},{12,28},{14,30},{16,0},... | collective-permute-start | bytes 196616 | tf_op jit(solution)/shard_map/ppermute | solution.py:756
  47.6 7.0 %collective-permute-start.16 = (bf16[4,4,16,128]{3,2,1,0:T(8,128)(2,1)S(1)}, bf16[4,4,16,128]{3,2,1,0:T(8,128)(2,1)S(1)}, u32[]{:S(2)}, u32[]{:S(2)}) collective-permute-start(bf16[4,4,16,128]{3,2,1,0:T(8,128)(2,1)S(1)} %get-tuple-element.132), channel_id=1, source_target_pairs={{0,8},{2,10},{4,12},{6,14},{8,0},{10,2},{12,4},{14,6},{16,24},{18,... | collective-permute-start | bytes 196616 | tf_op jit(solution)/shard_map/ppermute | solution.py:756
  48.1 10.6 %collective-permute-start.20 = (bf16[4,4,16,128]{3,2,1,0:T(8,128)(2,1)S(1)}, bf16[4,4,16,128]{3,2,1,0:T(8,128)(2,1)S(1)}, u32[]{:S(2)}, u32[]{:S(2)}) collective-permute-start(bf16[4,4,16,128]{3,2,1,0:T(8,128)(2,1)S(1)} %get-tuple-element.133.refs_3_), channel_id=1, source_target_pairs={{0,1},{1,0},{2,3},{3,2},{4,5},{5,4},{6,7},{7,6},{8,9},{9,8},{10,11... | collective-permute-start | bytes 196616 | tf_op jit(solution)/shard_map/ppermute | solution.py:760
  49.6 9.2 %collective-permute-start.17 = (bf16[4,4,16,128]{3,2,1,0:T(8,128)(2,1)S(1)}, bf16[4,4,16,128]{3,2,1,0:T(8,128)(2,1)S(1)}, u32[]{:S(2)}, u32[]{:S(2)}) collective-permute-start(bf16[4,4,16,128]{3,2,1,0:T(8,128)(2,1)S(1)} %collective-permute-done.14.refs_0_), channel_id=1, source_target_pairs={{0,1},{1,0},{2,3},{3,2},{4,5},{5,4},{6,7},{7,6},{8,9},{9,8},{10,11... | collective-permute-start | bytes 196616 | tf_op jit(solution)/shard_map/ppermute | solution.py:760
  53.7 5.1 %collective-permute-start.18 = (bf16[4,4,16,128]{3,2,1,0:T(8,128)(2,1)S(1)}, bf16[4,4,16,128]{3,2,1,0:T(8,128)(2,1)S(1)}, u32[]{:S(2)}, u32[]{:S(2)}) collective-permute-start(bf16[4,4,16,128]{3,2,1,0:T(8,128)(2,1)S(1)} %collective-permute-done.15.refs_1_), channel_id=1, source_target_pairs={{0,1},{1,0},{2,3},{3,2},{4,5},{5,4},{6,7},{7,6},{8,9},{9,8},{10,11... | collective-permute-start | bytes 196616 | tf_op jit(solution)/shard_map/ppermute | solution.py:760
  54.6 4.5 %collective-permute-start.19 = (bf16[4,4,16,128]{3,2,1,0:T(8,128)(2,1)S(1)}, bf16[4,4,16,128]{3,2,1,0:T(8,128)(2,1)S(1)}, u32[]{:S(2)}, u32[]{:S(2)}) collective-permute-start(bf16[4,4,16,128]{3,2,1,0:T(8,128)(2,1)S(1)} %collective-permute-done.16.refs_2_), channel_id=1, source_target_pairs={{0,1},{1,0},{2,3},{3,2},{4,5},{5,4},{6,7},{7,6},{8,9},{9,8},{10,11... | collective-permute-start | bytes 196616 | tf_op jit(solution)/shard_map/ppermute | solution.py:760

commit v8 on v7

--- a/solution.py
+++ b/solution.py
@@ -163,8 +163,13 @@
     transform(table[...], flow_at, cells_x, refs, pieces)
 
 
+def is_even(me, shards):
+    _, own_outer, own_inner = place(me, shards)
+    return lax.rem(own_outer * shards[1] + own_inner, 2) == 0
+
+
 def keep_kernel(shards, shards_y, pieces, me_ref, table_ref, flow_ref, *refs):
-    refs, (first, last, *rows) = refs[: len(pieces)], refs[len(pieces) :]
+    refs, (to_paired, to_other, low, high) = refs[: len(pieces)], refs[len(pieces) :]
     cells_x, positions, _ = flow_ref.shape
     outer, _ = shards
     block = refs[0].shape[1] * refs[0].shape[3]
@@ -176,22 +181,12 @@
     transform(
         jnp.concatenate(tables, axis=0), lambda x: flow_ref[x], cells_x, refs, pieces
     )
-    first[...] = flow_ref[0]
-    last[...] = flow_ref[cells_x - 1]
-    cells_z = rows[0].shape[1]
-    low, high = pl.ds(0, cells_z), pl.ds(positions - cells_z, cells_z)
-    if len(rows) > 1:
-        rows[0][...] = flow_ref[:, low]
-        rows[1][...] = flow_ref[:, high]
-    else:
-
-        @pl.when(own_y > 0)
-        def _():
-            rows[0][...] = flow_ref[:, low]
-
-        @pl.when(own_y == 0)
-        def _():
-            rows[0][...] = flow_ref[:, high]
+    even = is_even(me_ref[0], shards)
+    to_paired[...] = flow_ref[jnp.where(even, cells_x - 1, 0)]
+    to_other[...] = flow_ref[jnp.where(even, 0, cells_x - 1)]
+    cells_z = low.shape[1]
+    low[...] = flow_ref[:, pl.ds(0, cells_z)]
+    high[...] = flow_ref[:, pl.ds(positions - cells_z, cells_z)]
 
 
 def forward_yz(me, table, flow, step, shards, shards_y, pieces, cells_z=0):
@@ -215,7 +210,7 @@
         specs, scratch = in_vmem(2), []
         shapes += [jax.ShapeDtypeStruct((positions, channels), flow.dtype)] * 2
         edge = jax.ShapeDtypeStruct((cells_x, cells_z, channels), flow.dtype)
-        shapes += [edge] * (1 if shards_y == 2 else 2)
+        shapes += [edge] * 2
     return pl.pallas_call(
         kernel,
         in_specs=[IN_SMEM] + specs,
@@ -276,41 +271,37 @@
     )(me, *arrays)
 
 
-def halo_kernel(shards, shards_y, me_ref, first_ref, last_ref, front_ref, back_ref, *out_refs):
-    own_y, own_outer, own_inner = place(me_ref[0], shards)
-    even = lax.rem(own_outer * shards[1] + own_inner, 2) == 0
-    cells_x, cells_z, _ = front_ref.shape
-    cells_y = first_ref.shape[0] // cells_z
-
-    def fill(out_ref, x, plane_ref):
-        for y in range(cells_y):
-            out_ref[y + 1] = plane_ref[pl.ds(y * cells_z, cells_z), :]
-        row = front_ref[x]
-        out_ref[0] = jnp.where(own_y > 0, row, jnp.zeros_like(row))
-        row = back_ref[x]
-        out_ref[cells_y + 1] = jnp.where(own_y < shards_y - 1, row, jnp.zeros_like(row))
-
-    @pl.when(even)
+def edge_kernel(
+    choose, shards, me_ref, paired_ref, other_ref, low_ref, high_ref, out_ref
+):
+    cells_x, cells_z, _ = low_ref.shape
+    rows = paired_ref.shape[0]
+    own_y, _, _ = place(me_ref[0], shards)
+    is_low = choose(own_y)
+    even = is_even(me_ref[0], shards)
+    start = pl.multiple_of(jnp.where(is_low, 0, rows - cells_z), cells_z)
+    paired, other = (ref[pl.ds(start, cells_z), :] for ref in (paired_ref, other_ref))
+    out_ref[0] = jnp.where(even, other, paired)
+    out_ref[1 + cells_x] = jnp.where(even, paired, other)
+
+    @pl.when(is_low)
     def _():
-        fill(out_refs[0], cells_x - 1, last_ref)
-        fill(out_refs[1], 0, first_ref)
-
-    @pl.when(jnp.logical_not(even))
+        out_ref[1 : 1 + cells_x] = low_ref[...]
+
+    @pl.when(jnp.logical_not(is_low))
     def _():
-        fill(out_refs[0], 0, first_ref)
-        fill(out_refs[1], cells_x - 1, last_ref)
-
-
-def halo_planes(me, first, last, front, back, shards, shards_y):
-    cells_x, cells_z, channels = front.shape
-    shape = (first.shape[0] // cells_z + 2, cells_z, channels)
+        out_ref[1 : 1 + cells_x] = high_ref[...]
+
+
+def y_edge(me, paired, other, low, high, shards, choose):
+    cells_x, cells_z, channels = low.shape
     return pl.pallas_call(
-        functools.partial(halo_kernel, shards, shards_y),
+        functools.partial(edge_kernel, choose, shards),
         in_specs=[IN_SMEM] + in_vmem(4),
-        out_specs=in_vmem(2),
-        out_shape=[jax.ShapeDtypeStruct(shape, first.dtype)] * 2,
+        out_specs=in_vmem(1)[0],
+        out_shape=jax.ShapeDtypeStruct((cells_x + 2, cells_z, channels), low.dtype),
         compiler_params=pltpu.CompilerParams(vmem_limit_bytes=10 << 20),
-    )(me, first, last, front, back)
+    )(me, paired, other, low, high)
 
 
 def preload_kernel(first, weight_ref, out_ref, sems):
@@ -477,27 +468,27 @@
 def convolution_kernel(x, cells_x, width, shards, shards_y, me_ref, *refs):
     flow_ref, paired_ref, other_ref, front_ref, back_ref, kernel_ref, out_ref, padded = refs
     _, cells_y, cells_z, channels = out_ref.shape
-    own_y, own_outer, own_inner = place(me_ref[0], shards)
-    even = lax.rem(own_outer * shards[1] + own_inner, 2) == 0
+    own_y, _, _ = place(me_ref[0], shards)
+    even = is_even(me_ref[0], shards)
     for plane in range(width + 2):
         p = x + plane - 1
+        row = front_ref[p + 1]
+        padded[plane, 0] = jnp.where(own_y > 0, row, jnp.zeros_like(row))
+        row = back_ref[p + 1]
+        last = own_y == shards_y - 1
+        padded[plane, cells_y + 1] = jnp.where(last, jnp.zeros_like(row), row)
         if 0 <= p < cells_x:
             padded[plane, 1 : cells_y + 1] = flow_ref[p]
-            row = front_ref[p]
-            padded[plane, 0] = jnp.where(own_y > 0, row, jnp.zeros_like(row))
-            row = back_ref[p]
-            last = own_y == shards_y - 1
-            padded[plane, cells_y + 1] = jnp.where(last, jnp.zeros_like(row), row)
         else:
             use_paired = jnp.logical_not(even) if p < 0 else even
 
             @pl.when(use_paired)
             def _(plane=plane):
-                padded[plane] = paired_ref[...]
+                padded[plane, 1 : cells_y + 1] = paired_ref[...]
 
             @pl.when(jnp.logical_not(use_paired))
             def _(plane=plane):
-                padded[plane] = other_ref[...]
+                padded[plane, 1 : cells_y + 1] = other_ref[...]
 
     rows = 4 if cells_y % 4 == 0 else 1
     columns = [(k, d) for k in range(width) for d in range(3)]
@@ -791,34 +782,38 @@
         sent, columns, weight = barrier((sent, columns, weight))
         for into, piece in zip(arrived, sent):
             into.append(over_y(piece, step, shards_y))
+    loaded = [preload(weight, 0, early // 2)] if early > 1 else []
+    loaded, columns = barrier((loaded, columns))
     kept = forward_yz(me, table, columns, 0, shards, shards_y, pieces, cells_z)
-    kept, (first, last, *ends) = kept[: len(pieces)], kept[len(pieces) :]
-    if shards_y == 2:
-        front = back = over_y(ends[0], 1, shards_y)
-    else:
-        front, back = neighbours(*ends, "gy")
-    loaded = [preload(weight, 0, early)] if early else []
-    loaded, arrived[0] = barrier((loaded, arrived[0]))
+    kept, (*ends, low, high) = kept[: len(pieces)], kept[len(pieces) :]
+    planes = [with_neighbour(end, start, "gx") for start, end in enumerate(ends)]
 
     by_outer = []
     for piece, own, parts in zip(pieces, kept, arrived):
         for step, total in zip(piece, add_pieces(own, parts)):
             by_outer.append(exchange(total, step, shards, True) if step else total)
     if early:
-        loaded.append(preload(weight, early, early))
-    by_outer, loaded, weight = barrier((by_outer, loaded, weight))
-    by_inner = regroup(me, by_outer, shards, True)
+        loaded.append(preload(weight, early // 2, early))
+    by_outer, loaded, weight = barrier((by_outer[::-1], loaded, weight))
+    by_inner = regroup(me, by_outer[::-1], shards, True)
     by_inner, weight = barrier((by_inner, weight))
     rows = [
         exchange(by_inner[step], step, shards, False) if step else by_inner[0]
         for step in far_first(inner)
     ]
     if early:
-        loaded.append(preload(weight, 2 * early, 1))
-
-    rows, loaded, first, last, front, back = barrier((rows, loaded, first, last, front, back))
-    planes = halo_planes(me, first, last, front, back, shards, shards_y)
-    planes = [with_neighbour(plane, start, "gx") for start, plane in enumerate(planes)]
+        loaded.append(preload(weight, early + early // 2, early))
+
+    rows, loaded, planes = barrier((rows, loaded, planes))
+    if shards_y == 2:
+        edge = y_edge(me, *planes, low, high, shards, lambda own: own > 0)
+        front = back = over_y(edge, 1, shards_y)
+    else:
+        ends = [
+            y_edge(me, *planes, low, high, shards, lambda own, limit=limit: own < limit)
+            for limit in (shards_y, 0)
+        ]
+        front, back = neighbours(*ends, "gy")
     returned = mixing(
         me,
         rows,
@@ -828,7 +823,8 @@
         loaded,
         shards,
     )
-    returned, planes = barrier((list(returned), planes))
+    returned, front, back = barrier((list(returned), front, back))
+    planes = [plane.reshape(cells_y, cells_z, channels) for plane in planes]
     halos = (*planes, front, back)
     width = 2 if cells_x % 2 == 0 else 1
     convolved = [

time: 62.1 us -> 60.4 us (0.973)
  starting transfers between devices: 28.1 us -> 21.3 us
  waiting for transfers between devices: 5.9 us -> 11.1 us
    ppermute x12, starting transfers between devices: 18.1 us -> 12.8 us  [exchange(): return lax.ppermute(array, 'gx', pairs)]
    ppermute x12, waiting for transfers between devices: 5.06 us -> 8.03 us  [exchange(): return lax.ppermute(array, 'gx', pairs)]
    ppermute x7, waiting for transfers between devices: 0.84 us -> 3.1 us  [over_y(): lax.ppermute(array, 'gy', [(i, (i + step) % shards_y) for i in range(shar...]
    ppermute x7, starting transfers between devices: 9.09 us -> 7.73 us  [over_y(): lax.ppermute(array, 'gy', [(i, (i + step) % shards_y) for i in range(shar...]
  transfers between devices with their start and end apart: 21 -> 21, of which waited for: 7 -> 6; matrix products, arithmetic and copies ran while one was open for 0% -> 0% of each run, Pallas kernels for 35% -> 36%
where the time goes in v8:
time: 60.4 us; the launch traced here: 60.3 us
  Pallas kernels  27.5 us (46%)
  starting transfers between devices  21.3 us (35%)
  waiting for transfers between devices  11.1 us (18%)
    ppermute x12, starting transfers between devices, exchange(): return lax.ppermute(array, 'gx', pairs)  12.8 us
    pallas_call x3, Pallas kernels, preload(): pl.pallas_call(functools.partial(preload_kernel, 2 * pair), in_specs=[pl....  9.15 us
    ppermute x12, waiting for transfers between devices, exchange(): return lax.ppermute(array, 'gx', pairs)  8.03 us
    ppermute x7, starting transfers between devices, over_y(): lax.ppermute(array, 'gy', [(i, (i + step) % shards_y) for i in range(shar...  7.73 us
    pallas_call x2, Pallas kernels, convolution(): pl.pallas_call(functools.partial(convolution_kernel, x, cells_x, width, s...  6 us
    pallas_call x1, Pallas kernels, mixing(): pl.pallas_call(functools.partial(mixing_kernel, shards, len(loaded)), in_...  5.93 us
    pallas_call x2, Pallas kernels, forward_yz(): pl.pallas_call(kernel, in_specs=[IN_SMEM] + specs, out_specs=in_vmem(len(...  3.41 us
    ppermute x7, waiting for transfers between devices, over_y(): lax.ppermute(array, 'gy', [(i, (i + step) % shards_y) for i in range(shar...  3.1 us
  transfers between devices with their start and end apart: 21, of which 6 were waited for; matrix products, arithmetic and copies ran while one was open for 0% of the time, Pallas kernels for 36%

profile of v8, /device:TPU:0, one launch (start us, length us, event | category | flops | bytes accessed | tf_op | source)
XLA Modules:
  0.0 60.3 jit_solution(2500816625374577050)
XLA Ops:
  0.0 3.0 %shard_map.82 = (bf16[2,4,4,16,128]{4,3,2,1,0:T(8,128)(2,1)}, bf16[2,4,4,16,128]{4,3,2,1,0:T(8,128)(2,1)}) custom-call(s32[1]{0:T(128)} %bitcast.me_ref, bf16[2,512,1024]{2,1,0:T(8,128)(2,1)} %constant.18.clone.table_ref, bf16[4,1024,128]{2,1,0:T(8,128)(2,1)} %bitcast.6), custom_call_target="tpu_custom_call" | custom-call | flops 268435456 | bytes 1572864 | tf_op jit(solution)/shard_map/pallas_call | solution.py:214
  3.0 0.0 copy-start
  3.0 0.0 copy-start.1
  3.0 3.0 %collective-permute-start = (bf16[2,4,4,16,128]{4,3,2,1,0:T(8,128)(2,1)}, bf16[2,4,4,16,128]{4,3,2,1,0:T(8,128)(2,1)S(1)}, u32[]{:S(2)}, u32[]{:S(2)}) collective-permute-start(bf16[2,4,4,16,128]{4,3,2,1,0:T(8,128)(2,1)} %get-tuple-element.73), channel_id=1, source_target_pairs={{0,1},{1,0},{2,3},{3,2},{4,5},{5,4},{6,7},{7,6},{8,9},{9,8},{10,11... | collective-permute-start | bytes 393224 | tf_op jit(solution)/shard_map/ppermute | solution.py:751
  6.0 0.1 collective-permute-start.2
  6.1 2.2 %shard_map.83.refs_7_ = bf16[2,64,128,128]{3,2,1,0:T(8,128)(2,1)S(1)} custom-call(bf16[16,64,128,128]{3,2,1,0:T(8,128)(2,1)} %bitcast.13), custom_call_target="tpu_custom_call" | custom-call | bytes 4194304 | tf_op jit(solution)/shard_map/pallas_call | solution.py:327
  8.4 0.4 shard_map.84
  8.8 0.1 collective-permute-start.8
  8.9 0.7 %collective-permute-start.9 = (bf16[1024,128]{1,0:T(8,128)(2,1)S(1)}, bf16[1024,128]{1,0:T(8,128)(2,1)S(1)}, u32[]{:S(2)}, u32[]{:S(2)}) collective-permute-start(bf16[1024,128]{1,0:T(8,128)(2,1)S(1)} %get-tuple-element.98), channel_id=1, source_target_pairs={{2,4},{6,8},{10,12},{14,16},{18,20},{22,24},{26,28},{4,2},{8,6},{1... | collective-permute-start | bytes 786440 | tf_op jit(solution)/shard_map/ppermute | solution.py:736
  9.6 3.0 %collective-permute-done.2.refs_1_ = bf16[2,4,4,16,128]{4,3,2,1,0:T(8,128)(2,1)S(1)} collective-permute-done((bf16[2,4,4,16,128]{4,3,2,1,0:T(8,128)(2,1)}, bf16[2,4,4,16,128]{4,3,2,1,0:T(8,128)(2,1)S(1)}, u32[]{:S(2)}, u32[]{:S(2)}) %collective-permute-start.2) | collective-permute-done | bytes 131104 | tf_op jit(solution)/shard_map/ppermute | solution.py:751
  12.6 2.9 %collective-permute-start.3 = (bf16[4,4,16,128]{3,2,1,0:T(8,128)(2,1)S(1)}, bf16[4,4,16,128]{3,2,1,0:T(8,128)(2,1)S(1)}, u32[]{:S(2)}, u32[]{:S(2)}) collective-permute-start(bf16[4,4,16,128]{3,2,1,0:T(8,128)(2,1)S(1)} %get-tuple-element.78), channel_id=1, source_target_pairs={{0,16},{2,18},{4,20},{6,22},{8,24},{10,26},{12,28},{14,30},{16,0},... | collective-permute-start | bytes 196616 | tf_op jit(solution)/shard_map/ppermute | solution.py:747
  15.5 1.3 %collective-permute-start.4 = (bf16[4,4,16,128]{3,2,1,0:T(8,128)(2,1)S(1)}, bf16[4,4,16,128]{3,2,1,0:T(8,128)(2,1)S(1)}, u32[]{:S(2)}, u32[]{:S(2)}) collective-permute-start(bf16[4,4,16,128]{3,2,1,0:T(8,128)(2,1)S(1)} %get-tuple-element.79), channel_id=1, source_target_pairs={{0,24},{2,26},{4,28},{6,30},{8,16},{10,18},{12,20},{14,22},{16,8},... | collective-permute-start | bytes 196616 | tf_op jit(solution)/shard_map/ppermute | solution.py:747
  16.8 0.0 collective-permute-done.refs_1_
  16.9 0.3 collective-permute-start.1
  17.2 3.5 %shard_map.87.refs_8_ = bf16[4,64,128,128]{3,2,1,0:T(8,128)(2,1)S(1)} custom-call(bf16[16,64,128,128]{3,2,1,0:T(8,128)(2,1)} %bitcast.14), custom_call_target="tpu_custom_call" | custom-call | bytes 8388608 | tf_op jit(solution)/shard_map/pallas_call | solution.py:327
  20.6 3.5 %collective-permute-done.3.refs_1_ = bf16[4,4,16,128]{3,2,1,0:T(8,128)(2,1)S(1)} collective-permute-done((bf16[4,4,16,128]{3,2,1,0:T(8,128)(2,1)S(1)}, bf16[4,4,16,128]{3,2,1,0:T(8,128)(2,1)S(1)}, u32[]{:S(2)}, u32[]{:S(2)}) %collective-permute-start.3) | collective-permute-done | bytes 65568 | tf_op jit(solution)/shard_map/ppermute | solution.py:747
  24.2 0.0 collective-permute-done.4.refs_0_
  24.2 0.0 collective-permute-done.1.refs_2_
  24.2 0.0 copy-start.3
  24.2 0.0 copy-start.4
  24.2 0.1 collective-permute-start.5
  24.3 0.1 collective-permute-start.6
  24.4 1.8 %collective-permute-start.7 = (bf16[4,4,16,128]{3,2,1,0:T(8,128)(2,1)S(1)}, bf16[4,4,16,128]{3,2,1,0:T(8,128)(2,1)S(1)}, u32[]{:S(2)}, u32[]{:S(2)}) collective-permute-start(bf16[4,4,16,128]{3,2,1,0:T(8,128)(2,1)S(1)} %get-tuple-element.92), channel_id=1, source_target_pairs={{0,2},{2,0},{4,6},{6,4},{8,10},{10,8},{12,14},{14,12},{16,18},{18,... | collective-permute-start | bytes 196616 | tf_op jit(solution)/shard_map/ppermute | solution.py:747
  26.1 3.5 %shard_map.89.refs_9_ = bf16[4,64,128,128]{3,2,1,0:T(8,128)(2,1)S(1)} custom-call(bf16[16,64,128,128]{3,2,1,0:T(8,128)(2,1)} %bitcast.15), custom_call_target="tpu_custom_call" | custom-call | bytes 8388608 | tf_op jit(solution)/shard_map/pallas_call | solution.py:327
  29.6 0.0 collective-permute-done.9.other_ref
  29.6 0.0 collective-permute-done.5.refs_0_
  29.7 0.0 copy-start.6
  29.7 1.6 %collective-permute-start.10 = (bf16[6,64,128]{2,1,0:T(8,128)(2,1)S(1)}, bf16[6,64,128]{2,1,0:T(8,128)(2,1)S(1)}, u32[]{:S(2)}, u32[]{:S(2)}) collective-permute-start(bf16[6,64,128]{2,1,0:T(8,128)(2,1)S(1)} %shard_map.91), channel_id=1, source_target_pairs={{0,1},{1,0},{2,3},{3,2},{4,5},{5,4},{6,7},{7,6},{8,9},{9,8},{10,11... | collective-permute-start | bytes 294920 | tf_op jit(solution)/shard_map/ppermute | solution.py:751
  31.3 5.9 %shard_map.90 = (bf16[4,4,16,128]{3,2,1,0:T(8,128)(2,1)S(1)}, bf16[4,4,16,128]{3,2,1,0:T(8,128)(2,1)S(1)}, bf16[4,4,16,128]{3,2,1,0:T(8,128)(2,1)S(1)}, bf16[4,4,16,128]{3,2,1,0:T(8,128)(2,1)S(1)}) custom-call(s32[1]{0:T(128)} %bitcast.me_ref, bf16[4,4,16,128]{3,2,1,0:T(8,128)(2,1)S(1)} %collective-permute-done.5.refs_0_, ...), custom_call_target="tpu_custom_call" | custom-call | flops 134217728 | bytes 33554432 | tf_op jit(solution)/shard_map/pallas_call | solution.py:446
  37.2 0.0 collective-permute-done.10.refs_3_.refs_4_
  37.3 0.1 collective-permute-start.11
  37.4 1.3 %collective-permute-start.12 = (bf16[4,4,16,128]{3,2,1,0:T(8,128)(2,1)S(1)}, bf16[4,4,16,128]{3,2,1,0:T(8,128)(2,1)S(1)}, u32[]{:S(2)}, u32[]{:S(2)}) collective-permute-start(bf16[4,4,16,128]{3,2,1,0:T(8,128)(2,1)S(1)} %get-tuple-element.115), channel_id=1, source_target_pairs={{0,4},{2,6},{4,0},{6,2},{8,12},{10,14},{12,8},{14,10},{16,20},{18,... | collective-permute-start | bytes 196616 | tf_op jit(solution)/shard_map/ppermute | solution.py:747
  38.7 0.5 collective-permute-start.13
  39.2 3.0 %shard_map.92.refs_8_ = bf16[2,16,64,128]{3,2,1,0:T(8,128)(2,1)S(1)} custom-call(s32[1]{0:T(128)} %bitcast.me_ref, bf16[4,16,64,128]{3,2,1,0:T(8,128)(2,1)S(1)} %copy-done.1, bf16[16,64,128]{2,1,0:T(8,128)(2,1)S(1)} %bitcast.8, bf16[16,64,128]{2,1,0:T(8,128)(2,1)S(1)} %bitcast.10, bf16[6,64,128]{2,1,0:T(8,128)(2,1)S(1)} %collective-permute-done.10.refs_3_.refs_4_, ...), custom_call_target="tpu_custom_call" | custom-call | flops 2717908992 | bytes 1310720 | tf_op jit(solution)/shard_map/pallas_call | solution.py:532
  42.2 0.0 collective-permute-done.11.refs_0_
  42.2 0.7 %collective-permute-done.12.refs_1_ = bf16[4,4,16,128]{3,2,1,0:T(8,128)(2,1)S(1)} collective-permute-done((bf16[4,4,16,128]{3,2,1,0:T(8,128)(2,1)S(1)}, bf16[4,4,16,128]{3,2,1,0:T(8,128)(2,1)S(1)}, u32[]{:S(2)}, u32[]{:S(2)}) %collective-permute-start.12) | collective-permute-done | bytes 65568 | tf_op jit(solution)/shard_map/ppermute | solution.py:747
  42.9 2.0 %collective-permute-start.14 = (bf16[4,4,16,128]{3,2,1,0:T(8,128)(2,1)S(1)}, bf16[4,4,16,128]{3,2,1,0:T(8,128)(2,1)S(1)}, u32[]{:S(2)}, u32[]{:S(2)}) collective-permute-start(bf16[4,4,16,128]{3,2,1,0:T(8,128)(2,1)S(1)} %get-tuple-element.124), channel_id=1, source_target_pairs={{0,24},{2,26},{4,28},{6,30},{8,16},{10,18},{12,20},{14,22},{16,8},... | collective-permute-start | bytes 196616 | tf_op jit(solution)/shard_map/ppermute | solution.py:747
  44.9 0.8 %collective-permute-start.15 = (bf16[4,4,16,128]{3,2,1,0:T(8,128)(2,1)S(1)}, bf16[4,4,16,128]{3,2,1,0:T(8,128)(2,1)S(1)}, u32[]{:S(2)}, u32[]{:S(2)}) collective-permute-start(bf16[4,4,16,128]{3,2,1,0:T(8,128)(2,1)S(1)} %get-tuple-element.125), channel_id=1, source_target_pairs={{0,16},{2,18},{4,20},{6,22},{8,24},{10,26},{12,28},{14,30},{16,0},... | collective-permute-start | bytes 196616 | tf_op jit(solution)/shard_map/ppermute | solution.py:747
  45.7 1.7 %collective-permute-start.16 = (bf16[4,4,16,128]{3,2,1,0:T(8,128)(2,1)S(1)}, bf16[4,4,16,128]{3,2,1,0:T(8,128)(2,1)S(1)}, u32[]{:S(2)}, u32[]{:S(2)}) collective-permute-start(bf16[4,4,16,128]{3,2,1,0:T(8,128)(2,1)S(1)} %get-tuple-element.126), channel_id=1, source_target_pairs={{0,8},{2,10},{4,12},{6,14},{8,0},{10,2},{12,4},{14,6},{16,24},{18,... | collective-permute-start | bytes 196616 | tf_op jit(solution)/shard_map/ppermute | solution.py:747
  47.4 0.5 collective-permute-start.20
  47.9 1.9 %collective-permute-done.14.refs_0_ = bf16[4,4,16,128]{3,2,1,0:T(8,128)(2,1)S(1)} collective-permute-done((bf16[4,4,16,128]{3,2,1,0:T(8,128)(2,1)S(1)}, bf16[4,4,16,128]{3,2,1,0:T(8,128)(2,1)S(1)}, u32[]{:S(2)}, u32[]{:S(2)}) %collective-permute-start.14) | collective-permute-done | bytes 65568 | tf_op jit(solution)/shard_map/ppermute | solution.py:747
  49.8 0.5 collective-permute-start.17
  50.3 1.9 %collective-permute-done.15.refs_1_ = bf16[4,4,16,128]{3,2,1,0:T(8,128)(2,1)S(1)} collective-permute-done((bf16[4,4,16,128]{3,2,1,0:T(8,128)(2,1)S(1)}, bf16[4,4,16,128]{3,2,1,0:T(8,128)(2,1)S(1)}, u32[]{:S(2)}, u32[]{:S(2)}) %collective-permute-start.15) | collective-permute-done | bytes 65568 | tf_op jit(solution)/shard_map/ppermute | solution.py:747
  52.2 0.5 collective-permute-start.18
  52.7 1.5 %collective-permute-start.19 = (bf16[4,4,16,128]{3,2,1,0:T(8,128)(2,1)S(1)}, bf16[4,4,16,128]{3,2,1,0:T(8,128)(2,1)S(1)}, u32[]{:S(2)}, u32[]{:S(2)}) collective-permute-start(bf16[4,4,16,128]{3,2,1,0:T(8,128)(2,1)S(1)} %collective-permute-done.16.refs_2_), channel_id=1, source_target_pairs={{0,1},{1,0},{2,3},{3,2},{4,5},{5,4},{6,7},{7,6},{8,9},{9,8},{10,11... | collective-permute-start | bytes 196616 | tf_op jit(solution)/shard_map/ppermute | solution.py:751
  54.2 3.0 %shard_map.94.refs_9_ = bf16[2,16,64,128]{3,2,1,0:T(8,128)(2,1)S(1)} custom-call(s32[1]{0:T(128)} %bitcast.me_ref, bf16[4,16,64,128]{3,2,1,0:T(8,128)(2,1)S(1)} %copy-done.1, bf16[16,64,128]{2,1,0:T(8,128)(2,1)S(1)} %bitcast.9, bf16[16,64,128]{2,1,0:T(8,128)(2,1)S(1)} %bitcast.11, bf16[6,64,128]{2,1,0:T(8,128)(2,1)S(1)} %collective-permute-done.10.refs_3_.refs_4_, ...), custom_call_target="tpu_custom_call" | custom-call | flops 2717908992 | bytes 1310720 | tf_op jit(solution)/shard_map/pallas_call | solution.py:532
  57.3 0.1 collective-permute-done.19.refs_6_
  57.4 2.9 %shard_map.95 = bf16[4,16,64,128]{3,2,1,0:T(8,128)(2,1)} custom-call(s32[1]{0:T(128)} %bitcast.me_ref, bf16[2,1024,512]{2,1,0:T(8,128)(2,1)S(1)} %copy-done.2, bf16[4,4,16,128]{3,2,1,0:T(8,128)(2,1)S(1)} %collective-permute-done.14.refs_0_, bf16[4,4,16,128]{3,2,1,0:T(8,128)(2,1)S(1)} %collective-permute-done.15.refs_1_, ...), custom_call_target="tpu_custom_call" | custom-call | flops 536870912 | bytes 3145728 | tf_op jit(solution)/shard_map/pallas_call | solution.py:590
  (22 shorter events, 0.2 us)
Async XLA Ops:
  3.0 5.4 %copy-start = (bf16[2,512,1024]{2,1,0:T(8,128)(2,1)S(1)}, bf16[2,512,1024]{2,1,0:T(8,128)(2,1)}, u32[]{:S(2)}) copy-start(bf16[2,512,1024]{2,1,0:T(8,128)(2,1)} %constant.18.clone.table_ref) | copy-start | bytes 6291460
  3.0 5.3 %copy-start.1 = (bf16[4,16,64,128]{3,2,1,0:T(8,128)(2,1)S(1)}, bf16[4,16,64,128]{3,2,1,0:T(8,128)(2,1)}, u32[]{:S(2)}) copy-start(bf16[4,16,64,128]{3,2,1,0:T(8,128)(2,1)} %refs_0_.3) | copy-start | bytes 3145732
  3.0 13.8 %collective-permute-start = (bf16[2,4,4,16,128]{4,3,2,1,0:T(8,128)(2,1)}, bf16[2,4,4,16,128]{4,3,2,1,0:T(8,128)(2,1)S(1)}, u32[]{:S(2)}, u32[]{:S(2)}) collective-permute-start(bf16[2,4,4,16,128]{4,3,2,1,0:T(8,128)(2,1)} %get-tuple-element.73), channel_id=1, source_target_pairs={{0,1},{1,0},{2,3},{3,2},{4,5},{5,4},{6,7},{7,6},{8,9},{9,8},{10,11... | collective-permute-start | bytes 393224 | tf_op jit(solution)/shard_map/ppermute | solution.py:751
  6.0 6.5 %collective-permute-start.2 = (bf16[2,4,4,16,128]{4,3,2,1,0:T(8,128)(2,1)}, bf16[2,4,4,16,128]{4,3,2,1,0:T(8,128)(2,1)S(1)}, u32[]{:S(2)}, u32[]{:S(2)}) collective-permute-start(bf16[2,4,4,16,128]{4,3,2,1,0:T(8,128)(2,1)} %get-tuple-element.77), channel_id=1, source_target_pairs={{0,1},{1,0},{2,3},{3,2},{4,5},{5,4},{6,7},{7,6},{8,9},{9,8},{10,11... | collective-permute-start | bytes 393224 | tf_op jit(solution)/shard_map/ppermute | solution.py:751
  8.8 20.8 %collective-permute-start.8 = (bf16[1024,128]{1,0:T(8,128)(2,1)S(1)}, bf16[1024,128]{1,0:T(8,128)(2,1)S(1)}, u32[]{:S(2)}, u32[]{:S(2)}) collective-permute-start(bf16[1024,128]{1,0:T(8,128)(2,1)S(1)} %get-tuple-element.97), channel_id=1, source_target_pairs={{0,2},{4,6},{8,10},{12,14},{16,18},{20,22},{24,26},{28,30},{2,0},{... | collective-permute-start | bytes 786440 | tf_op jit(solution)/shard_map/ppermute | solution.py:736
  8.9 20.8 %collective-permute-start.9 = (bf16[1024,128]{1,0:T(8,128)(2,1)S(1)}, bf16[1024,128]{1,0:T(8,128)(2,1)S(1)}, u32[]{:S(2)}, u32[]{:S(2)}) collective-permute-start(bf16[1024,128]{1,0:T(8,128)(2,1)S(1)} %get-tuple-element.98), channel_id=1, source_target_pairs={{2,4},{6,8},{10,12},{14,16},{18,20},{22,24},{26,28},{4,2},{8,6},{1... | collective-permute-start | bytes 786440 | tf_op jit(solution)/shard_map/ppermute | solution.py:736
  12.6 11.6 %collective-permute-start.3 = (bf16[4,4,16,128]{3,2,1,0:T(8,128)(2,1)S(1)}, bf16[4,4,16,128]{3,2,1,0:T(8,128)(2,1)S(1)}, u32[]{:S(2)}, u32[]{:S(2)}) collective-permute-start(bf16[4,4,16,128]{3,2,1,0:T(8,128)(2,1)S(1)} %get-tuple-element.78), channel_id=1, source_target_pairs={{0,16},{2,18},{4,20},{6,22},{8,24},{10,26},{12,28},{14,30},{16,0},... | collective-permute-start | bytes 196616 | tf_op jit(solution)/shard_map/ppermute | solution.py:747
  15.5 8.7 %collective-permute-start.4 = (bf16[4,4,16,128]{3,2,1,0:T(8,128)(2,1)S(1)}, bf16[4,4,16,128]{3,2,1,0:T(8,128)(2,1)S(1)}, u32[]{:S(2)}, u32[]{:S(2)}) collective-permute-start(bf16[4,4,16,128]{3,2,1,0:T(8,128)(2,1)S(1)} %get-tuple-element.79), channel_id=1, source_target_pairs={{0,24},{2,26},{4,28},{6,30},{8,16},{10,18},{12,20},{14,22},{16,8},... | collective-permute-start | bytes 196616 | tf_op jit(solution)/shard_map/ppermute | solution.py:747
  16.9 7.3 %collective-permute-start.1 = (bf16[4,4,16,128]{3,2,1,0:T(8,128)(2,1)S(1)}, bf16[4,4,16,128]{3,2,1,0:T(8,128)(2,1)S(1)}, u32[]{:S(2)}, u32[]{:S(2)}) collective-permute-start(bf16[4,4,16,128]{3,2,1,0:T(8,128)(2,1)S(1)} %get-tuple-element.75), channel_id=1, source_target_pairs={{0,8},{2,10},{4,12},{6,14},{8,0},{10,2},{12,4},{14,6},{16,24},{18,... | collective-permute-start | bytes 196616 | tf_op jit(solution)/shard_map/ppermute | solution.py:747
  24.2 7.1 %copy-start.3 = (bf16[256,128]{1,0:T(8,128)(2,1)S(1)}, bf16[256,128]{1,0:T(8,128)(2,1)}, u32[]{:S(2)}) copy-start(bf16[256,128]{1,0:T(8,128)(2,1)} %constant.19.clone.refs_4_) | copy-start | bytes 196612
  24.2 7.1 %copy-start.4 = (bf16[128,128]{1,0:T(8,128)(2,1)S(1)}, bf16[128,128]{1,0:T(8,128)(2,1)}, u32[]{:S(2)}) copy-start(bf16[128,128]{1,0:T(8,128)(2,1)} %constant.20.clone.refs_5_) | copy-start | bytes 98308
  24.2 5.4 %collective-permute-start.5 = (bf16[4,4,16,128]{3,2,1,0:T(8,128)(2,1)S(1)}, bf16[4,4,16,128]{3,2,1,0:T(8,128)(2,1)S(1)}, u32[]{:S(2)}, u32[]{:S(2)}) collective-permute-start(bf16[4,4,16,128]{3,2,1,0:T(8,128)(2,1)S(1)} %get-tuple-element.90), channel_id=1, source_target_pairs={{0,6},{2,4},{4,2},{6,0},{8,14},{10,12},{12,10},{14,8},{16,22},{18,... | collective-permute-start | bytes 196616 | tf_op jit(solution)/shard_map/ppermute | solution.py:747
  24.3 5.4 %collective-permute-start.6 = (bf16[4,4,16,128]{3,2,1,0:T(8,128)(2,1)S(1)}, bf16[4,4,16,128]{3,2,1,0:T(8,128)(2,1)S(1)}, u32[]{:S(2)}, u32[]{:S(2)}) collective-permute-start(bf16[4,4,16,128]{3,2,1,0:T(8,128)(2,1)S(1)} %get-tuple-element.91), channel_id=1, source_target_pairs={{0,4},{2,6},{4,0},{6,2},{8,12},{10,14},{12,8},{14,10},{16,20},{18,... | collective-permute-start | bytes 196616 | tf_op jit(solution)/shard_map/ppermute | solution.py:747
  24.4 5.3 %collective-permute-start.7 = (bf16[4,4,16,128]{3,2,1,0:T(8,128)(2,1)S(1)}, bf16[4,4,16,128]{3,2,1,0:T(8,128)(2,1)S(1)}, u32[]{:S(2)}, u32[]{:S(2)}) collective-permute-start(bf16[4,4,16,128]{3,2,1,0:T(8,128)(2,1)S(1)} %get-tuple-element.92), channel_id=1, source_target_pairs={{0,2},{2,0},{4,6},{6,4},{8,10},{10,8},{12,14},{14,12},{16,18},{18,... | collective-permute-start | bytes 196616 | tf_op jit(solution)/shard_map/ppermute | solution.py:747
  29.7 9.5 %copy-start.6 = (bf16[3,3,3,128,128]{4,3,2,1,0:T(8,128)(2,1)S(1)}, bf16[3,3,3,128,128]{4,3,2,1,0:T(8,128)(2,1)}, u32[]{:S(2)}) copy-start(bf16[3,3,3,128,128]{4,3,2,1,0:T(8,128)(2,1)} %refs_5_.4) | copy-start | bytes 2654212
  29.7 7.5 %collective-permute-start.10 = (bf16[6,64,128]{2,1,0:T(8,128)(2,1)S(1)}, bf16[6,64,128]{2,1,0:T(8,128)(2,1)S(1)}, u32[]{:S(2)}, u32[]{:S(2)}) collective-permute-start(bf16[6,64,128]{2,1,0:T(8,128)(2,1)S(1)} %shard_map.91), channel_id=1, source_target_pairs={{0,1},{1,0},{2,3},{3,2},{4,5},{5,4},{6,7},{7,6},{8,9},{9,8},{10,11... | collective-permute-start | bytes 294920 | tf_op jit(solution)/shard_map/ppermute | solution.py:751
  37.3 4.9 %collective-permute-start.11 = (bf16[4,4,16,128]{3,2,1,0:T(8,128)(2,1)S(1)}, bf16[4,4,16,128]{3,2,1,0:T(8,128)(2,1)S(1)}, u32[]{:S(2)}, u32[]{:S(2)}) collective-permute-start(bf16[4,4,16,128]{3,2,1,0:T(8,128)(2,1)S(1)} %get-tuple-element.114), channel_id=1, source_target_pairs={{0,6},{2,4},{4,2},{6,0},{8,14},{10,12},{12,10},{14,8},{16,22},{18,... | collective-permute-start | bytes 196616 | tf_op jit(solution)/shard_map/ppermute | solution.py:747
  37.4 5.5 %collective-permute-start.12 = (bf16[4,4,16,128]{3,2,1,0:T(8,128)(2,1)S(1)}, bf16[4,4,16,128]{3,2,1,0:T(8,128)(2,1)S(1)}, u32[]{:S(2)}, u32[]{:S(2)}) collective-permute-start(bf16[4,4,16,128]{3,2,1,0:T(8,128)(2,1)S(1)} %get-tuple-element.115), channel_id=1, source_target_pairs={{0,4},{2,6},{4,0},{6,2},{8,12},{10,14},{12,8},{14,10},{16,20},{18,... | collective-permute-start | bytes 196616 | tf_op jit(solution)/shard_map/ppermute | solution.py:747
  38.7 4.2 %collective-permute-start.13 = (bf16[4,4,16,128]{3,2,1,0:T(8,128)(2,1)S(1)}, bf16[4,4,16,128]{3,2,1,0:T(8,128)(2,1)S(1)}, u32[]{:S(2)}, u32[]{:S(2)}) collective-permute-start(bf16[4,4,16,128]{3,2,1,0:T(8,128)(2,1)S(1)} %get-tuple-element.116), channel_id=1, source_target_pairs={{0,2},{2,0},{4,6},{6,4},{8,10},{10,8},{12,14},{14,12},{16,18},{18,... | collective-permute-start | bytes 196616 | tf_op jit(solution)/shard_map/ppermute | solution.py:747
  39.2 18.2 %copy-start.2 = (bf16[2,1024,512]{2,1,0:T(8,128)(2,1)S(1)}, bf16[2,1024,512]{2,1,0:T(8,128)(2,1)}, u32[]{:S(2)}) copy-start(bf16[2,1024,512]{2,1,0:T(8,128)(2,1)} %constant.21.clone.table_ref) | copy-start | bytes 6291460
  39.2 18.2 %copy-start.5 = (f32[128]{0:T(128)S(1)}, f32[128]{0:T(128)}, u32[]{:S(2)}) copy-start(f32[128]{0:T(128)} %param.11) | copy-start | bytes 1540
  42.9 6.8 %collective-permute-start.14 = (bf16[4,4,16,128]{3,2,1,0:T(8,128)(2,1)S(1)}, bf16[4,4,16,128]{3,2,1,0:T(8,128)(2,1)S(1)}, u32[]{:S(2)}, u32[]{:S(2)}) collective-permute-start(bf16[4,4,16,128]{3,2,1,0:T(8,128)(2,1)S(1)} %get-tuple-element.124), channel_id=1, source_target_pairs={{0,24},{2,26},{4,28},{6,30},{8,16},{10,18},{12,20},{14,22},{16,8},... | collective-permute-start | bytes 196616 | tf_op jit(solution)/shard_map/ppermute | solution.py:747
  44.9 7.3 %collective-permute-start.15 = (bf16[4,4,16,128]{3,2,1,0:T(8,128)(2,1)S(1)}, bf16[4,4,16,128]{3,2,1,0:T(8,128)(2,1)S(1)}, u32[]{:S(2)}, u32[]{:S(2)}) collective-permute-start(bf16[4,4,16,128]{3,2,1,0:T(8,128)(2,1)S(1)} %get-tuple-element.125), channel_id=1, source_target_pairs={{0,16},{2,18},{4,20},{6,22},{8,24},{10,26},{12,28},{14,30},{16,0},... | collective-permute-start | bytes 196616 | tf_op jit(solution)/shard_map/ppermute | solution.py:747
  45.7 7.0 %collective-permute-start.16 = (bf16[4,4,16,128]{3,2,1,0:T(8,128)(2,1)S(1)}, bf16[4,4,16,128]{3,2,1,0:T(8,128)(2,1)S(1)}, u32[]{:S(2)}, u32[]{:S(2)}) collective-permute-start(bf16[4,4,16,128]{3,2,1,0:T(8,128)(2,1)S(1)} %get-tuple-element.126), channel_id=1, source_target_pairs={{0,8},{2,10},{4,12},{6,14},{8,0},{10,2},{12,4},{14,6},{16,24},{18,... | collective-permute-start | bytes 196616 | tf_op jit(solution)/shard_map/ppermute | solution.py:747
  47.4 9.8 %collective-permute-start.20 = (bf16[4,4,16,128]{3,2,1,0:T(8,128)(2,1)S(1)}, bf16[4,4,16,128]{3,2,1,0:T(8,128)(2,1)S(1)}, u32[]{:S(2)}, u32[]{:S(2)}) collective-permute-start(bf16[4,4,16,128]{3,2,1,0:T(8,128)(2,1)S(1)} %get-tuple-element.127.refs_3_), channel_id=1, source_target_pairs={{0,1},{1,0},{2,3},{3,2},{4,5},{5,4},{6,7},{7,6},{8,9},{9,8},{10,11... | collective-permute-start | bytes 196616 | tf_op jit(solution)/shard_map/ppermute | solution.py:751
  49.8 7.4 %collective-permute-start.17 = (bf16[4,4,16,128]{3,2,1,0:T(8,128)(2,1)S(1)}, bf16[4,4,16,128]{3,2,1,0:T(8,128)(2,1)S(1)}, u32[]{:S(2)}, u32[]{:S(2)}) collective-permute-start(bf16[4,4,16,128]{3,2,1,0:T(8,128)(2,1)S(1)} %collective-permute-done.14.refs_0_), channel_id=1, source_target_pairs={{0,1},{1,0},{2,3},{3,2},{4,5},{5,4},{6,7},{7,6},{8,9},{9,8},{10,11... | collective-permute-start | bytes 196616 | tf_op jit(solution)/shard_map/ppermute | solution.py:751
  52.2 5.1 %collective-permute-start.18 = (bf16[4,4,16,128]{3,2,1,0:T(8,128)(2,1)S(1)}, bf16[4,4,16,128]{3,2,1,0:T(8,128)(2,1)S(1)}, u32[]{:S(2)}, u32[]{:S(2)}) collective-permute-start(bf16[4,4,16,128]{3,2,1,0:T(8,128)(2,1)S(1)} %collective-permute-done.15.refs_1_), channel_id=1, source_target_pairs={{0,1},{1,0},{2,3},{3,2},{4,5},{5,4},{6,7},{7,6},{8,9},{9,8},{10,11... | collective-permute-start | bytes 196616 | tf_op jit(solution)/shard_map/ppermute | solution.py:751
  52.7 4.6 %collective-permute-start.19 = (bf16[4,4,16,128]{3,2,1,0:T(8,128)(2,1)S(1)}, bf16[4,4,16,128]{3,2,1,0:T(8,128)(2,1)S(1)}, u32[]{:S(2)}, u32[]{:S(2)}) collective-permute-start(bf16[4,4,16,128]{3,2,1,0:T(8,128)(2,1)S(1)} %collective-permute-done.16.refs_2_), channel_id=1, source_target_pairs={{0,1},{1,0},{2,3},{3,2},{4,5},{5,4},{6,7},{7,6},{8,9},{9,8},{10,11... | collective-permute-start | bytes 196616 | tf_op jit(solution)/shard_map/ppermute | solution.py:751

commit v9 on v8

--- a/solution.py
+++ b/solution.py
@@ -55,14 +55,14 @@
     turn_z = rounded(turn_z.real) + 1j * rounded(turn_z.imag)
     turn_y = wave(frequencies(MY), np.arange(full_y), full_y, MY**-0.5)
     mode_y, mode_z = item_modes(shards_x, shards_y, pairs)
-    table = np.empty((shards_y, cells_y, cells_z, shards_y, shards_x, pairs, 2), np.float32)
+    table = np.empty((shards_y, shards_y, cells_y, cells_z, shards_x, pairs, 2), np.float32)
     for own in range(shards_y):
         rows = turn_y[:, own * cells_y : (own + 1) * cells_y]
         product = rows[mode_y][..., :, None] * turn_z[mode_z][..., None, :]
-        product = np.moveaxis(product, (3, 4), (0, 1))
+        product = np.moveaxis(product, (3, 4), (1, 2))
         table[own, ..., 0] = product.real
         table[own, ..., 1] = -product.imag
-    return table.reshape(shards_y, cells_y * cells_z, -1).astype(jnp.bfloat16)
+    return table.reshape(shards_y**2, cells_y * cells_z, -1).astype(jnp.bfloat16)
 
 
 def forward_x_table(full_x):
@@ -135,6 +135,7 @@
 
 def send_kernel(shards, shards_y, pieces, step, me_ref, table_ref, flow_ref, *refs):
     *refs, table, flow, table_sems, flow_sems = refs
+    refs, plane_refs = refs[: len(pieces)], refs[len(pieces) :]
     cells_x = flow.shape[0]
     outer, _ = shards
     block = refs[0].shape[1] * refs[0].shape[3]
@@ -161,6 +162,10 @@
         return flow[x]
 
     transform(table[...], flow_at, cells_x, refs, pieces)
+    if plane_refs:
+        even = is_even(me_ref[0], shards)
+        plane_refs[0][...] = flow[jnp.where(even, cells_x - 1, 0)]
+        plane_refs[1][...] = flow[jnp.where(even, 0, cells_x - 1)]
 
 
 def is_even(me, shards):
@@ -169,7 +174,7 @@
 
 
 def keep_kernel(shards, shards_y, pieces, me_ref, table_ref, flow_ref, *refs):
-    refs, (to_paired, to_other, low, high) = refs[: len(pieces)], refs[len(pieces) :]
+    refs, (low, high) = refs[: len(pieces)], refs[len(pieces) :]
     cells_x, positions, _ = flow_ref.shape
     outer, _ = shards
     block = refs[0].shape[1] * refs[0].shape[3]
@@ -181,9 +186,6 @@
     transform(
         jnp.concatenate(tables, axis=0), lambda x: flow_ref[x], cells_x, refs, pieces
     )
-    even = is_even(me_ref[0], shards)
-    to_paired[...] = flow_ref[jnp.where(even, cells_x - 1, 0)]
-    to_other[...] = flow_ref[jnp.where(even, 0, cells_x - 1)]
     cells_z = low.shape[1]
     low[...] = flow_ref[:, pl.ds(0, cells_z)]
     high[...] = flow_ref[:, pl.ds(positions - cells_z, cells_z)]
@@ -196,6 +198,8 @@
     unit = (inner, cells_x, rows // (outer * inner), channels)
     dtype = jnp.bfloat16 if step else jnp.float32
     shapes = [jax.ShapeDtypeStruct((len(piece), *unit), dtype) for piece in pieces]
+    if step == 1:
+        shapes += [jax.ShapeDtypeStruct((positions, channels), flow.dtype)] * 2
     if step:
         kernel = functools.partial(send_kernel, shards, shards_y, pieces, step)
         specs = [pl.BlockSpec(memory_space=pltpu.HBM)] * 2
@@ -208,7 +212,6 @@
     else:
         kernel = functools.partial(keep_kernel, shards, shards_y, pieces)
         specs, scratch = in_vmem(2), []
-        shapes += [jax.ShapeDtypeStruct((positions, channels), flow.dtype)] * 2
         edge = jax.ShapeDtypeStruct((cells_x, cells_z, channels), flow.dtype)
         shapes += [edge] * 2
     return pl.pallas_call(
@@ -544,68 +547,155 @@
     )(me, flow, *halos, kernel)
 
 
-def final_kernel(shards, shards_y, me_ref, table_ref, *refs):
+def bundled_slots(count):
+    slots = [0] + far_first(count)[:-1]
+    cut = (count + 1) // 2
+    return [part for part in (slots[:cut], slots[cut:]) if part]
+
+
+def bundle_kernel(*refs):
+    *in_refs, out_ref = refs
+    for i, ref in enumerate(in_refs):
+        out_ref[i] = ref[...]
+
+
+def bundle(arrays):
+    shape = (len(arrays), *arrays[0].shape)
+    return pl.pallas_call(
+        bundle_kernel,
+        in_specs=in_vmem(len(arrays)),
+        out_specs=in_vmem(1)[0],
+        out_shape=jax.ShapeDtypeStruct(shape, arrays[0].dtype),
+        cost_estimate=pl.CostEstimate(
+            flops=math.prod(shape), bytes_accessed=0, transcendentals=0
+        ),
+        compiler_params=pltpu.CompilerParams(vmem_limit_bytes=10 << 20),
+    )(*arrays)
+
+
+def gather_pieces(me, shards, pieces, held):
     outer, inner = shards
+    _, own_outer, own_inner = place(me, shards)
+    for number, slot, ref in pieces:
+        cells_x, rows = ref.shape[1:3]
+        source = (number * outer + origin(own_outer, slot, outer)) * inner
+        for part in range(inner):
+            at = (source + origin(own_inner, part, inner)) * rows
+            for x in range(cells_x):
+                held[x, pl.ds(pl.multiple_of(at, rows), rows), :] = ref[part, x]
+
+
+def inverse(me, shards, shards_y, steps, table_ref, held, part, x, width, positions):
+    own_y, _, _ = place(me, shards)
+    columns = [held[x + i] for i in range(width)]
+    depth = table_ref.shape[2]
+    total = None
+    for number, step in enumerate(steps):
+        source = lax.rem(own_y + (shards_y - step), shards_y)
+        rows = pl.ds(pl.multiple_of(part * positions, positions), positions)
+        table = table_ref[own_y * shards_y + source, rows, :]
+        block = [column[number * depth : (number + 1) * depth] for column in columns]
+        product = dot(table, jnp.concatenate(block, axis=1))
+        total = product if total is None else total + product
+    return total
+
+
+def own_part_kernel(shards, shards_y, me_ref, table_ref, *refs):
     *piece_refs, bias_ref, out_ref, held = refs
     cells_x, cells_y, cells_z, channels = out_ref.shape
     width = 2 if cells_x % 2 == 0 else 1
     count = -(-cells_x // width)
     piece_refs, convolved_refs = piece_refs[:-count], piece_refs[-count:]
-    own_y, own_outer, own_inner = place(me_ref[0], shards)
-    rows = piece_refs[0].shape[2]
-
-    @pl.when(pl.program_id(0) == 0)
+    slots = far_first(shards[0])
+    gather_pieces(me_ref[0], shards, [(0, *p) for p in zip(slots, piece_refs)], held)
+    bias = bias_ref[...]
+    rows = 4 if cells_y % 4 == 0 else 1
+    positions = rows * cells_z
+
+    def chunk(part, carry):
+        for x in range(0, cells_x, width):
+            total = inverse(
+                me_ref[0], shards, shards_y, [0], table_ref, held, part, x, width, positions
+            )
+            for i in range(width):
+                spectral = total[:, i * channels : (i + 1) * channels]
+                convolved = convolved_refs[x // width][i, pl.ds(part * rows, rows)]
+                value = spectral.reshape(rows, cells_z, channels) + convolved + bias
+                out_ref[x + i, pl.ds(part * rows, rows)] = value
+        return carry
+
+    lax.fori_loop(0, cells_y // rows, chunk, 0)
+
+
+def last_part_kernel(shards, shards_y, me_ref, table_ref, *refs):
+    *bundle_refs, partial_ref, out_ref, held = refs
+    cells_x, cells_y, cells_z, channels = out_ref.shape
+    bundles = bundled_slots(shards[0])
+    steps = list(range(1, shards_y))
+    width = 2 if cells_x % 2 == 0 else 1
+    part = pl.program_id(0)
+
+    @pl.when(part == 0)
     def _():
-        for number, ref in enumerate(piece_refs):
-            step, slot = divmod(number, outer)
-            slot = far_first(outer)[slot]
-            source_y = lax.rem(own_y + (shards_y - step), shards_y)
-            source = source_y * outer + origin(own_outer, slot, outer)
-            for part in range(inner):
-                at = (source * inner + origin(own_inner, part, inner)) * rows
-                for x in range(cells_x):
-                    held[x, pl.ds(pl.multiple_of(at, rows), rows), :] = ref[part, x]
-
-    bias = bias_ref[...]
-    part = pl.program_id(0)
-    count = cells_y * cells_z
-    table = table_ref[own_y, pl.ds(pl.multiple_of(part * count, count), count), :]
+        pieces = []
+        for i, ref in enumerate(bundle_refs):
+            number, bundle = divmod(i, len(bundles))
+            pieces += [(number, slot, ref.at[j]) for j, slot in enumerate(bundles[bundle])]
+        gather_pieces(me_ref[0], shards, pieces, held)
+
     for x in range(0, cells_x, width):
-        columns = [held[x + i] for i in range(width)]
-        total = dot(table, jnp.concatenate(columns, axis=1))
+        total = inverse(
+            me_ref[0], shards, shards_y, steps, table_ref, held, part, x, width,
+            cells_y * cells_z,
+        )
         for i in range(width):
             spectral = total[:, i * channels : (i + 1) * channels]
-            spectral = spectral.reshape(cells_y, cells_z, channels)
-            convolved = convolved_refs[x // width][i, pl.ds(part * cells_y, cells_y)]
-            value = spectral + convolved.astype(jnp.float32) + bias
+            value = partial_ref[x + i, pl.ds(part * cells_y, cells_y)]
+            value = value + spectral.reshape(cells_y, cells_z, channels)
             out_ref[x + i] = jax.nn.gelu(value, approximate=True).astype(out_ref.dtype)
 
 
-def final(me, table, pieces, convolved, bias, shards, shards_y):
+def own_part(me, table, pieces, convolved, bias, shards, shards_y):
     width, cells_y, cells_z, channels = convolved[0].shape
-    cells_x = width * len(convolved)
+    shape = (width * len(convolved), cells_y, cells_z, channels)
+    depth = table.shape[2]
+    return pl.pallas_call(
+        functools.partial(own_part_kernel, shards, shards_y),
+        in_specs=[IN_SMEM] + in_vmem(2 + len(pieces) + len(convolved)),
+        out_specs=in_vmem(1)[0],
+        out_shape=jax.ShapeDtypeStruct(shape, jnp.float32),
+        scratch_shapes=[pltpu.VMEM((shape[0], depth, channels), jnp.bfloat16)],
+        compiler_params=pltpu.CompilerParams(vmem_limit_bytes=14 << 20),
+        cost_estimate=pl.CostEstimate(
+            flops=2 * math.prod(shape) * depth,
+            bytes_accessed=6 * math.prod(shape),
+            transcendentals=0,
+        ),
+    )(me, table, *pieces, *convolved, bias)
+
+
+def last_part(me, table, pieces, partial, shards, shards_y):
+    cells_x, cells_y, cells_z, channels = partial.shape
     parts = 4 if cells_y % 4 == 0 else 1
     block = (cells_x, cells_y // parts, cells_z, channels)
-    depth = table.shape[2]
+    depth = table.shape[2] * (shards_y - 1)
     return pl.pallas_call(
-        functools.partial(final_kernel, shards, shards_y),
+        functools.partial(last_part_kernel, shards, shards_y),
         grid_spec=pltpu.PrefetchScalarGridSpec(
             num_scalar_prefetch=1,
             grid=(parts,),
-            in_specs=[
-                *in_vmem(2 + len(pieces) + len(convolved)),
-            ],
+            in_specs=in_vmem(2 + len(pieces)),
             out_specs=pl.BlockSpec(block, lambda i, me: (0, i, 0, 0)),
             scratch_shapes=[pltpu.VMEM((cells_x, depth, channels), jnp.bfloat16)],
         ),
-        out_shape=jax.ShapeDtypeStruct((cells_x, cells_y, cells_z, channels), jnp.bfloat16),
-        compiler_params=pltpu.CompilerParams(vmem_limit_bytes=10 << 20),
+        out_shape=jax.ShapeDtypeStruct(partial.shape, jnp.bfloat16),
+        compiler_params=pltpu.CompilerParams(vmem_limit_bytes=14 << 20),
         cost_estimate=pl.CostEstimate(
-            flops=2 * table.shape[1] * depth * cells_x * channels,
-            bytes_accessed=6 * len(convolved) * convolved[0].size,
-            transcendentals=len(convolved) * convolved[0].size,
+            flops=2 * partial.size * depth,
+            bytes_accessed=6 * partial.size,
+            transcendentals=partial.size,
         ),
-    )(me, table, *pieces, *convolved, bias)
+    )(me, table, *pieces, partial)
 
 
 def with_halo(array, sides, width):
@@ -782,11 +872,13 @@
         sent, columns, weight = barrier((sent, columns, weight))
         for into, piece in zip(arrived, sent):
             into.append(over_y(piece, step, shards_y))
+        if step == 1:
+            ends = sent[len(pieces) :]
+            planes = [with_neighbour(end, start, "gx") for start, end in enumerate(ends)]
     loaded = [preload(weight, 0, early // 2)] if early > 1 else []
     loaded, columns = barrier((loaded, columns))
     kept = forward_yz(me, table, columns, 0, shards, shards_y, pieces, cells_z)
-    kept, (*ends, low, high) = kept[: len(pieces)], kept[len(pieces) :]
-    planes = [with_neighbour(end, start, "gx") for start, end in enumerate(ends)]
+    kept, (low, high) = kept[: len(pieces)], kept[len(pieces) :]
 
     by_outer = []
     for piece, own, parts in zip(pieces, kept, arrived):
@@ -842,18 +934,16 @@
         exchange(returned[step], step, shards, True) if step else returned[0]
         for step in far_first(outer)
     ]
-    coefficients = list(returned)
+    returned[0], convolved[-1] = barrier((returned[0], convolved[-1]))
+    by_slot = dict(zip(far_first(outer), returned))
+    bundles = [bundle([by_slot[slot] for slot in slots]) for slots in bundled_slots(outer)]
+    others = []
     for step in range(1, shards_y):
-        coefficients += [over_y(part, step, shards_y) for part in returned]
-    return final(
-        me,
-        jnp.asarray(backward_yz_table(*sizes)),
-        coefficients,
-        convolved,
-        bias.reshape(1, channels),
-        shards,
-        shards_y,
-    )
+        others += [over_y(part, step, shards_y) for part in bundles]
+    table = jnp.asarray(backward_yz_table(*sizes))
+    bias = bias.reshape(1, channels)
+    partial = own_part(me, table, returned, convolved, bias, shards, shards_y)
+    return last_part(me, table, others, partial, shards, shards_y)
 
 
 def solution(mesh):

time: 60.4 us -> 59.6 us (0.987)
  waiting for transfers between devices: 11.1 us -> 9.67 us
  Pallas kernels: 27.5 us -> 28.3 us
    ppermute x12, waiting for transfers between devices: 8.03 us -> 3.92 us  [exchange(): return lax.ppermute(array, 'gx', pairs)]
    ppermute x7 -> x5, waiting for transfers between devices: 3.1 us -> 5.74 us  [over_y(): lax.ppermute(array, 'gy', [(i, (i + step) % shards_y) for i in range(shar...]
    ppermute x7 -> x5, starting transfers between devices: 7.73 us -> 5.82 us  [over_y(): lax.ppermute(array, 'gy', [(i, (i + step) % shards_y) for i in range(shar...]
    ppermute x12, starting transfers between devices: 12.8 us -> 14.7 us  [exchange(): return lax.ppermute(array, 'gx', pairs)]
    pallas_call x1 -> x4, Pallas kernels: 2.9 us -> 3.53 us  [the longest x1 2.53 us: last_part(): pl.pallas_call(functools.partial(last_part_kernel, shards, shards_y), gri...]
  transfers between devices with their start and end apart: 21 -> 19, of which waited for: 6 -> 9; matrix products, arithmetic and copies ran while one was open for 0% -> 0% of each run, Pallas kernels for 36% -> 38%
where the time goes in v9:
time: 59.6 us; the launch traced here: 59.4 us
  Pallas kernels  28.3 us (47%)
  starting transfers between devices  21.2 us (36%)
  waiting for transfers between devices  9.67 us (16%)
    ppermute x12, starting transfers between devices, exchange(): return lax.ppermute(array, 'gx', pairs)  14.7 us
    pallas_call x3, Pallas kernels, preload(): pl.pallas_call(functools.partial(preload_kernel, 2 * pair), in_specs=[pl....  9.15 us
    pallas_call x2, Pallas kernels, convolution(): pl.pallas_call(functools.partial(convolution_kernel, x, cells_x, width, s...  5.99 us
    pallas_call x1, Pallas kernels, mixing(): pl.pallas_call(functools.partial(mixing_kernel, shards, len(loaded)), in_...  5.93 us
    ppermute x5, starting transfers between devices, over_y(): lax.ppermute(array, 'gy', [(i, (i + step) % shards_y) for i in range(shar...  5.82 us
    ppermute x5, waiting for transfers between devices, over_y(): lax.ppermute(array, 'gy', [(i, (i + step) % shards_y) for i in range(shar...  5.74 us
    ppermute x12, waiting for transfers between devices, exchange(): return lax.ppermute(array, 'gx', pairs)  3.92 us
    pallas_call x2, Pallas kernels, forward_yz(): pl.pallas_call(kernel, in_specs=[IN_SMEM] + specs, out_specs=in_vmem(len(...  3.58 us
  transfers between devices with their start and end apart: 19, of which 9 were waited for; matrix products, arithmetic and copies ran while one was open for 0% of the time, Pallas kernels for 38%

profile of v9, /device:TPU:0, one launch (start us, length us, event | category | flops | bytes accessed | tf_op | source)
XLA Modules:
  0.0 59.4 jit_solution(11928353126386660715)
XLA Ops:
  0.0 3.1 %shard_map.82 = (bf16[2,4,4,16,128]{4,3,2,1,0:T(8,128)(2,1)}, bf16[2,4,4,16,128]{4,3,2,1,0:T(8,128)(2,1)}, bf16[1024,128]{1,0:T(8,128)(2,1)}, bf16[1024,128]{1,0:T(8,128)(2,1)}) custom-call(s32[1]{0:T(128)} %bitcast.me_ref, bf16[2,512,1024]{2,1,0:T(8,128)(2,1)} %constant.18.clone.table_ref, bf16[4,1024,128]{2,1,0:T(8,128)(2,1)} %bitcast.6), custom_call_target="tpu_custom_call" | custom-call | flops 268435456 | bytes 1572864 | tf_op jit(solution)/shard_map/pallas_call | solution.py:217
  3.2 0.0 copy-start.1
  3.2 0.0 copy-start.2
  3.2 3.0 %collective-permute-start.2 = (bf16[2,4,4,16,128]{4,3,2,1,0:T(8,128)(2,1)}, bf16[2,4,4,16,128]{4,3,2,1,0:T(8,128)(2,1)S(1)}, u32[]{:S(2)}, u32[]{:S(2)}) collective-permute-start(bf16[2,4,4,16,128]{4,3,2,1,0:T(8,128)(2,1)} %get-tuple-element.83), channel_id=1, source_target_pairs={{0,1},{1,0},{2,3},{3,2},{4,5},{5,4},{6,7},{7,6},{8,9},{9,8},{10,11... | collective-permute-start | bytes 393224 | tf_op jit(solution)/shard_map/ppermute | solution.py:841
  6.2 0.1 collective-permute-start
  6.3 0.0 collective-permute-start.8
  6.3 0.7 %collective-permute-start.9 = (bf16[1024,128]{1,0:T(8,128)(2,1)}, bf16[1024,128]{1,0:T(8,128)(2,1)S(1)}, u32[]{:S(2)}, u32[]{:S(2)}) collective-permute-start(bf16[1024,128]{1,0:T(8,128)(2,1)} %get-tuple-element.104), channel_id=1, source_target_pairs={{2,4},{6,8},{10,12},{14,16},{18,20},{22,24},{26,28},{4,2},{8,6},{1... | collective-permute-start | bytes 786440 | tf_op jit(solution)/shard_map/ppermute | solution.py:826
  7.0 2.2 %shard_map.83.refs_7_ = bf16[2,64,128,128]{3,2,1,0:T(8,128)(2,1)S(1)} custom-call(bf16[16,64,128,128]{3,2,1,0:T(8,128)(2,1)} %bitcast.13), custom_call_target="tpu_custom_call" | custom-call | bytes 4194304 | tf_op jit(solution)/shard_map/pallas_call | solution.py:330
  9.2 0.4 shard_map.84
  9.7 1.1 %collective-permute-done.2.refs_1_ = bf16[2,4,4,16,128]{4,3,2,1,0:T(8,128)(2,1)S(1)} collective-permute-done((bf16[2,4,4,16,128]{4,3,2,1,0:T(8,128)(2,1)}, bf16[2,4,4,16,128]{4,3,2,1,0:T(8,128)(2,1)S(1)}, u32[]{:S(2)}, u32[]{:S(2)}) %collective-permute-start.2) | collective-permute-done | bytes 131104 | tf_op jit(solution)/shard_map/ppermute | solution.py:841
  10.8 4.7 %collective-permute-start.3 = (bf16[4,4,16,128]{3,2,1,0:T(8,128)(2,1)S(1)}, bf16[4,4,16,128]{3,2,1,0:T(8,128)(2,1)S(1)}, u32[]{:S(2)}, u32[]{:S(2)}) collective-permute-start(bf16[4,4,16,128]{3,2,1,0:T(8,128)(2,1)S(1)} %get-tuple-element.84), channel_id=1, source_target_pairs={{0,16},{2,18},{4,20},{6,22},{8,24},{10,26},{12,28},{14,30},{16,0},... | collective-permute-start | bytes 196616 | tf_op jit(solution)/shard_map/ppermute | solution.py:837
  15.5 1.3 %collective-permute-start.4 = (bf16[4,4,16,128]{3,2,1,0:T(8,128)(2,1)S(1)}, bf16[4,4,16,128]{3,2,1,0:T(8,128)(2,1)S(1)}, u32[]{:S(2)}, u32[]{:S(2)}) collective-permute-start(bf16[4,4,16,128]{3,2,1,0:T(8,128)(2,1)S(1)} %get-tuple-element.85), channel_id=1, source_target_pairs={{0,24},{2,26},{4,28},{6,30},{8,16},{10,18},{12,20},{14,22},{16,8},... | collective-permute-start | bytes 196616 | tf_op jit(solution)/shard_map/ppermute | solution.py:837
  16.9 0.3 collective-permute-start.1
  17.2 3.5 %shard_map.87.refs_8_ = bf16[4,64,128,128]{3,2,1,0:T(8,128)(2,1)S(1)} custom-call(bf16[16,64,128,128]{3,2,1,0:T(8,128)(2,1)} %bitcast.14), custom_call_target="tpu_custom_call" | custom-call | bytes 8388608 | tf_op jit(solution)/shard_map/pallas_call | solution.py:330
  20.7 0.8 %collective-permute-done.3.refs_1_ = bf16[4,4,16,128]{3,2,1,0:T(8,128)(2,1)S(1)} collective-permute-done((bf16[4,4,16,128]{3,2,1,0:T(8,128)(2,1)S(1)}, bf16[4,4,16,128]{3,2,1,0:T(8,128)(2,1)S(1)}, u32[]{:S(2)}, u32[]{:S(2)}) %collective-permute-start.3) | collective-permute-done | bytes 65568 | tf_op jit(solution)/shard_map/ppermute | solution.py:837
  21.4 0.5 collective-permute-done.4.refs_0_
  21.9 0.4 collective-permute-done.1.refs_2_
  22.3 0.0 copy-start.3
  22.3 0.0 copy-start.4
  22.3 0.5 collective-permute-start.5
  22.8 0.8 %collective-permute-start.6 = (bf16[4,4,16,128]{3,2,1,0:T(8,128)(2,1)S(1)}, bf16[4,4,16,128]{3,2,1,0:T(8,128)(2,1)S(1)}, u32[]{:S(2)}, u32[]{:S(2)}) collective-permute-start(bf16[4,4,16,128]{3,2,1,0:T(8,128)(2,1)S(1)} %get-tuple-element.97), channel_id=1, source_target_pairs={{0,4},{2,6},{4,0},{6,2},{8,12},{10,14},{12,8},{14,10},{16,20},{18,... | collective-permute-start | bytes 196616 | tf_op jit(solution)/shard_map/ppermute | solution.py:837
  23.6 0.6 collective-permute-start.7
  24.2 3.5 %shard_map.89.refs_9_ = bf16[4,64,128,128]{3,2,1,0:T(8,128)(2,1)S(1)} custom-call(bf16[16,64,128,128]{3,2,1,0:T(8,128)(2,1)} %bitcast.15), custom_call_target="tpu_custom_call" | custom-call | bytes 8388608 | tf_op jit(solution)/shard_map/pallas_call | solution.py:330
  27.7 0.0 collective-permute-done.8.paired_ref
  27.7 0.0 collective-permute-done.5.refs_0_
  27.7 0.1 collective-permute-done.6.refs_1_
  27.8 0.0 copy-start.6
  27.9 1.9 %collective-permute-start.10 = (bf16[6,64,128]{2,1,0:T(8,128)(2,1)S(1)}, bf16[6,64,128]{2,1,0:T(8,128)(2,1)S(1)}, u32[]{:S(2)}, u32[]{:S(2)}) collective-permute-start(bf16[6,64,128]{2,1,0:T(8,128)(2,1)S(1)} %shard_map.91), channel_id=1, source_target_pairs={{0,1},{1,0},{2,3},{3,2},{4,5},{5,4},{6,7},{7,6},{8,9},{9,8},{10,11... | collective-permute-start | bytes 294920 | tf_op jit(solution)/shard_map/ppermute | solution.py:841
  29.7 5.9 %shard_map.90 = (bf16[4,4,16,128]{3,2,1,0:T(8,128)(2,1)S(1)}, bf16[4,4,16,128]{3,2,1,0:T(8,128)(2,1)S(1)}, bf16[4,4,16,128]{3,2,1,0:T(8,128)(2,1)S(1)}, bf16[4,4,16,128]{3,2,1,0:T(8,128)(2,1)S(1)}) custom-call(s32[1]{0:T(128)} %bitcast.me_ref, bf16[4,4,16,128]{3,2,1,0:T(8,128)(2,1)S(1)} %collective-permute-done.5.refs_0_, ...), custom_call_target="tpu_custom_call" | custom-call | flops 134217728 | bytes 33554432 | tf_op jit(solution)/shard_map/pallas_call | solution.py:449
  35.7 0.0 collective-permute-done.10.refs_3_.refs_4_
  35.7 0.9 %collective-permute-start.11 = (bf16[4,4,16,128]{3,2,1,0:T(8,128)(2,1)S(1)}, bf16[4,4,16,128]{3,2,1,0:T(8,128)(2,1)S(1)}, u32[]{:S(2)}, u32[]{:S(2)}) collective-permute-start(bf16[4,4,16,128]{3,2,1,0:T(8,128)(2,1)S(1)} %get-tuple-element.120), channel_id=1, source_target_pairs={{0,6},{2,4},{4,2},{6,0},{8,14},{10,12},{12,10},{14,8},{16,22},{18,... | collective-permute-start | bytes 196616 | tf_op jit(solution)/shard_map/ppermute | solution.py:837
  36.5 0.6 %collective-permute-start.12 = (bf16[4,4,16,128]{3,2,1,0:T(8,128)(2,1)S(1)}, bf16[4,4,16,128]{3,2,1,0:T(8,128)(2,1)S(1)}, u32[]{:S(2)}, u32[]{:S(2)}) collective-permute-start(bf16[4,4,16,128]{3,2,1,0:T(8,128)(2,1)S(1)} %get-tuple-element.121), channel_id=1, source_target_pairs={{0,4},{2,6},{4,0},{6,2},{8,12},{10,14},{12,8},{14,10},{16,20},{18,... | collective-permute-start | bytes 196616 | tf_op jit(solution)/shard_map/ppermute | solution.py:837
  37.2 0.4 collective-permute-start.13
  37.6 3.0 %shard_map.92.refs_4_ = bf16[2,16,64,128]{3,2,1,0:T(8,128)(2,1)S(1)} custom-call(s32[1]{0:T(128)} %bitcast.me_ref, bf16[4,16,64,128]{3,2,1,0:T(8,128)(2,1)S(1)} %copy-done.2, bf16[16,64,128]{2,1,0:T(8,128)(2,1)S(1)} %bitcast.8, bf16[16,64,128]{2,1,0:T(8,128)(2,1)S(1)} %bitcast.10, bf16[6,64,128]{2,1,0:T(8,128)(2,1)S(1)} %collective-permute-done.10.refs_3_.refs_4_, ...), custom_call_target="tpu_custom_call" | custom-call | flops 2717908992 | bytes 1310720 | tf_op jit(solution)/shard_map/pallas_call | solution.py:535
  40.6 0.0 collective-permute-done.11.refs_0_
  40.6 0.9 %collective-permute-done.12.refs_1_ = bf16[4,4,16,128]{3,2,1,0:T(8,128)(2,1)S(1)} collective-permute-done((bf16[4,4,16,128]{3,2,1,0:T(8,128)(2,1)S(1)}, bf16[4,4,16,128]{3,2,1,0:T(8,128)(2,1)S(1)}, u32[]{:S(2)}, u32[]{:S(2)}) %collective-permute-start.12) | collective-permute-done | bytes 65568 | tf_op jit(solution)/shard_map/ppermute | solution.py:837
  41.5 3.2 %collective-permute-start.14 = (bf16[4,4,16,128]{3,2,1,0:T(8,128)(2,1)S(1)}, bf16[4,4,16,128]{3,2,1,0:T(8,128)(2,1)S(1)}, u32[]{:S(2)}, u32[]{:S(2)}) collective-permute-start(bf16[4,4,16,128]{3,2,1,0:T(8,128)(2,1)S(1)} %get-tuple-element.131), channel_id=1, source_target_pairs={{0,24},{2,26},{4,28},{6,30},{8,16},{10,18},{12,20},{14,22},{16,8},... | collective-permute-start | bytes 196616 | tf_op jit(solution)/shard_map/ppermute | solution.py:837
  44.8 0.0 collective-permute-start.16
  44.8 1.2 %collective-permute-start.17 = (bf16[4,4,16,128]{3,2,1,0:T(8,128)(2,1)S(1)}, bf16[4,4,16,128]{3,2,1,0:T(8,128)(2,1)S(1)}, u32[]{:S(2)}, u32[]{:S(2)}) collective-permute-start(bf16[4,4,16,128]{3,2,1,0:T(8,128)(2,1)S(1)} %get-tuple-element.134), channel_id=1, source_target_pairs={{0,8},{2,10},{4,12},{6,14},{8,0},{10,2},{12,4},{14,6},{16,24},{18,... | collective-permute-start | bytes 196616 | tf_op jit(solution)/shard_map/ppermute | solution.py:837
  46.0 3.0 %shard_map.94.refs_5_ = bf16[2,16,64,128]{3,2,1,0:T(8,128)(2,1)S(1)} custom-call(s32[1]{0:T(128)} %bitcast.me_ref, bf16[4,16,64,128]{3,2,1,0:T(8,128)(2,1)S(1)} %copy-done.2, bf16[16,64,128]{2,1,0:T(8,128)(2,1)S(1)} %bitcast.9, bf16[16,64,128]{2,1,0:T(8,128)(2,1)S(1)} %bitcast.11, bf16[6,64,128]{2,1,0:T(8,128)(2,1)S(1)} %collective-permute-done.10.refs_3_.refs_4_, ...), custom_call_target="tpu_custom_call" | custom-call | flops 2717908992 | bytes 1310720 | tf_op jit(solution)/shard_map/pallas_call | solution.py:535
  49.0 0.0 collective-permute-done.14.refs_1_.refs_0_
  49.0 0.3 collective-permute-start.15
  49.3 1.4 %collective-permute-done.16.refs_0_.refs_1_ = bf16[4,4,16,128]{3,2,1,0:T(8,128)(2,1)S(1)} collective-permute-done((bf16[4,4,16,128]{3,2,1,0:T(8,128)(2,1)S(1)}, bf16[4,4,16,128]{3,2,1,0:T(8,128)(2,1)S(1)}, u32[]{:S(2)}, u32[]{:S(2)}) %collective-permute-start.16) | collective-permute-done | bytes 65568 | tf_op jit(solution)/shard_map/ppermute | solution.py:837
  50.7 0.5 collective-permute-start.18
  51.2 1.0 %shard_map.97.refs_2_ = f32[4,16,64,128]{3,2,1,0:T(8,128)S(1)} custom-call(s32[1]{0:T(128)} %bitcast.me_ref, bf16[4,1024,256]{2,1,0:T(8,128)(2,1)S(1)} %copy-done, bf16[4,4,16,128]{3,2,1,0:T(8,128)(2,1)S(1)} %collective-permute-done.14.refs_1_.refs_0_, bf16[4,4,16,128]{3,2,1,0:T(8,128)(2,1)S(1)} %collective-permute-done.16.refs_0_.refs_1_, ...), custom_call_target="tpu_custom_call" | custom-call | flops 268435456 | bytes 3145728 | tf_op jit(solution)/shard_map/pallas_call | solution.py:662
  52.2 2.6 %collective-permute-done.15.refs_0_ = bf16[2,4,4,16,128]{4,3,2,1,0:T(8,128)(2,1)S(1)} collective-permute-done((bf16[2,4,4,16,128]{4,3,2,1,0:T(8,128)(2,1)S(1)}, bf16[2,4,4,16,128]{4,3,2,1,0:T(8,128)(2,1)S(1)}, u32[]{:S(2)}, u32[]{:S(2)}) %collective-permute-start.15) | collective-permute-done | bytes 131104 | tf_op jit(solution)/shard_map/ppermute | solution.py:841
  54.8 2.1 %collective-permute-done.18.refs_1_ = bf16[2,4,4,16,128]{4,3,2,1,0:T(8,128)(2,1)S(1)} collective-permute-done((bf16[2,4,4,16,128]{4,3,2,1,0:T(8,128)(2,1)S(1)}, bf16[2,4,4,16,128]{4,3,2,1,0:T(8,128)(2,1)S(1)}, u32[]{:S(2)}, u32[]{:S(2)}) %collective-permute-start.18) | collective-permute-done | bytes 131104 | tf_op jit(solution)/shard_map/ppermute | solution.py:841
  56.9 2.5 %shard_map.98 = bf16[4,16,64,128]{3,2,1,0:T(8,128)(2,1)} custom-call(s32[1]{0:T(128)} %bitcast.me_ref, bf16[4,1024,256]{2,1,0:T(8,128)(2,1)S(1)} %copy-done, bf16[2,4,4,16,128]{4,3,2,1,0:T(8,128)(2,1)S(1)} %collective-permute-done.15.refs_0_, bf16[2,4,4,16,128]{4,3,2,1,0:T(8,128)(2,1)S(1)} %collective-permute-done.18.refs_1_, ...), custom_call_target="tpu_custom_call" | custom-call | flops 268435456 | bytes 3145728 | tf_op jit(solution)/shard_map/pallas_call | solution.py:682
  (21 shorter events, 0.2 us)
Async XLA Ops:
  3.2 6.0 %copy-start.1 = (bf16[2,512,1024]{2,1,0:T(8,128)(2,1)S(1)}, bf16[2,512,1024]{2,1,0:T(8,128)(2,1)}, u32[]{:S(2)}) copy-start(bf16[2,512,1024]{2,1,0:T(8,128)(2,1)} %constant.18.clone.table_ref) | copy-start | bytes 6291460
  3.2 6.0 %copy-start.2 = (bf16[4,16,64,128]{3,2,1,0:T(8,128)(2,1)S(1)}, bf16[4,16,64,128]{3,2,1,0:T(8,128)(2,1)}, u32[]{:S(2)}) copy-start(bf16[4,16,64,128]{3,2,1,0:T(8,128)(2,1)} %refs_0_.3) | copy-start | bytes 3145732
  3.2 7.6 %collective-permute-start.2 = (bf16[2,4,4,16,128]{4,3,2,1,0:T(8,128)(2,1)}, bf16[2,4,4,16,128]{4,3,2,1,0:T(8,128)(2,1)S(1)}, u32[]{:S(2)}, u32[]{:S(2)}) collective-permute-start(bf16[2,4,4,16,128]{4,3,2,1,0:T(8,128)(2,1)} %get-tuple-element.83), channel_id=1, source_target_pairs={{0,1},{1,0},{2,3},{3,2},{4,5},{5,4},{6,7},{7,6},{8,9},{9,8},{10,11... | collective-permute-start | bytes 393224 | tf_op jit(solution)/shard_map/ppermute | solution.py:841
  6.2 10.6 %collective-permute-start = (bf16[2,4,4,16,128]{4,3,2,1,0:T(8,128)(2,1)}, bf16[2,4,4,16,128]{4,3,2,1,0:T(8,128)(2,1)S(1)}, u32[]{:S(2)}, u32[]{:S(2)}) collective-permute-start(bf16[2,4,4,16,128]{4,3,2,1,0:T(8,128)(2,1)} %get-tuple-element.79), channel_id=1, source_target_pairs={{0,1},{1,0},{2,3},{3,2},{4,5},{5,4},{6,7},{7,6},{8,9},{9,8},{10,11... | collective-permute-start | bytes 393224 | tf_op jit(solution)/shard_map/ppermute | solution.py:841
  6.3 21.4 %collective-permute-start.8 = (bf16[1024,128]{1,0:T(8,128)(2,1)}, bf16[1024,128]{1,0:T(8,128)(2,1)S(1)}, u32[]{:S(2)}, u32[]{:S(2)}) collective-permute-start(bf16[1024,128]{1,0:T(8,128)(2,1)} %get-tuple-element.103), channel_id=1, source_target_pairs={{0,2},{4,6},{8,10},{12,14},{16,18},{20,22},{24,26},{28,30},{2,0},{... | collective-permute-start | bytes 786440 | tf_op jit(solution)/shard_map/ppermute | solution.py:826
  6.3 21.4 %collective-permute-start.9 = (bf16[1024,128]{1,0:T(8,128)(2,1)}, bf16[1024,128]{1,0:T(8,128)(2,1)S(1)}, u32[]{:S(2)}, u32[]{:S(2)}) collective-permute-start(bf16[1024,128]{1,0:T(8,128)(2,1)} %get-tuple-element.104), channel_id=1, source_target_pairs={{2,4},{6,8},{10,12},{14,16},{18,20},{22,24},{26,28},{4,2},{8,6},{1... | collective-permute-start | bytes 786440 | tf_op jit(solution)/shard_map/ppermute | solution.py:826
  10.8 10.6 %collective-permute-start.3 = (bf16[4,4,16,128]{3,2,1,0:T(8,128)(2,1)S(1)}, bf16[4,4,16,128]{3,2,1,0:T(8,128)(2,1)S(1)}, u32[]{:S(2)}, u32[]{:S(2)}) collective-permute-start(bf16[4,4,16,128]{3,2,1,0:T(8,128)(2,1)S(1)} %get-tuple-element.84), channel_id=1, source_target_pairs={{0,16},{2,18},{4,20},{6,22},{8,24},{10,26},{12,28},{14,30},{16,0},... | collective-permute-start | bytes 196616 | tf_op jit(solution)/shard_map/ppermute | solution.py:837
  15.5 6.4 %collective-permute-start.4 = (bf16[4,4,16,128]{3,2,1,0:T(8,128)(2,1)S(1)}, bf16[4,4,16,128]{3,2,1,0:T(8,128)(2,1)S(1)}, u32[]{:S(2)}, u32[]{:S(2)}) collective-permute-start(bf16[4,4,16,128]{3,2,1,0:T(8,128)(2,1)S(1)} %get-tuple-element.85), channel_id=1, source_target_pairs={{0,24},{2,26},{4,28},{6,30},{8,16},{10,18},{12,20},{14,22},{16,8},... | collective-permute-start | bytes 196616 | tf_op jit(solution)/shard_map/ppermute | solution.py:837
  16.9 5.4 %collective-permute-start.1 = (bf16[4,4,16,128]{3,2,1,0:T(8,128)(2,1)S(1)}, bf16[4,4,16,128]{3,2,1,0:T(8,128)(2,1)S(1)}, u32[]{:S(2)}, u32[]{:S(2)}) collective-permute-start(bf16[4,4,16,128]{3,2,1,0:T(8,128)(2,1)S(1)} %get-tuple-element.81), channel_id=1, source_target_pairs={{0,8},{2,10},{4,12},{6,14},{8,0},{10,2},{12,4},{14,6},{16,24},{18,... | collective-permute-start | bytes 196616 | tf_op jit(solution)/shard_map/ppermute | solution.py:837
  22.3 7.4 %copy-start.3 = (bf16[256,128]{1,0:T(8,128)(2,1)S(1)}, bf16[256,128]{1,0:T(8,128)(2,1)}, u32[]{:S(2)}) copy-start(bf16[256,128]{1,0:T(8,128)(2,1)} %constant.19.clone.refs_4_) | copy-start | bytes 196612
  22.3 7.4 %copy-start.4 = (bf16[128,128]{1,0:T(8,128)(2,1)S(1)}, bf16[128,128]{1,0:T(8,128)(2,1)}, u32[]{:S(2)}) copy-start(bf16[128,128]{1,0:T(8,128)(2,1)} %constant.20.clone.refs_5_) | copy-start | bytes 98308
  22.3 5.4 %collective-permute-start.5 = (bf16[4,4,16,128]{3,2,1,0:T(8,128)(2,1)S(1)}, bf16[4,4,16,128]{3,2,1,0:T(8,128)(2,1)S(1)}, u32[]{:S(2)}, u32[]{:S(2)}) collective-permute-start(bf16[4,4,16,128]{3,2,1,0:T(8,128)(2,1)S(1)} %get-tuple-element.96), channel_id=1, source_target_pairs={{0,6},{2,4},{4,2},{6,0},{8,14},{10,12},{12,10},{14,8},{16,22},{18,... | collective-permute-start | bytes 196616 | tf_op jit(solution)/shard_map/ppermute | solution.py:837
  22.8 5.0 %collective-permute-start.6 = (bf16[4,4,16,128]{3,2,1,0:T(8,128)(2,1)S(1)}, bf16[4,4,16,128]{3,2,1,0:T(8,128)(2,1)S(1)}, u32[]{:S(2)}, u32[]{:S(2)}) collective-permute-start(bf16[4,4,16,128]{3,2,1,0:T(8,128)(2,1)S(1)} %get-tuple-element.97), channel_id=1, source_target_pairs={{0,4},{2,6},{4,0},{6,2},{8,12},{10,14},{12,8},{14,10},{16,20},{18,... | collective-permute-start | bytes 196616 | tf_op jit(solution)/shard_map/ppermute | solution.py:837
  23.6 4.2 %collective-permute-start.7 = (bf16[4,4,16,128]{3,2,1,0:T(8,128)(2,1)S(1)}, bf16[4,4,16,128]{3,2,1,0:T(8,128)(2,1)S(1)}, u32[]{:S(2)}, u32[]{:S(2)}) collective-permute-start(bf16[4,4,16,128]{3,2,1,0:T(8,128)(2,1)S(1)} %get-tuple-element.98), channel_id=1, source_target_pairs={{0,2},{2,0},{4,6},{6,4},{8,10},{10,8},{12,14},{14,12},{16,18},{18,... | collective-permute-start | bytes 196616 | tf_op jit(solution)/shard_map/ppermute | solution.py:837
  27.8 9.8 %copy-start.6 = (bf16[3,3,3,128,128]{4,3,2,1,0:T(8,128)(2,1)S(1)}, bf16[3,3,3,128,128]{4,3,2,1,0:T(8,128)(2,1)}, u32[]{:S(2)}) copy-start(bf16[3,3,3,128,128]{4,3,2,1,0:T(8,128)(2,1)} %refs_5_.4) | copy-start | bytes 2654212
  27.9 7.8 %collective-permute-start.10 = (bf16[6,64,128]{2,1,0:T(8,128)(2,1)S(1)}, bf16[6,64,128]{2,1,0:T(8,128)(2,1)S(1)}, u32[]{:S(2)}, u32[]{:S(2)}) collective-permute-start(bf16[6,64,128]{2,1,0:T(8,128)(2,1)S(1)} %shard_map.91), channel_id=1, source_target_pairs={{0,1},{1,0},{2,3},{3,2},{4,5},{5,4},{6,7},{7,6},{8,9},{9,8},{10,11... | collective-permute-start | bytes 294920 | tf_op jit(solution)/shard_map/ppermute | solution.py:841
  35.7 4.9 %collective-permute-start.11 = (bf16[4,4,16,128]{3,2,1,0:T(8,128)(2,1)S(1)}, bf16[4,4,16,128]{3,2,1,0:T(8,128)(2,1)S(1)}, u32[]{:S(2)}, u32[]{:S(2)}) collective-permute-start(bf16[4,4,16,128]{3,2,1,0:T(8,128)(2,1)S(1)} %get-tuple-element.120), channel_id=1, source_target_pairs={{0,6},{2,4},{4,2},{6,0},{8,14},{10,12},{12,10},{14,8},{16,22},{18,... | collective-permute-start | bytes 196616 | tf_op jit(solution)/shard_map/ppermute | solution.py:837
  36.5 5.0 %collective-permute-start.12 = (bf16[4,4,16,128]{3,2,1,0:T(8,128)(2,1)S(1)}, bf16[4,4,16,128]{3,2,1,0:T(8,128)(2,1)S(1)}, u32[]{:S(2)}, u32[]{:S(2)}) collective-permute-start(bf16[4,4,16,128]{3,2,1,0:T(8,128)(2,1)S(1)} %get-tuple-element.121), channel_id=1, source_target_pairs={{0,4},{2,6},{4,0},{6,2},{8,12},{10,14},{12,8},{14,10},{16,20},{18,... | collective-permute-start | bytes 196616 | tf_op jit(solution)/shard_map/ppermute | solution.py:837
  37.2 4.3 %collective-permute-start.13 = (bf16[4,4,16,128]{3,2,1,0:T(8,128)(2,1)S(1)}, bf16[4,4,16,128]{3,2,1,0:T(8,128)(2,1)S(1)}, u32[]{:S(2)}, u32[]{:S(2)}) collective-permute-start(bf16[4,4,16,128]{3,2,1,0:T(8,128)(2,1)S(1)} %get-tuple-element.122), channel_id=1, source_target_pairs={{0,2},{2,0},{4,6},{6,4},{8,10},{10,8},{12,14},{14,12},{16,18},{18,... | collective-permute-start | bytes 196616 | tf_op jit(solution)/shard_map/ppermute | solution.py:837
  41.5 7.5 %collective-permute-start.14 = (bf16[4,4,16,128]{3,2,1,0:T(8,128)(2,1)S(1)}, bf16[4,4,16,128]{3,2,1,0:T(8,128)(2,1)S(1)}, u32[]{:S(2)}, u32[]{:S(2)}) collective-permute-start(bf16[4,4,16,128]{3,2,1,0:T(8,128)(2,1)S(1)} %get-tuple-element.131), channel_id=1, source_target_pairs={{0,24},{2,26},{4,28},{6,30},{8,16},{10,18},{12,20},{14,22},{16,8},... | collective-permute-start | bytes 196616 | tf_op jit(solution)/shard_map/ppermute | solution.py:837
  44.8 5.9 %collective-permute-start.16 = (bf16[4,4,16,128]{3,2,1,0:T(8,128)(2,1)S(1)}, bf16[4,4,16,128]{3,2,1,0:T(8,128)(2,1)S(1)}, u32[]{:S(2)}, u32[]{:S(2)}) collective-permute-start(bf16[4,4,16,128]{3,2,1,0:T(8,128)(2,1)S(1)} %get-tuple-element.133), channel_id=1, source_target_pairs={{0,16},{2,18},{4,20},{6,22},{8,24},{10,26},{12,28},{14,30},{16,0},... | collective-permute-start | bytes 196616 | tf_op jit(solution)/shard_map/ppermute | solution.py:837
  44.8 6.5 %copy-start = (bf16[4,1024,256]{2,1,0:T(8,128)(2,1)S(1)}, bf16[4,1024,256]{2,1,0:T(8,128)(2,1)}, u32[]{:S(2)}) copy-start(bf16[4,1024,256]{2,1,0:T(8,128)(2,1)} %constant.21.clone.table_ref) | copy-start | bytes 6291460
  44.8 6.5 %copy-start.5 = (f32[128]{0:T(128)S(1)}, f32[128]{0:T(128)}, u32[]{:S(2)}) copy-start(f32[128]{0:T(128)} %param.11) | copy-start | bytes 1540
  44.8 5.9 %collective-permute-start.17 = (bf16[4,4,16,128]{3,2,1,0:T(8,128)(2,1)S(1)}, bf16[4,4,16,128]{3,2,1,0:T(8,128)(2,1)S(1)}, u32[]{:S(2)}, u32[]{:S(2)}) collective-permute-start(bf16[4,4,16,128]{3,2,1,0:T(8,128)(2,1)S(1)} %get-tuple-element.134), channel_id=1, source_target_pairs={{0,8},{2,10},{4,12},{6,14},{8,0},{10,2},{12,4},{14,6},{16,24},{18,... | collective-permute-start | bytes 196616 | tf_op jit(solution)/shard_map/ppermute | solution.py:837
  49.0 5.8 %collective-permute-start.15 = (bf16[2,4,4,16,128]{4,3,2,1,0:T(8,128)(2,1)S(1)}, bf16[2,4,4,16,128]{4,3,2,1,0:T(8,128)(2,1)S(1)}, u32[]{:S(2)}, u32[]{:S(2)}) collective-permute-start(bf16[2,4,4,16,128]{4,3,2,1,0:T(8,128)(2,1)S(1)} %shard_map.95), channel_id=1, source_target_pairs={{0,1},{1,0},{2,3},{3,2},{4,5},{5,4},{6,7},{7,6},{8,9},{9,8},{10,11... | collective-permute-start | bytes 393224 | tf_op jit(solution)/shard_map/ppermute | solution.py:841
  50.7 6.2 %collective-permute-start.18 = (bf16[2,4,4,16,128]{4,3,2,1,0:T(8,128)(2,1)S(1)}, bf16[2,4,4,16,128]{4,3,2,1,0:T(8,128)(2,1)S(1)}, u32[]{:S(2)}, u32[]{:S(2)}) collective-permute-start(bf16[2,4,4,16,128]{4,3,2,1,0:T(8,128)(2,1)S(1)} %shard_map.96), channel_id=1, source_target_pairs={{0,1},{1,0},{2,3},{3,2},{4,5},{5,4},{6,7},{7,6},{8,9},{9,8},{10,11... | collective-permute-start | bytes 393224 | tf_op jit(solution)/shard_map/ppermute | solution.py:841

commit v10 on v9

--- a/solution.py
+++ b/solution.py
@@ -493,7 +493,7 @@
             def _(plane=plane):
                 padded[plane, 1 : cells_y + 1] = other_ref[...]
 
-    rows = 4 if cells_y % 4 == 0 else 1
+    rows = 8 if cells_y % 8 == 0 else 1
     columns = [(k, d) for k in range(width) for d in range(3)]
     columns = [columns[i : i + 2] for i in range(0, len(columns), 2)]
     none = jnp.zeros((channels, channels), kernel_ref.dtype)
@@ -548,9 +548,8 @@
 
 
 def bundled_slots(count):
-    slots = [0] + far_first(count)[:-1]
-    cut = (count + 1) // 2
-    return [part for part in (slots[:cut], slots[cut:]) if part]
+    parts = ([0], [count - 1], far_first(count)[1:-1]) if count > 1 else ([0],)
+    return [part for part in parts if part]
 
 
 def bundle_kernel(*refs):
@@ -875,8 +874,7 @@
         if step == 1:
             ends = sent[len(pieces) :]
             planes = [with_neighbour(end, start, "gx") for start, end in enumerate(ends)]
-    loaded = [preload(weight, 0, early // 2)] if early > 1 else []
-    loaded, columns = barrier((loaded, columns))
+    loaded = []
     kept = forward_yz(me, table, columns, 0, shards, shards_y, pieces, cells_z)
     kept, (low, high) = kept[: len(pieces)], kept[len(pieces) :]
 
@@ -885,7 +883,7 @@
         for step, total in zip(piece, add_pieces(own, parts)):
             by_outer.append(exchange(total, step, shards, True) if step else total)
     if early:
-        loaded.append(preload(weight, early // 2, early))
+        loaded.append(preload(weight, 0, early))
     by_outer, loaded, weight = barrier((by_outer[::-1], loaded, weight))
     by_inner = regroup(me, by_outer[::-1], shards, True)
     by_inner, weight = barrier((by_inner, weight))
@@ -894,9 +892,10 @@
         for step in far_first(inner)
     ]
     if early:
-        loaded.append(preload(weight, early + early // 2, early))
-
-    rows, loaded, planes = barrier((rows, loaded, planes))
+        loaded.append(preload(weight, early, early))
+
+    rows, loaded, planes = barrier((rows, loaded, planes[::-1]))
+    planes = planes[::-1]
     if shards_y == 2:
         edge = y_edge(me, *planes, low, high, shards, lambda own: own > 0)
         front = back = over_y(edge, 1, shards_y)
@@ -934,9 +933,11 @@
         exchange(returned[step], step, shards, True) if step else returned[0]
         for step in far_first(outer)
     ]
-    returned[0], convolved[-1] = barrier((returned[0], convolved[-1]))
     by_slot = dict(zip(far_first(outer), returned))
-    bundles = [bundle([by_slot[slot] for slot in slots]) for slots in bundled_slots(outer)]
+    bundles = [
+        bundle([by_slot[slot] for slot in slots]) if slots[1:] else by_slot[slots[0]][None]
+        for slots in bundled_slots(outer)
+    ]
     others = []
     for step in range(1, shards_y):
         others += [over_y(part, step, shards_y) for part in bundles]

time: 59.6 us -> 60.7 us (1.018)
  local copies, waits for them, and re-layouts: 0.04 us -> 2.85 us
  Pallas kernels: 28.3 us -> 26.4 us
  starting transfers between devices: 21.2 us -> 23.1 us
  waiting for transfers between devices: 9.67 us -> 7.91 us
    ppermute x5 -> x6, waiting for transfers between devices: 5.74 us -> 1.31 us  [over_y(): lax.ppermute(array, 'gy', [(i, (i + step) % shards_y) for i in range(shar...]
    ppermute x2, starting transfers between devices: 0.67 us -> 4 us  [with_neighbour(): return lax.ppermute(array, axis, pairs + [(j, i) for i, j in pairs])]
    unnamed x14 -> x16, local copies, waits for them, and re-layouts: 0.04 us -> 2.85 us
    ppermute x12, waiting for transfers between devices: 3.92 us -> 6.59 us  [exchange(): return lax.ppermute(array, 'gx', pairs)]
    pallas_call x3 -> x2, Pallas kernels: 9.15 us -> 6.94 us  [preload(): pl.pallas_call(functools.partial(preload_kernel, 2 * pair), in_specs=[pl....]
    ppermute x12, starting transfers between devices: 14.7 us -> 12.6 us  [exchange(): return lax.ppermute(array, 'gx', pairs)]
    pallas_call x1, Pallas kernels: 5.93 us -> 6.99 us  [mixing(): pl.pallas_call(functools.partial(mixing_kernel, shards, len(loaded)), in_...]
    pallas_call x2, Pallas kernels: 5.99 us -> 5.27 us  [convolution(): pl.pallas_call(functools.partial(convolution_kernel, x, cells_x, width, s...]
  transfers between devices with their start and end apart: 19 -> 20, of which waited for: 9 -> 7; matrix products, arithmetic and copies ran while one was open for 0% -> 0% of each run, Pallas kernels for 38% -> 34%
where the time goes in v10:
time: 60.7 us; the launch traced here: 60.5 us
  Pallas kernels  26.4 us (43%)
  starting transfers between devices  23.1 us (38%)
  waiting for transfers between devices  7.91 us (13%)
  local copies, waits for them, and re-layouts  2.85 us (5%)
    ppermute x12, starting transfers between devices, exchange(): return lax.ppermute(array, 'gx', pairs)  12.6 us
    pallas_call x1, Pallas kernels, mixing(): pl.pallas_call(functools.partial(mixing_kernel, shards, len(loaded)), in_...  6.99 us
    pallas_call x2, Pallas kernels, preload(): pl.pallas_call(functools.partial(preload_kernel, 2 * pair), in_specs=[pl....  6.94 us
    ppermute x12, waiting for transfers between devices, exchange(): return lax.ppermute(array, 'gx', pairs)  6.59 us
    ppermute x6, starting transfers between devices, over_y(): lax.ppermute(array, 'gy', [(i, (i + step) % shards_y) for i in range(shar...  6.47 us
    pallas_call x2, Pallas kernels, convolution(): pl.pallas_call(functools.partial(convolution_kernel, x, cells_x, width, s...  5.27 us
    ppermute x2, starting transfers between devices, with_neighbour(): return lax.ppermute(array, axis, pairs + [(j, i) for i, j in pairs])  4 us
    pallas_call x2, Pallas kernels, forward_yz(): pl.pallas_call(kernel, in_specs=[IN_SMEM] + specs, out_specs=in_vmem(len(...  3.58 us
  transfers between devices with their start and end apart: 20, of which 7 were waited for; matrix products, arithmetic and copies ran while one was open for 0% of the time, Pallas kernels for 34%

profile of v10, /device:TPU:0, one launch (start us, length us, event | category | flops | bytes accessed | tf_op | source)
XLA Modules:
  0.0 60.5 jit_solution(11393427057235469155)
XLA Ops:
  0.0 3.1 %shard_map.82 = (bf16[2,4,4,16,128]{4,3,2,1,0:T(8,128)(2,1)}, bf16[2,4,4,16,128]{4,3,2,1,0:T(8,128)(2,1)}, bf16[1024,128]{1,0:T(8,128)(2,1)}, bf16[1024,128]{1,0:T(8,128)(2,1)}) custom-call(s32[1]{0:T(128)} %bitcast.me_ref, bf16[2,512,1024]{2,1,0:T(8,128)(2,1)} %constant.18.clone.table_ref, bf16[4,1024,128]{2,1,0:T(8,128)(2,1)} %bitcast.8), custom_call_target="tpu_custom_call" | custom-call | flops 268435456 | bytes 1572864 | tf_op jit(solution)/shard_map/pallas_call | solution.py:217
  3.2 3.0 %collective-permute-start.2 = (bf16[2,4,4,16,128]{4,3,2,1,0:T(8,128)(2,1)}, bf16[2,4,4,16,128]{4,3,2,1,0:T(8,128)(2,1)S(1)}, u32[]{:S(2)}, u32[]{:S(2)}) collective-permute-start(bf16[2,4,4,16,128]{4,3,2,1,0:T(8,128)(2,1)} %get-tuple-element.75), channel_id=1, source_target_pairs={{0,1},{1,0},{2,3},{3,2},{4,5},{5,4},{6,7},{7,6},{8,9},{9,8},{10,11... | collective-permute-start | bytes 393224 | tf_op jit(solution)/shard_map/ppermute | solution.py:840
  6.2 0.1 collective-permute-start
  6.3 0.7 %collective-permute-start.8 = (bf16[1024,128]{1,0:T(8,128)(2,1)}, bf16[1024,128]{1,0:T(8,128)(2,1)S(1)}, u32[]{:S(2)}, u32[]{:S(2)}) collective-permute-start(bf16[1024,128]{1,0:T(8,128)(2,1)} %get-tuple-element.94), channel_id=1, source_target_pairs={{2,4},{6,8},{10,12},{14,16},{18,20},{22,24},{26,28},{4,2},{8,6},{1... | collective-permute-start | bytes 786440 | tf_op jit(solution)/shard_map/ppermute | solution.py:825
  6.9 3.3 %collective-permute-start.9 = (bf16[1024,128]{1,0:T(8,128)(2,1)}, bf16[1024,128]{1,0:T(8,128)(2,1)S(1)}, u32[]{:S(2)}, u32[]{:S(2)}) collective-permute-start(bf16[1024,128]{1,0:T(8,128)(2,1)} %get-tuple-element.95), channel_id=1, source_target_pairs={{0,2},{4,6},{8,10},{12,14},{16,18},{20,22},{24,26},{28,30},{2,0},{... | collective-permute-start | bytes 786440 | tf_op jit(solution)/shard_map/ppermute | solution.py:825
  10.3 1.6 %copy-done.1 = bf16[2,512,1024]{2,1,0:T(8,128)(2,1)S(1)} copy-done((bf16[2,512,1024]{2,1,0:T(8,128)(2,1)S(1)}, bf16[2,512,1024]{2,1,0:T(8,128)(2,1)}, u32[]{:S(2)}) %copy-start.1) | copy-done | bytes 2097176
  11.9 1.2 %copy-done.2 = bf16[4,16,64,128]{3,2,1,0:T(8,128)(2,1)S(1)} copy-done((bf16[4,16,64,128]{3,2,1,0:T(8,128)(2,1)S(1)}, bf16[4,16,64,128]{3,2,1,0:T(8,128)(2,1)}, u32[]{:S(2)}) %copy-start.2) | copy-done | bytes 1048600
  13.1 0.4 shard_map.83
  13.6 2.7 %collective-permute-start.3 = (bf16[4,4,16,128]{3,2,1,0:T(8,128)(2,1)S(1)}, bf16[4,4,16,128]{3,2,1,0:T(8,128)(2,1)S(1)}, u32[]{:S(2)}, u32[]{:S(2)}) collective-permute-start(bf16[4,4,16,128]{3,2,1,0:T(8,128)(2,1)S(1)} %get-tuple-element.76), channel_id=1, source_target_pairs={{0,16},{2,18},{4,20},{6,22},{8,24},{10,26},{12,28},{14,30},{16,0},... | collective-permute-start | bytes 196616 | tf_op jit(solution)/shard_map/ppermute | solution.py:836
  16.2 1.3 %collective-permute-start.4 = (bf16[4,4,16,128]{3,2,1,0:T(8,128)(2,1)S(1)}, bf16[4,4,16,128]{3,2,1,0:T(8,128)(2,1)S(1)}, u32[]{:S(2)}, u32[]{:S(2)}) collective-permute-start(bf16[4,4,16,128]{3,2,1,0:T(8,128)(2,1)S(1)} %get-tuple-element.77), channel_id=1, source_target_pairs={{0,24},{2,26},{4,28},{6,30},{8,16},{10,18},{12,20},{14,22},{16,8},... | collective-permute-start | bytes 196616 | tf_op jit(solution)/shard_map/ppermute | solution.py:836
  17.6 0.0 collective-permute-done.refs_1_
  17.6 0.3 collective-permute-start.1
  17.9 3.5 %shard_map.86.refs_7_ = bf16[4,64,128,128]{3,2,1,0:T(8,128)(2,1)S(1)} custom-call(bf16[16,64,128,128]{3,2,1,0:T(8,128)(2,1)} %bitcast.17), custom_call_target="tpu_custom_call" | custom-call | bytes 8388608 | tf_op jit(solution)/shard_map/pallas_call | solution.py:330
  21.4 0.0 collective-permute-done.3.refs_1_
  21.4 1.2 %collective-permute-done.4.refs_0_ = bf16[4,4,16,128]{3,2,1,0:T(8,128)(2,1)S(1)} collective-permute-done((bf16[4,4,16,128]{3,2,1,0:T(8,128)(2,1)S(1)}, bf16[4,4,16,128]{3,2,1,0:T(8,128)(2,1)S(1)}, u32[]{:S(2)}, u32[]{:S(2)}) %collective-permute-start.4) | collective-permute-done | bytes 65568 | tf_op jit(solution)/shard_map/ppermute | solution.py:836
  22.6 0.3 collective-permute-done.1.refs_2_
  23.0 0.0 copy-start.4
  23.0 0.0 copy-start.5
  23.0 0.3 collective-permute-start.5
  23.3 1.5 %collective-permute-start.6 = (bf16[4,4,16,128]{3,2,1,0:T(8,128)(2,1)S(1)}, bf16[4,4,16,128]{3,2,1,0:T(8,128)(2,1)S(1)}, u32[]{:S(2)}, u32[]{:S(2)}) collective-permute-start(bf16[4,4,16,128]{3,2,1,0:T(8,128)(2,1)S(1)} %get-tuple-element.89), channel_id=1, source_target_pairs={{0,4},{2,6},{4,0},{6,2},{8,12},{10,14},{12,8},{14,10},{16,20},{18,... | collective-permute-start | bytes 196616 | tf_op jit(solution)/shard_map/ppermute | solution.py:836
  24.7 0.2 collective-permute-start.7
  24.9 3.5 %shard_map.88.refs_8_ = bf16[4,64,128,128]{3,2,1,0:T(8,128)(2,1)S(1)} custom-call(bf16[16,64,128,128]{3,2,1,0:T(8,128)(2,1)} %bitcast.18), custom_call_target="tpu_custom_call" | custom-call | bytes 8388608 | tf_op jit(solution)/shard_map/pallas_call | solution.py:330
  28.4 0.0 collective-permute-done.9.paired_ref
  28.4 0.0 collective-permute-done.5.refs_0_
  28.4 0.4 collective-permute-done.6.refs_1_
  28.9 0.0 collective-permute-done.7.refs_2_
  28.9 0.0 copy-start.3
  28.9 0.0 copy-start.7
  28.9 1.6 %collective-permute-start.10 = (bf16[6,64,128]{2,1,0:T(8,128)(2,1)S(1)}, bf16[6,64,128]{2,1,0:T(8,128)(2,1)S(1)}, u32[]{:S(2)}, u32[]{:S(2)}) collective-permute-start(bf16[6,64,128]{2,1,0:T(8,128)(2,1)S(1)} %shard_map.90), channel_id=1, source_target_pairs={{0,1},{1,0},{2,3},{3,2},{4,5},{5,4},{6,7},{7,6},{8,9},{9,8},{10,11... | collective-permute-start | bytes 294920 | tf_op jit(solution)/shard_map/ppermute | solution.py:840
  30.5 7.0 %shard_map.89 = (bf16[4,4,16,128]{3,2,1,0:T(8,128)(2,1)S(1)}, bf16[4,4,16,128]{3,2,1,0:T(8,128)(2,1)S(1)}, bf16[4,4,16,128]{3,2,1,0:T(8,128)(2,1)S(1)}, bf16[4,4,16,128]{3,2,1,0:T(8,128)(2,1)S(1)}) custom-call(s32[1]{0:T(128)} %bitcast.me_ref, bf16[4,4,16,128]{3,2,1,0:T(8,128)(2,1)S(1)} %collective-permute-done.5.refs_0_, ...), custom_call_target="tpu_custom_call" | custom-call | flops 134217728 | bytes 33554432 | tf_op jit(solution)/shard_map/pallas_call | solution.py:449
  37.5 0.0 collective-permute-done.10.refs_3_.refs_4_
  37.5 0.6 collective-permute-start.11
  38.1 0.9 %collective-permute-start.12 = (bf16[4,4,16,128]{3,2,1,0:T(8,128)(2,1)S(1)}, bf16[4,4,16,128]{3,2,1,0:T(8,128)(2,1)S(1)}, u32[]{:S(2)}, u32[]{:S(2)}) collective-permute-start(bf16[4,4,16,128]{3,2,1,0:T(8,128)(2,1)S(1)} %get-tuple-element.111), channel_id=1, source_target_pairs={{0,4},{2,6},{4,0},{6,2},{8,12},{10,14},{12,8},{14,10},{16,20},{18,... | collective-permute-start | bytes 196616 | tf_op jit(solution)/shard_map/ppermute | solution.py:836
  39.0 0.5 collective-permute-start.13
  39.4 2.6 %shard_map.91.refs_4_ = bf16[2,16,64,128]{3,2,1,0:T(8,128)(2,1)S(1)} custom-call(s32[1]{0:T(128)} %bitcast.me_ref, bf16[4,16,64,128]{3,2,1,0:T(8,128)(2,1)S(1)} %copy-done.3, bf16[16,64,128]{2,1,0:T(8,128)(2,1)S(1)} %bitcast.12, bf16[16,64,128]{2,1,0:T(8,128)(2,1)S(1)} %bitcast.10, bf16[6,64,128]{2,1,0:T(8,128)(2,1)S(1)} %collective-permute-done.10.refs_3_.refs_4_, ...), custom_call_target="tpu_custom_call" | custom-call | flops 2717908992 | bytes 1310720 | tf_op jit(solution)/shard_map/pallas_call | solution.py:535
  42.1 1.2 %collective-permute-done.12.refs_1_ = bf16[4,4,16,128]{3,2,1,0:T(8,128)(2,1)S(1)} collective-permute-done((bf16[4,4,16,128]{3,2,1,0:T(8,128)(2,1)S(1)}, bf16[4,4,16,128]{3,2,1,0:T(8,128)(2,1)S(1)}, u32[]{:S(2)}, u32[]{:S(2)}) %collective-permute-start.12) | collective-permute-done | bytes 65568 | tf_op jit(solution)/shard_map/ppermute | solution.py:836
  43.3 0.0 collective-permute-done.13.refs_2_
  43.3 2.7 %collective-permute-start.15 = (bf16[4,4,16,128]{3,2,1,0:T(8,128)(2,1)S(1)}, bf16[4,4,16,128]{3,2,1,0:T(8,128)(2,1)S(1)}, u32[]{:S(2)}, u32[]{:S(2)}) collective-permute-start(bf16[4,4,16,128]{3,2,1,0:T(8,128)(2,1)S(1)} %get-tuple-element.121), channel_id=1, source_target_pairs={{0,24},{2,26},{4,28},{6,30},{8,16},{10,18},{12,20},{14,22},{16,8},... | collective-permute-start | bytes 196616 | tf_op jit(solution)/shard_map/ppermute | solution.py:836
  46.0 1.7 %collective-permute-start.18 = (bf16[4,4,16,128]{3,2,1,0:T(8,128)(2,1)S(1)}, bf16[4,4,16,128]{3,2,1,0:T(8,128)(2,1)S(1)}, u32[]{:S(2)}, u32[]{:S(2)}) collective-permute-start(bf16[4,4,16,128]{3,2,1,0:T(8,128)(2,1)S(1)} %get-tuple-element.123), channel_id=1, source_target_pairs={{0,8},{2,10},{4,12},{6,14},{8,0},{10,2},{12,4},{14,6},{16,24},{18,... | collective-permute-start | bytes 196616 | tf_op jit(solution)/shard_map/ppermute | solution.py:836
  47.7 0.6 collective-permute-start.14
  48.3 1.4 %collective-permute-done.15.refs_0_ = bf16[4,4,16,128]{3,2,1,0:T(8,128)(2,1)S(1)} collective-permute-done((bf16[4,4,16,128]{3,2,1,0:T(8,128)(2,1)S(1)}, bf16[4,4,16,128]{3,2,1,0:T(8,128)(2,1)S(1)}, u32[]{:S(2)}, u32[]{:S(2)}) %collective-permute-start.15) | collective-permute-done | bytes 65568 | tf_op jit(solution)/shard_map/ppermute | solution.py:836
  49.8 0.7 %collective-permute-start.16 = (bf16[1,4,4,16,128]{4,3,2,1,0:T(8,128)(2,1)S(1)}, bf16[1,4,4,16,128]{4,3,2,1,0:T(8,128)(2,1)S(1)}, u32[]{:S(2)}, u32[]{:S(2)}) collective-permute-start(bf16[1,4,4,16,128]{4,3,2,1,0:T(8,128)(2,1)S(1)} %bitcast.15), channel_id=1, source_target_pairs={{0,1},{1,0},{2,3},{3,2},{4,5},{5,4},{6,7},{7,6},{8,9},{9,8},{10,11... | collective-permute-start | bytes 196616 | tf_op jit(solution)/shard_map/ppermute | solution.py:840
  50.4 2.0 %collective-permute-done.17.refs_0_.refs_1_ = bf16[4,4,16,128]{3,2,1,0:T(8,128)(2,1)S(1)} collective-permute-done((bf16[4,4,16,128]{3,2,1,0:T(8,128)(2,1)S(1)}, bf16[4,4,16,128]{3,2,1,0:T(8,128)(2,1)S(1)}, u32[]{:S(2)}, u32[]{:S(2)}) %collective-permute-start.17) | collective-permute-done | bytes 65568 | tf_op jit(solution)/shard_map/ppermute | solution.py:836
  52.5 0.5 collective-permute-start.19
  53.0 2.6 %shard_map.94.refs_5_ = bf16[2,16,64,128]{3,2,1,0:T(8,128)(2,1)S(1)} custom-call(s32[1]{0:T(128)} %bitcast.me_ref, bf16[4,16,64,128]{3,2,1,0:T(8,128)(2,1)S(1)} %copy-done.3, bf16[16,64,128]{2,1,0:T(8,128)(2,1)S(1)} %bitcast.13, bf16[16,64,128]{2,1,0:T(8,128)(2,1)S(1)} %bitcast.11, bf16[6,64,128]{2,1,0:T(8,128)(2,1)S(1)} %collective-permute-done.10.refs_3_.refs_4_, ...), custom_call_target="tpu_custom_call" | custom-call | flops 2717908992 | bytes 1310720 | tf_op jit(solution)/shard_map/pallas_call | solution.py:535
  55.6 1.0 %shard_map.95.refs_3_ = f32[4,16,64,128]{3,2,1,0:T(8,128)S(1)} custom-call(s32[1]{0:T(128)} %bitcast.me_ref, bf16[4,1024,256]{2,1,0:T(8,128)(2,1)S(1)} %copy-done, bf16[4,4,16,128]{3,2,1,0:T(8,128)(2,1)S(1)} %collective-permute-done.15.refs_0_, bf16[4,4,16,128]{3,2,1,0:T(8,128)(2,1)S(1)} %collective-permute-done.17.refs_0_.refs_1_, ...), custom_call_target="tpu_custom_call" | custom-call | flops 268435456 | bytes 3145728 | tf_op jit(solution)/shard_map/pallas_call | solution.py:661
  56.6 1.3 %collective-permute-done.19.refs_2_ = bf16[2,4,4,16,128]{4,3,2,1,0:T(8,128)(2,1)S(1)} collective-permute-done((bf16[2,4,4,16,128]{4,3,2,1,0:T(8,128)(2,1)S(1)}, bf16[2,4,4,16,128]{4,3,2,1,0:T(8,128)(2,1)S(1)}, u32[]{:S(2)}, u32[]{:S(2)}) %collective-permute-start.19) | collective-permute-done | bytes 131104 | tf_op jit(solution)/shard_map/ppermute | solution.py:840
  57.9 2.5 %shard_map.96 = bf16[4,16,64,128]{3,2,1,0:T(8,128)(2,1)} custom-call(s32[1]{0:T(128)} %bitcast.me_ref, bf16[4,1024,256]{2,1,0:T(8,128)(2,1)S(1)} %copy-done, bf16[1,4,4,16,128]{4,3,2,1,0:T(8,128)(2,1)S(1)} %collective-permute-done.14.refs_0_, bf16[1,4,4,16,128]{4,3,2,1,0:T(8,128)(2,1)S(1)} %collective-permute-done.16.refs_1_, ...), custom_call_target="tpu_custom_call" | custom-call | flops 268435456 | bytes 3145728 | tf_op jit(solution)/shard_map/pallas_call | solution.py:681
  (23 shorter events, 0.1 us)
Async XLA Ops:
  3.2 10.4 %collective-permute-start.2 = (bf16[2,4,4,16,128]{4,3,2,1,0:T(8,128)(2,1)}, bf16[2,4,4,16,128]{4,3,2,1,0:T(8,128)(2,1)S(1)}, u32[]{:S(2)}, u32[]{:S(2)}) collective-permute-start(bf16[2,4,4,16,128]{4,3,2,1,0:T(8,128)(2,1)} %get-tuple-element.75), channel_id=1, source_target_pairs={{0,1},{1,0},{2,3},{3,2},{4,5},{5,4},{6,7},{7,6},{8,9},{9,8},{10,11... | collective-permute-start | bytes 393224 | tf_op jit(solution)/shard_map/ppermute | solution.py:840
  6.2 11.4 %collective-permute-start = (bf16[2,4,4,16,128]{4,3,2,1,0:T(8,128)(2,1)}, bf16[2,4,4,16,128]{4,3,2,1,0:T(8,128)(2,1)S(1)}, u32[]{:S(2)}, u32[]{:S(2)}) collective-permute-start(bf16[2,4,4,16,128]{4,3,2,1,0:T(8,128)(2,1)} %get-tuple-element.71), channel_id=1, source_target_pairs={{0,1},{1,0},{2,3},{3,2},{4,5},{5,4},{6,7},{7,6},{8,9},{9,8},{10,11... | collective-permute-start | bytes 393224 | tf_op jit(solution)/shard_map/ppermute | solution.py:840
  6.3 22.1 %collective-permute-start.8 = (bf16[1024,128]{1,0:T(8,128)(2,1)}, bf16[1024,128]{1,0:T(8,128)(2,1)S(1)}, u32[]{:S(2)}, u32[]{:S(2)}) collective-permute-start(bf16[1024,128]{1,0:T(8,128)(2,1)} %get-tuple-element.94), channel_id=1, source_target_pairs={{2,4},{6,8},{10,12},{14,16},{18,20},{22,24},{26,28},{4,2},{8,6},{1... | collective-permute-start | bytes 786440 | tf_op jit(solution)/shard_map/ppermute | solution.py:825
  6.9 21.5 %collective-permute-start.9 = (bf16[1024,128]{1,0:T(8,128)(2,1)}, bf16[1024,128]{1,0:T(8,128)(2,1)S(1)}, u32[]{:S(2)}, u32[]{:S(2)}) collective-permute-start(bf16[1024,128]{1,0:T(8,128)(2,1)} %get-tuple-element.95), channel_id=1, source_target_pairs={{0,2},{4,6},{8,10},{12,14},{16,18},{20,22},{24,26},{28,30},{2,0},{... | collective-permute-start | bytes 786440 | tf_op jit(solution)/shard_map/ppermute | solution.py:825
  10.3 1.6 %copy-start.1 = (bf16[2,512,1024]{2,1,0:T(8,128)(2,1)S(1)}, bf16[2,512,1024]{2,1,0:T(8,128)(2,1)}, u32[]{:S(2)}) copy-start(bf16[2,512,1024]{2,1,0:T(8,128)(2,1)} %constant.18.clone.table_ref) | copy-start | bytes 6291460
  11.9 1.2 %copy-start.2 = (bf16[4,16,64,128]{3,2,1,0:T(8,128)(2,1)S(1)}, bf16[4,16,64,128]{3,2,1,0:T(8,128)(2,1)}, u32[]{:S(2)}) copy-start(bf16[4,16,64,128]{3,2,1,0:T(8,128)(2,1)} %refs_0_.3) | copy-start | bytes 3145732
  13.6 7.8 %collective-permute-start.3 = (bf16[4,4,16,128]{3,2,1,0:T(8,128)(2,1)S(1)}, bf16[4,4,16,128]{3,2,1,0:T(8,128)(2,1)S(1)}, u32[]{:S(2)}, u32[]{:S(2)}) collective-permute-start(bf16[4,4,16,128]{3,2,1,0:T(8,128)(2,1)S(1)} %get-tuple-element.76), channel_id=1, source_target_pairs={{0,16},{2,18},{4,20},{6,22},{8,24},{10,26},{12,28},{14,30},{16,0},... | collective-permute-start | bytes 196616 | tf_op jit(solution)/shard_map/ppermute | solution.py:836
  16.2 6.4 %collective-permute-start.4 = (bf16[4,4,16,128]{3,2,1,0:T(8,128)(2,1)S(1)}, bf16[4,4,16,128]{3,2,1,0:T(8,128)(2,1)S(1)}, u32[]{:S(2)}, u32[]{:S(2)}) collective-permute-start(bf16[4,4,16,128]{3,2,1,0:T(8,128)(2,1)S(1)} %get-tuple-element.77), channel_id=1, source_target_pairs={{0,24},{2,26},{4,28},{6,30},{8,16},{10,18},{12,20},{14,22},{16,8},... | collective-permute-start | bytes 196616 | tf_op jit(solution)/shard_map/ppermute | solution.py:836
  17.6 5.3 %collective-permute-start.1 = (bf16[4,4,16,128]{3,2,1,0:T(8,128)(2,1)S(1)}, bf16[4,4,16,128]{3,2,1,0:T(8,128)(2,1)S(1)}, u32[]{:S(2)}, u32[]{:S(2)}) collective-permute-start(bf16[4,4,16,128]{3,2,1,0:T(8,128)(2,1)S(1)} %get-tuple-element.73), channel_id=1, source_target_pairs={{0,8},{2,10},{4,12},{6,14},{8,0},{10,2},{12,4},{14,6},{16,24},{18,... | collective-permute-start | bytes 196616 | tf_op jit(solution)/shard_map/ppermute | solution.py:836
  23.0 7.5 %copy-start.4 = (bf16[256,128]{1,0:T(8,128)(2,1)S(1)}, bf16[256,128]{1,0:T(8,128)(2,1)}, u32[]{:S(2)}) copy-start(bf16[256,128]{1,0:T(8,128)(2,1)} %constant.19.clone.refs_4_) | copy-start | bytes 196612
  23.0 7.5 %copy-start.5 = (bf16[128,128]{1,0:T(8,128)(2,1)S(1)}, bf16[128,128]{1,0:T(8,128)(2,1)}, u32[]{:S(2)}) copy-start(bf16[128,128]{1,0:T(8,128)(2,1)} %constant.20.clone.refs_5_) | copy-start | bytes 98308
  23.0 5.4 %collective-permute-start.5 = (bf16[4,4,16,128]{3,2,1,0:T(8,128)(2,1)S(1)}, bf16[4,4,16,128]{3,2,1,0:T(8,128)(2,1)S(1)}, u32[]{:S(2)}, u32[]{:S(2)}) collective-permute-start(bf16[4,4,16,128]{3,2,1,0:T(8,128)(2,1)S(1)} %get-tuple-element.88), channel_id=1, source_target_pairs={{0,6},{2,4},{4,2},{6,0},{8,14},{10,12},{12,10},{14,8},{16,22},{18,... | collective-permute-start | bytes 196616 | tf_op jit(solution)/shard_map/ppermute | solution.py:836
  23.3 5.6 %collective-permute-start.6 = (bf16[4,4,16,128]{3,2,1,0:T(8,128)(2,1)S(1)}, bf16[4,4,16,128]{3,2,1,0:T(8,128)(2,1)S(1)}, u32[]{:S(2)}, u32[]{:S(2)}) collective-permute-start(bf16[4,4,16,128]{3,2,1,0:T(8,128)(2,1)S(1)} %get-tuple-element.89), channel_id=1, source_target_pairs={{0,4},{2,6},{4,0},{6,2},{8,12},{10,14},{12,8},{14,10},{16,20},{18,... | collective-permute-start | bytes 196616 | tf_op jit(solution)/shard_map/ppermute | solution.py:836
  24.7 4.1 %collective-permute-start.7 = (bf16[4,4,16,128]{3,2,1,0:T(8,128)(2,1)S(1)}, bf16[4,4,16,128]{3,2,1,0:T(8,128)(2,1)S(1)}, u32[]{:S(2)}, u32[]{:S(2)}) collective-permute-start(bf16[4,4,16,128]{3,2,1,0:T(8,128)(2,1)S(1)} %get-tuple-element.90), channel_id=1, source_target_pairs={{0,2},{2,0},{4,6},{6,4},{8,10},{10,8},{12,14},{14,12},{16,18},{18,... | collective-permute-start | bytes 196616 | tf_op jit(solution)/shard_map/ppermute | solution.py:836
  28.9 10.6 %copy-start.3 = (bf16[4,16,64,128]{3,2,1,0:T(8,128)(2,1)S(1)}, bf16[4,16,64,128]{3,2,1,0:T(8,128)(2,1)}, u32[]{:S(2)}) copy-start(bf16[4,16,64,128]{3,2,1,0:T(8,128)(2,1)} %refs_0_.3) | copy-start | bytes 3145732
  28.9 10.5 %copy-start.7 = (bf16[3,3,3,128,128]{4,3,2,1,0:T(8,128)(2,1)S(1)}, bf16[3,3,3,128,128]{4,3,2,1,0:T(8,128)(2,1)}, u32[]{:S(2)}) copy-start(bf16[3,3,3,128,128]{4,3,2,1,0:T(8,128)(2,1)} %refs_5_.4) | copy-start | bytes 2654212
  28.9 8.6 %collective-permute-start.10 = (bf16[6,64,128]{2,1,0:T(8,128)(2,1)S(1)}, bf16[6,64,128]{2,1,0:T(8,128)(2,1)S(1)}, u32[]{:S(2)}, u32[]{:S(2)}) collective-permute-start(bf16[6,64,128]{2,1,0:T(8,128)(2,1)S(1)} %shard_map.90), channel_id=1, source_target_pairs={{0,1},{1,0},{2,3},{3,2},{4,5},{5,4},{6,7},{7,6},{8,9},{9,8},{10,11... | collective-permute-start | bytes 294920 | tf_op jit(solution)/shard_map/ppermute | solution.py:840
  37.5 4.6 %collective-permute-start.11 = (bf16[4,4,16,128]{3,2,1,0:T(8,128)(2,1)S(1)}, bf16[4,4,16,128]{3,2,1,0:T(8,128)(2,1)S(1)}, u32[]{:S(2)}, u32[]{:S(2)}) collective-permute-start(bf16[4,4,16,128]{3,2,1,0:T(8,128)(2,1)S(1)} %get-tuple-element.110), channel_id=1, source_target_pairs={{0,6},{2,4},{4,2},{6,0},{8,14},{10,12},{12,10},{14,8},{16,22},{18,... | collective-permute-start | bytes 196616 | tf_op jit(solution)/shard_map/ppermute | solution.py:836
  38.1 5.2 %collective-permute-start.12 = (bf16[4,4,16,128]{3,2,1,0:T(8,128)(2,1)S(1)}, bf16[4,4,16,128]{3,2,1,0:T(8,128)(2,1)S(1)}, u32[]{:S(2)}, u32[]{:S(2)}) collective-permute-start(bf16[4,4,16,128]{3,2,1,0:T(8,128)(2,1)S(1)} %get-tuple-element.111), channel_id=1, source_target_pairs={{0,4},{2,6},{4,0},{6,2},{8,12},{10,14},{12,8},{14,10},{16,20},{18,... | collective-permute-start | bytes 196616 | tf_op jit(solution)/shard_map/ppermute | solution.py:836
  39.0 4.3 %collective-permute-start.13 = (bf16[4,4,16,128]{3,2,1,0:T(8,128)(2,1)S(1)}, bf16[4,4,16,128]{3,2,1,0:T(8,128)(2,1)S(1)}, u32[]{:S(2)}, u32[]{:S(2)}) collective-permute-start(bf16[4,4,16,128]{3,2,1,0:T(8,128)(2,1)S(1)} %get-tuple-element.112), channel_id=1, source_target_pairs={{0,2},{2,0},{4,6},{6,4},{8,10},{10,8},{12,14},{14,12},{16,18},{18,... | collective-permute-start | bytes 196616 | tf_op jit(solution)/shard_map/ppermute | solution.py:836
  39.4 16.2 %copy-start = (bf16[4,1024,256]{2,1,0:T(8,128)(2,1)S(1)}, bf16[4,1024,256]{2,1,0:T(8,128)(2,1)}, u32[]{:S(2)}) copy-start(bf16[4,1024,256]{2,1,0:T(8,128)(2,1)} %constant.21.clone.table_ref) | copy-start | bytes 6291460
  39.4 16.2 %copy-start.6 = (f32[128]{0:T(128)S(1)}, f32[128]{0:T(128)}, u32[]{:S(2)}) copy-start(f32[128]{0:T(128)} %param.11) | copy-start | bytes 1540
  43.3 6.5 %collective-permute-start.15 = (bf16[4,4,16,128]{3,2,1,0:T(8,128)(2,1)S(1)}, bf16[4,4,16,128]{3,2,1,0:T(8,128)(2,1)S(1)}, u32[]{:S(2)}, u32[]{:S(2)}) collective-permute-start(bf16[4,4,16,128]{3,2,1,0:T(8,128)(2,1)S(1)} %get-tuple-element.121), channel_id=1, source_target_pairs={{0,24},{2,26},{4,28},{6,30},{8,16},{10,18},{12,20},{14,22},{16,8},... | collective-permute-start | bytes 196616 | tf_op jit(solution)/shard_map/ppermute | solution.py:836
  46.0 6.4 %collective-permute-start.17 = (bf16[4,4,16,128]{3,2,1,0:T(8,128)(2,1)S(1)}, bf16[4,4,16,128]{3,2,1,0:T(8,128)(2,1)S(1)}, u32[]{:S(2)}, u32[]{:S(2)}) collective-permute-start(bf16[4,4,16,128]{3,2,1,0:T(8,128)(2,1)S(1)} %get-tuple-element.122), channel_id=1, source_target_pairs={{0,16},{2,18},{4,20},{6,22},{8,24},{10,26},{12,28},{14,30},{16,0},... | collective-permute-start | bytes 196616 | tf_op jit(solution)/shard_map/ppermute | solution.py:836
  46.0 6.4 %collective-permute-start.18 = (bf16[4,4,16,128]{3,2,1,0:T(8,128)(2,1)S(1)}, bf16[4,4,16,128]{3,2,1,0:T(8,128)(2,1)S(1)}, u32[]{:S(2)}, u32[]{:S(2)}) collective-permute-start(bf16[4,4,16,128]{3,2,1,0:T(8,128)(2,1)S(1)} %get-tuple-element.123), channel_id=1, source_target_pairs={{0,8},{2,10},{4,12},{6,14},{8,0},{10,2},{12,4},{14,6},{16,24},{18,... | collective-permute-start | bytes 196616 | tf_op jit(solution)/shard_map/ppermute | solution.py:836
  47.7 8.9 %collective-permute-start.14 = (bf16[1,4,4,16,128]{4,3,2,1,0:T(8,128)(2,1)S(1)}, bf16[1,4,4,16,128]{4,3,2,1,0:T(8,128)(2,1)S(1)}, u32[]{:S(2)}, u32[]{:S(2)}) collective-permute-start(bf16[1,4,4,16,128]{4,3,2,1,0:T(8,128)(2,1)S(1)} %bitcast.14), channel_id=1, source_target_pairs={{0,1},{1,0},{2,3},{3,2},{4,5},{5,4},{6,7},{7,6},{8,9},{9,8},{10,11... | collective-permute-start | bytes 196616 | tf_op jit(solution)/shard_map/ppermute | solution.py:840
  49.8 6.8 %collective-permute-start.16 = (bf16[1,4,4,16,128]{4,3,2,1,0:T(8,128)(2,1)S(1)}, bf16[1,4,4,16,128]{4,3,2,1,0:T(8,128)(2,1)S(1)}, u32[]{:S(2)}, u32[]{:S(2)}) collective-permute-start(bf16[1,4,4,16,128]{4,3,2,1,0:T(8,128)(2,1)S(1)} %bitcast.15), channel_id=1, source_target_pairs={{0,1},{1,0},{2,3},{3,2},{4,5},{5,4},{6,7},{7,6},{8,9},{9,8},{10,11... | collective-permute-start | bytes 196616 | tf_op jit(solution)/shard_map/ppermute | solution.py:840
  52.5 5.5 %collective-permute-start.19 = (bf16[2,4,4,16,128]{4,3,2,1,0:T(8,128)(2,1)S(1)}, bf16[2,4,4,16,128]{4,3,2,1,0:T(8,128)(2,1)S(1)}, u32[]{:S(2)}, u32[]{:S(2)}) collective-permute-start(bf16[2,4,4,16,128]{4,3,2,1,0:T(8,128)(2,1)S(1)} %shard_map.93), channel_id=1, source_target_pairs={{0,1},{1,0},{2,3},{3,2},{4,5},{5,4},{6,7},{7,6},{8,9},{9,8},{10,11... | collective-permute-start | bytes 393224 | tf_op jit(solution)/shard_map/ppermute | solution.py:840

commit v11 on v9

--- a/solution.py
+++ b/solution.py
@@ -135,7 +135,6 @@
 
 def send_kernel(shards, shards_y, pieces, step, me_ref, table_ref, flow_ref, *refs):
     *refs, table, flow, table_sems, flow_sems = refs
-    refs, plane_refs = refs[: len(pieces)], refs[len(pieces) :]
     cells_x = flow.shape[0]
     outer, _ = shards
     block = refs[0].shape[1] * refs[0].shape[3]
@@ -162,10 +161,6 @@
         return flow[x]
 
     transform(table[...], flow_at, cells_x, refs, pieces)
-    if plane_refs:
-        even = is_even(me_ref[0], shards)
-        plane_refs[0][...] = flow[jnp.where(even, cells_x - 1, 0)]
-        plane_refs[1][...] = flow[jnp.where(even, 0, cells_x - 1)]
 
 
 def is_even(me, shards):
@@ -174,7 +169,7 @@
 
 
 def keep_kernel(shards, shards_y, pieces, me_ref, table_ref, flow_ref, *refs):
-    refs, (low, high) = refs[: len(pieces)], refs[len(pieces) :]
+    refs, (first, last, *edges) = refs[: len(pieces)], refs[len(pieces) :]
     cells_x, positions, _ = flow_ref.shape
     outer, _ = shards
     block = refs[0].shape[1] * refs[0].shape[3]
@@ -186,9 +181,22 @@
     transform(
         jnp.concatenate(tables, axis=0), lambda x: flow_ref[x], cells_x, refs, pieces
     )
-    cells_z = low.shape[1]
-    low[...] = flow_ref[:, pl.ds(0, cells_z)]
-    high[...] = flow_ref[:, pl.ds(positions - cells_z, cells_z)]
+    first[...] = flow_ref[0]
+    last[...] = flow_ref[cells_x - 1]
+    cells_z = edges[0].shape[1]
+    low, high = pl.ds(0, cells_z), pl.ds(positions - cells_z, cells_z)
+    if len(edges) > 1:
+        edges[0][...] = flow_ref[:, low]
+        edges[1][...] = flow_ref[:, high]
+    else:
+
+        @pl.when(own_y > 0)
+        def _():
+            edges[0][...] = flow_ref[:, low]
+
+        @pl.when(own_y == 0)
+        def _():
+            edges[0][...] = flow_ref[:, high]
 
 
 def forward_yz(me, table, flow, step, shards, shards_y, pieces, cells_z=0):
@@ -198,8 +206,6 @@
     unit = (inner, cells_x, rows // (outer * inner), channels)
     dtype = jnp.bfloat16 if step else jnp.float32
     shapes = [jax.ShapeDtypeStruct((len(piece), *unit), dtype) for piece in pieces]
-    if step == 1:
-        shapes += [jax.ShapeDtypeStruct((positions, channels), flow.dtype)] * 2
     if step:
         kernel = functools.partial(send_kernel, shards, shards_y, pieces, step)
         specs = [pl.BlockSpec(memory_space=pltpu.HBM)] * 2
@@ -212,8 +218,9 @@
     else:
         kernel = functools.partial(keep_kernel, shards, shards_y, pieces)
         specs, scratch = in_vmem(2), []
+        shapes += [jax.ShapeDtypeStruct((positions, channels), flow.dtype)] * 2
         edge = jax.ShapeDtypeStruct((cells_x, cells_z, channels), flow.dtype)
-        shapes += [edge] * 2
+        shapes += [edge] * (1 if shards_y == 2 else 2)
     return pl.pallas_call(
         kernel,
         in_specs=[IN_SMEM] + specs,
@@ -274,37 +281,41 @@
     )(me, *arrays)
 
 
-def edge_kernel(
-    choose, shards, me_ref, paired_ref, other_ref, low_ref, high_ref, out_ref
-):
-    cells_x, cells_z, _ = low_ref.shape
-    rows = paired_ref.shape[0]
+def halo_kernel(shards, shards_y, me_ref, first_ref, last_ref, front_ref, back_ref, *out_refs):
     own_y, _, _ = place(me_ref[0], shards)
-    is_low = choose(own_y)
     even = is_even(me_ref[0], shards)
-    start = pl.multiple_of(jnp.where(is_low, 0, rows - cells_z), cells_z)
-    paired, other = (ref[pl.ds(start, cells_z), :] for ref in (paired_ref, other_ref))
-    out_ref[0] = jnp.where(even, other, paired)
-    out_ref[1 + cells_x] = jnp.where(even, paired, other)
-
-    @pl.when(is_low)
+    cells_x, cells_z, _ = front_ref.shape
+    cells_y = first_ref.shape[0] // cells_z
+
+    def fill(out_ref, x, plane_ref):
+        for y in range(cells_y):
+            out_ref[y + 1] = plane_ref[pl.ds(y * cells_z, cells_z), :]
+        row = front_ref[x]
+        out_ref[0] = jnp.where(own_y > 0, row, jnp.zeros_like(row))
+        row = back_ref[x]
+        out_ref[cells_y + 1] = jnp.where(own_y < shards_y - 1, row, jnp.zeros_like(row))
+
+    @pl.when(even)
     def _():
-        out_ref[1 : 1 + cells_x] = low_ref[...]
-
-    @pl.when(jnp.logical_not(is_low))
+        fill(out_refs[0], cells_x - 1, last_ref)
+        fill(out_refs[1], 0, first_ref)
+
+    @pl.when(jnp.logical_not(even))
     def _():
-        out_ref[1 : 1 + cells_x] = high_ref[...]
-
-
-def y_edge(me, paired, other, low, high, shards, choose):
-    cells_x, cells_z, channels = low.shape
+        fill(out_refs[0], 0, first_ref)
+        fill(out_refs[1], cells_x - 1, last_ref)
+
+
+def halo_planes(me, first, last, front, back, shards, shards_y):
+    cells_x, cells_z, channels = front.shape
+    shape = (first.shape[0] // cells_z + 2, cells_z, channels)
     return pl.pallas_call(
-        functools.partial(edge_kernel, choose, shards),
+        functools.partial(halo_kernel, shards, shards_y),
         in_specs=[IN_SMEM] + in_vmem(4),
-        out_specs=in_vmem(1)[0],
-        out_shape=jax.ShapeDtypeStruct((cells_x + 2, cells_z, channels), low.dtype),
+        out_specs=in_vmem(2),
+        out_shape=[jax.ShapeDtypeStruct(shape, first.dtype)] * 2,
         compiler_params=pltpu.CompilerParams(vmem_limit_bytes=10 << 20),
-    )(me, paired, other, low, high)
+    )(me, first, last, front, back)
 
 
 def preload_kernel(first, weight_ref, out_ref, sems):
@@ -333,7 +344,7 @@
         out_specs=in_vmem(1)[0],
         out_shape=jax.ShapeDtypeStruct(shape, weight.dtype),
         scratch_shapes=[pltpu.SemaphoreType.DMA((2 * 2 * count,))],
-        compiler_params=pltpu.CompilerParams(vmem_limit_bytes=36 << 20),
+        compiler_params=pltpu.CompilerParams(vmem_limit_bytes=34 << 20),
         cost_estimate=pl.CostEstimate(
             flops=0, bytes_accessed=2 * math.prod(shape), transcendentals=0
         ),
@@ -475,25 +486,25 @@
     even = is_even(me_ref[0], shards)
     for plane in range(width + 2):
         p = x + plane - 1
-        row = front_ref[p + 1]
-        padded[plane, 0] = jnp.where(own_y > 0, row, jnp.zeros_like(row))
-        row = back_ref[p + 1]
-        last = own_y == shards_y - 1
-        padded[plane, cells_y + 1] = jnp.where(last, jnp.zeros_like(row), row)
         if 0 <= p < cells_x:
             padded[plane, 1 : cells_y + 1] = flow_ref[p]
+            row = front_ref[p]
+            padded[plane, 0] = jnp.where(own_y > 0, row, jnp.zeros_like(row))
+            row = back_ref[p]
+            last = own_y == shards_y - 1
+            padded[plane, cells_y + 1] = jnp.where(last, jnp.zeros_like(row), row)
         else:
             use_paired = jnp.logical_not(even) if p < 0 else even
 
             @pl.when(use_paired)
             def _(plane=plane):
-                padded[plane, 1 : cells_y + 1] = paired_ref[...]
+                padded[plane] = paired_ref[...]
 
             @pl.when(jnp.logical_not(use_paired))
             def _(plane=plane):
-                padded[plane, 1 : cells_y + 1] = other_ref[...]
-
-    rows = 4 if cells_y % 4 == 0 else 1
+                padded[plane] = other_ref[...]
+
+    rows = 8 if cells_y % 8 == 0 else 1
     columns = [(k, d) for k in range(width) for d in range(3)]
     columns = [columns[i : i + 2] for i in range(0, len(columns), 2)]
     none = jnp.zeros((channels, channels), kernel_ref.dtype)
@@ -548,9 +559,7 @@
 
 
 def bundled_slots(count):
-    slots = [0] + far_first(count)[:-1]
-    cut = (count + 1) // 2
-    return [part for part in (slots[:cut], slots[cut:]) if part]
+    return [[0] + far_first(count)[:-1]]
 
 
 def bundle_kernel(*refs):
@@ -872,20 +881,21 @@
         sent, columns, weight = barrier((sent, columns, weight))
         for into, piece in zip(arrived, sent):
             into.append(over_y(piece, step, shards_y))
-        if step == 1:
-            ends = sent[len(pieces) :]
-            planes = [with_neighbour(end, start, "gx") for start, end in enumerate(ends)]
-    loaded = [preload(weight, 0, early // 2)] if early > 1 else []
+    loaded = [preload(weight, 0, early)] if early else []
     loaded, columns = barrier((loaded, columns))
     kept = forward_yz(me, table, columns, 0, shards, shards_y, pieces, cells_z)
-    kept, (low, high) = kept[: len(pieces)], kept[len(pieces) :]
+    kept, (first, last, *ends) = kept[: len(pieces)], kept[len(pieces) :]
+    if shards_y == 2:
+        front = back = over_y(ends[0], 1, shards_y)
+    else:
+        front, back = neighbours(*ends, "gy")
 
     by_outer = []
     for piece, own, parts in zip(pieces, kept, arrived):
         for step, total in zip(piece, add_pieces(own, parts)):
             by_outer.append(exchange(total, step, shards, True) if step else total)
     if early:
-        loaded.append(preload(weight, early // 2, early))
+        loaded.append(preload(weight, early, early))
     by_outer, loaded, weight = barrier((by_outer[::-1], loaded, weight))
     by_inner = regroup(me, by_outer[::-1], shards, True)
     by_inner, weight = barrier((by_inner, weight))
@@ -894,18 +904,11 @@
         for step in far_first(inner)
     ]
     if early:
-        loaded.append(preload(weight, early + early // 2, early))
-
-    rows, loaded, planes = barrier((rows, loaded, planes))
-    if shards_y == 2:
-        edge = y_edge(me, *planes, low, high, shards, lambda own: own > 0)
-        front = back = over_y(edge, 1, shards_y)
-    else:
-        ends = [
-            y_edge(me, *planes, low, high, shards, lambda own, limit=limit: own < limit)
-            for limit in (shards_y, 0)
-        ]
-        front, back = neighbours(*ends, "gy")
+        loaded.append(preload(weight, 2 * early, early))
+
+    rows, loaded, first, last, front, back = barrier((rows, loaded, first, last, front, back))
+    paired, other = halo_planes(me, first, last, front, back, shards, shards_y)
+    paired, other = with_neighbour(paired, 0, "gx"), with_neighbour(other, 1, "gx")
     returned = mixing(
         me,
         rows,
@@ -915,9 +918,8 @@
         loaded,
         shards,
     )
-    returned, front, back = barrier((list(returned), front, back))
-    planes = [plane.reshape(cells_y, cells_z, channels) for plane in planes]
-    halos = (*planes, front, back)
+    returned, paired, other = barrier((list(returned), paired, other))
+    halos = (paired, other, front, back)
     width = 2 if cells_x % 2 == 0 else 1
     convolved = [
         convolution(me, x, width, flow, halos, conv_weight, shards, shards_y)
@@ -934,7 +936,6 @@
         exchange(returned[step], step, shards, True) if step else returned[0]
         for step in far_first(outer)
     ]
-    returned[0], convolved[-1] = barrier((returned[0], convolved[-1]))
     by_slot = dict(zip(far_first(outer), returned))
     bundles = [bundle([by_slot[slot] for slot in slots]) for slots in bundled_slots(outer)]
     others = []

time: 59.6 us -> 63.7 us (1.069)
  starting transfers between devices: 21.2 us -> 23 us
  waiting for transfers between devices: 9.67 us -> 11.3 us
    ppermute x12, waiting for transfers between devices: 3.92 us -> 6.87 us  [exchange(): return lax.ppermute(array, 'gx', pairs)]
    ppermute x12, starting transfers between devices: 14.7 us -> 16.8 us  [exchange(): return lax.ppermute(array, 'gx', pairs)]
    ppermute x5 -> x4, waiting for transfers between devices: 5.74 us -> 4.46 us  [over_y(): lax.ppermute(array, 'gy', [(i, (i + step) % shards_y) for i in range(shar...]
    pallas_call x3, Pallas kernels: 9.15 us -> 10.4 us  [preload(): pl.pallas_call(functools.partial(preload_kernel, 2 * pair), in_specs=[pl....]
    pallas_call x2, Pallas kernels: 5.99 us -> 5.26 us  [convolution(): pl.pallas_call(functools.partial(convolution_kernel, x, cells_x, width, s...]
    ppermute x5 -> x4, starting transfers between devices: 5.82 us -> 5.21 us  [over_y(): lax.ppermute(array, 'gy', [(i, (i + step) % shards_y) for i in range(shar...]
  transfers between devices with their start and end apart: 19 -> 18, of which waited for: 9 -> 6; matrix products, arithmetic and copies ran while one was open for 0% -> 0% of each run, Pallas kernels for 38% -> 37%
where the time goes in v11:
time: 63.7 us; the launch traced here: 63.5 us
  Pallas kernels  28.9 us (45%)
  starting transfers between devices  23 us (36%)
  waiting for transfers between devices  11.3 us (18%)
    ppermute x12, starting transfers between devices, exchange(): return lax.ppermute(array, 'gx', pairs)  16.8 us
    pallas_call x3, Pallas kernels, preload(): pl.pallas_call(functools.partial(preload_kernel, 2 * pair), in_specs=[pl....  10.4 us
    ppermute x12, waiting for transfers between devices, exchange(): return lax.ppermute(array, 'gx', pairs)  6.87 us
    pallas_call x1, Pallas kernels, mixing(): pl.pallas_call(functools.partial(mixing_kernel, shards, len(loaded)), in_...  6.1 us
    pallas_call x2, Pallas kernels, convolution(): pl.pallas_call(functools.partial(convolution_kernel, x, cells_x, width, s...  5.26 us
    ppermute x4, starting transfers between devices, over_y(): lax.ppermute(array, 'gy', [(i, (i + step) % shards_y) for i in range(shar...  5.21 us
    ppermute x4, waiting for transfers between devices, over_y(): lax.ppermute(array, 'gy', [(i, (i + step) % shards_y) for i in range(shar...  4.46 us
    pallas_call x2, Pallas kernels, forward_yz(): pl.pallas_call(kernel, in_specs=[IN_SMEM] + specs, out_specs=in_vmem(len(...  3.43 us
  transfers between devices with their start and end apart: 18, of which 6 were waited for; matrix products, arithmetic and copies ran while one was open for 0% of the time, Pallas kernels for 37%

profile of v11, /device:TPU:0, one launch (start us, length us, event | category | flops | bytes accessed | tf_op | source)
XLA Modules:
  0.0 63.5 jit_solution(15607114691971648610)
XLA Ops:
  0.0 3.0 %shard_map.82 = (bf16[2,4,4,16,128]{4,3,2,1,0:T(8,128)(2,1)}, bf16[2,4,4,16,128]{4,3,2,1,0:T(8,128)(2,1)}) custom-call(s32[1]{0:T(128)} %bitcast.me_ref, bf16[2,512,1024]{2,1,0:T(8,128)(2,1)} %constant.18.clone.table_ref, bf16[4,1024,128]{2,1,0:T(8,128)(2,1)} %bitcast.4), custom_call_target="tpu_custom_call" | custom-call | flops 268435456 | bytes 1572864 | tf_op jit(solution)/shard_map/pallas_call | solution.py:224
  3.0 0.0 copy-start.1
  3.0 0.0 copy-start.2
  3.0 3.0 %collective-permute-start.2 = (bf16[2,4,4,16,128]{4,3,2,1,0:T(8,128)(2,1)}, bf16[2,4,4,16,128]{4,3,2,1,0:T(8,128)(2,1)S(1)}, u32[]{:S(2)}, u32[]{:S(2)}) collective-permute-start(bf16[2,4,4,16,128]{4,3,2,1,0:T(8,128)(2,1)} %get-tuple-element.80), channel_id=1, source_target_pairs={{0,1},{1,0},{2,3},{3,2},{4,5},{5,4},{6,7},{7,6},{8,9},{9,8},{10,11... | collective-permute-start | bytes 393224 | tf_op jit(solution)/shard_map/ppermute | solution.py:850
  6.1 0.1 collective-permute-start
  6.1 3.5 %shard_map.83.refs_7_ = bf16[4,64,128,128]{3,2,1,0:T(8,128)(2,1)S(1)} custom-call(bf16[16,64,128,128]{3,2,1,0:T(8,128)(2,1)} %bitcast.7), custom_call_target="tpu_custom_call" | custom-call | bytes 8388608 | tf_op jit(solution)/shard_map/pallas_call | solution.py:341
  9.6 0.4 shard_map.84
  10.1 0.5 collective-permute-done.2.refs_1_
  10.6 3.2 %collective-permute-start.3 = (bf16[4,4,16,128]{3,2,1,0:T(8,128)(2,1)S(1)}, bf16[4,4,16,128]{3,2,1,0:T(8,128)(2,1)S(1)}, u32[]{:S(2)}, u32[]{:S(2)}) collective-permute-start(bf16[4,4,16,128]{3,2,1,0:T(8,128)(2,1)S(1)} %get-tuple-element.81), channel_id=1, source_target_pairs={{0,16},{2,18},{4,20},{6,22},{8,24},{10,26},{12,28},{14,30},{16,0},... | collective-permute-start | bytes 196616 | tf_op jit(solution)/shard_map/ppermute | solution.py:846
  13.8 1.4 %collective-permute-start.4 = (bf16[4,4,16,128]{3,2,1,0:T(8,128)(2,1)S(1)}, bf16[4,4,16,128]{3,2,1,0:T(8,128)(2,1)S(1)}, u32[]{:S(2)}, u32[]{:S(2)}) collective-permute-start(bf16[4,4,16,128]{3,2,1,0:T(8,128)(2,1)S(1)} %get-tuple-element.82), channel_id=1, source_target_pairs={{0,24},{2,26},{4,28},{6,30},{8,16},{10,18},{12,20},{14,22},{16,8},... | collective-permute-start | bytes 196616 | tf_op jit(solution)/shard_map/ppermute | solution.py:846
  15.2 0.0 collective-permute-done.refs_1_
  15.2 0.3 collective-permute-start.1
  15.5 1.5 %collective-permute-start.8 = (bf16[4,64,128]{2,1,0:T(8,128)(2,1)S(1)}, bf16[4,64,128]{2,1,0:T(8,128)(2,1)S(1)}, u32[]{:S(2)}, u32[]{:S(2)}) collective-permute-start(bf16[4,64,128]{2,1,0:T(8,128)(2,1)S(1)} %get-tuple-element.102), channel_id=1, source_target_pairs={{0,1},{1,0},{2,3},{3,2},{4,5},{5,4},{6,7},{7,6},{8,9},{9,8},{10,11... | collective-permute-start | bytes 196616 | tf_op jit(solution)/shard_map/ppermute | solution.py:850
  17.0 3.5 %shard_map.87.refs_8_ = bf16[4,64,128,128]{3,2,1,0:T(8,128)(2,1)S(1)} custom-call(bf16[16,64,128,128]{3,2,1,0:T(8,128)(2,1)} %bitcast.8), custom_call_target="tpu_custom_call" | custom-call | bytes 8388608 | tf_op jit(solution)/shard_map/pallas_call | solution.py:341
  20.5 0.0 collective-permute-done.3.refs_1_
  20.5 0.0 collective-permute-done.4.refs_0_
  20.5 0.0 collective-permute-done.1.refs_2_
  20.6 0.0 copy-start.3
  20.6 0.0 copy-start.4
  20.6 0.1 collective-permute-start.5
  20.7 1.6 %collective-permute-start.6 = (bf16[4,4,16,128]{3,2,1,0:T(8,128)(2,1)S(1)}, bf16[4,4,16,128]{3,2,1,0:T(8,128)(2,1)S(1)}, u32[]{:S(2)}, u32[]{:S(2)}) collective-permute-start(bf16[4,4,16,128]{3,2,1,0:T(8,128)(2,1)S(1)} %get-tuple-element.94), channel_id=1, source_target_pairs={{0,4},{2,6},{4,0},{6,2},{8,12},{10,14},{12,8},{14,10},{16,20},{18,... | collective-permute-start | bytes 196616 | tf_op jit(solution)/shard_map/ppermute | solution.py:846
  22.2 0.3 collective-permute-start.7
  22.5 3.5 %shard_map.89.refs_9_ = bf16[4,64,128,128]{3,2,1,0:T(8,128)(2,1)S(1)} custom-call(bf16[16,64,128,128]{3,2,1,0:T(8,128)(2,1)} %bitcast.9), custom_call_target="tpu_custom_call" | custom-call | bytes 8388608 | tf_op jit(solution)/shard_map/pallas_call | solution.py:341
  26.0 0.0 collective-permute-done.8.front_ref.back_ref.refs_3_.refs_4_
  26.0 0.4 collective-permute-done.6.refs_1_
  26.5 0.1 shard_map.91
  26.5 0.1 collective-permute-start.9
  26.6 0.8 %collective-permute-start.10 = (bf16[18,64,128]{2,1,0:T(8,128)(2,1)S(1)}, bf16[18,64,128]{2,1,0:T(8,128)(2,1)S(1)}, u32[]{:S(2)}, u32[]{:S(2)}) collective-permute-start(bf16[18,64,128]{2,1,0:T(8,128)(2,1)S(1)} %get-tuple-element.119), channel_id=1, source_target_pairs={{2,4},{6,8},{10,12},{14,16},{18,20},{22,24},{26,28},{4,2},{8,6},{1... | collective-permute-start | bytes 884744 | tf_op jit(solution)/shard_map/ppermute | solution.py:835
  27.5 6.1 %shard_map.90 = (bf16[4,4,16,128]{3,2,1,0:T(8,128)(2,1)S(1)}, bf16[4,4,16,128]{3,2,1,0:T(8,128)(2,1)S(1)}, bf16[4,4,16,128]{3,2,1,0:T(8,128)(2,1)S(1)}, bf16[4,4,16,128]{3,2,1,0:T(8,128)(2,1)S(1)}) custom-call(s32[1]{0:T(128)} %bitcast.me_ref, bf16[4,4,16,128]{3,2,1,0:T(8,128)(2,1)S(1)} %collective-permute-done.5.refs_0_, ...), custom_call_target="tpu_custom_call" | custom-call | flops 134217728 | bytes 33554432 | tf_op jit(solution)/shard_map/pallas_call | solution.py:460
  33.6 0.0 collective-permute-done.9.refs_1_
  33.6 0.0 copy-start
  33.6 0.0 copy-start.5
  33.6 4.3 %collective-permute-start.11 = (bf16[4,4,16,128]{3,2,1,0:T(8,128)(2,1)S(1)}, bf16[4,4,16,128]{3,2,1,0:T(8,128)(2,1)S(1)}, u32[]{:S(2)}, u32[]{:S(2)}) collective-permute-start(bf16[4,4,16,128]{3,2,1,0:T(8,128)(2,1)S(1)} %get-tuple-element.120), channel_id=1, source_target_pairs={{0,6},{2,4},{4,2},{6,0},{8,14},{10,12},{12,10},{14,8},{16,22},{18,... | collective-permute-start | bytes 196616 | tf_op jit(solution)/shard_map/ppermute | solution.py:846
  37.9 1.2 %collective-permute-start.12 = (bf16[4,4,16,128]{3,2,1,0:T(8,128)(2,1)S(1)}, bf16[4,4,16,128]{3,2,1,0:T(8,128)(2,1)S(1)}, u32[]{:S(2)}, u32[]{:S(2)}) collective-permute-start(bf16[4,4,16,128]{3,2,1,0:T(8,128)(2,1)S(1)} %get-tuple-element.121), channel_id=1, source_target_pairs={{0,4},{2,6},{4,0},{6,2},{8,12},{10,14},{12,8},{14,10},{16,20},{18,... | collective-permute-start | bytes 196616 | tf_op jit(solution)/shard_map/ppermute | solution.py:846
  39.1 0.1 collective-permute-start.13
  39.2 2.6 %shard_map.92.refs_4_ = bf16[2,16,64,128]{3,2,1,0:T(8,128)(2,1)S(1)} custom-call(s32[1]{0:T(128)} %bitcast.me_ref, bf16[4,16,64,128]{3,2,1,0:T(8,128)(2,1)S(1)} %copy-done.2, bf16[18,64,128]{2,1,0:T(8,128)(2,1)S(1)} %collective-permute-done.9.refs_1_, bf16[18,64,128]{2,1,0:T(8,128)(2,1)S(1)} %collective-permute-done.10.refs_2_, ...), custom_call_target="tpu_custom_call" | custom-call | flops 2717908992 | bytes 1310720 | tf_op jit(solution)/shard_map/pallas_call | solution.py:546
  41.8 0.8 %collective-permute-done.12.refs_1_ = bf16[4,4,16,128]{3,2,1,0:T(8,128)(2,1)S(1)} collective-permute-done((bf16[4,4,16,128]{3,2,1,0:T(8,128)(2,1)S(1)}, bf16[4,4,16,128]{3,2,1,0:T(8,128)(2,1)S(1)}, u32[]{:S(2)}, u32[]{:S(2)}) %collective-permute-start.12) | collective-permute-done | bytes 65568 | tf_op jit(solution)/shard_map/ppermute | solution.py:846
  42.6 3.6 %collective-permute-start.14 = (bf16[4,4,16,128]{3,2,1,0:T(8,128)(2,1)S(1)}, bf16[4,4,16,128]{3,2,1,0:T(8,128)(2,1)S(1)}, u32[]{:S(2)}, u32[]{:S(2)}) collective-permute-start(bf16[4,4,16,128]{3,2,1,0:T(8,128)(2,1)S(1)} %get-tuple-element.131), channel_id=1, source_target_pairs={{0,24},{2,26},{4,28},{6,30},{8,16},{10,18},{12,20},{14,22},{16,8},... | collective-permute-start | bytes 196616 | tf_op jit(solution)/shard_map/ppermute | solution.py:846
  46.2 0.8 %collective-permute-start.15 = (bf16[4,4,16,128]{3,2,1,0:T(8,128)(2,1)S(1)}, bf16[4,4,16,128]{3,2,1,0:T(8,128)(2,1)S(1)}, u32[]{:S(2)}, u32[]{:S(2)}) collective-permute-start(bf16[4,4,16,128]{3,2,1,0:T(8,128)(2,1)S(1)} %get-tuple-element.132), channel_id=1, source_target_pairs={{0,16},{2,18},{4,20},{6,22},{8,24},{10,26},{12,28},{14,30},{16,0},... | collective-permute-start | bytes 196616 | tf_op jit(solution)/shard_map/ppermute | solution.py:846
  47.0 0.1 collective-permute-start.16
  47.2 1.6 %collective-permute-done.14.refs_1_.refs_0_ = bf16[4,4,16,128]{3,2,1,0:T(8,128)(2,1)S(1)} collective-permute-done((bf16[4,4,16,128]{3,2,1,0:T(8,128)(2,1)S(1)}, bf16[4,4,16,128]{3,2,1,0:T(8,128)(2,1)S(1)}, u32[]{:S(2)}, u32[]{:S(2)}) %collective-permute-start.14) | collective-permute-done | bytes 65568 | tf_op jit(solution)/shard_map/ppermute | solution.py:846
  48.8 4.0 %collective-permute-done.15.refs_2_.refs_1_ = bf16[4,4,16,128]{3,2,1,0:T(8,128)(2,1)S(1)} collective-permute-done((bf16[4,4,16,128]{3,2,1,0:T(8,128)(2,1)S(1)}, bf16[4,4,16,128]{3,2,1,0:T(8,128)(2,1)S(1)}, u32[]{:S(2)}, u32[]{:S(2)}) %collective-permute-start.15) | collective-permute-done | bytes 65568 | tf_op jit(solution)/shard_map/ppermute | solution.py:846
  52.8 0.0 collective-permute-done.16.refs_3_.refs_2_
  52.8 0.6 collective-permute-start.17
  53.4 2.6 %shard_map.95.refs_5_ = bf16[2,16,64,128]{3,2,1,0:T(8,128)(2,1)S(1)} custom-call(s32[1]{0:T(128)} %bitcast.me_ref, bf16[4,16,64,128]{3,2,1,0:T(8,128)(2,1)S(1)} %copy-done.2, bf16[18,64,128]{2,1,0:T(8,128)(2,1)S(1)} %collective-permute-done.9.refs_1_, bf16[18,64,128]{2,1,0:T(8,128)(2,1)S(1)} %collective-permute-done.10.refs_2_, ...), custom_call_target="tpu_custom_call" | custom-call | flops 2717908992 | bytes 1310720 | tf_op jit(solution)/shard_map/pallas_call | solution.py:546
  56.1 1.0 %shard_map.96.refs_1_ = f32[4,16,64,128]{3,2,1,0:T(8,128)S(1)} custom-call(s32[1]{0:T(128)} %bitcast.me_ref, bf16[4,1024,256]{2,1,0:T(8,128)(2,1)S(1)} %copy-done, bf16[4,4,16,128]{3,2,1,0:T(8,128)(2,1)S(1)} %collective-permute-done.14.refs_1_.refs_0_, bf16[4,4,16,128]{3,2,1,0:T(8,128)(2,1)S(1)} %collective-permute-done.15.refs_2_.refs_1_, ...), custom_call_target="tpu_custom_call" | custom-call | flops 268435456 | bytes 3145728 | tf_op jit(solution)/shard_map/pallas_call | solution.py:671
  57.0 4.0 %collective-permute-done.17.refs_0_ = bf16[4,4,4,16,128]{4,3,2,1,0:T(8,128)(2,1)S(1)} collective-permute-done((bf16[4,4,4,16,128]{4,3,2,1,0:T(8,128)(2,1)S(1)}, bf16[4,4,4,16,128]{4,3,2,1,0:T(8,128)(2,1)S(1)}, u32[]{:S(2)}, u32[]{:S(2)}) %collective-permute-start.17) | collective-permute-done | bytes 262176 | tf_op jit(solution)/shard_map/ppermute | solution.py:850
  61.0 2.5 %shard_map.97 = bf16[4,16,64,128]{3,2,1,0:T(8,128)(2,1)} custom-call(s32[1]{0:T(128)} %bitcast.me_ref, bf16[4,1024,256]{2,1,0:T(8,128)(2,1)S(1)} %copy-done, bf16[4,4,4,16,128]{4,3,2,1,0:T(8,128)(2,1)S(1)} %collective-permute-done.17.refs_0_, f32[4,16,64,128]{3,2,1,0:T(8,128)S(1)} %shard_map.96.refs_1_), custom_call_target="tpu_custom_call" | custom-call | flops 268435456 | bytes 3145728 | tf_op jit(solution)/shard_map/pallas_call | solution.py:691
  (18 shorter events, 0.2 us)
Async XLA Ops:
  3.0 6.6 %copy-start.1 = (bf16[2,512,1024]{2,1,0:T(8,128)(2,1)S(1)}, bf16[2,512,1024]{2,1,0:T(8,128)(2,1)}, u32[]{:S(2)}) copy-start(bf16[2,512,1024]{2,1,0:T(8,128)(2,1)} %constant.18.clone.table_ref) | copy-start | bytes 6291460
  3.0 6.6 %copy-start.2 = (bf16[4,16,64,128]{3,2,1,0:T(8,128)(2,1)S(1)}, bf16[4,16,64,128]{3,2,1,0:T(8,128)(2,1)}, u32[]{:S(2)}) copy-start(bf16[4,16,64,128]{3,2,1,0:T(8,128)(2,1)} %refs_0_.3) | copy-start | bytes 3145732
  3.0 7.6 %collective-permute-start.2 = (bf16[2,4,4,16,128]{4,3,2,1,0:T(8,128)(2,1)}, bf16[2,4,4,16,128]{4,3,2,1,0:T(8,128)(2,1)S(1)}, u32[]{:S(2)}, u32[]{:S(2)}) collective-permute-start(bf16[2,4,4,16,128]{4,3,2,1,0:T(8,128)(2,1)} %get-tuple-element.80), channel_id=1, source_target_pairs={{0,1},{1,0},{2,3},{3,2},{4,5},{5,4},{6,7},{7,6},{8,9},{9,8},{10,11... | collective-permute-start | bytes 393224 | tf_op jit(solution)/shard_map/ppermute | solution.py:850
  6.1 9.1 %collective-permute-start = (bf16[2,4,4,16,128]{4,3,2,1,0:T(8,128)(2,1)}, bf16[2,4,4,16,128]{4,3,2,1,0:T(8,128)(2,1)S(1)}, u32[]{:S(2)}, u32[]{:S(2)}) collective-permute-start(bf16[2,4,4,16,128]{4,3,2,1,0:T(8,128)(2,1)} %get-tuple-element.76), channel_id=1, source_target_pairs={{0,1},{1,0},{2,3},{3,2},{4,5},{5,4},{6,7},{7,6},{8,9},{9,8},{10,11... | collective-permute-start | bytes 393224 | tf_op jit(solution)/shard_map/ppermute | solution.py:850
  10.6 9.9 %collective-permute-start.3 = (bf16[4,4,16,128]{3,2,1,0:T(8,128)(2,1)S(1)}, bf16[4,4,16,128]{3,2,1,0:T(8,128)(2,1)S(1)}, u32[]{:S(2)}, u32[]{:S(2)}) collective-permute-start(bf16[4,4,16,128]{3,2,1,0:T(8,128)(2,1)S(1)} %get-tuple-element.81), channel_id=1, source_target_pairs={{0,16},{2,18},{4,20},{6,22},{8,24},{10,26},{12,28},{14,30},{16,0},... | collective-permute-start | bytes 196616 | tf_op jit(solution)/shard_map/ppermute | solution.py:846
  13.8 6.7 %collective-permute-start.4 = (bf16[4,4,16,128]{3,2,1,0:T(8,128)(2,1)S(1)}, bf16[4,4,16,128]{3,2,1,0:T(8,128)(2,1)S(1)}, u32[]{:S(2)}, u32[]{:S(2)}) collective-permute-start(bf16[4,4,16,128]{3,2,1,0:T(8,128)(2,1)S(1)} %get-tuple-element.82), channel_id=1, source_target_pairs={{0,24},{2,26},{4,28},{6,30},{8,16},{10,18},{12,20},{14,22},{16,8},... | collective-permute-start | bytes 196616 | tf_op jit(solution)/shard_map/ppermute | solution.py:846
  15.2 5.3 %collective-permute-start.1 = (bf16[4,4,16,128]{3,2,1,0:T(8,128)(2,1)S(1)}, bf16[4,4,16,128]{3,2,1,0:T(8,128)(2,1)S(1)}, u32[]{:S(2)}, u32[]{:S(2)}) collective-permute-start(bf16[4,4,16,128]{3,2,1,0:T(8,128)(2,1)S(1)} %get-tuple-element.78), channel_id=1, source_target_pairs={{0,8},{2,10},{4,12},{6,14},{8,0},{10,2},{12,4},{14,6},{16,24},{18,... | collective-permute-start | bytes 196616 | tf_op jit(solution)/shard_map/ppermute | solution.py:846
  15.5 10.5 %collective-permute-start.8 = (bf16[4,64,128]{2,1,0:T(8,128)(2,1)S(1)}, bf16[4,64,128]{2,1,0:T(8,128)(2,1)S(1)}, u32[]{:S(2)}, u32[]{:S(2)}) collective-permute-start(bf16[4,64,128]{2,1,0:T(8,128)(2,1)S(1)} %get-tuple-element.102), channel_id=1, source_target_pairs={{0,1},{1,0},{2,3},{3,2},{4,5},{5,4},{6,7},{7,6},{8,9},{9,8},{10,11... | collective-permute-start | bytes 196616 | tf_op jit(solution)/shard_map/ppermute | solution.py:850
  20.6 6.9 %copy-start.3 = (bf16[256,128]{1,0:T(8,128)(2,1)S(1)}, bf16[256,128]{1,0:T(8,128)(2,1)}, u32[]{:S(2)}) copy-start(bf16[256,128]{1,0:T(8,128)(2,1)} %constant.19.clone.refs_4_) | copy-start | bytes 196612
  20.6 6.9 %copy-start.4 = (bf16[128,128]{1,0:T(8,128)(2,1)S(1)}, bf16[128,128]{1,0:T(8,128)(2,1)}, u32[]{:S(2)}) copy-start(bf16[128,128]{1,0:T(8,128)(2,1)} %constant.20.clone.refs_5_) | copy-start | bytes 98308
  20.6 5.4 %collective-permute-start.5 = (bf16[4,4,16,128]{3,2,1,0:T(8,128)(2,1)S(1)}, bf16[4,4,16,128]{3,2,1,0:T(8,128)(2,1)S(1)}, u32[]{:S(2)}, u32[]{:S(2)}) collective-permute-start(bf16[4,4,16,128]{3,2,1,0:T(8,128)(2,1)S(1)} %get-tuple-element.93), channel_id=1, source_target_pairs={{0,6},{2,4},{4,2},{6,0},{8,14},{10,12},{12,10},{14,8},{16,22},{18,... | collective-permute-start | bytes 196616 | tf_op jit(solution)/shard_map/ppermute | solution.py:846
  20.7 5.8 %collective-permute-start.6 = (bf16[4,4,16,128]{3,2,1,0:T(8,128)(2,1)S(1)}, bf16[4,4,16,128]{3,2,1,0:T(8,128)(2,1)S(1)}, u32[]{:S(2)}, u32[]{:S(2)}) collective-permute-start(bf16[4,4,16,128]{3,2,1,0:T(8,128)(2,1)S(1)} %get-tuple-element.94), channel_id=1, source_target_pairs={{0,4},{2,6},{4,0},{6,2},{8,12},{10,14},{12,8},{14,10},{16,20},{18,... | collective-permute-start | bytes 196616 | tf_op jit(solution)/shard_map/ppermute | solution.py:846
  22.2 4.2 %collective-permute-start.7 = (bf16[4,4,16,128]{3,2,1,0:T(8,128)(2,1)S(1)}, bf16[4,4,16,128]{3,2,1,0:T(8,128)(2,1)S(1)}, u32[]{:S(2)}, u32[]{:S(2)}) collective-permute-start(bf16[4,4,16,128]{3,2,1,0:T(8,128)(2,1)S(1)} %get-tuple-element.95), channel_id=1, source_target_pairs={{0,2},{2,0},{4,6},{6,4},{8,10},{10,8},{12,14},{14,12},{16,18},{18,... | collective-permute-start | bytes 196616 | tf_op jit(solution)/shard_map/ppermute | solution.py:846
  26.5 7.1 %collective-permute-start.9 = (bf16[18,64,128]{2,1,0:T(8,128)(2,1)S(1)}, bf16[18,64,128]{2,1,0:T(8,128)(2,1)S(1)}, u32[]{:S(2)}, u32[]{:S(2)}) collective-permute-start(bf16[18,64,128]{2,1,0:T(8,128)(2,1)S(1)} %get-tuple-element.118), channel_id=1, source_target_pairs={{0,2},{4,6},{8,10},{12,14},{16,18},{20,22},{24,26},{28,30},{2,0},{... | collective-permute-start | bytes 884744 | tf_op jit(solution)/shard_map/ppermute | solution.py:835
  26.6 12.5 %copy-start.6 = (bf16[3,3,3,128,128]{4,3,2,1,0:T(8,128)(2,1)S(1)}, bf16[3,3,3,128,128]{4,3,2,1,0:T(8,128)(2,1)}, u32[]{:S(2)}) copy-start(bf16[3,3,3,128,128]{4,3,2,1,0:T(8,128)(2,1)} %refs_5_.4) | copy-start | bytes 2654212
  26.6 6.9 %collective-permute-start.10 = (bf16[18,64,128]{2,1,0:T(8,128)(2,1)S(1)}, bf16[18,64,128]{2,1,0:T(8,128)(2,1)S(1)}, u32[]{:S(2)}, u32[]{:S(2)}) collective-permute-start(bf16[18,64,128]{2,1,0:T(8,128)(2,1)S(1)} %get-tuple-element.119), channel_id=1, source_target_pairs={{2,4},{6,8},{10,12},{14,16},{18,20},{22,24},{26,28},{4,2},{8,6},{1... | collective-permute-start | bytes 884744 | tf_op jit(solution)/shard_map/ppermute | solution.py:835
  33.6 22.4 %copy-start = (bf16[4,1024,256]{2,1,0:T(8,128)(2,1)S(1)}, bf16[4,1024,256]{2,1,0:T(8,128)(2,1)}, u32[]{:S(2)}) copy-start(bf16[4,1024,256]{2,1,0:T(8,128)(2,1)} %constant.21.clone.table_ref) | copy-start | bytes 6291460
  33.6 22.4 %copy-start.5 = (f32[128]{0:T(128)S(1)}, f32[128]{0:T(128)}, u32[]{:S(2)}) copy-start(f32[128]{0:T(128)} %param.11) | copy-start | bytes 1540
  33.6 8.2 %collective-permute-start.11 = (bf16[4,4,16,128]{3,2,1,0:T(8,128)(2,1)S(1)}, bf16[4,4,16,128]{3,2,1,0:T(8,128)(2,1)S(1)}, u32[]{:S(2)}, u32[]{:S(2)}) collective-permute-start(bf16[4,4,16,128]{3,2,1,0:T(8,128)(2,1)S(1)} %get-tuple-element.120), channel_id=1, source_target_pairs={{0,6},{2,4},{4,2},{6,0},{8,14},{10,12},{12,10},{14,8},{16,22},{18,... | collective-permute-start | bytes 196616 | tf_op jit(solution)/shard_map/ppermute | solution.py:846
  37.9 4.7 %collective-permute-start.12 = (bf16[4,4,16,128]{3,2,1,0:T(8,128)(2,1)S(1)}, bf16[4,4,16,128]{3,2,1,0:T(8,128)(2,1)S(1)}, u32[]{:S(2)}, u32[]{:S(2)}) collective-permute-start(bf16[4,4,16,128]{3,2,1,0:T(8,128)(2,1)S(1)} %get-tuple-element.121), channel_id=1, source_target_pairs={{0,4},{2,6},{4,0},{6,2},{8,12},{10,14},{12,8},{14,10},{16,20},{18,... | collective-permute-start | bytes 196616 | tf_op jit(solution)/shard_map/ppermute | solution.py:846
  39.1 3.5 %collective-permute-start.13 = (bf16[4,4,16,128]{3,2,1,0:T(8,128)(2,1)S(1)}, bf16[4,4,16,128]{3,2,1,0:T(8,128)(2,1)S(1)}, u32[]{:S(2)}, u32[]{:S(2)}) collective-permute-start(bf16[4,4,16,128]{3,2,1,0:T(8,128)(2,1)S(1)} %get-tuple-element.122), channel_id=1, source_target_pairs={{0,2},{2,0},{4,6},{6,4},{8,10},{10,8},{12,14},{14,12},{16,18},{18,... | collective-permute-start | bytes 196616 | tf_op jit(solution)/shard_map/ppermute | solution.py:846
  42.6 6.2 %collective-permute-start.14 = (bf16[4,4,16,128]{3,2,1,0:T(8,128)(2,1)S(1)}, bf16[4,4,16,128]{3,2,1,0:T(8,128)(2,1)S(1)}, u32[]{:S(2)}, u32[]{:S(2)}) collective-permute-start(bf16[4,4,16,128]{3,2,1,0:T(8,128)(2,1)S(1)} %get-tuple-element.131), channel_id=1, source_target_pairs={{0,24},{2,26},{4,28},{6,30},{8,16},{10,18},{12,20},{14,22},{16,8},... | collective-permute-start | bytes 196616 | tf_op jit(solution)/shard_map/ppermute | solution.py:846
  46.2 6.6 %collective-permute-start.15 = (bf16[4,4,16,128]{3,2,1,0:T(8,128)(2,1)S(1)}, bf16[4,4,16,128]{3,2,1,0:T(8,128)(2,1)S(1)}, u32[]{:S(2)}, u32[]{:S(2)}) collective-permute-start(bf16[4,4,16,128]{3,2,1,0:T(8,128)(2,1)S(1)} %get-tuple-element.132), channel_id=1, source_target_pairs={{0,16},{2,18},{4,20},{6,22},{8,24},{10,26},{12,28},{14,30},{16,0},... | collective-permute-start | bytes 196616 | tf_op jit(solution)/shard_map/ppermute | solution.py:846
  47.0 5.8 %collective-permute-start.16 = (bf16[4,4,16,128]{3,2,1,0:T(8,128)(2,1)S(1)}, bf16[4,4,16,128]{3,2,1,0:T(8,128)(2,1)S(1)}, u32[]{:S(2)}, u32[]{:S(2)}) collective-permute-start(bf16[4,4,16,128]{3,2,1,0:T(8,128)(2,1)S(1)} %get-tuple-element.133), channel_id=1, source_target_pairs={{0,8},{2,10},{4,12},{6,14},{8,0},{10,2},{12,4},{14,6},{16,24},{18,... | collective-permute-start | bytes 196616 | tf_op jit(solution)/shard_map/ppermute | solution.py:846
  52.8 8.2 %collective-permute-start.17 = (bf16[4,4,4,16,128]{4,3,2,1,0:T(8,128)(2,1)S(1)}, bf16[4,4,4,16,128]{4,3,2,1,0:T(8,128)(2,1)S(1)}, u32[]{:S(2)}, u32[]{:S(2)}) collective-permute-start(bf16[4,4,4,16,128]{4,3,2,1,0:T(8,128)(2,1)S(1)} %shard_map.94), channel_id=1, source_target_pairs={{0,1},{1,0},{2,3},{3,2},{4,5},{5,4},{6,7},{7,6},{8,9},{9,8},{10,11... | collective-permute-start | bytes 786440 | tf_op jit(solution)/shard_map/ppermute | solution.py:850

commit v12 on v11

--- a/solution.py
+++ b/solution.py
@@ -559,7 +559,8 @@
 
 
 def bundled_slots(count):
-    return [[0] + far_first(count)[:-1]]
+    parts = ([0], [count - 1], far_first(count)[1:-1]) if count > 1 else ([0],)
+    return [part for part in parts if part]
 
 
 def bundle_kernel(*refs):
@@ -904,7 +905,7 @@
         for step in far_first(inner)
     ]
     if early:
-        loaded.append(preload(weight, 2 * early, early))
+        loaded.append(preload(weight, 2 * early, max(early // 2, 1)))
 
     rows, loaded, first, last, front, back = barrier((rows, loaded, first, last, front, back))
     paired, other = halo_planes(me, first, last, front, back, shards, shards_y)
@@ -918,7 +919,7 @@
         loaded,
         shards,
     )
-    returned, paired, other = barrier((list(returned), paired, other))
+    returned, other, paired = barrier((list(returned), other, paired))
     halos = (paired, other, front, back)
     width = 2 if cells_x % 2 == 0 else 1
     convolved = [
@@ -937,7 +938,10 @@
         for step in far_first(outer)
     ]
     by_slot = dict(zip(far_first(outer), returned))
-    bundles = [bundle([by_slot[slot] for slot in slots]) for slots in bundled_slots(outer)]
+    bundles = [
+        bundle([by_slot[slot] for slot in slots]) if slots[1:] else by_slot[slots[0]][None]
+        for slots in bundled_slots(outer)
+    ]
     others = []
     for step in range(1, shards_y):
         others += [over_y(part, step, shards_y) for part in bundles]

time: 63.7 us -> 59.9 us (0.940)
  waiting for transfers between devices: 11.3 us -> 8.99 us
  Pallas kernels: 28.9 us -> 27.5 us
    ppermute x4 -> x6, waiting for transfers between devices: 4.46 us -> 1.32 us  [over_y(): lax.ppermute(array, 'gy', [(i, (i + step) % shards_y) for i in range(shar...]
    ppermute x12, starting transfers between devices: 16.8 us -> 14.3 us  [exchange(): return lax.ppermute(array, 'gx', pairs)]
    ppermute x2, starting transfers between devices: 0.92 us -> 2.78 us  [with_neighbour(): return lax.ppermute(array, axis, pairs + [(j, i) for i, j in pairs])]
    pallas_call x3, Pallas kernels: 10.4 us -> 9.15 us  [preload(): pl.pallas_call(functools.partial(preload_kernel, 2 * pair), in_specs=[pl....]
    ppermute x12, waiting for transfers between devices: 6.87 us -> 7.67 us  [exchange(): return lax.ppermute(array, 'gx', pairs)]
    ppermute x4 -> x6, starting transfers between devices: 5.21 us -> 5.8 us  [over_y(): lax.ppermute(array, 'gy', [(i, (i + step) % shards_y) for i in range(shar...]
  transfers between devices with their start and end apart: 18 -> 20, of which waited for: 6 -> 7; matrix products, arithmetic and copies ran while one was open for 0% -> 0% of each run, Pallas kernels for 37% -> 37%
where the time goes in v12:
time: 59.9 us; the launch traced here: 59.8 us
  Pallas kernels  27.5 us (46%)
  starting transfers between devices  22.9 us (38%)
  waiting for transfers between devices  8.99 us (15%)
    ppermute x12, starting transfers between devices, exchange(): return lax.ppermute(array, 'gx', pairs)  14.3 us
    pallas_call x3, Pallas kernels, preload(): pl.pallas_call(functools.partial(preload_kernel, 2 * pair), in_specs=[pl....  9.15 us
    ppermute x12, waiting for transfers between devices, exchange(): return lax.ppermute(array, 'gx', pairs)  7.67 us
    pallas_call x1, Pallas kernels, mixing(): pl.pallas_call(functools.partial(mixing_kernel, shards, len(loaded)), in_...  6.07 us
    ppermute x6, starting transfers between devices, over_y(): lax.ppermute(array, 'gy', [(i, (i + step) % shards_y) for i in range(shar...  5.8 us
    pallas_call x2, Pallas kernels, convolution(): pl.pallas_call(functools.partial(convolution_kernel, x, cells_x, width, s...  5.21 us
    pallas_call x2, Pallas kernels, forward_yz(): pl.pallas_call(kernel, in_specs=[IN_SMEM] + specs, out_specs=in_vmem(len(...  3.43 us
    ppermute x2, starting transfers between devices, with_neighbour(): return lax.ppermute(array, axis, pairs + [(j, i) for i, j in pairs])  2.78 us
  transfers between devices with their start and end apart: 20, of which 7 were waited for; matrix products, arithmetic and copies ran while one was open for 0% of the time, Pallas kernels for 37%

profile of v12, /device:TPU:0, one launch (start us, length us, event | category | flops | bytes accessed | tf_op | source)
XLA Modules:
  0.0 59.8 jit_solution(13141176580636490968)
XLA Ops:
  0.0 3.0 %shard_map.82 = (bf16[2,4,4,16,128]{4,3,2,1,0:T(8,128)(2,1)}, bf16[2,4,4,16,128]{4,3,2,1,0:T(8,128)(2,1)}) custom-call(s32[1]{0:T(128)} %bitcast.me_ref, bf16[2,512,1024]{2,1,0:T(8,128)(2,1)} %constant.18.clone.table_ref, bf16[4,1024,128]{2,1,0:T(8,128)(2,1)} %bitcast.6), custom_call_target="tpu_custom_call" | custom-call | flops 268435456 | bytes 1572864 | tf_op jit(solution)/shard_map/pallas_call | solution.py:224
  3.0 0.0 copy-start.1
  3.0 0.0 copy-start.2
  3.0 3.0 %collective-permute-start.2 = (bf16[2,4,4,16,128]{4,3,2,1,0:T(8,128)(2,1)}, bf16[2,4,4,16,128]{4,3,2,1,0:T(8,128)(2,1)S(1)}, u32[]{:S(2)}, u32[]{:S(2)}) collective-permute-start(bf16[2,4,4,16,128]{4,3,2,1,0:T(8,128)(2,1)} %get-tuple-element.80), channel_id=1, source_target_pairs={{0,1},{1,0},{2,3},{3,2},{4,5},{5,4},{6,7},{7,6},{8,9},{9,8},{10,11... | collective-permute-start | bytes 393224 | tf_op jit(solution)/shard_map/ppermute | solution.py:851
  6.0 0.1 collective-permute-start
  6.1 3.5 %shard_map.83.refs_7_ = bf16[4,64,128,128]{3,2,1,0:T(8,128)(2,1)S(1)} custom-call(bf16[16,64,128,128]{3,2,1,0:T(8,128)(2,1)} %bitcast.11), custom_call_target="tpu_custom_call" | custom-call | bytes 8388608 | tf_op jit(solution)/shard_map/pallas_call | solution.py:341
  9.6 0.4 shard_map.84
  10.1 0.5 collective-permute-done.2.refs_1_
  10.6 3.2 %collective-permute-start.3 = (bf16[4,4,16,128]{3,2,1,0:T(8,128)(2,1)S(1)}, bf16[4,4,16,128]{3,2,1,0:T(8,128)(2,1)S(1)}, u32[]{:S(2)}, u32[]{:S(2)}) collective-permute-start(bf16[4,4,16,128]{3,2,1,0:T(8,128)(2,1)S(1)} %get-tuple-element.81), channel_id=1, source_target_pairs={{0,16},{2,18},{4,20},{6,22},{8,24},{10,26},{12,28},{14,30},{16,0},... | collective-permute-start | bytes 196616 | tf_op jit(solution)/shard_map/ppermute | solution.py:847
  13.8 1.4 %collective-permute-start.4 = (bf16[4,4,16,128]{3,2,1,0:T(8,128)(2,1)S(1)}, bf16[4,4,16,128]{3,2,1,0:T(8,128)(2,1)S(1)}, u32[]{:S(2)}, u32[]{:S(2)}) collective-permute-start(bf16[4,4,16,128]{3,2,1,0:T(8,128)(2,1)S(1)} %get-tuple-element.82), channel_id=1, source_target_pairs={{0,24},{2,26},{4,28},{6,30},{8,16},{10,18},{12,20},{14,22},{16,8},... | collective-permute-start | bytes 196616 | tf_op jit(solution)/shard_map/ppermute | solution.py:847
  15.2 0.0 collective-permute-done.refs_1_
  15.2 0.3 collective-permute-start.1
  15.5 1.5 %collective-permute-start.8 = (bf16[4,64,128]{2,1,0:T(8,128)(2,1)S(1)}, bf16[4,64,128]{2,1,0:T(8,128)(2,1)S(1)}, u32[]{:S(2)}, u32[]{:S(2)}) collective-permute-start(bf16[4,64,128]{2,1,0:T(8,128)(2,1)S(1)} %get-tuple-element.102), channel_id=1, source_target_pairs={{0,1},{1,0},{2,3},{3,2},{4,5},{5,4},{6,7},{7,6},{8,9},{9,8},{10,11... | collective-permute-start | bytes 196616 | tf_op jit(solution)/shard_map/ppermute | solution.py:851
  17.0 3.5 %shard_map.87.refs_8_ = bf16[4,64,128,128]{3,2,1,0:T(8,128)(2,1)S(1)} custom-call(bf16[16,64,128,128]{3,2,1,0:T(8,128)(2,1)} %bitcast.12), custom_call_target="tpu_custom_call" | custom-call | bytes 8388608 | tf_op jit(solution)/shard_map/pallas_call | solution.py:341
  20.5 0.0 collective-permute-done.4.refs_0_
  20.5 0.0 collective-permute-done.1.refs_2_
  20.6 0.0 copy-start.3
  20.6 0.0 copy-start.4
  20.6 0.1 collective-permute-start.5
  20.7 1.6 %collective-permute-start.6 = (bf16[4,4,16,128]{3,2,1,0:T(8,128)(2,1)S(1)}, bf16[4,4,16,128]{3,2,1,0:T(8,128)(2,1)S(1)}, u32[]{:S(2)}, u32[]{:S(2)}) collective-permute-start(bf16[4,4,16,128]{3,2,1,0:T(8,128)(2,1)S(1)} %get-tuple-element.94), channel_id=1, source_target_pairs={{0,4},{2,6},{4,0},{6,2},{8,12},{10,14},{12,8},{14,10},{16,20},{18,... | collective-permute-start | bytes 196616 | tf_op jit(solution)/shard_map/ppermute | solution.py:847
  22.2 0.3 collective-permute-start.7
  22.5 2.2 %shard_map.89.refs_9_ = bf16[2,64,128,128]{3,2,1,0:T(8,128)(2,1)S(1)} custom-call(bf16[16,64,128,128]{3,2,1,0:T(8,128)(2,1)} %bitcast.13), custom_call_target="tpu_custom_call" | custom-call | bytes 4194304 | tf_op jit(solution)/shard_map/pallas_call | solution.py:341
  24.7 0.3 collective-permute-done.5.refs_0_
  25.0 1.5 %collective-permute-done.6.refs_1_ = bf16[4,4,16,128]{3,2,1,0:T(8,128)(2,1)S(1)} collective-permute-done((bf16[4,4,16,128]{3,2,1,0:T(8,128)(2,1)S(1)}, bf16[4,4,16,128]{3,2,1,0:T(8,128)(2,1)S(1)}, u32[]{:S(2)}, u32[]{:S(2)}) %collective-permute-start.6) | collective-permute-done | bytes 65568 | tf_op jit(solution)/shard_map/ppermute | solution.py:847
  26.4 0.1 shard_map.91
  26.5 0.7 %collective-permute-start.9 = (bf16[18,64,128]{2,1,0:T(8,128)(2,1)S(1)}, bf16[18,64,128]{2,1,0:T(8,128)(2,1)S(1)}, u32[]{:S(2)}, u32[]{:S(2)}) collective-permute-start(bf16[18,64,128]{2,1,0:T(8,128)(2,1)S(1)} %get-tuple-element.118), channel_id=1, source_target_pairs={{2,4},{6,8},{10,12},{14,16},{18,20},{22,24},{26,28},{4,2},{8,6},{1... | collective-permute-start | bytes 884744 | tf_op jit(solution)/shard_map/ppermute | solution.py:836
  27.2 0.0 copy-start.6
  27.2 2.1 %collective-permute-start.10 = (bf16[18,64,128]{2,1,0:T(8,128)(2,1)S(1)}, bf16[18,64,128]{2,1,0:T(8,128)(2,1)S(1)}, u32[]{:S(2)}, u32[]{:S(2)}) collective-permute-start(bf16[18,64,128]{2,1,0:T(8,128)(2,1)S(1)} %get-tuple-element.119), channel_id=1, source_target_pairs={{0,2},{4,6},{8,10},{12,14},{16,18},{20,22},{24,26},{28,30},{2,0},{... | collective-permute-start | bytes 884744 | tf_op jit(solution)/shard_map/ppermute | solution.py:836
  29.3 6.1 %shard_map.90 = (bf16[4,4,16,128]{3,2,1,0:T(8,128)(2,1)S(1)}, bf16[4,4,16,128]{3,2,1,0:T(8,128)(2,1)S(1)}, bf16[4,4,16,128]{3,2,1,0:T(8,128)(2,1)S(1)}, bf16[4,4,16,128]{3,2,1,0:T(8,128)(2,1)S(1)}) custom-call(s32[1]{0:T(128)} %bitcast.me_ref, bf16[4,4,16,128]{3,2,1,0:T(8,128)(2,1)S(1)} %collective-permute-done.5.refs_0_, ...), custom_call_target="tpu_custom_call" | custom-call | flops 134217728 | bytes 33554432 | tf_op jit(solution)/shard_map/pallas_call | solution.py:460
  35.4 2.3 %collective-permute-start.11 = (bf16[4,4,16,128]{3,2,1,0:T(8,128)(2,1)S(1)}, bf16[4,4,16,128]{3,2,1,0:T(8,128)(2,1)S(1)}, u32[]{:S(2)}, u32[]{:S(2)}) collective-permute-start(bf16[4,4,16,128]{3,2,1,0:T(8,128)(2,1)S(1)} %get-tuple-element.120), channel_id=1, source_target_pairs={{0,6},{2,4},{4,2},{6,0},{8,14},{10,12},{12,10},{14,8},{16,22},{18,... | collective-permute-start | bytes 196616 | tf_op jit(solution)/shard_map/ppermute | solution.py:847
  37.7 0.7 %collective-permute-start.12 = (bf16[4,4,16,128]{3,2,1,0:T(8,128)(2,1)S(1)}, bf16[4,4,16,128]{3,2,1,0:T(8,128)(2,1)S(1)}, u32[]{:S(2)}, u32[]{:S(2)}) collective-permute-start(bf16[4,4,16,128]{3,2,1,0:T(8,128)(2,1)S(1)} %get-tuple-element.121), channel_id=1, source_target_pairs={{0,4},{2,6},{4,0},{6,2},{8,12},{10,14},{12,8},{14,10},{16,20},{18,... | collective-permute-start | bytes 196616 | tf_op jit(solution)/shard_map/ppermute | solution.py:847
  38.4 0.1 collective-permute-start.13
  38.5 2.6 %shard_map.92.refs_4_ = bf16[2,16,64,128]{3,2,1,0:T(8,128)(2,1)S(1)} custom-call(s32[1]{0:T(128)} %bitcast.me_ref, bf16[4,16,64,128]{3,2,1,0:T(8,128)(2,1)S(1)} %copy-done.2, bf16[18,64,128]{2,1,0:T(8,128)(2,1)S(1)} %collective-permute-done.10.refs_1_, bf16[18,64,128]{2,1,0:T(8,128)(2,1)S(1)} %collective-permute-done.9.refs_2_, ...), custom_call_target="tpu_custom_call" | custom-call | flops 2717908992 | bytes 1310720 | tf_op jit(solution)/shard_map/pallas_call | solution.py:546
  41.1 1.4 %collective-permute-done.12.refs_1_ = bf16[4,4,16,128]{3,2,1,0:T(8,128)(2,1)S(1)} collective-permute-done((bf16[4,4,16,128]{3,2,1,0:T(8,128)(2,1)S(1)}, bf16[4,4,16,128]{3,2,1,0:T(8,128)(2,1)S(1)}, u32[]{:S(2)}, u32[]{:S(2)}) %collective-permute-start.12) | collective-permute-done | bytes 65568 | tf_op jit(solution)/shard_map/ppermute | solution.py:847
  42.5 3.0 %collective-permute-start.15 = (bf16[4,4,16,128]{3,2,1,0:T(8,128)(2,1)S(1)}, bf16[4,4,16,128]{3,2,1,0:T(8,128)(2,1)S(1)}, u32[]{:S(2)}, u32[]{:S(2)}) collective-permute-start(bf16[4,4,16,128]{3,2,1,0:T(8,128)(2,1)S(1)} %get-tuple-element.131), channel_id=1, source_target_pairs={{0,24},{2,26},{4,28},{6,30},{8,16},{10,18},{12,20},{14,22},{16,8},... | collective-permute-start | bytes 196616 | tf_op jit(solution)/shard_map/ppermute | solution.py:847
  45.5 0.9 %collective-permute-start.17 = (bf16[4,4,16,128]{3,2,1,0:T(8,128)(2,1)S(1)}, bf16[4,4,16,128]{3,2,1,0:T(8,128)(2,1)S(1)}, u32[]{:S(2)}, u32[]{:S(2)}) collective-permute-start(bf16[4,4,16,128]{3,2,1,0:T(8,128)(2,1)S(1)} %get-tuple-element.132), channel_id=1, source_target_pairs={{0,16},{2,18},{4,20},{6,22},{8,24},{10,26},{12,28},{14,30},{16,0},... | collective-permute-start | bytes 196616 | tf_op jit(solution)/shard_map/ppermute | solution.py:847
  46.4 0.6 %collective-permute-start.18 = (bf16[4,4,16,128]{3,2,1,0:T(8,128)(2,1)S(1)}, bf16[4,4,16,128]{3,2,1,0:T(8,128)(2,1)S(1)}, u32[]{:S(2)}, u32[]{:S(2)}) collective-permute-start(bf16[4,4,16,128]{3,2,1,0:T(8,128)(2,1)S(1)} %get-tuple-element.133), channel_id=1, source_target_pairs={{0,8},{2,10},{4,12},{6,14},{8,0},{10,2},{12,4},{14,6},{16,24},{18,... | collective-permute-start | bytes 196616 | tf_op jit(solution)/shard_map/ppermute | solution.py:847
  47.0 0.3 collective-permute-start.14
  47.3 1.5 %collective-permute-done.15.refs_0_ = bf16[4,4,16,128]{3,2,1,0:T(8,128)(2,1)S(1)} collective-permute-done((bf16[4,4,16,128]{3,2,1,0:T(8,128)(2,1)S(1)}, bf16[4,4,16,128]{3,2,1,0:T(8,128)(2,1)S(1)}, u32[]{:S(2)}, u32[]{:S(2)}) %collective-permute-start.15) | collective-permute-done | bytes 65568 | tf_op jit(solution)/shard_map/ppermute | solution.py:847
  48.8 0.3 collective-permute-start.16
  49.1 3.0 %collective-permute-done.17.refs_0_.refs_1_ = bf16[4,4,16,128]{3,2,1,0:T(8,128)(2,1)S(1)} collective-permute-done((bf16[4,4,16,128]{3,2,1,0:T(8,128)(2,1)S(1)}, bf16[4,4,16,128]{3,2,1,0:T(8,128)(2,1)S(1)}, u32[]{:S(2)}, u32[]{:S(2)}) %collective-permute-start.17) | collective-permute-done | bytes 65568 | tf_op jit(solution)/shard_map/ppermute | solution.py:847
  52.2 0.0 copy-start
  52.2 0.0 copy-start.5
  52.2 0.6 collective-permute-start.19
  52.8 2.6 %shard_map.95.refs_5_ = bf16[2,16,64,128]{3,2,1,0:T(8,128)(2,1)S(1)} custom-call(s32[1]{0:T(128)} %bitcast.me_ref, bf16[4,16,64,128]{3,2,1,0:T(8,128)(2,1)S(1)} %copy-done.2, bf16[18,64,128]{2,1,0:T(8,128)(2,1)S(1)} %collective-permute-done.10.refs_1_, bf16[18,64,128]{2,1,0:T(8,128)(2,1)S(1)} %collective-permute-done.9.refs_2_, ...), custom_call_target="tpu_custom_call" | custom-call | flops 2717908992 | bytes 1310720 | tf_op jit(solution)/shard_map/pallas_call | solution.py:546
  55.4 1.0 %shard_map.96.refs_3_ = f32[4,16,64,128]{3,2,1,0:T(8,128)S(1)} custom-call(s32[1]{0:T(128)} %bitcast.me_ref, bf16[4,1024,256]{2,1,0:T(8,128)(2,1)S(1)} %copy-done, bf16[4,4,16,128]{3,2,1,0:T(8,128)(2,1)S(1)} %collective-permute-done.15.refs_0_, bf16[4,4,16,128]{3,2,1,0:T(8,128)(2,1)S(1)} %collective-permute-done.17.refs_0_.refs_1_, ...), custom_call_target="tpu_custom_call" | custom-call | flops 268435456 | bytes 3145728 | tf_op jit(solution)/shard_map/pallas_call | solution.py:672
  56.4 0.8 %collective-permute-done.19.refs_2_ = bf16[2,4,4,16,128]{4,3,2,1,0:T(8,128)(2,1)S(1)} collective-permute-done((bf16[2,4,4,16,128]{4,3,2,1,0:T(8,128)(2,1)S(1)}, bf16[2,4,4,16,128]{4,3,2,1,0:T(8,128)(2,1)S(1)}, u32[]{:S(2)}, u32[]{:S(2)}) %collective-permute-start.19) | collective-permute-done | bytes 131104 | tf_op jit(solution)/shard_map/ppermute | solution.py:851
  57.2 2.5 %shard_map.97 = bf16[4,16,64,128]{3,2,1,0:T(8,128)(2,1)} custom-call(s32[1]{0:T(128)} %bitcast.me_ref, bf16[4,1024,256]{2,1,0:T(8,128)(2,1)S(1)} %copy-done, bf16[1,4,4,16,128]{4,3,2,1,0:T(8,128)(2,1)S(1)} %collective-permute-done.14.refs_0_, bf16[1,4,4,16,128]{4,3,2,1,0:T(8,128)(2,1)S(1)} %collective-permute-done.16.refs_1_, ...), custom_call_target="tpu_custom_call" | custom-call | flops 268435456 | bytes 3145728 | tf_op jit(solution)/shard_map/pallas_call | solution.py:692
  (22 shorter events, 0.2 us)
Async XLA Ops:
  3.0 6.6 %copy-start.1 = (bf16[2,512,1024]{2,1,0:T(8,128)(2,1)S(1)}, bf16[2,512,1024]{2,1,0:T(8,128)(2,1)}, u32[]{:S(2)}) copy-start(bf16[2,512,1024]{2,1,0:T(8,128)(2,1)} %constant.18.clone.table_ref) | copy-start | bytes 6291460
  3.0 6.6 %copy-start.2 = (bf16[4,16,64,128]{3,2,1,0:T(8,128)(2,1)S(1)}, bf16[4,16,64,128]{3,2,1,0:T(8,128)(2,1)}, u32[]{:S(2)}) copy-start(bf16[4,16,64,128]{3,2,1,0:T(8,128)(2,1)} %refs_0_.3) | copy-start | bytes 3145732
  3.0 7.6 %collective-permute-start.2 = (bf16[2,4,4,16,128]{4,3,2,1,0:T(8,128)(2,1)}, bf16[2,4,4,16,128]{4,3,2,1,0:T(8,128)(2,1)S(1)}, u32[]{:S(2)}, u32[]{:S(2)}) collective-permute-start(bf16[2,4,4,16,128]{4,3,2,1,0:T(8,128)(2,1)} %get-tuple-element.80), channel_id=1, source_target_pairs={{0,1},{1,0},{2,3},{3,2},{4,5},{5,4},{6,7},{7,6},{8,9},{9,8},{10,11... | collective-permute-start | bytes 393224 | tf_op jit(solution)/shard_map/ppermute | solution.py:851
  6.0 9.1 %collective-permute-start = (bf16[2,4,4,16,128]{4,3,2,1,0:T(8,128)(2,1)}, bf16[2,4,4,16,128]{4,3,2,1,0:T(8,128)(2,1)S(1)}, u32[]{:S(2)}, u32[]{:S(2)}) collective-permute-start(bf16[2,4,4,16,128]{4,3,2,1,0:T(8,128)(2,1)} %get-tuple-element.76), channel_id=1, source_target_pairs={{0,1},{1,0},{2,3},{3,2},{4,5},{5,4},{6,7},{7,6},{8,9},{9,8},{10,11... | collective-permute-start | bytes 393224 | tf_op jit(solution)/shard_map/ppermute | solution.py:851
  10.6 9.9 %collective-permute-start.3 = (bf16[4,4,16,128]{3,2,1,0:T(8,128)(2,1)S(1)}, bf16[4,4,16,128]{3,2,1,0:T(8,128)(2,1)S(1)}, u32[]{:S(2)}, u32[]{:S(2)}) collective-permute-start(bf16[4,4,16,128]{3,2,1,0:T(8,128)(2,1)S(1)} %get-tuple-element.81), channel_id=1, source_target_pairs={{0,16},{2,18},{4,20},{6,22},{8,24},{10,26},{12,28},{14,30},{16,0},... | collective-permute-start | bytes 196616 | tf_op jit(solution)/shard_map/ppermute | solution.py:847
  13.8 6.7 %collective-permute-start.4 = (bf16[4,4,16,128]{3,2,1,0:T(8,128)(2,1)S(1)}, bf16[4,4,16,128]{3,2,1,0:T(8,128)(2,1)S(1)}, u32[]{:S(2)}, u32[]{:S(2)}) collective-permute-start(bf16[4,4,16,128]{3,2,1,0:T(8,128)(2,1)S(1)} %get-tuple-element.82), channel_id=1, source_target_pairs={{0,24},{2,26},{4,28},{6,30},{8,16},{10,18},{12,20},{14,22},{16,8},... | collective-permute-start | bytes 196616 | tf_op jit(solution)/shard_map/ppermute | solution.py:847
  15.2 5.3 %collective-permute-start.1 = (bf16[4,4,16,128]{3,2,1,0:T(8,128)(2,1)S(1)}, bf16[4,4,16,128]{3,2,1,0:T(8,128)(2,1)S(1)}, u32[]{:S(2)}, u32[]{:S(2)}) collective-permute-start(bf16[4,4,16,128]{3,2,1,0:T(8,128)(2,1)S(1)} %get-tuple-element.78), channel_id=1, source_target_pairs={{0,8},{2,10},{4,12},{6,14},{8,0},{10,2},{12,4},{14,6},{16,24},{18,... | collective-permute-start | bytes 196616 | tf_op jit(solution)/shard_map/ppermute | solution.py:847
  15.5 9.2 %collective-permute-start.8 = (bf16[4,64,128]{2,1,0:T(8,128)(2,1)S(1)}, bf16[4,64,128]{2,1,0:T(8,128)(2,1)S(1)}, u32[]{:S(2)}, u32[]{:S(2)}) collective-permute-start(bf16[4,64,128]{2,1,0:T(8,128)(2,1)S(1)} %get-tuple-element.102), channel_id=1, source_target_pairs={{0,1},{1,0},{2,3},{3,2},{4,5},{5,4},{6,7},{7,6},{8,9},{9,8},{10,11... | collective-permute-start | bytes 196616 | tf_op jit(solution)/shard_map/ppermute | solution.py:851
  20.6 8.8 %copy-start.3 = (bf16[256,128]{1,0:T(8,128)(2,1)S(1)}, bf16[256,128]{1,0:T(8,128)(2,1)}, u32[]{:S(2)}) copy-start(bf16[256,128]{1,0:T(8,128)(2,1)} %constant.19.clone.refs_4_) | copy-start | bytes 196612
  20.6 8.7 %copy-start.4 = (bf16[128,128]{1,0:T(8,128)(2,1)S(1)}, bf16[128,128]{1,0:T(8,128)(2,1)}, u32[]{:S(2)}) copy-start(bf16[128,128]{1,0:T(8,128)(2,1)} %constant.20.clone.refs_5_) | copy-start | bytes 98308
  20.6 4.4 %collective-permute-start.5 = (bf16[4,4,16,128]{3,2,1,0:T(8,128)(2,1)S(1)}, bf16[4,4,16,128]{3,2,1,0:T(8,128)(2,1)S(1)}, u32[]{:S(2)}, u32[]{:S(2)}) collective-permute-start(bf16[4,4,16,128]{3,2,1,0:T(8,128)(2,1)S(1)} %get-tuple-element.93), channel_id=1, source_target_pairs={{0,6},{2,4},{4,2},{6,0},{8,14},{10,12},{12,10},{14,8},{16,22},{18,... | collective-permute-start | bytes 196616 | tf_op jit(solution)/shard_map/ppermute | solution.py:847
  20.7 5.8 %collective-permute-start.6 = (bf16[4,4,16,128]{3,2,1,0:T(8,128)(2,1)S(1)}, bf16[4,4,16,128]{3,2,1,0:T(8,128)(2,1)S(1)}, u32[]{:S(2)}, u32[]{:S(2)}) collective-permute-start(bf16[4,4,16,128]{3,2,1,0:T(8,128)(2,1)S(1)} %get-tuple-element.94), channel_id=1, source_target_pairs={{0,4},{2,6},{4,0},{6,2},{8,12},{10,14},{12,8},{14,10},{16,20},{18,... | collective-permute-start | bytes 196616 | tf_op jit(solution)/shard_map/ppermute | solution.py:847
  22.2 4.2 %collective-permute-start.7 = (bf16[4,4,16,128]{3,2,1,0:T(8,128)(2,1)S(1)}, bf16[4,4,16,128]{3,2,1,0:T(8,128)(2,1)S(1)}, u32[]{:S(2)}, u32[]{:S(2)}) collective-permute-start(bf16[4,4,16,128]{3,2,1,0:T(8,128)(2,1)S(1)} %get-tuple-element.95), channel_id=1, source_target_pairs={{0,2},{2,0},{4,6},{6,4},{8,10},{10,8},{12,14},{14,12},{16,18},{18,... | collective-permute-start | bytes 196616 | tf_op jit(solution)/shard_map/ppermute | solution.py:847
  26.5 8.9 %collective-permute-start.9 = (bf16[18,64,128]{2,1,0:T(8,128)(2,1)S(1)}, bf16[18,64,128]{2,1,0:T(8,128)(2,1)S(1)}, u32[]{:S(2)}, u32[]{:S(2)}) collective-permute-start(bf16[18,64,128]{2,1,0:T(8,128)(2,1)S(1)} %get-tuple-element.118), channel_id=1, source_target_pairs={{2,4},{6,8},{10,12},{14,16},{18,20},{22,24},{26,28},{4,2},{8,6},{1... | collective-permute-start | bytes 884744 | tf_op jit(solution)/shard_map/ppermute | solution.py:836
  27.2 11.3 %copy-start.6 = (bf16[3,3,3,128,128]{4,3,2,1,0:T(8,128)(2,1)S(1)}, bf16[3,3,3,128,128]{4,3,2,1,0:T(8,128)(2,1)}, u32[]{:S(2)}) copy-start(bf16[3,3,3,128,128]{4,3,2,1,0:T(8,128)(2,1)} %refs_5_.4) | copy-start | bytes 2654212
  27.2 8.2 %collective-permute-start.10 = (bf16[18,64,128]{2,1,0:T(8,128)(2,1)S(1)}, bf16[18,64,128]{2,1,0:T(8,128)(2,1)S(1)}, u32[]{:S(2)}, u32[]{:S(2)}) collective-permute-start(bf16[18,64,128]{2,1,0:T(8,128)(2,1)S(1)} %get-tuple-element.119), channel_id=1, source_target_pairs={{0,2},{4,6},{8,10},{12,14},{16,18},{20,22},{24,26},{28,30},{2,0},{... | collective-permute-start | bytes 884744 | tf_op jit(solution)/shard_map/ppermute | solution.py:836
  35.4 5.7 %collective-permute-start.11 = (bf16[4,4,16,128]{3,2,1,0:T(8,128)(2,1)S(1)}, bf16[4,4,16,128]{3,2,1,0:T(8,128)(2,1)S(1)}, u32[]{:S(2)}, u32[]{:S(2)}) collective-permute-start(bf16[4,4,16,128]{3,2,1,0:T(8,128)(2,1)S(1)} %get-tuple-element.120), channel_id=1, source_target_pairs={{0,6},{2,4},{4,2},{6,0},{8,14},{10,12},{12,10},{14,8},{16,22},{18,... | collective-permute-start | bytes 196616 | tf_op jit(solution)/shard_map/ppermute | solution.py:847
  37.7 4.8 %collective-permute-start.12 = (bf16[4,4,16,128]{3,2,1,0:T(8,128)(2,1)S(1)}, bf16[4,4,16,128]{3,2,1,0:T(8,128)(2,1)S(1)}, u32[]{:S(2)}, u32[]{:S(2)}) collective-permute-start(bf16[4,4,16,128]{3,2,1,0:T(8,128)(2,1)S(1)} %get-tuple-element.121), channel_id=1, source_target_pairs={{0,4},{2,6},{4,0},{6,2},{8,12},{10,14},{12,8},{14,10},{16,20},{18,... | collective-permute-start | bytes 196616 | tf_op jit(solution)/shard_map/ppermute | solution.py:847
  38.4 4.1 %collective-permute-start.13 = (bf16[4,4,16,128]{3,2,1,0:T(8,128)(2,1)S(1)}, bf16[4,4,16,128]{3,2,1,0:T(8,128)(2,1)S(1)}, u32[]{:S(2)}, u32[]{:S(2)}) collective-permute-start(bf16[4,4,16,128]{3,2,1,0:T(8,128)(2,1)S(1)} %get-tuple-element.122), channel_id=1, source_target_pairs={{0,2},{2,0},{4,6},{6,4},{8,10},{10,8},{12,14},{14,12},{16,18},{18,... | collective-permute-start | bytes 196616 | tf_op jit(solution)/shard_map/ppermute | solution.py:847
  42.5 6.2 %collective-permute-start.15 = (bf16[4,4,16,128]{3,2,1,0:T(8,128)(2,1)S(1)}, bf16[4,4,16,128]{3,2,1,0:T(8,128)(2,1)S(1)}, u32[]{:S(2)}, u32[]{:S(2)}) collective-permute-start(bf16[4,4,16,128]{3,2,1,0:T(8,128)(2,1)S(1)} %get-tuple-element.131), channel_id=1, source_target_pairs={{0,24},{2,26},{4,28},{6,30},{8,16},{10,18},{12,20},{14,22},{16,8},... | collective-permute-start | bytes 196616 | tf_op jit(solution)/shard_map/ppermute | solution.py:847
  45.5 6.6 %collective-permute-start.17 = (bf16[4,4,16,128]{3,2,1,0:T(8,128)(2,1)S(1)}, bf16[4,4,16,128]{3,2,1,0:T(8,128)(2,1)S(1)}, u32[]{:S(2)}, u32[]{:S(2)}) collective-permute-start(bf16[4,4,16,128]{3,2,1,0:T(8,128)(2,1)S(1)} %get-tuple-element.132), channel_id=1, source_target_pairs={{0,16},{2,18},{4,20},{6,22},{8,24},{10,26},{12,28},{14,30},{16,0},... | collective-permute-start | bytes 196616 | tf_op jit(solution)/shard_map/ppermute | solution.py:847
  46.4 5.8 %collective-permute-start.18 = (bf16[4,4,16,128]{3,2,1,0:T(8,128)(2,1)S(1)}, bf16[4,4,16,128]{3,2,1,0:T(8,128)(2,1)S(1)}, u32[]{:S(2)}, u32[]{:S(2)}) collective-permute-start(bf16[4,4,16,128]{3,2,1,0:T(8,128)(2,1)S(1)} %get-tuple-element.133), channel_id=1, source_target_pairs={{0,8},{2,10},{4,12},{6,14},{8,0},{10,2},{12,4},{14,6},{16,24},{18,... | collective-permute-start | bytes 196616 | tf_op jit(solution)/shard_map/ppermute | solution.py:847
  47.0 9.4 %collective-permute-start.14 = (bf16[1,4,4,16,128]{4,3,2,1,0:T(8,128)(2,1)S(1)}, bf16[1,4,4,16,128]{4,3,2,1,0:T(8,128)(2,1)S(1)}, u32[]{:S(2)}, u32[]{:S(2)}) collective-permute-start(bf16[1,4,4,16,128]{4,3,2,1,0:T(8,128)(2,1)S(1)} %bitcast.8), channel_id=1, source_target_pairs={{0,1},{1,0},{2,3},{3,2},{4,5},{5,4},{6,7},{7,6},{8,9},{9,8},{10,11... | collective-permute-start | bytes 196616 | tf_op jit(solution)/shard_map/ppermute | solution.py:851
  48.8 7.6 %collective-permute-start.16 = (bf16[1,4,4,16,128]{4,3,2,1,0:T(8,128)(2,1)S(1)}, bf16[1,4,4,16,128]{4,3,2,1,0:T(8,128)(2,1)S(1)}, u32[]{:S(2)}, u32[]{:S(2)}) collective-permute-start(bf16[1,4,4,16,128]{4,3,2,1,0:T(8,128)(2,1)S(1)} %bitcast.9), channel_id=1, source_target_pairs={{0,1},{1,0},{2,3},{3,2},{4,5},{5,4},{6,7},{7,6},{8,9},{9,8},{10,11... | collective-permute-start | bytes 196616 | tf_op jit(solution)/shard_map/ppermute | solution.py:851
  52.2 3.2 %copy-start = (bf16[4,1024,256]{2,1,0:T(8,128)(2,1)S(1)}, bf16[4,1024,256]{2,1,0:T(8,128)(2,1)}, u32[]{:S(2)}) copy-start(bf16[4,1024,256]{2,1,0:T(8,128)(2,1)} %constant.21.clone.table_ref) | copy-start | bytes 6291460
  52.2 3.2 %copy-start.5 = (f32[128]{0:T(128)S(1)}, f32[128]{0:T(128)}, u32[]{:S(2)}) copy-start(f32[128]{0:T(128)} %param.11) | copy-start | bytes 1540
  52.2 5.0 %collective-permute-start.19 = (bf16[2,4,4,16,128]{4,3,2,1,0:T(8,128)(2,1)S(1)}, bf16[2,4,4,16,128]{4,3,2,1,0:T(8,128)(2,1)S(1)}, u32[]{:S(2)}, u32[]{:S(2)}) collective-permute-start(bf16[2,4,4,16,128]{4,3,2,1,0:T(8,128)(2,1)S(1)} %shard_map.94), channel_id=1, source_target_pairs={{0,1},{1,0},{2,3},{3,2},{4,5},{5,4},{6,7},{7,6},{8,9},{9,8},{10,11... | collective-permute-start | bytes 393224 | tf_op jit(solution)/shard_map/ppermute | solution.py:851

commit v13 on v12

--- a/solution.py
+++ b/solution.py
@@ -482,7 +482,8 @@
 def convolution_kernel(x, cells_x, width, shards, shards_y, me_ref, *refs):
     flow_ref, paired_ref, other_ref, front_ref, back_ref, kernel_ref, out_ref, padded = refs
     _, cells_y, cells_z, channels = out_ref.shape
-    own_y, _, _ = place(me_ref[0], shards)
+    own_y, own_outer, own_inner = place(me_ref[0], shards)
+    own_x = own_outer * shards[1] + own_inner
     even = is_even(me_ref[0], shards)
     for plane in range(width + 2):
         p = x + plane - 1
@@ -495,12 +496,17 @@
             padded[plane, cells_y + 1] = jnp.where(last, jnp.zeros_like(row), row)
         else:
             use_paired = jnp.logical_not(even) if p < 0 else even
-
-            @pl.when(use_paired)
+            outside = own_x == (0 if p < 0 else shards[0] * shards[1] - 1)
+
+            @pl.when(outside)
+            def _(plane=plane):
+                padded[plane] = jnp.zeros(padded.shape[1:], padded.dtype)
+
+            @pl.when(jnp.logical_and(jnp.logical_not(outside), use_paired))
             def _(plane=plane):
                 padded[plane] = paired_ref[...]
 
-            @pl.when(jnp.logical_not(use_paired))
+            @pl.when(jnp.logical_not(jnp.logical_or(outside, use_paired)))
             def _(plane=plane):
                 padded[plane] = other_ref[...]
 
@@ -833,7 +839,9 @@
 def with_neighbour(array, start, axis):
     size = lax.axis_size(axis)
     pairs = [(i, i + 1) for i in range(start, size - 1, 2)]
-    return lax.ppermute(array, axis, pairs + [(j, i) for i, j in pairs])
+    alone = set(range(size)) - {i for pair in pairs for i in pair}
+    pairs += [(j, i) for i, j in pairs] + [(i, i) for i in sorted(alone)]
+    return lax.ppermute(array, axis, pairs)
 
 
 def exchange(array, step, shards, along_outer):

time: 59.9 us -> 59.9 us (level)
  no operation moved by 1% of the time
where the time goes in v13:
time: 59.9 us; the launch traced here: 59.8 us
  Pallas kernels  27.6 us (46%)
  starting transfers between devices  22.9 us (38%)
  waiting for transfers between devices  8.96 us (15%)
    ppermute x12, starting transfers between devices, exchange(): return lax.ppermute(array, 'gx', pairs)  14.3 us
    pallas_call x3, Pallas kernels, preload(): pl.pallas_call(functools.partial(preload_kernel, 2 * pair), in_specs=[pl....  9.15 us
    ppermute x12, waiting for transfers between devices, exchange(): return lax.ppermute(array, 'gx', pairs)  7.64 us
    pallas_call x1, Pallas kernels, mixing(): pl.pallas_call(functools.partial(mixing_kernel, shards, len(loaded)), in_...  6.07 us
    ppermute x6, starting transfers between devices, over_y(): lax.ppermute(array, 'gy', [(i, (i + step) % shards_y) for i in range(shar...  5.8 us
    pallas_call x2, Pallas kernels, convolution(): pl.pallas_call(functools.partial(convolution_kernel, x, cells_x, width, s...  5.24 us
    pallas_call x2, Pallas kernels, forward_yz(): pl.pallas_call(kernel, in_specs=[IN_SMEM] + specs, out_specs=in_vmem(len(...  3.43 us
    ppermute x2, starting transfers between devices, with_neighbour(): return lax.ppermute(array, axis, pairs)  2.78 us
  transfers between devices with their start and end apart: 20, of which 7 were waited for; matrix products, arithmetic and copies ran while one was open for 0% of the time, Pallas kernels for 37%

profile of v13, /device:TPU:0, one launch (start us, length us, event | category | flops | bytes accessed | tf_op | source)
XLA Modules:
  0.0 59.8 jit_solution(6786704570454778799)
XLA Ops:
  0.0 3.0 %shard_map.82 = (bf16[2,4,4,16,128]{4,3,2,1,0:T(8,128)(2,1)}, bf16[2,4,4,16,128]{4,3,2,1,0:T(8,128)(2,1)}) custom-call(s32[1]{0:T(128)} %bitcast.me_ref, bf16[2,512,1024]{2,1,0:T(8,128)(2,1)} %constant.18.clone.table_ref, bf16[4,1024,128]{2,1,0:T(8,128)(2,1)} %bitcast.6), custom_call_target="tpu_custom_call" | custom-call | flops 268435456 | bytes 1572864 | tf_op jit(solution)/shard_map/pallas_call | solution.py:224
  3.0 0.0 copy-start.1
  3.0 0.0 copy-start.2
  3.0 3.0 %collective-permute-start.2 = (bf16[2,4,4,16,128]{4,3,2,1,0:T(8,128)(2,1)}, bf16[2,4,4,16,128]{4,3,2,1,0:T(8,128)(2,1)S(1)}, u32[]{:S(2)}, u32[]{:S(2)}) collective-permute-start(bf16[2,4,4,16,128]{4,3,2,1,0:T(8,128)(2,1)} %get-tuple-element.80), channel_id=1, source_target_pairs={{0,1},{1,0},{2,3},{3,2},{4,5},{5,4},{6,7},{7,6},{8,9},{9,8},{10,11... | collective-permute-start | bytes 393224 | tf_op jit(solution)/shard_map/ppermute | solution.py:859
  6.0 0.1 collective-permute-start
  6.1 3.5 %shard_map.83.refs_7_ = bf16[4,64,128,128]{3,2,1,0:T(8,128)(2,1)S(1)} custom-call(bf16[16,64,128,128]{3,2,1,0:T(8,128)(2,1)} %bitcast.11), custom_call_target="tpu_custom_call" | custom-call | bytes 8388608 | tf_op jit(solution)/shard_map/pallas_call | solution.py:341
  9.6 0.4 shard_map.84
  10.1 0.5 collective-permute-done.2.refs_1_
  10.6 3.2 %collective-permute-start.3 = (bf16[4,4,16,128]{3,2,1,0:T(8,128)(2,1)S(1)}, bf16[4,4,16,128]{3,2,1,0:T(8,128)(2,1)S(1)}, u32[]{:S(2)}, u32[]{:S(2)}) collective-permute-start(bf16[4,4,16,128]{3,2,1,0:T(8,128)(2,1)S(1)} %get-tuple-element.81), channel_id=1, source_target_pairs={{0,16},{2,18},{4,20},{6,22},{8,24},{10,26},{12,28},{14,30},{16,0},... | collective-permute-start | bytes 196616 | tf_op jit(solution)/shard_map/ppermute | solution.py:855
  13.8 1.4 %collective-permute-start.4 = (bf16[4,4,16,128]{3,2,1,0:T(8,128)(2,1)S(1)}, bf16[4,4,16,128]{3,2,1,0:T(8,128)(2,1)S(1)}, u32[]{:S(2)}, u32[]{:S(2)}) collective-permute-start(bf16[4,4,16,128]{3,2,1,0:T(8,128)(2,1)S(1)} %get-tuple-element.82), channel_id=1, source_target_pairs={{0,24},{2,26},{4,28},{6,30},{8,16},{10,18},{12,20},{14,22},{16,8},... | collective-permute-start | bytes 196616 | tf_op jit(solution)/shard_map/ppermute | solution.py:855
  15.2 0.0 collective-permute-done.refs_1_
  15.2 0.3 collective-permute-start.1
  15.5 1.5 %collective-permute-start.8 = (bf16[4,64,128]{2,1,0:T(8,128)(2,1)S(1)}, bf16[4,64,128]{2,1,0:T(8,128)(2,1)S(1)}, u32[]{:S(2)}, u32[]{:S(2)}) collective-permute-start(bf16[4,64,128]{2,1,0:T(8,128)(2,1)S(1)} %get-tuple-element.102), channel_id=1, source_target_pairs={{0,1},{1,0},{2,3},{3,2},{4,5},{5,4},{6,7},{7,6},{8,9},{9,8},{10,11... | collective-permute-start | bytes 196616 | tf_op jit(solution)/shard_map/ppermute | solution.py:859
  17.0 3.5 %shard_map.87.refs_8_ = bf16[4,64,128,128]{3,2,1,0:T(8,128)(2,1)S(1)} custom-call(bf16[16,64,128,128]{3,2,1,0:T(8,128)(2,1)} %bitcast.12), custom_call_target="tpu_custom_call" | custom-call | bytes 8388608 | tf_op jit(solution)/shard_map/pallas_call | solution.py:341
  20.5 0.0 collective-permute-done.4.refs_0_
  20.5 0.0 collective-permute-done.1.refs_2_
  20.6 0.0 copy-start.3
  20.6 0.0 copy-start.4
  20.6 0.1 collective-permute-start.5
  20.7 1.6 %collective-permute-start.6 = (bf16[4,4,16,128]{3,2,1,0:T(8,128)(2,1)S(1)}, bf16[4,4,16,128]{3,2,1,0:T(8,128)(2,1)S(1)}, u32[]{:S(2)}, u32[]{:S(2)}) collective-permute-start(bf16[4,4,16,128]{3,2,1,0:T(8,128)(2,1)S(1)} %get-tuple-element.94), channel_id=1, source_target_pairs={{0,4},{2,6},{4,0},{6,2},{8,12},{10,14},{12,8},{14,10},{16,20},{18,... | collective-permute-start | bytes 196616 | tf_op jit(solution)/shard_map/ppermute | solution.py:855
  22.2 0.3 collective-permute-start.7
  22.5 2.2 %shard_map.89.refs_9_ = bf16[2,64,128,128]{3,2,1,0:T(8,128)(2,1)S(1)} custom-call(bf16[16,64,128,128]{3,2,1,0:T(8,128)(2,1)} %bitcast.13), custom_call_target="tpu_custom_call" | custom-call | bytes 4194304 | tf_op jit(solution)/shard_map/pallas_call | solution.py:341
  24.7 0.3 collective-permute-done.5.refs_0_
  25.0 1.5 %collective-permute-done.6.refs_1_ = bf16[4,4,16,128]{3,2,1,0:T(8,128)(2,1)S(1)} collective-permute-done((bf16[4,4,16,128]{3,2,1,0:T(8,128)(2,1)S(1)}, bf16[4,4,16,128]{3,2,1,0:T(8,128)(2,1)S(1)}, u32[]{:S(2)}, u32[]{:S(2)}) %collective-permute-start.6) | collective-permute-done | bytes 65568 | tf_op jit(solution)/shard_map/ppermute | solution.py:855
  26.4 0.1 shard_map.91
  26.5 0.7 %collective-permute-start.9 = (bf16[18,64,128]{2,1,0:T(8,128)(2,1)S(1)}, bf16[18,64,128]{2,1,0:T(8,128)(2,1)S(1)}, u32[]{:S(2)}, u32[]{:S(2)}) collective-permute-start(bf16[18,64,128]{2,1,0:T(8,128)(2,1)S(1)} %get-tuple-element.118), channel_id=1, source_target_pairs={{2,4},{6,8},{10,12},{14,16},{18,20},{22,24},{26,28},{4,2},{8,6},{1... | collective-permute-start | bytes 884744 | tf_op jit(solution)/shard_map/ppermute | solution.py:844
  27.2 0.0 copy-start.6
  27.2 2.1 %collective-permute-start.10 = (bf16[18,64,128]{2,1,0:T(8,128)(2,1)S(1)}, bf16[18,64,128]{2,1,0:T(8,128)(2,1)S(1)}, u32[]{:S(2)}, u32[]{:S(2)}) collective-permute-start(bf16[18,64,128]{2,1,0:T(8,128)(2,1)S(1)} %get-tuple-element.119), channel_id=1, source_target_pairs={{0,2},{4,6},{8,10},{12,14},{16,18},{20,22},{24,26},{28,30},{2,0},{... | collective-permute-start | bytes 884744 | tf_op jit(solution)/shard_map/ppermute | solution.py:844
  29.3 6.1 %shard_map.90 = (bf16[4,4,16,128]{3,2,1,0:T(8,128)(2,1)S(1)}, bf16[4,4,16,128]{3,2,1,0:T(8,128)(2,1)S(1)}, bf16[4,4,16,128]{3,2,1,0:T(8,128)(2,1)S(1)}, bf16[4,4,16,128]{3,2,1,0:T(8,128)(2,1)S(1)}) custom-call(s32[1]{0:T(128)} %bitcast.me_ref, bf16[4,4,16,128]{3,2,1,0:T(8,128)(2,1)S(1)} %collective-permute-done.5.refs_0_, ...), custom_call_target="tpu_custom_call" | custom-call | flops 134217728 | bytes 33554432 | tf_op jit(solution)/shard_map/pallas_call | solution.py:460
  35.4 2.3 %collective-permute-start.11 = (bf16[4,4,16,128]{3,2,1,0:T(8,128)(2,1)S(1)}, bf16[4,4,16,128]{3,2,1,0:T(8,128)(2,1)S(1)}, u32[]{:S(2)}, u32[]{:S(2)}) collective-permute-start(bf16[4,4,16,128]{3,2,1,0:T(8,128)(2,1)S(1)} %get-tuple-element.120), channel_id=1, source_target_pairs={{0,6},{2,4},{4,2},{6,0},{8,14},{10,12},{12,10},{14,8},{16,22},{18,... | collective-permute-start | bytes 196616 | tf_op jit(solution)/shard_map/ppermute | solution.py:855
  37.7 0.7 %collective-permute-start.12 = (bf16[4,4,16,128]{3,2,1,0:T(8,128)(2,1)S(1)}, bf16[4,4,16,128]{3,2,1,0:T(8,128)(2,1)S(1)}, u32[]{:S(2)}, u32[]{:S(2)}) collective-permute-start(bf16[4,4,16,128]{3,2,1,0:T(8,128)(2,1)S(1)} %get-tuple-element.121), channel_id=1, source_target_pairs={{0,4},{2,6},{4,0},{6,2},{8,12},{10,14},{12,8},{14,10},{16,20},{18,... | collective-permute-start | bytes 196616 | tf_op jit(solution)/shard_map/ppermute | solution.py:855
  38.4 0.1 collective-permute-start.13
  38.5 2.6 %shard_map.92.refs_4_ = bf16[2,16,64,128]{3,2,1,0:T(8,128)(2,1)S(1)} custom-call(s32[1]{0:T(128)} %bitcast.me_ref, bf16[4,16,64,128]{3,2,1,0:T(8,128)(2,1)S(1)} %copy-done.2, bf16[18,64,128]{2,1,0:T(8,128)(2,1)S(1)} %collective-permute-done.10.refs_1_, bf16[18,64,128]{2,1,0:T(8,128)(2,1)S(1)} %collective-permute-done.9.refs_2_, ...), custom_call_target="tpu_custom_call" | custom-call | flops 2717908992 | bytes 1310720 | tf_op jit(solution)/shard_map/pallas_call | solution.py:552
  41.2 1.3 %collective-permute-done.12.refs_1_ = bf16[4,4,16,128]{3,2,1,0:T(8,128)(2,1)S(1)} collective-permute-done((bf16[4,4,16,128]{3,2,1,0:T(8,128)(2,1)S(1)}, bf16[4,4,16,128]{3,2,1,0:T(8,128)(2,1)S(1)}, u32[]{:S(2)}, u32[]{:S(2)}) %collective-permute-start.12) | collective-permute-done | bytes 65568 | tf_op jit(solution)/shard_map/ppermute | solution.py:855
  42.5 3.0 %collective-permute-start.15 = (bf16[4,4,16,128]{3,2,1,0:T(8,128)(2,1)S(1)}, bf16[4,4,16,128]{3,2,1,0:T(8,128)(2,1)S(1)}, u32[]{:S(2)}, u32[]{:S(2)}) collective-permute-start(bf16[4,4,16,128]{3,2,1,0:T(8,128)(2,1)S(1)} %get-tuple-element.131), channel_id=1, source_target_pairs={{0,24},{2,26},{4,28},{6,30},{8,16},{10,18},{12,20},{14,22},{16,8},... | collective-permute-start | bytes 196616 | tf_op jit(solution)/shard_map/ppermute | solution.py:855
  45.5 0.9 %collective-permute-start.17 = (bf16[4,4,16,128]{3,2,1,0:T(8,128)(2,1)S(1)}, bf16[4,4,16,128]{3,2,1,0:T(8,128)(2,1)S(1)}, u32[]{:S(2)}, u32[]{:S(2)}) collective-permute-start(bf16[4,4,16,128]{3,2,1,0:T(8,128)(2,1)S(1)} %get-tuple-element.132), channel_id=1, source_target_pairs={{0,16},{2,18},{4,20},{6,22},{8,24},{10,26},{12,28},{14,30},{16,0},... | collective-permute-start | bytes 196616 | tf_op jit(solution)/shard_map/ppermute | solution.py:855
  46.4 0.6 %collective-permute-start.18 = (bf16[4,4,16,128]{3,2,1,0:T(8,128)(2,1)S(1)}, bf16[4,4,16,128]{3,2,1,0:T(8,128)(2,1)S(1)}, u32[]{:S(2)}, u32[]{:S(2)}) collective-permute-start(bf16[4,4,16,128]{3,2,1,0:T(8,128)(2,1)S(1)} %get-tuple-element.133), channel_id=1, source_target_pairs={{0,8},{2,10},{4,12},{6,14},{8,0},{10,2},{12,4},{14,6},{16,24},{18,... | collective-permute-start | bytes 196616 | tf_op jit(solution)/shard_map/ppermute | solution.py:855
  47.0 0.3 collective-permute-start.14
  47.3 1.5 %collective-permute-done.15.refs_0_ = bf16[4,4,16,128]{3,2,1,0:T(8,128)(2,1)S(1)} collective-permute-done((bf16[4,4,16,128]{3,2,1,0:T(8,128)(2,1)S(1)}, bf16[4,4,16,128]{3,2,1,0:T(8,128)(2,1)S(1)}, u32[]{:S(2)}, u32[]{:S(2)}) %collective-permute-start.15) | collective-permute-done | bytes 65568 | tf_op jit(solution)/shard_map/ppermute | solution.py:855
  48.8 0.3 collective-permute-start.16
  49.1 3.0 %collective-permute-done.17.refs_0_.refs_1_ = bf16[4,4,16,128]{3,2,1,0:T(8,128)(2,1)S(1)} collective-permute-done((bf16[4,4,16,128]{3,2,1,0:T(8,128)(2,1)S(1)}, bf16[4,4,16,128]{3,2,1,0:T(8,128)(2,1)S(1)}, u32[]{:S(2)}, u32[]{:S(2)}) %collective-permute-start.17) | collective-permute-done | bytes 65568 | tf_op jit(solution)/shard_map/ppermute | solution.py:855
  52.2 0.0 copy-start
  52.2 0.0 copy-start.5
  52.2 0.6 collective-permute-start.19
  52.8 2.6 %shard_map.95.refs_5_ = bf16[2,16,64,128]{3,2,1,0:T(8,128)(2,1)S(1)} custom-call(s32[1]{0:T(128)} %bitcast.me_ref, bf16[4,16,64,128]{3,2,1,0:T(8,128)(2,1)S(1)} %copy-done.2, bf16[18,64,128]{2,1,0:T(8,128)(2,1)S(1)} %collective-permute-done.10.refs_1_, bf16[18,64,128]{2,1,0:T(8,128)(2,1)S(1)} %collective-permute-done.9.refs_2_, ...), custom_call_target="tpu_custom_call" | custom-call | flops 2717908992 | bytes 1310720 | tf_op jit(solution)/shard_map/pallas_call | solution.py:552
  55.4 1.0 %shard_map.96.refs_3_ = f32[4,16,64,128]{3,2,1,0:T(8,128)S(1)} custom-call(s32[1]{0:T(128)} %bitcast.me_ref, bf16[4,1024,256]{2,1,0:T(8,128)(2,1)S(1)} %copy-done, bf16[4,4,16,128]{3,2,1,0:T(8,128)(2,1)S(1)} %collective-permute-done.15.refs_0_, bf16[4,4,16,128]{3,2,1,0:T(8,128)(2,1)S(1)} %collective-permute-done.17.refs_0_.refs_1_, ...), custom_call_target="tpu_custom_call" | custom-call | flops 268435456 | bytes 3145728 | tf_op jit(solution)/shard_map/pallas_call | solution.py:678
  56.4 0.8 %collective-permute-done.19.refs_2_ = bf16[2,4,4,16,128]{4,3,2,1,0:T(8,128)(2,1)S(1)} collective-permute-done((bf16[2,4,4,16,128]{4,3,2,1,0:T(8,128)(2,1)S(1)}, bf16[2,4,4,16,128]{4,3,2,1,0:T(8,128)(2,1)S(1)}, u32[]{:S(2)}, u32[]{:S(2)}) %collective-permute-start.19) | collective-permute-done | bytes 131104 | tf_op jit(solution)/shard_map/ppermute | solution.py:859
  57.2 2.5 %shard_map.97 = bf16[4,16,64,128]{3,2,1,0:T(8,128)(2,1)} custom-call(s32[1]{0:T(128)} %bitcast.me_ref, bf16[4,1024,256]{2,1,0:T(8,128)(2,1)S(1)} %copy-done, bf16[1,4,4,16,128]{4,3,2,1,0:T(8,128)(2,1)S(1)} %collective-permute-done.14.refs_0_, bf16[1,4,4,16,128]{4,3,2,1,0:T(8,128)(2,1)S(1)} %collective-permute-done.16.refs_1_, ...), custom_call_target="tpu_custom_call" | custom-call | flops 268435456 | bytes 3145728 | tf_op jit(solution)/shard_map/pallas_call | solution.py:698
  (22 shorter events, 0.2 us)
Async XLA Ops:
  3.0 6.6 %copy-start.1 = (bf16[2,512,1024]{2,1,0:T(8,128)(2,1)S(1)}, bf16[2,512,1024]{2,1,0:T(8,128)(2,1)}, u32[]{:S(2)}) copy-start(bf16[2,512,1024]{2,1,0:T(8,128)(2,1)} %constant.18.clone.table_ref) | copy-start | bytes 6291460
  3.0 6.6 %copy-start.2 = (bf16[4,16,64,128]{3,2,1,0:T(8,128)(2,1)S(1)}, bf16[4,16,64,128]{3,2,1,0:T(8,128)(2,1)}, u32[]{:S(2)}) copy-start(bf16[4,16,64,128]{3,2,1,0:T(8,128)(2,1)} %refs_0_.3) | copy-start | bytes 3145732
  3.0 7.6 %collective-permute-start.2 = (bf16[2,4,4,16,128]{4,3,2,1,0:T(8,128)(2,1)}, bf16[2,4,4,16,128]{4,3,2,1,0:T(8,128)(2,1)S(1)}, u32[]{:S(2)}, u32[]{:S(2)}) collective-permute-start(bf16[2,4,4,16,128]{4,3,2,1,0:T(8,128)(2,1)} %get-tuple-element.80), channel_id=1, source_target_pairs={{0,1},{1,0},{2,3},{3,2},{4,5},{5,4},{6,7},{7,6},{8,9},{9,8},{10,11... | collective-permute-start | bytes 393224 | tf_op jit(solution)/shard_map/ppermute | solution.py:859
  6.0 9.1 %collective-permute-start = (bf16[2,4,4,16,128]{4,3,2,1,0:T(8,128)(2,1)}, bf16[2,4,4,16,128]{4,3,2,1,0:T(8,128)(2,1)S(1)}, u32[]{:S(2)}, u32[]{:S(2)}) collective-permute-start(bf16[2,4,4,16,128]{4,3,2,1,0:T(8,128)(2,1)} %get-tuple-element.76), channel_id=1, source_target_pairs={{0,1},{1,0},{2,3},{3,2},{4,5},{5,4},{6,7},{7,6},{8,9},{9,8},{10,11... | collective-permute-start | bytes 393224 | tf_op jit(solution)/shard_map/ppermute | solution.py:859
  10.6 9.9 %collective-permute-start.3 = (bf16[4,4,16,128]{3,2,1,0:T(8,128)(2,1)S(1)}, bf16[4,4,16,128]{3,2,1,0:T(8,128)(2,1)S(1)}, u32[]{:S(2)}, u32[]{:S(2)}) collective-permute-start(bf16[4,4,16,128]{3,2,1,0:T(8,128)(2,1)S(1)} %get-tuple-element.81), channel_id=1, source_target_pairs={{0,16},{2,18},{4,20},{6,22},{8,24},{10,26},{12,28},{14,30},{16,0},... | collective-permute-start | bytes 196616 | tf_op jit(solution)/shard_map/ppermute | solution.py:855
  13.8 6.7 %collective-permute-start.4 = (bf16[4,4,16,128]{3,2,1,0:T(8,128)(2,1)S(1)}, bf16[4,4,16,128]{3,2,1,0:T(8,128)(2,1)S(1)}, u32[]{:S(2)}, u32[]{:S(2)}) collective-permute-start(bf16[4,4,16,128]{3,2,1,0:T(8,128)(2,1)S(1)} %get-tuple-element.82), channel_id=1, source_target_pairs={{0,24},{2,26},{4,28},{6,30},{8,16},{10,18},{12,20},{14,22},{16,8},... | collective-permute-start | bytes 196616 | tf_op jit(solution)/shard_map/ppermute | solution.py:855
  15.2 5.3 %collective-permute-start.1 = (bf16[4,4,16,128]{3,2,1,0:T(8,128)(2,1)S(1)}, bf16[4,4,16,128]{3,2,1,0:T(8,128)(2,1)S(1)}, u32[]{:S(2)}, u32[]{:S(2)}) collective-permute-start(bf16[4,4,16,128]{3,2,1,0:T(8,128)(2,1)S(1)} %get-tuple-element.78), channel_id=1, source_target_pairs={{0,8},{2,10},{4,12},{6,14},{8,0},{10,2},{12,4},{14,6},{16,24},{18,... | collective-permute-start | bytes 196616 | tf_op jit(solution)/shard_map/ppermute | solution.py:855
  15.5 9.2 %collective-permute-start.8 = (bf16[4,64,128]{2,1,0:T(8,128)(2,1)S(1)}, bf16[4,64,128]{2,1,0:T(8,128)(2,1)S(1)}, u32[]{:S(2)}, u32[]{:S(2)}) collective-permute-start(bf16[4,64,128]{2,1,0:T(8,128)(2,1)S(1)} %get-tuple-element.102), channel_id=1, source_target_pairs={{0,1},{1,0},{2,3},{3,2},{4,5},{5,4},{6,7},{7,6},{8,9},{9,8},{10,11... | collective-permute-start | bytes 196616 | tf_op jit(solution)/shard_map/ppermute | solution.py:859
  20.6 8.8 %copy-start.3 = (bf16[256,128]{1,0:T(8,128)(2,1)S(1)}, bf16[256,128]{1,0:T(8,128)(2,1)}, u32[]{:S(2)}) copy-start(bf16[256,128]{1,0:T(8,128)(2,1)} %constant.19.clone.refs_4_) | copy-start | bytes 196612
  20.6 8.7 %copy-start.4 = (bf16[128,128]{1,0:T(8,128)(2,1)S(1)}, bf16[128,128]{1,0:T(8,128)(2,1)}, u32[]{:S(2)}) copy-start(bf16[128,128]{1,0:T(8,128)(2,1)} %constant.20.clone.refs_5_) | copy-start | bytes 98308
  20.6 4.4 %collective-permute-start.5 = (bf16[4,4,16,128]{3,2,1,0:T(8,128)(2,1)S(1)}, bf16[4,4,16,128]{3,2,1,0:T(8,128)(2,1)S(1)}, u32[]{:S(2)}, u32[]{:S(2)}) collective-permute-start(bf16[4,4,16,128]{3,2,1,0:T(8,128)(2,1)S(1)} %get-tuple-element.93), channel_id=1, source_target_pairs={{0,6},{2,4},{4,2},{6,0},{8,14},{10,12},{12,10},{14,8},{16,22},{18,... | collective-permute-start | bytes 196616 | tf_op jit(solution)/shard_map/ppermute | solution.py:855
  20.7 5.8 %collective-permute-start.6 = (bf16[4,4,16,128]{3,2,1,0:T(8,128)(2,1)S(1)}, bf16[4,4,16,128]{3,2,1,0:T(8,128)(2,1)S(1)}, u32[]{:S(2)}, u32[]{:S(2)}) collective-permute-start(bf16[4,4,16,128]{3,2,1,0:T(8,128)(2,1)S(1)} %get-tuple-element.94), channel_id=1, source_target_pairs={{0,4},{2,6},{4,0},{6,2},{8,12},{10,14},{12,8},{14,10},{16,20},{18,... | collective-permute-start | bytes 196616 | tf_op jit(solution)/shard_map/ppermute | solution.py:855
  22.2 4.2 %collective-permute-start.7 = (bf16[4,4,16,128]{3,2,1,0:T(8,128)(2,1)S(1)}, bf16[4,4,16,128]{3,2,1,0:T(8,128)(2,1)S(1)}, u32[]{:S(2)}, u32[]{:S(2)}) collective-permute-start(bf16[4,4,16,128]{3,2,1,0:T(8,128)(2,1)S(1)} %get-tuple-element.95), channel_id=1, source_target_pairs={{0,2},{2,0},{4,6},{6,4},{8,10},{10,8},{12,14},{14,12},{16,18},{18,... | collective-permute-start | bytes 196616 | tf_op jit(solution)/shard_map/ppermute | solution.py:855
  26.5 8.9 %collective-permute-start.9 = (bf16[18,64,128]{2,1,0:T(8,128)(2,1)S(1)}, bf16[18,64,128]{2,1,0:T(8,128)(2,1)S(1)}, u32[]{:S(2)}, u32[]{:S(2)}) collective-permute-start(bf16[18,64,128]{2,1,0:T(8,128)(2,1)S(1)} %get-tuple-element.118), channel_id=1, source_target_pairs={{2,4},{6,8},{10,12},{14,16},{18,20},{22,24},{26,28},{4,2},{8,6},{1... | collective-permute-start | bytes 884744 | tf_op jit(solution)/shard_map/ppermute | solution.py:844
  27.2 11.3 %copy-start.6 = (bf16[3,3,3,128,128]{4,3,2,1,0:T(8,128)(2,1)S(1)}, bf16[3,3,3,128,128]{4,3,2,1,0:T(8,128)(2,1)}, u32[]{:S(2)}) copy-start(bf16[3,3,3,128,128]{4,3,2,1,0:T(8,128)(2,1)} %refs_5_.4) | copy-start | bytes 2654212
  27.2 8.2 %collective-permute-start.10 = (bf16[18,64,128]{2,1,0:T(8,128)(2,1)S(1)}, bf16[18,64,128]{2,1,0:T(8,128)(2,1)S(1)}, u32[]{:S(2)}, u32[]{:S(2)}) collective-permute-start(bf16[18,64,128]{2,1,0:T(8,128)(2,1)S(1)} %get-tuple-element.119), channel_id=1, source_target_pairs={{0,2},{4,6},{8,10},{12,14},{16,18},{20,22},{24,26},{28,30},{2,0},{... | collective-permute-start | bytes 884744 | tf_op jit(solution)/shard_map/ppermute | solution.py:844
  35.4 5.8 %collective-permute-start.11 = (bf16[4,4,16,128]{3,2,1,0:T(8,128)(2,1)S(1)}, bf16[4,4,16,128]{3,2,1,0:T(8,128)(2,1)S(1)}, u32[]{:S(2)}, u32[]{:S(2)}) collective-permute-start(bf16[4,4,16,128]{3,2,1,0:T(8,128)(2,1)S(1)} %get-tuple-element.120), channel_id=1, source_target_pairs={{0,6},{2,4},{4,2},{6,0},{8,14},{10,12},{12,10},{14,8},{16,22},{18,... | collective-permute-start | bytes 196616 | tf_op jit(solution)/shard_map/ppermute | solution.py:855
  37.7 4.8 %collective-permute-start.12 = (bf16[4,4,16,128]{3,2,1,0:T(8,128)(2,1)S(1)}, bf16[4,4,16,128]{3,2,1,0:T(8,128)(2,1)S(1)}, u32[]{:S(2)}, u32[]{:S(2)}) collective-permute-start(bf16[4,4,16,128]{3,2,1,0:T(8,128)(2,1)S(1)} %get-tuple-element.121), channel_id=1, source_target_pairs={{0,4},{2,6},{4,0},{6,2},{8,12},{10,14},{12,8},{14,10},{16,20},{18,... | collective-permute-start | bytes 196616 | tf_op jit(solution)/shard_map/ppermute | solution.py:855
  38.4 4.1 %collective-permute-start.13 = (bf16[4,4,16,128]{3,2,1,0:T(8,128)(2,1)S(1)}, bf16[4,4,16,128]{3,2,1,0:T(8,128)(2,1)S(1)}, u32[]{:S(2)}, u32[]{:S(2)}) collective-permute-start(bf16[4,4,16,128]{3,2,1,0:T(8,128)(2,1)S(1)} %get-tuple-element.122), channel_id=1, source_target_pairs={{0,2},{2,0},{4,6},{6,4},{8,10},{10,8},{12,14},{14,12},{16,18},{18,... | collective-permute-start | bytes 196616 | tf_op jit(solution)/shard_map/ppermute | solution.py:855
  42.5 6.2 %collective-permute-start.15 = (bf16[4,4,16,128]{3,2,1,0:T(8,128)(2,1)S(1)}, bf16[4,4,16,128]{3,2,1,0:T(8,128)(2,1)S(1)}, u32[]{:S(2)}, u32[]{:S(2)}) collective-permute-start(bf16[4,4,16,128]{3,2,1,0:T(8,128)(2,1)S(1)} %get-tuple-element.131), channel_id=1, source_target_pairs={{0,24},{2,26},{4,28},{6,30},{8,16},{10,18},{12,20},{14,22},{16,8},... | collective-permute-start | bytes 196616 | tf_op jit(solution)/shard_map/ppermute | solution.py:855
  45.5 6.6 %collective-permute-start.17 = (bf16[4,4,16,128]{3,2,1,0:T(8,128)(2,1)S(1)}, bf16[4,4,16,128]{3,2,1,0:T(8,128)(2,1)S(1)}, u32[]{:S(2)}, u32[]{:S(2)}) collective-permute-start(bf16[4,4,16,128]{3,2,1,0:T(8,128)(2,1)S(1)} %get-tuple-element.132), channel_id=1, source_target_pairs={{0,16},{2,18},{4,20},{6,22},{8,24},{10,26},{12,28},{14,30},{16,0},... | collective-permute-start | bytes 196616 | tf_op jit(solution)/shard_map/ppermute | solution.py:855
  46.4 5.8 %collective-permute-start.18 = (bf16[4,4,16,128]{3,2,1,0:T(8,128)(2,1)S(1)}, bf16[4,4,16,128]{3,2,1,0:T(8,128)(2,1)S(1)}, u32[]{:S(2)}, u32[]{:S(2)}) collective-permute-start(bf16[4,4,16,128]{3,2,1,0:T(8,128)(2,1)S(1)} %get-tuple-element.133), channel_id=1, source_target_pairs={{0,8},{2,10},{4,12},{6,14},{8,0},{10,2},{12,4},{14,6},{16,24},{18,... | collective-permute-start | bytes 196616 | tf_op jit(solution)/shard_map/ppermute | solution.py:855
  47.0 9.4 %collective-permute-start.14 = (bf16[1,4,4,16,128]{4,3,2,1,0:T(8,128)(2,1)S(1)}, bf16[1,4,4,16,128]{4,3,2,1,0:T(8,128)(2,1)S(1)}, u32[]{:S(2)}, u32[]{:S(2)}) collective-permute-start(bf16[1,4,4,16,128]{4,3,2,1,0:T(8,128)(2,1)S(1)} %bitcast.8), channel_id=1, source_target_pairs={{0,1},{1,0},{2,3},{3,2},{4,5},{5,4},{6,7},{7,6},{8,9},{9,8},{10,11... | collective-permute-start | bytes 196616 | tf_op jit(solution)/shard_map/ppermute | solution.py:859
  48.8 7.6 %collective-permute-start.16 = (bf16[1,4,4,16,128]{4,3,2,1,0:T(8,128)(2,1)S(1)}, bf16[1,4,4,16,128]{4,3,2,1,0:T(8,128)(2,1)S(1)}, u32[]{:S(2)}, u32[]{:S(2)}) collective-permute-start(bf16[1,4,4,16,128]{4,3,2,1,0:T(8,128)(2,1)S(1)} %bitcast.9), channel_id=1, source_target_pairs={{0,1},{1,0},{2,3},{3,2},{4,5},{5,4},{6,7},{7,6},{8,9},{9,8},{10,11... | collective-permute-start | bytes 196616 | tf_op jit(solution)/shard_map/ppermute | solution.py:859
  52.2 3.2 %copy-start = (bf16[4,1024,256]{2,1,0:T(8,128)(2,1)S(1)}, bf16[4,1024,256]{2,1,0:T(8,128)(2,1)}, u32[]{:S(2)}) copy-start(bf16[4,1024,256]{2,1,0:T(8,128)(2,1)} %constant.21.clone.table_ref) | copy-start | bytes 6291460
  52.2 3.2 %copy-start.5 = (f32[128]{0:T(128)S(1)}, f32[128]{0:T(128)}, u32[]{:S(2)}) copy-start(f32[128]{0:T(128)} %param.11) | copy-start | bytes 1540
  52.2 5.0 %collective-permute-start.19 = (bf16[2,4,4,16,128]{4,3,2,1,0:T(8,128)(2,1)S(1)}, bf16[2,4,4,16,128]{4,3,2,1,0:T(8,128)(2,1)S(1)}, u32[]{:S(2)}, u32[]{:S(2)}) collective-permute-start(bf16[2,4,4,16,128]{4,3,2,1,0:T(8,128)(2,1)S(1)} %shard_map.94), channel_id=1, source_target_pairs={{0,1},{1,0},{2,3},{3,2},{4,5},{5,4},{6,7},{7,6},{8,9},{9,8},{10,11... | collective-permute-start | bytes 393224 | tf_op jit(solution)/shard_map/ppermute | solution.py:859

commit v14 on v12

--- a/solution.py
+++ b/solution.py
@@ -504,7 +504,7 @@
             def _(plane=plane):
                 padded[plane] = other_ref[...]
 
-    rows = 8 if cells_y % 8 == 0 else 1
+    rows = 16 if cells_y % 16 == 0 else 1
     columns = [(k, d) for k in range(width) for d in range(3)]
     columns = [columns[i : i + 2] for i in range(0, len(columns), 2)]
     none = jnp.zeros((channels, channels), kernel_ref.dtype)
@@ -610,49 +610,27 @@
     return total
 
 
-def own_part_kernel(shards, shards_y, me_ref, table_ref, *refs):
+def final_kernel(shards, shards_y, me_ref, table_ref, *refs):
+    outer, _ = shards
     *piece_refs, bias_ref, out_ref, held = refs
     cells_x, cells_y, cells_z, channels = out_ref.shape
     width = 2 if cells_x % 2 == 0 else 1
     count = -(-cells_x // width)
     piece_refs, convolved_refs = piece_refs[:-count], piece_refs[-count:]
-    slots = far_first(shards[0])
-    gather_pieces(me_ref[0], shards, [(0, *p) for p in zip(slots, piece_refs)], held)
-    bias = bias_ref[...]
-    rows = 4 if cells_y % 4 == 0 else 1
-    positions = rows * cells_z
-
-    def chunk(part, carry):
-        for x in range(0, cells_x, width):
-            total = inverse(
-                me_ref[0], shards, shards_y, [0], table_ref, held, part, x, width, positions
-            )
-            for i in range(width):
-                spectral = total[:, i * channels : (i + 1) * channels]
-                convolved = convolved_refs[x // width][i, pl.ds(part * rows, rows)]
-                value = spectral.reshape(rows, cells_z, channels) + convolved + bias
-                out_ref[x + i, pl.ds(part * rows, rows)] = value
-        return carry
-
-    lax.fori_loop(0, cells_y // rows, chunk, 0)
-
-
-def last_part_kernel(shards, shards_y, me_ref, table_ref, *refs):
-    *bundle_refs, partial_ref, out_ref, held = refs
-    cells_x, cells_y, cells_z, channels = out_ref.shape
-    bundles = bundled_slots(shards[0])
-    steps = list(range(1, shards_y))
-    width = 2 if cells_x % 2 == 0 else 1
+    bundles = bundled_slots(outer)
+    steps = list(range(shards_y))
     part = pl.program_id(0)
 
     @pl.when(part == 0)
     def _():
-        pieces = []
-        for i, ref in enumerate(bundle_refs):
-            number, bundle = divmod(i, len(bundles))
-            pieces += [(number, slot, ref.at[j]) for j, slot in enumerate(bundles[bundle])]
+        pieces = [(0, *piece) for piece in zip(far_first(outer), piece_refs)]
+        for i, ref in enumerate(piece_refs[outer:]):
+            number, place_in = divmod(i, len(bundles))
+            for j, slot in enumerate(bundles[place_in]):
+                pieces.append((number + 1, slot, ref.at[j]))
         gather_pieces(me_ref[0], shards, pieces, held)
 
+    bias = bias_ref[...]
     for x in range(0, cells_x, width):
         total = inverse(
             me_ref[0], shards, shards_y, steps, table_ref, held, part, x, width,
@@ -660,52 +638,35 @@
         )
         for i in range(width):
             spectral = total[:, i * channels : (i + 1) * channels]
-            value = partial_ref[x + i, pl.ds(part * cells_y, cells_y)]
-            value = value + spectral.reshape(cells_y, cells_z, channels)
+            convolved = convolved_refs[x // width][i, pl.ds(part * cells_y, cells_y)]
+            value = spectral.reshape(cells_y, cells_z, channels) + convolved + bias
             out_ref[x + i] = jax.nn.gelu(value, approximate=True).astype(out_ref.dtype)
 
 
-def own_part(me, table, pieces, convolved, bias, shards, shards_y):
+def final(me, table, pieces, convolved, bias, shards, shards_y):
     width, cells_y, cells_z, channels = convolved[0].shape
-    shape = (width * len(convolved), cells_y, cells_z, channels)
-    depth = table.shape[2]
+    cells_x = width * len(convolved)
+    parts = 4 if cells_y % 4 == 0 else 1
+    block = (cells_x, cells_y // parts, cells_z, channels)
+    shape = (cells_x, cells_y, cells_z, channels)
+    depth = table.shape[2] * shards_y
     return pl.pallas_call(
-        functools.partial(own_part_kernel, shards, shards_y),
-        in_specs=[IN_SMEM] + in_vmem(2 + len(pieces) + len(convolved)),
-        out_specs=in_vmem(1)[0],
-        out_shape=jax.ShapeDtypeStruct(shape, jnp.float32),
-        scratch_shapes=[pltpu.VMEM((shape[0], depth, channels), jnp.bfloat16)],
+        functools.partial(final_kernel, shards, shards_y),
+        grid_spec=pltpu.PrefetchScalarGridSpec(
+            num_scalar_prefetch=1,
+            grid=(parts,),
+            in_specs=in_vmem(2 + len(pieces) + len(convolved)),
+            out_specs=pl.BlockSpec(block, lambda i, me: (0, i, 0, 0)),
+            scratch_shapes=[pltpu.VMEM((cells_x, depth, channels), jnp.bfloat16)],
+        ),
+        out_shape=jax.ShapeDtypeStruct(shape, jnp.bfloat16),
         compiler_params=pltpu.CompilerParams(vmem_limit_bytes=14 << 20),
         cost_estimate=pl.CostEstimate(
             flops=2 * math.prod(shape) * depth,
             bytes_accessed=6 * math.prod(shape),
-            transcendentals=0,
+            transcendentals=math.prod(shape),
         ),
     )(me, table, *pieces, *convolved, bias)
-
-
-def last_part(me, table, pieces, partial, shards, shards_y):
-    cells_x, cells_y, cells_z, channels = partial.shape
-    parts = 4 if cells_y % 4 == 0 else 1
-    block = (cells_x, cells_y // parts, cells_z, channels)
-    depth = table.shape[2] * (shards_y - 1)
-    return pl.pallas_call(
-        functools.partial(last_part_kernel, shards, shards_y),
-        grid_spec=pltpu.PrefetchScalarGridSpec(
-            num_scalar_prefetch=1,
-            grid=(parts,),
-            in_specs=in_vmem(2 + len(pieces)),
-            out_specs=pl.BlockSpec(block, lambda i, me: (0, i, 0, 0)),
-            scratch_shapes=[pltpu.VMEM((cells_x, depth, channels), jnp.bfloat16)],
-        ),
-        out_shape=jax.ShapeDtypeStruct(partial.shape, jnp.bfloat16),
-        compiler_params=pltpu.CompilerParams(vmem_limit_bytes=14 << 20),
-        cost_estimate=pl.CostEstimate(
-            flops=2 * partial.size * depth,
-            bytes_accessed=6 * partial.size,
-            transcendentals=partial.size,
-        ),
-    )(me, table, *pieces, partial)
 
 
 def with_halo(array, sides, width):
@@ -947,8 +908,7 @@
         others += [over_y(part, step, shards_y) for part in bundles]
     table = jnp.asarray(backward_yz_table(*sizes))
     bias = bias.reshape(1, channels)
-    partial = own_part(me, table, returned, convolved, bias, shards, shards_y)
-    return last_part(me, table, others, partial, shards, shards_y)
+    return final(me, table, [*returned, *others], convolved, bias, shards, shards_y)
 
 
 def solution(mesh):

time: 59.9 us -> 60.4 us (level)
  waiting for transfers between devices: 8.99 us -> 10.4 us
  Pallas kernels: 27.5 us -> 26.5 us
    ppermute x6, waiting for transfers between devices: 1.32 us -> 2.51 us  [over_y(): lax.ppermute(array, 'gy', [(i, (i + step) % shards_y) for i in range(shar...]
    pallas_call x2 -> x1, Pallas kernels: 3.52 us -> 2.91 us  [final(): pl.pallas_call(functools.partial(final_kernel, shards, shards_y), grid_sp...]
  transfers between devices with their start and end apart: 20 -> 20, of which waited for: 7 -> 7; matrix products, arithmetic and copies ran while one was open for 0% -> 0% of each run, Pallas kernels for 37% -> 34%
where the time goes in v14:
time: 60.4 us; the launch traced here: 60.2 us
  Pallas kernels  26.5 us (44%)
  starting transfers between devices  22.9 us (38%)
  waiting for transfers between devices  10.4 us (17%)
    ppermute x12, starting transfers between devices, exchange(): return lax.ppermute(array, 'gx', pairs)  14.4 us
    pallas_call x3, Pallas kernels, preload(): pl.pallas_call(functools.partial(preload_kernel, 2 * pair), in_specs=[pl....  9.15 us
    ppermute x12, waiting for transfers between devices, exchange(): return lax.ppermute(array, 'gx', pairs)  7.88 us
    pallas_call x1, Pallas kernels, mixing(): pl.pallas_call(functools.partial(mixing_kernel, shards, len(loaded)), in_...  6.07 us
    ppermute x6, starting transfers between devices, over_y(): lax.ppermute(array, 'gy', [(i, (i + step) % shards_y) for i in range(shar...  5.81 us
    pallas_call x2, Pallas kernels, convolution(): pl.pallas_call(functools.partial(convolution_kernel, x, cells_x, width, s...  4.81 us
    pallas_call x2, Pallas kernels, forward_yz(): pl.pallas_call(kernel, in_specs=[IN_SMEM] + specs, out_specs=in_vmem(len(...  3.43 us
    pallas_call x1, Pallas kernels, final(): pl.pallas_call(functools.partial(final_kernel, shards, shards_y), grid_sp...  2.91 us
  transfers between devices with their start and end apart: 20, of which 7 were waited for; matrix products, arithmetic and copies ran while one was open for 0% of the time, Pallas kernels for 34%

profile of v14, /device:TPU:0, one launch (start us, length us, event | category | flops | bytes accessed | tf_op | source)
XLA Modules:
  0.0 60.2 jit_solution(7415753375389721931)
XLA Ops:
  0.0 3.0 %shard_map.82 = (bf16[2,4,4,16,128]{4,3,2,1,0:T(8,128)(2,1)}, bf16[2,4,4,16,128]{4,3,2,1,0:T(8,128)(2,1)}) custom-call(s32[1]{0:T(128)} %bitcast.me_ref, bf16[2,512,1024]{2,1,0:T(8,128)(2,1)} %constant.18.clone.table_ref, bf16[4,1024,128]{2,1,0:T(8,128)(2,1)} %bitcast.6), custom_call_target="tpu_custom_call" | custom-call | flops 268435456 | bytes 1572864 | tf_op jit(solution)/shard_map/pallas_call | solution.py:224
  3.0 0.0 copy-start
  3.0 0.0 copy-start.1
  3.0 3.0 %collective-permute-start.2 = (bf16[2,4,4,16,128]{4,3,2,1,0:T(8,128)(2,1)}, bf16[2,4,4,16,128]{4,3,2,1,0:T(8,128)(2,1)S(1)}, u32[]{:S(2)}, u32[]{:S(2)}) collective-permute-start(bf16[2,4,4,16,128]{4,3,2,1,0:T(8,128)(2,1)} %get-tuple-element.80), channel_id=1, source_target_pairs={{0,1},{1,0},{2,3},{3,2},{4,5},{5,4},{6,7},{7,6},{8,9},{9,8},{10,11... | collective-permute-start | bytes 393224 | tf_op jit(solution)/shard_map/ppermute | solution.py:812
  6.0 0.1 collective-permute-start
  6.1 3.5 %shard_map.83.refs_7_ = bf16[4,64,128,128]{3,2,1,0:T(8,128)(2,1)S(1)} custom-call(bf16[16,64,128,128]{3,2,1,0:T(8,128)(2,1)} %bitcast.11), custom_call_target="tpu_custom_call" | custom-call | bytes 8388608 | tf_op jit(solution)/shard_map/pallas_call | solution.py:341
  9.6 0.4 shard_map.84
  10.1 0.5 collective-permute-done.2.refs_1_
  10.6 3.2 %collective-permute-start.3 = (bf16[4,4,16,128]{3,2,1,0:T(8,128)(2,1)S(1)}, bf16[4,4,16,128]{3,2,1,0:T(8,128)(2,1)S(1)}, u32[]{:S(2)}, u32[]{:S(2)}) collective-permute-start(bf16[4,4,16,128]{3,2,1,0:T(8,128)(2,1)S(1)} %get-tuple-element.81), channel_id=1, source_target_pairs={{0,16},{2,18},{4,20},{6,22},{8,24},{10,26},{12,28},{14,30},{16,0},... | collective-permute-start | bytes 196616 | tf_op jit(solution)/shard_map/ppermute | solution.py:808
  13.8 1.4 %collective-permute-start.4 = (bf16[4,4,16,128]{3,2,1,0:T(8,128)(2,1)S(1)}, bf16[4,4,16,128]{3,2,1,0:T(8,128)(2,1)S(1)}, u32[]{:S(2)}, u32[]{:S(2)}) collective-permute-start(bf16[4,4,16,128]{3,2,1,0:T(8,128)(2,1)S(1)} %get-tuple-element.82), channel_id=1, source_target_pairs={{0,24},{2,26},{4,28},{6,30},{8,16},{10,18},{12,20},{14,22},{16,8},... | collective-permute-start | bytes 196616 | tf_op jit(solution)/shard_map/ppermute | solution.py:808
  15.2 0.0 collective-permute-done.refs_1_
  15.2 0.3 collective-permute-start.1
  15.5 1.5 %collective-permute-start.8 = (bf16[4,64,128]{2,1,0:T(8,128)(2,1)S(1)}, bf16[4,64,128]{2,1,0:T(8,128)(2,1)S(1)}, u32[]{:S(2)}, u32[]{:S(2)}) collective-permute-start(bf16[4,64,128]{2,1,0:T(8,128)(2,1)S(1)} %get-tuple-element.102), channel_id=1, source_target_pairs={{0,1},{1,0},{2,3},{3,2},{4,5},{5,4},{6,7},{7,6},{8,9},{9,8},{10,11... | collective-permute-start | bytes 196616 | tf_op jit(solution)/shard_map/ppermute | solution.py:812
  17.0 3.5 %shard_map.87.refs_8_ = bf16[4,64,128,128]{3,2,1,0:T(8,128)(2,1)S(1)} custom-call(bf16[16,64,128,128]{3,2,1,0:T(8,128)(2,1)} %bitcast.12), custom_call_target="tpu_custom_call" | custom-call | bytes 8388608 | tf_op jit(solution)/shard_map/pallas_call | solution.py:341
  20.5 0.0 collective-permute-done.3.refs_1_
  20.5 0.0 collective-permute-done.1.refs_2_
  20.6 0.0 copy-start.3
  20.6 0.0 copy-start.4
  20.6 0.1 collective-permute-start.5
  20.7 1.6 %collective-permute-start.6 = (bf16[4,4,16,128]{3,2,1,0:T(8,128)(2,1)S(1)}, bf16[4,4,16,128]{3,2,1,0:T(8,128)(2,1)S(1)}, u32[]{:S(2)}, u32[]{:S(2)}) collective-permute-start(bf16[4,4,16,128]{3,2,1,0:T(8,128)(2,1)S(1)} %get-tuple-element.94), channel_id=1, source_target_pairs={{0,4},{2,6},{4,0},{6,2},{8,12},{10,14},{12,8},{14,10},{16,20},{18,... | collective-permute-start | bytes 196616 | tf_op jit(solution)/shard_map/ppermute | solution.py:808
  22.2 0.3 collective-permute-start.7
  22.5 2.2 %shard_map.89.refs_9_ = bf16[2,64,128,128]{3,2,1,0:T(8,128)(2,1)S(1)} custom-call(bf16[16,64,128,128]{3,2,1,0:T(8,128)(2,1)} %bitcast.13), custom_call_target="tpu_custom_call" | custom-call | bytes 4194304 | tf_op jit(solution)/shard_map/pallas_call | solution.py:341
  24.7 0.0 collective-permute-done.8.front_ref.back_ref.refs_3_.refs_4_
  24.7 0.3 collective-permute-done.5.refs_0_
  25.0 1.5 %collective-permute-done.6.refs_1_ = bf16[4,4,16,128]{3,2,1,0:T(8,128)(2,1)S(1)} collective-permute-done((bf16[4,4,16,128]{3,2,1,0:T(8,128)(2,1)S(1)}, bf16[4,4,16,128]{3,2,1,0:T(8,128)(2,1)S(1)}, u32[]{:S(2)}, u32[]{:S(2)}) %collective-permute-start.6) | collective-permute-done | bytes 65568 | tf_op jit(solution)/shard_map/ppermute | solution.py:808
  26.4 0.1 shard_map.91
  26.5 0.7 %collective-permute-start.9 = (bf16[18,64,128]{2,1,0:T(8,128)(2,1)S(1)}, bf16[18,64,128]{2,1,0:T(8,128)(2,1)S(1)}, u32[]{:S(2)}, u32[]{:S(2)}) collective-permute-start(bf16[18,64,128]{2,1,0:T(8,128)(2,1)S(1)} %get-tuple-element.118), channel_id=1, source_target_pairs={{2,4},{6,8},{10,12},{14,16},{18,20},{22,24},{26,28},{4,2},{8,6},{1... | collective-permute-start | bytes 884744 | tf_op jit(solution)/shard_map/ppermute | solution.py:797
  27.2 0.0 copy-start.6
  27.2 2.1 %collective-permute-start.10 = (bf16[18,64,128]{2,1,0:T(8,128)(2,1)S(1)}, bf16[18,64,128]{2,1,0:T(8,128)(2,1)S(1)}, u32[]{:S(2)}, u32[]{:S(2)}) collective-permute-start(bf16[18,64,128]{2,1,0:T(8,128)(2,1)S(1)} %get-tuple-element.119), channel_id=1, source_target_pairs={{0,2},{4,6},{8,10},{12,14},{16,18},{20,22},{24,26},{28,30},{2,0},{... | collective-permute-start | bytes 884744 | tf_op jit(solution)/shard_map/ppermute | solution.py:797
  29.3 6.1 %shard_map.90 = (bf16[4,4,16,128]{3,2,1,0:T(8,128)(2,1)S(1)}, bf16[4,4,16,128]{3,2,1,0:T(8,128)(2,1)S(1)}, bf16[4,4,16,128]{3,2,1,0:T(8,128)(2,1)S(1)}, bf16[4,4,16,128]{3,2,1,0:T(8,128)(2,1)S(1)}) custom-call(s32[1]{0:T(128)} %bitcast.me_ref, bf16[4,4,16,128]{3,2,1,0:T(8,128)(2,1)S(1)} %collective-permute-done.5.refs_0_, ...), custom_call_target="tpu_custom_call" | custom-call | flops 134217728 | bytes 33554432 | tf_op jit(solution)/shard_map/pallas_call | solution.py:460
  35.4 0.0 copy-start.2
  35.4 0.0 copy-start.5
  35.4 2.3 %collective-permute-start.11 = (bf16[4,4,16,128]{3,2,1,0:T(8,128)(2,1)S(1)}, bf16[4,4,16,128]{3,2,1,0:T(8,128)(2,1)S(1)}, u32[]{:S(2)}, u32[]{:S(2)}) collective-permute-start(bf16[4,4,16,128]{3,2,1,0:T(8,128)(2,1)S(1)} %get-tuple-element.120), channel_id=1, source_target_pairs={{0,6},{2,4},{4,2},{6,0},{8,14},{10,12},{12,10},{14,8},{16,22},{18,... | collective-permute-start | bytes 196616 | tf_op jit(solution)/shard_map/ppermute | solution.py:808
  37.7 0.8 %collective-permute-start.12 = (bf16[4,4,16,128]{3,2,1,0:T(8,128)(2,1)S(1)}, bf16[4,4,16,128]{3,2,1,0:T(8,128)(2,1)S(1)}, u32[]{:S(2)}, u32[]{:S(2)}) collective-permute-start(bf16[4,4,16,128]{3,2,1,0:T(8,128)(2,1)S(1)} %get-tuple-element.121), channel_id=1, source_target_pairs={{0,4},{2,6},{4,0},{6,2},{8,12},{10,14},{12,8},{14,10},{16,20},{18,... | collective-permute-start | bytes 196616 | tf_op jit(solution)/shard_map/ppermute | solution.py:808
  38.5 0.0 collective-permute-start.13
  38.6 2.4 %shard_map.92.refs_7_ = bf16[2,16,64,128]{3,2,1,0:T(8,128)(2,1)S(1)} custom-call(s32[1]{0:T(128)} %bitcast.me_ref, bf16[4,16,64,128]{3,2,1,0:T(8,128)(2,1)S(1)} %copy-done.1, bf16[18,64,128]{2,1,0:T(8,128)(2,1)S(1)} %collective-permute-done.10.refs_1_, bf16[18,64,128]{2,1,0:T(8,128)(2,1)S(1)} %collective-permute-done.9.refs_2_, ...), custom_call_target="tpu_custom_call" | custom-call | flops 2717908992 | bytes 1310720 | tf_op jit(solution)/shard_map/pallas_call | solution.py:546
  41.0 1.6 %collective-permute-done.12.refs_1_ = bf16[4,4,16,128]{3,2,1,0:T(8,128)(2,1)S(1)} collective-permute-done((bf16[4,4,16,128]{3,2,1,0:T(8,128)(2,1)S(1)}, bf16[4,4,16,128]{3,2,1,0:T(8,128)(2,1)S(1)}, u32[]{:S(2)}, u32[]{:S(2)}) %collective-permute-start.12) | collective-permute-done | bytes 65568 | tf_op jit(solution)/shard_map/ppermute | solution.py:808
  42.6 3.0 %collective-permute-start.14 = (bf16[4,4,16,128]{3,2,1,0:T(8,128)(2,1)S(1)}, bf16[4,4,16,128]{3,2,1,0:T(8,128)(2,1)S(1)}, u32[]{:S(2)}, u32[]{:S(2)}) collective-permute-start(bf16[4,4,16,128]{3,2,1,0:T(8,128)(2,1)S(1)} %get-tuple-element.130), channel_id=1, source_target_pairs={{0,24},{2,26},{4,28},{6,30},{8,16},{10,18},{12,20},{14,22},{16,8},... | collective-permute-start | bytes 196616 | tf_op jit(solution)/shard_map/ppermute | solution.py:808
  45.6 0.8 %collective-permute-start.15 = (bf16[4,4,16,128]{3,2,1,0:T(8,128)(2,1)S(1)}, bf16[4,4,16,128]{3,2,1,0:T(8,128)(2,1)S(1)}, u32[]{:S(2)}, u32[]{:S(2)}) collective-permute-start(bf16[4,4,16,128]{3,2,1,0:T(8,128)(2,1)S(1)} %get-tuple-element.131), channel_id=1, source_target_pairs={{0,16},{2,18},{4,20},{6,22},{8,24},{10,26},{12,28},{14,30},{16,0},... | collective-permute-start | bytes 196616 | tf_op jit(solution)/shard_map/ppermute | solution.py:808
  46.5 0.6 collective-permute-start.16
  47.1 0.3 collective-permute-start.17
  47.3 1.5 %collective-permute-done.14.refs_0_ = bf16[4,4,16,128]{3,2,1,0:T(8,128)(2,1)S(1)} collective-permute-done((bf16[4,4,16,128]{3,2,1,0:T(8,128)(2,1)S(1)}, bf16[4,4,16,128]{3,2,1,0:T(8,128)(2,1)S(1)}, u32[]{:S(2)}, u32[]{:S(2)}) %collective-permute-start.14) | collective-permute-done | bytes 65568 | tf_op jit(solution)/shard_map/ppermute | solution.py:808
  48.8 0.3 collective-permute-start.18
  49.2 3.0 %collective-permute-done.15.refs_0_.refs_1_ = bf16[4,4,16,128]{3,2,1,0:T(8,128)(2,1)S(1)} collective-permute-done((bf16[4,4,16,128]{3,2,1,0:T(8,128)(2,1)S(1)}, bf16[4,4,16,128]{3,2,1,0:T(8,128)(2,1)S(1)}, u32[]{:S(2)}, u32[]{:S(2)}) %collective-permute-start.15) | collective-permute-done | bytes 65568 | tf_op jit(solution)/shard_map/ppermute | solution.py:808
  52.2 0.6 collective-permute-start.19
  52.8 2.4 %shard_map.95.refs_8_ = bf16[2,16,64,128]{3,2,1,0:T(8,128)(2,1)S(1)} custom-call(s32[1]{0:T(128)} %bitcast.me_ref, bf16[4,16,64,128]{3,2,1,0:T(8,128)(2,1)S(1)} %copy-done.1, bf16[18,64,128]{2,1,0:T(8,128)(2,1)S(1)} %collective-permute-done.10.refs_1_, bf16[18,64,128]{2,1,0:T(8,128)(2,1)S(1)} %collective-permute-done.9.refs_2_, ...), custom_call_target="tpu_custom_call" | custom-call | flops 2717908992 | bytes 1310720 | tf_op jit(solution)/shard_map/pallas_call | solution.py:546
  55.3 2.0 %collective-permute-done.19.refs_6_ = bf16[2,4,4,16,128]{4,3,2,1,0:T(8,128)(2,1)S(1)} collective-permute-done((bf16[2,4,4,16,128]{4,3,2,1,0:T(8,128)(2,1)S(1)}, bf16[2,4,4,16,128]{4,3,2,1,0:T(8,128)(2,1)S(1)}, u32[]{:S(2)}, u32[]{:S(2)}) %collective-permute-start.19) | collective-permute-done | bytes 131104 | tf_op jit(solution)/shard_map/ppermute | solution.py:812
  57.3 2.9 %shard_map.96 = bf16[4,16,64,128]{3,2,1,0:T(8,128)(2,1)} custom-call(s32[1]{0:T(128)} %bitcast.me_ref, bf16[4,1024,256]{2,1,0:T(8,128)(2,1)S(1)} %copy-done.2, bf16[4,4,16,128]{3,2,1,0:T(8,128)(2,1)S(1)} %collective-permute-done.14.refs_0_, bf16[4,4,16,128]{3,2,1,0:T(8,128)(2,1)S(1)} %collective-permute-done.15.refs_0_.refs_1_, ...), custom_call_target="tpu_custom_call" | custom-call | flops 536870912 | bytes 3145728 | tf_op jit(solution)/shard_map/pallas_call | solution.py:653
  (21 shorter events, 0.2 us)
Async XLA Ops:
  3.0 6.6 %copy-start = (bf16[2,512,1024]{2,1,0:T(8,128)(2,1)S(1)}, bf16[2,512,1024]{2,1,0:T(8,128)(2,1)}, u32[]{:S(2)}) copy-start(bf16[2,512,1024]{2,1,0:T(8,128)(2,1)} %constant.18.clone.table_ref) | copy-start | bytes 6291460
  3.0 6.6 %copy-start.1 = (bf16[4,16,64,128]{3,2,1,0:T(8,128)(2,1)S(1)}, bf16[4,16,64,128]{3,2,1,0:T(8,128)(2,1)}, u32[]{:S(2)}) copy-start(bf16[4,16,64,128]{3,2,1,0:T(8,128)(2,1)} %refs_0_.3) | copy-start | bytes 3145732
  3.0 7.6 %collective-permute-start.2 = (bf16[2,4,4,16,128]{4,3,2,1,0:T(8,128)(2,1)}, bf16[2,4,4,16,128]{4,3,2,1,0:T(8,128)(2,1)S(1)}, u32[]{:S(2)}, u32[]{:S(2)}) collective-permute-start(bf16[2,4,4,16,128]{4,3,2,1,0:T(8,128)(2,1)} %get-tuple-element.80), channel_id=1, source_target_pairs={{0,1},{1,0},{2,3},{3,2},{4,5},{5,4},{6,7},{7,6},{8,9},{9,8},{10,11... | collective-permute-start | bytes 393224 | tf_op jit(solution)/shard_map/ppermute | solution.py:812
  6.0 9.1 %collective-permute-start = (bf16[2,4,4,16,128]{4,3,2,1,0:T(8,128)(2,1)}, bf16[2,4,4,16,128]{4,3,2,1,0:T(8,128)(2,1)S(1)}, u32[]{:S(2)}, u32[]{:S(2)}) collective-permute-start(bf16[2,4,4,16,128]{4,3,2,1,0:T(8,128)(2,1)} %get-tuple-element.76), channel_id=1, source_target_pairs={{0,1},{1,0},{2,3},{3,2},{4,5},{5,4},{6,7},{7,6},{8,9},{9,8},{10,11... | collective-permute-start | bytes 393224 | tf_op jit(solution)/shard_map/ppermute | solution.py:812
  10.6 9.9 %collective-permute-start.3 = (bf16[4,4,16,128]{3,2,1,0:T(8,128)(2,1)S(1)}, bf16[4,4,16,128]{3,2,1,0:T(8,128)(2,1)S(1)}, u32[]{:S(2)}, u32[]{:S(2)}) collective-permute-start(bf16[4,4,16,128]{3,2,1,0:T(8,128)(2,1)S(1)} %get-tuple-element.81), channel_id=1, source_target_pairs={{0,16},{2,18},{4,20},{6,22},{8,24},{10,26},{12,28},{14,30},{16,0},... | collective-permute-start | bytes 196616 | tf_op jit(solution)/shard_map/ppermute | solution.py:808
  13.8 6.7 %collective-permute-start.4 = (bf16[4,4,16,128]{3,2,1,0:T(8,128)(2,1)S(1)}, bf16[4,4,16,128]{3,2,1,0:T(8,128)(2,1)S(1)}, u32[]{:S(2)}, u32[]{:S(2)}) collective-permute-start(bf16[4,4,16,128]{3,2,1,0:T(8,128)(2,1)S(1)} %get-tuple-element.82), channel_id=1, source_target_pairs={{0,24},{2,26},{4,28},{6,30},{8,16},{10,18},{12,20},{14,22},{16,8},... | collective-permute-start | bytes 196616 | tf_op jit(solution)/shard_map/ppermute | solution.py:808
  15.2 5.3 %collective-permute-start.1 = (bf16[4,4,16,128]{3,2,1,0:T(8,128)(2,1)S(1)}, bf16[4,4,16,128]{3,2,1,0:T(8,128)(2,1)S(1)}, u32[]{:S(2)}, u32[]{:S(2)}) collective-permute-start(bf16[4,4,16,128]{3,2,1,0:T(8,128)(2,1)S(1)} %get-tuple-element.78), channel_id=1, source_target_pairs={{0,8},{2,10},{4,12},{6,14},{8,0},{10,2},{12,4},{14,6},{16,24},{18,... | collective-permute-start | bytes 196616 | tf_op jit(solution)/shard_map/ppermute | solution.py:808
  15.5 9.2 %collective-permute-start.8 = (bf16[4,64,128]{2,1,0:T(8,128)(2,1)S(1)}, bf16[4,64,128]{2,1,0:T(8,128)(2,1)S(1)}, u32[]{:S(2)}, u32[]{:S(2)}) collective-permute-start(bf16[4,64,128]{2,1,0:T(8,128)(2,1)S(1)} %get-tuple-element.102), channel_id=1, source_target_pairs={{0,1},{1,0},{2,3},{3,2},{4,5},{5,4},{6,7},{7,6},{8,9},{9,8},{10,11... | collective-permute-start | bytes 196616 | tf_op jit(solution)/shard_map/ppermute | solution.py:812
  20.6 8.8 %copy-start.3 = (bf16[256,128]{1,0:T(8,128)(2,1)S(1)}, bf16[256,128]{1,0:T(8,128)(2,1)}, u32[]{:S(2)}) copy-start(bf16[256,128]{1,0:T(8,128)(2,1)} %constant.19.clone.refs_4_) | copy-start | bytes 196612
  20.6 8.7 %copy-start.4 = (bf16[128,128]{1,0:T(8,128)(2,1)S(1)}, bf16[128,128]{1,0:T(8,128)(2,1)}, u32[]{:S(2)}) copy-start(bf16[128,128]{1,0:T(8,128)(2,1)} %constant.20.clone.refs_5_) | copy-start | bytes 98308
  20.6 4.4 %collective-permute-start.5 = (bf16[4,4,16,128]{3,2,1,0:T(8,128)(2,1)S(1)}, bf16[4,4,16,128]{3,2,1,0:T(8,128)(2,1)S(1)}, u32[]{:S(2)}, u32[]{:S(2)}) collective-permute-start(bf16[4,4,16,128]{3,2,1,0:T(8,128)(2,1)S(1)} %get-tuple-element.93), channel_id=1, source_target_pairs={{0,6},{2,4},{4,2},{6,0},{8,14},{10,12},{12,10},{14,8},{16,22},{18,... | collective-permute-start | bytes 196616 | tf_op jit(solution)/shard_map/ppermute | solution.py:808
  20.7 5.8 %collective-permute-start.6 = (bf16[4,4,16,128]{3,2,1,0:T(8,128)(2,1)S(1)}, bf16[4,4,16,128]{3,2,1,0:T(8,128)(2,1)S(1)}, u32[]{:S(2)}, u32[]{:S(2)}) collective-permute-start(bf16[4,4,16,128]{3,2,1,0:T(8,128)(2,1)S(1)} %get-tuple-element.94), channel_id=1, source_target_pairs={{0,4},{2,6},{4,0},{6,2},{8,12},{10,14},{12,8},{14,10},{16,20},{18,... | collective-permute-start | bytes 196616 | tf_op jit(solution)/shard_map/ppermute | solution.py:808
  22.2 4.2 %collective-permute-start.7 = (bf16[4,4,16,128]{3,2,1,0:T(8,128)(2,1)S(1)}, bf16[4,4,16,128]{3,2,1,0:T(8,128)(2,1)S(1)}, u32[]{:S(2)}, u32[]{:S(2)}) collective-permute-start(bf16[4,4,16,128]{3,2,1,0:T(8,128)(2,1)S(1)} %get-tuple-element.95), channel_id=1, source_target_pairs={{0,2},{2,0},{4,6},{6,4},{8,10},{10,8},{12,14},{14,12},{16,18},{18,... | collective-permute-start | bytes 196616 | tf_op jit(solution)/shard_map/ppermute | solution.py:808
  26.5 8.9 %collective-permute-start.9 = (bf16[18,64,128]{2,1,0:T(8,128)(2,1)S(1)}, bf16[18,64,128]{2,1,0:T(8,128)(2,1)S(1)}, u32[]{:S(2)}, u32[]{:S(2)}) collective-permute-start(bf16[18,64,128]{2,1,0:T(8,128)(2,1)S(1)} %get-tuple-element.118), channel_id=1, source_target_pairs={{2,4},{6,8},{10,12},{14,16},{18,20},{22,24},{26,28},{4,2},{8,6},{1... | collective-permute-start | bytes 884744 | tf_op jit(solution)/shard_map/ppermute | solution.py:797
  27.2 11.4 %copy-start.6 = (bf16[3,3,3,128,128]{4,3,2,1,0:T(8,128)(2,1)S(1)}, bf16[3,3,3,128,128]{4,3,2,1,0:T(8,128)(2,1)}, u32[]{:S(2)}) copy-start(bf16[3,3,3,128,128]{4,3,2,1,0:T(8,128)(2,1)} %refs_5_.4) | copy-start | bytes 2654212
  27.2 8.2 %collective-permute-start.10 = (bf16[18,64,128]{2,1,0:T(8,128)(2,1)S(1)}, bf16[18,64,128]{2,1,0:T(8,128)(2,1)S(1)}, u32[]{:S(2)}, u32[]{:S(2)}) collective-permute-start(bf16[18,64,128]{2,1,0:T(8,128)(2,1)S(1)} %get-tuple-element.119), channel_id=1, source_target_pairs={{0,2},{4,6},{8,10},{12,14},{16,18},{20,22},{24,26},{28,30},{2,0},{... | collective-permute-start | bytes 884744 | tf_op jit(solution)/shard_map/ppermute | solution.py:797
  35.4 21.9 %copy-start.2 = (bf16[4,1024,256]{2,1,0:T(8,128)(2,1)S(1)}, bf16[4,1024,256]{2,1,0:T(8,128)(2,1)}, u32[]{:S(2)}) copy-start(bf16[4,1024,256]{2,1,0:T(8,128)(2,1)} %constant.21.clone.table_ref) | copy-start | bytes 6291460
  35.4 21.9 %copy-start.5 = (f32[128]{0:T(128)S(1)}, f32[128]{0:T(128)}, u32[]{:S(2)}) copy-start(f32[128]{0:T(128)} %param.11) | copy-start | bytes 1540
  35.4 5.5 %collective-permute-start.11 = (bf16[4,4,16,128]{3,2,1,0:T(8,128)(2,1)S(1)}, bf16[4,4,16,128]{3,2,1,0:T(8,128)(2,1)S(1)}, u32[]{:S(2)}, u32[]{:S(2)}) collective-permute-start(bf16[4,4,16,128]{3,2,1,0:T(8,128)(2,1)S(1)} %get-tuple-element.120), channel_id=1, source_target_pairs={{0,6},{2,4},{4,2},{6,0},{8,14},{10,12},{12,10},{14,8},{16,22},{18,... | collective-permute-start | bytes 196616 | tf_op jit(solution)/shard_map/ppermute | solution.py:808
  37.7 4.9 %collective-permute-start.12 = (bf16[4,4,16,128]{3,2,1,0:T(8,128)(2,1)S(1)}, bf16[4,4,16,128]{3,2,1,0:T(8,128)(2,1)S(1)}, u32[]{:S(2)}, u32[]{:S(2)}) collective-permute-start(bf16[4,4,16,128]{3,2,1,0:T(8,128)(2,1)S(1)} %get-tuple-element.121), channel_id=1, source_target_pairs={{0,4},{2,6},{4,0},{6,2},{8,12},{10,14},{12,8},{14,10},{16,20},{18,... | collective-permute-start | bytes 196616 | tf_op jit(solution)/shard_map/ppermute | solution.py:808
  38.5 4.0 %collective-permute-start.13 = (bf16[4,4,16,128]{3,2,1,0:T(8,128)(2,1)S(1)}, bf16[4,4,16,128]{3,2,1,0:T(8,128)(2,1)S(1)}, u32[]{:S(2)}, u32[]{:S(2)}) collective-permute-start(bf16[4,4,16,128]{3,2,1,0:T(8,128)(2,1)S(1)} %get-tuple-element.122), channel_id=1, source_target_pairs={{0,2},{2,0},{4,6},{6,4},{8,10},{10,8},{12,14},{14,12},{16,18},{18,... | collective-permute-start | bytes 196616 | tf_op jit(solution)/shard_map/ppermute | solution.py:808
  42.6 6.2 %collective-permute-start.14 = (bf16[4,4,16,128]{3,2,1,0:T(8,128)(2,1)S(1)}, bf16[4,4,16,128]{3,2,1,0:T(8,128)(2,1)S(1)}, u32[]{:S(2)}, u32[]{:S(2)}) collective-permute-start(bf16[4,4,16,128]{3,2,1,0:T(8,128)(2,1)S(1)} %get-tuple-element.130), channel_id=1, source_target_pairs={{0,24},{2,26},{4,28},{6,30},{8,16},{10,18},{12,20},{14,22},{16,8},... | collective-permute-start | bytes 196616 | tf_op jit(solution)/shard_map/ppermute | solution.py:808
  45.6 6.6 %collective-permute-start.15 = (bf16[4,4,16,128]{3,2,1,0:T(8,128)(2,1)S(1)}, bf16[4,4,16,128]{3,2,1,0:T(8,128)(2,1)S(1)}, u32[]{:S(2)}, u32[]{:S(2)}) collective-permute-start(bf16[4,4,16,128]{3,2,1,0:T(8,128)(2,1)S(1)} %get-tuple-element.131), channel_id=1, source_target_pairs={{0,16},{2,18},{4,20},{6,22},{8,24},{10,26},{12,28},{14,30},{16,0},... | collective-permute-start | bytes 196616 | tf_op jit(solution)/shard_map/ppermute | solution.py:808
  46.5 5.8 %collective-permute-start.16 = (bf16[4,4,16,128]{3,2,1,0:T(8,128)(2,1)S(1)}, bf16[4,4,16,128]{3,2,1,0:T(8,128)(2,1)S(1)}, u32[]{:S(2)}, u32[]{:S(2)}) collective-permute-start(bf16[4,4,16,128]{3,2,1,0:T(8,128)(2,1)S(1)} %get-tuple-element.132), channel_id=1, source_target_pairs={{0,8},{2,10},{4,12},{6,14},{8,0},{10,2},{12,4},{14,6},{16,24},{18,... | collective-permute-start | bytes 196616 | tf_op jit(solution)/shard_map/ppermute | solution.py:808
  47.1 8.2 %collective-permute-start.17 = (bf16[1,4,4,16,128]{4,3,2,1,0:T(8,128)(2,1)S(1)}, bf16[1,4,4,16,128]{4,3,2,1,0:T(8,128)(2,1)S(1)}, u32[]{:S(2)}, u32[]{:S(2)}) collective-permute-start(bf16[1,4,4,16,128]{4,3,2,1,0:T(8,128)(2,1)S(1)} %bitcast.8), channel_id=1, source_target_pairs={{0,1},{1,0},{2,3},{3,2},{4,5},{5,4},{6,7},{7,6},{8,9},{9,8},{10,11... | collective-permute-start | bytes 196616 | tf_op jit(solution)/shard_map/ppermute | solution.py:812
  48.8 6.4 %collective-permute-start.18 = (bf16[1,4,4,16,128]{4,3,2,1,0:T(8,128)(2,1)S(1)}, bf16[1,4,4,16,128]{4,3,2,1,0:T(8,128)(2,1)S(1)}, u32[]{:S(2)}, u32[]{:S(2)}) collective-permute-start(bf16[1,4,4,16,128]{4,3,2,1,0:T(8,128)(2,1)S(1)} %bitcast.9), channel_id=1, source_target_pairs={{0,1},{1,0},{2,3},{3,2},{4,5},{5,4},{6,7},{7,6},{8,9},{9,8},{10,11... | collective-permute-start | bytes 196616 | tf_op jit(solution)/shard_map/ppermute | solution.py:812
  52.2 5.0 %collective-permute-start.19 = (bf16[2,4,4,16,128]{4,3,2,1,0:T(8,128)(2,1)S(1)}, bf16[2,4,4,16,128]{4,3,2,1,0:T(8,128)(2,1)S(1)}, u32[]{:S(2)}, u32[]{:S(2)}) collective-permute-start(bf16[2,4,4,16,128]{4,3,2,1,0:T(8,128)(2,1)S(1)} %shard_map.94), channel_id=1, source_target_pairs={{0,1},{1,0},{2,3},{3,2},{4,5},{5,4},{6,7},{7,6},{8,9},{9,8},{10,11... | collective-permute-start | bytes 393224 | tf_op jit(solution)/shard_map/ppermute | solution.py:812

commit v15 on v9

--- a/solution.py
+++ b/solution.py
@@ -493,7 +493,7 @@
             def _(plane=plane):
                 padded[plane, 1 : cells_y + 1] = other_ref[...]
 
-    rows = 4 if cells_y % 4 == 0 else 1
+    rows = 16 if cells_y % 16 == 0 else 1
     columns = [(k, d) for k in range(width) for d in range(3)]
     columns = [columns[i : i + 2] for i in range(0, len(columns), 2)]
     none = jnp.zeros((channels, channels), kernel_ref.dtype)
@@ -676,7 +676,7 @@
 
 def last_part(me, table, pieces, partial, shards, shards_y):
     cells_x, cells_y, cells_z, channels = partial.shape
-    parts = 4 if cells_y % 4 == 0 else 1
+    parts = 2 if cells_y % 2 == 0 else 1
     block = (cells_x, cells_y // parts, cells_z, channels)
     depth = table.shape[2] * (shards_y - 1)
     return pl.pallas_call(

time: 59.6 us -> 58.4 us (0.980)
  Pallas kernels: 28.3 us -> 26.5 us
  waiting for transfers between devices: 9.67 us -> 10.3 us
    ppermute x12, waiting for transfers between devices: 3.92 us -> 5.08 us  [exchange(): return lax.ppermute(array, 'gx', pairs)]
    pallas_call x2, Pallas kernels: 5.99 us -> 4.84 us  [convolution(): pl.pallas_call(functools.partial(convolution_kernel, x, cells_x, width, s...]
    pallas_call x1, Pallas kernels: 2.53 us -> 1.93 us  [last_part(): pl.pallas_call(functools.partial(last_part_kernel, shards, shards_y), gri...]
  transfers between devices with their start and end apart: 19 -> 19, of which waited for: 9 -> 10; matrix products, arithmetic and copies ran while one was open for 0% -> 0% of each run, Pallas kernels for 38% -> 37%
where the time goes in v15:
time: 58.4 us; the launch traced here: 58.2 us
  Pallas kernels  26.5 us (45%)
  starting transfers between devices  21.2 us (36%)
  waiting for transfers between devices  10.3 us (18%)
    ppermute x12, starting transfers between devices, exchange(): return lax.ppermute(array, 'gx', pairs)  14.7 us
    pallas_call x3, Pallas kernels, preload(): pl.pallas_call(functools.partial(preload_kernel, 2 * pair), in_specs=[pl....  9.15 us
    pallas_call x1, Pallas kernels, mixing(): pl.pallas_call(functools.partial(mixing_kernel, shards, len(loaded)), in_...  5.93 us
    ppermute x5, starting transfers between devices, over_y(): lax.ppermute(array, 'gy', [(i, (i + step) % shards_y) for i in range(shar...  5.82 us
    ppermute x5, waiting for transfers between devices, over_y(): lax.ppermute(array, 'gy', [(i, (i + step) % shards_y) for i in range(shar...  5.18 us
    ppermute x12, waiting for transfers between devices, exchange(): return lax.ppermute(array, 'gx', pairs)  5.08 us
    pallas_call x2, Pallas kernels, convolution(): pl.pallas_call(functools.partial(convolution_kernel, x, cells_x, width, s...  4.84 us
    pallas_call x2, Pallas kernels, forward_yz(): pl.pallas_call(kernel, in_specs=[IN_SMEM] + specs, out_specs=in_vmem(len(...  3.58 us
  transfers between devices with their start and end apart: 19, of which 10 were waited for; matrix products, arithmetic and copies ran while one was open for 0% of the time, Pallas kernels for 37%

profile of v15, /device:TPU:0, one launch (start us, length us, event | category | flops | bytes accessed | tf_op | source)
XLA Modules:
  0.0 58.2 jit_solution(16117407696944332937)
XLA Ops:
  0.0 3.1 %shard_map.82 = (bf16[2,4,4,16,128]{4,3,2,1,0:T(8,128)(2,1)}, bf16[2,4,4,16,128]{4,3,2,1,0:T(8,128)(2,1)}, bf16[1024,128]{1,0:T(8,128)(2,1)}, bf16[1024,128]{1,0:T(8,128)(2,1)}) custom-call(s32[1]{0:T(128)} %bitcast.me_ref, bf16[2,512,1024]{2,1,0:T(8,128)(2,1)} %constant.18.clone.table_ref, bf16[4,1024,128]{2,1,0:T(8,128)(2,1)} %bitcast.6), custom_call_target="tpu_custom_call" | custom-call | flops 268435456 | bytes 1572864 | tf_op jit(solution)/shard_map/pallas_call | solution.py:217
  3.2 0.0 copy-start.1
  3.2 0.0 copy-start.2
  3.2 3.0 %collective-permute-start.2 = (bf16[2,4,4,16,128]{4,3,2,1,0:T(8,128)(2,1)}, bf16[2,4,4,16,128]{4,3,2,1,0:T(8,128)(2,1)S(1)}, u32[]{:S(2)}, u32[]{:S(2)}) collective-permute-start(bf16[2,4,4,16,128]{4,3,2,1,0:T(8,128)(2,1)} %get-tuple-element.83), channel_id=1, source_target_pairs={{0,1},{1,0},{2,3},{3,2},{4,5},{5,4},{6,7},{7,6},{8,9},{9,8},{10,11... | collective-permute-start | bytes 393224 | tf_op jit(solution)/shard_map/ppermute | solution.py:841
  6.2 0.1 collective-permute-start
  6.3 0.7 %collective-permute-start.9 = (bf16[1024,128]{1,0:T(8,128)(2,1)}, bf16[1024,128]{1,0:T(8,128)(2,1)S(1)}, u32[]{:S(2)}, u32[]{:S(2)}) collective-permute-start(bf16[1024,128]{1,0:T(8,128)(2,1)} %get-tuple-element.104), channel_id=1, source_target_pairs={{2,4},{6,8},{10,12},{14,16},{18,20},{22,24},{26,28},{4,2},{8,6},{1... | collective-permute-start | bytes 786440 | tf_op jit(solution)/shard_map/ppermute | solution.py:826
  7.0 2.2 %shard_map.83.refs_7_ = bf16[2,64,128,128]{3,2,1,0:T(8,128)(2,1)S(1)} custom-call(bf16[16,64,128,128]{3,2,1,0:T(8,128)(2,1)} %bitcast.13), custom_call_target="tpu_custom_call" | custom-call | bytes 4194304 | tf_op jit(solution)/shard_map/pallas_call | solution.py:330
  9.2 0.4 shard_map.84
  9.7 1.1 %collective-permute-done.2.refs_1_ = bf16[2,4,4,16,128]{4,3,2,1,0:T(8,128)(2,1)S(1)} collective-permute-done((bf16[2,4,4,16,128]{4,3,2,1,0:T(8,128)(2,1)}, bf16[2,4,4,16,128]{4,3,2,1,0:T(8,128)(2,1)S(1)}, u32[]{:S(2)}, u32[]{:S(2)}) %collective-permute-start.2) | collective-permute-done | bytes 131104 | tf_op jit(solution)/shard_map/ppermute | solution.py:841
  10.8 4.7 %collective-permute-start.3 = (bf16[4,4,16,128]{3,2,1,0:T(8,128)(2,1)S(1)}, bf16[4,4,16,128]{3,2,1,0:T(8,128)(2,1)S(1)}, u32[]{:S(2)}, u32[]{:S(2)}) collective-permute-start(bf16[4,4,16,128]{3,2,1,0:T(8,128)(2,1)S(1)} %get-tuple-element.84), channel_id=1, source_target_pairs={{0,16},{2,18},{4,20},{6,22},{8,24},{10,26},{12,28},{14,30},{16,0},... | collective-permute-start | bytes 196616 | tf_op jit(solution)/shard_map/ppermute | solution.py:837
  15.5 1.3 %collective-permute-start.4 = (bf16[4,4,16,128]{3,2,1,0:T(8,128)(2,1)S(1)}, bf16[4,4,16,128]{3,2,1,0:T(8,128)(2,1)S(1)}, u32[]{:S(2)}, u32[]{:S(2)}) collective-permute-start(bf16[4,4,16,128]{3,2,1,0:T(8,128)(2,1)S(1)} %get-tuple-element.85), channel_id=1, source_target_pairs={{0,24},{2,26},{4,28},{6,30},{8,16},{10,18},{12,20},{14,22},{16,8},... | collective-permute-start | bytes 196616 | tf_op jit(solution)/shard_map/ppermute | solution.py:837
  16.8 0.0 collective-permute-done.refs_1_
  16.9 0.3 collective-permute-start.1
  17.2 3.5 %shard_map.87.refs_8_ = bf16[4,64,128,128]{3,2,1,0:T(8,128)(2,1)S(1)} custom-call(bf16[16,64,128,128]{3,2,1,0:T(8,128)(2,1)} %bitcast.14), custom_call_target="tpu_custom_call" | custom-call | bytes 8388608 | tf_op jit(solution)/shard_map/pallas_call | solution.py:330
  20.7 0.8 %collective-permute-done.3.refs_1_ = bf16[4,4,16,128]{3,2,1,0:T(8,128)(2,1)S(1)} collective-permute-done((bf16[4,4,16,128]{3,2,1,0:T(8,128)(2,1)S(1)}, bf16[4,4,16,128]{3,2,1,0:T(8,128)(2,1)S(1)}, u32[]{:S(2)}, u32[]{:S(2)}) %collective-permute-start.3) | collective-permute-done | bytes 65568 | tf_op jit(solution)/shard_map/ppermute | solution.py:837
  21.4 0.5 collective-permute-done.4.refs_0_
  21.9 0.4 collective-permute-done.1.refs_2_
  22.3 0.0 copy-start.3
  22.3 0.0 copy-start.4
  22.3 0.5 collective-permute-start.5
  22.8 0.8 %collective-permute-start.6 = (bf16[4,4,16,128]{3,2,1,0:T(8,128)(2,1)S(1)}, bf16[4,4,16,128]{3,2,1,0:T(8,128)(2,1)S(1)}, u32[]{:S(2)}, u32[]{:S(2)}) collective-permute-start(bf16[4,4,16,128]{3,2,1,0:T(8,128)(2,1)S(1)} %get-tuple-element.97), channel_id=1, source_target_pairs={{0,4},{2,6},{4,0},{6,2},{8,12},{10,14},{12,8},{14,10},{16,20},{18,... | collective-permute-start | bytes 196616 | tf_op jit(solution)/shard_map/ppermute | solution.py:837
  23.6 0.6 collective-permute-start.7
  24.2 3.5 %shard_map.89.refs_9_ = bf16[4,64,128,128]{3,2,1,0:T(8,128)(2,1)S(1)} custom-call(bf16[16,64,128,128]{3,2,1,0:T(8,128)(2,1)} %bitcast.15), custom_call_target="tpu_custom_call" | custom-call | bytes 8388608 | tf_op jit(solution)/shard_map/pallas_call | solution.py:330
  27.7 0.0 collective-permute-done.8.paired_ref
  27.7 0.0 collective-permute-done.9.other_ref
  27.7 0.1 collective-permute-done.6.refs_1_
  27.8 0.0 collective-permute-done.7.refs_2_
  27.8 0.0 copy-start.6
  27.9 1.9 %collective-permute-start.10 = (bf16[6,64,128]{2,1,0:T(8,128)(2,1)S(1)}, bf16[6,64,128]{2,1,0:T(8,128)(2,1)S(1)}, u32[]{:S(2)}, u32[]{:S(2)}) collective-permute-start(bf16[6,64,128]{2,1,0:T(8,128)(2,1)S(1)} %shard_map.91), channel_id=1, source_target_pairs={{0,1},{1,0},{2,3},{3,2},{4,5},{5,4},{6,7},{7,6},{8,9},{9,8},{10,11... | collective-permute-start | bytes 294920 | tf_op jit(solution)/shard_map/ppermute | solution.py:841
  29.7 5.9 %shard_map.90 = (bf16[4,4,16,128]{3,2,1,0:T(8,128)(2,1)S(1)}, bf16[4,4,16,128]{3,2,1,0:T(8,128)(2,1)S(1)}, bf16[4,4,16,128]{3,2,1,0:T(8,128)(2,1)S(1)}, bf16[4,4,16,128]{3,2,1,0:T(8,128)(2,1)S(1)}) custom-call(s32[1]{0:T(128)} %bitcast.me_ref, bf16[4,4,16,128]{3,2,1,0:T(8,128)(2,1)S(1)} %collective-permute-done.5.refs_0_, ...), custom_call_target="tpu_custom_call" | custom-call | flops 134217728 | bytes 33554432 | tf_op jit(solution)/shard_map/pallas_call | solution.py:449
  35.7 0.9 %collective-permute-start.11 = (bf16[4,4,16,128]{3,2,1,0:T(8,128)(2,1)S(1)}, bf16[4,4,16,128]{3,2,1,0:T(8,128)(2,1)S(1)}, u32[]{:S(2)}, u32[]{:S(2)}) collective-permute-start(bf16[4,4,16,128]{3,2,1,0:T(8,128)(2,1)S(1)} %get-tuple-element.120), channel_id=1, source_target_pairs={{0,6},{2,4},{4,2},{6,0},{8,14},{10,12},{12,10},{14,8},{16,22},{18,... | collective-permute-start | bytes 196616 | tf_op jit(solution)/shard_map/ppermute | solution.py:837
  36.5 0.6 %collective-permute-start.12 = (bf16[4,4,16,128]{3,2,1,0:T(8,128)(2,1)S(1)}, bf16[4,4,16,128]{3,2,1,0:T(8,128)(2,1)S(1)}, u32[]{:S(2)}, u32[]{:S(2)}) collective-permute-start(bf16[4,4,16,128]{3,2,1,0:T(8,128)(2,1)S(1)} %get-tuple-element.121), channel_id=1, source_target_pairs={{0,4},{2,6},{4,0},{6,2},{8,12},{10,14},{12,8},{14,10},{16,20},{18,... | collective-permute-start | bytes 196616 | tf_op jit(solution)/shard_map/ppermute | solution.py:837
  37.2 0.4 collective-permute-start.13
  37.6 2.4 %shard_map.92.refs_4_ = bf16[2,16,64,128]{3,2,1,0:T(8,128)(2,1)S(1)} custom-call(s32[1]{0:T(128)} %bitcast.me_ref, bf16[4,16,64,128]{3,2,1,0:T(8,128)(2,1)S(1)} %copy-done.2, bf16[16,64,128]{2,1,0:T(8,128)(2,1)S(1)} %bitcast.8, bf16[16,64,128]{2,1,0:T(8,128)(2,1)S(1)} %bitcast.10, bf16[6,64,128]{2,1,0:T(8,128)(2,1)S(1)} %collective-permute-done.10.refs_3_.refs_4_, ...), custom_call_target="tpu_custom_call" | custom-call | flops 2717908992 | bytes 1310720 | tf_op jit(solution)/shard_map/pallas_call | solution.py:535
  40.0 0.1 collective-permute-done.11.refs_0_
  40.1 1.4 %collective-permute-done.12.refs_1_ = bf16[4,4,16,128]{3,2,1,0:T(8,128)(2,1)S(1)} collective-permute-done((bf16[4,4,16,128]{3,2,1,0:T(8,128)(2,1)S(1)}, bf16[4,4,16,128]{3,2,1,0:T(8,128)(2,1)S(1)}, u32[]{:S(2)}, u32[]{:S(2)}) %collective-permute-start.12) | collective-permute-done | bytes 65568 | tf_op jit(solution)/shard_map/ppermute | solution.py:837
  41.5 0.0 collective-permute-done.13.refs_2_
  41.5 3.2 %collective-permute-start.14 = (bf16[4,4,16,128]{3,2,1,0:T(8,128)(2,1)S(1)}, bf16[4,4,16,128]{3,2,1,0:T(8,128)(2,1)S(1)}, u32[]{:S(2)}, u32[]{:S(2)}) collective-permute-start(bf16[4,4,16,128]{3,2,1,0:T(8,128)(2,1)S(1)} %get-tuple-element.131), channel_id=1, source_target_pairs={{0,24},{2,26},{4,28},{6,30},{8,16},{10,18},{12,20},{14,22},{16,8},... | collective-permute-start | bytes 196616 | tf_op jit(solution)/shard_map/ppermute | solution.py:837
  44.8 0.0 collective-permute-start.16
  44.8 1.2 %collective-permute-start.17 = (bf16[4,4,16,128]{3,2,1,0:T(8,128)(2,1)S(1)}, bf16[4,4,16,128]{3,2,1,0:T(8,128)(2,1)S(1)}, u32[]{:S(2)}, u32[]{:S(2)}) collective-permute-start(bf16[4,4,16,128]{3,2,1,0:T(8,128)(2,1)S(1)} %get-tuple-element.134), channel_id=1, source_target_pairs={{0,8},{2,10},{4,12},{6,14},{8,0},{10,2},{12,4},{14,6},{16,24},{18,... | collective-permute-start | bytes 196616 | tf_op jit(solution)/shard_map/ppermute | solution.py:837
  46.0 2.4 %shard_map.94.refs_5_ = bf16[2,16,64,128]{3,2,1,0:T(8,128)(2,1)S(1)} custom-call(s32[1]{0:T(128)} %bitcast.me_ref, bf16[4,16,64,128]{3,2,1,0:T(8,128)(2,1)S(1)} %copy-done.2, bf16[16,64,128]{2,1,0:T(8,128)(2,1)S(1)} %bitcast.9, bf16[16,64,128]{2,1,0:T(8,128)(2,1)S(1)} %bitcast.11, bf16[6,64,128]{2,1,0:T(8,128)(2,1)S(1)} %collective-permute-done.10.refs_3_.refs_4_, ...), custom_call_target="tpu_custom_call" | custom-call | flops 2717908992 | bytes 1310720 | tf_op jit(solution)/shard_map/pallas_call | solution.py:535
  48.5 0.3 collective-permute-start.15
  48.8 1.9 %collective-permute-done.16.refs_0_.refs_1_ = bf16[4,4,16,128]{3,2,1,0:T(8,128)(2,1)S(1)} collective-permute-done((bf16[4,4,16,128]{3,2,1,0:T(8,128)(2,1)S(1)}, bf16[4,4,16,128]{3,2,1,0:T(8,128)(2,1)S(1)}, u32[]{:S(2)}, u32[]{:S(2)}) %collective-permute-start.16) | collective-permute-done | bytes 65568 | tf_op jit(solution)/shard_map/ppermute | solution.py:837
  50.7 0.5 collective-permute-start.18
  51.2 1.0 %shard_map.97.refs_2_ = f32[4,16,64,128]{3,2,1,0:T(8,128)S(1)} custom-call(s32[1]{0:T(128)} %bitcast.me_ref, bf16[4,1024,256]{2,1,0:T(8,128)(2,1)S(1)} %copy-done, bf16[4,4,16,128]{3,2,1,0:T(8,128)(2,1)S(1)} %collective-permute-done.14.refs_1_.refs_0_, bf16[4,4,16,128]{3,2,1,0:T(8,128)(2,1)S(1)} %collective-permute-done.16.refs_0_.refs_1_, ...), custom_call_target="tpu_custom_call" | custom-call | flops 268435456 | bytes 3145728 | tf_op jit(solution)/shard_map/pallas_call | solution.py:662
  52.2 1.4 %collective-permute-done.15.refs_0_ = bf16[2,4,4,16,128]{4,3,2,1,0:T(8,128)(2,1)S(1)} collective-permute-done((bf16[2,4,4,16,128]{4,3,2,1,0:T(8,128)(2,1)S(1)}, bf16[2,4,4,16,128]{4,3,2,1,0:T(8,128)(2,1)S(1)}, u32[]{:S(2)}, u32[]{:S(2)}) %collective-permute-start.15) | collective-permute-done | bytes 131104 | tf_op jit(solution)/shard_map/ppermute | solution.py:841
  53.6 2.7 %collective-permute-done.18.refs_1_ = bf16[2,4,4,16,128]{4,3,2,1,0:T(8,128)(2,1)S(1)} collective-permute-done((bf16[2,4,4,16,128]{4,3,2,1,0:T(8,128)(2,1)S(1)}, bf16[2,4,4,16,128]{4,3,2,1,0:T(8,128)(2,1)S(1)}, u32[]{:S(2)}, u32[]{:S(2)}) %collective-permute-start.18) | collective-permute-done | bytes 131104 | tf_op jit(solution)/shard_map/ppermute | solution.py:841
  56.3 1.9 %shard_map.98 = bf16[4,16,64,128]{3,2,1,0:T(8,128)(2,1)} custom-call(s32[1]{0:T(128)} %bitcast.me_ref, bf16[4,1024,256]{2,1,0:T(8,128)(2,1)S(1)} %copy-done, bf16[2,4,4,16,128]{4,3,2,1,0:T(8,128)(2,1)S(1)} %collective-permute-done.15.refs_0_, bf16[2,4,4,16,128]{4,3,2,1,0:T(8,128)(2,1)S(1)} %collective-permute-done.18.refs_1_, ...), custom_call_target="tpu_custom_call" | custom-call | flops 268435456 | bytes 3145728 | tf_op jit(solution)/shard_map/pallas_call | solution.py:682
  (21 shorter events, 0.2 us)
Async XLA Ops:
  3.2 6.0 %copy-start.1 = (bf16[2,512,1024]{2,1,0:T(8,128)(2,1)S(1)}, bf16[2,512,1024]{2,1,0:T(8,128)(2,1)}, u32[]{:S(2)}) copy-start(bf16[2,512,1024]{2,1,0:T(8,128)(2,1)} %constant.18.clone.table_ref) | copy-start | bytes 6291460
  3.2 6.0 %copy-start.2 = (bf16[4,16,64,128]{3,2,1,0:T(8,128)(2,1)S(1)}, bf16[4,16,64,128]{3,2,1,0:T(8,128)(2,1)}, u32[]{:S(2)}) copy-start(bf16[4,16,64,128]{3,2,1,0:T(8,128)(2,1)} %refs_0_.3) | copy-start | bytes 3145732
  3.2 7.6 %collective-permute-start.2 = (bf16[2,4,4,16,128]{4,3,2,1,0:T(8,128)(2,1)}, bf16[2,4,4,16,128]{4,3,2,1,0:T(8,128)(2,1)S(1)}, u32[]{:S(2)}, u32[]{:S(2)}) collective-permute-start(bf16[2,4,4,16,128]{4,3,2,1,0:T(8,128)(2,1)} %get-tuple-element.83), channel_id=1, source_target_pairs={{0,1},{1,0},{2,3},{3,2},{4,5},{5,4},{6,7},{7,6},{8,9},{9,8},{10,11... | collective-permute-start | bytes 393224 | tf_op jit(solution)/shard_map/ppermute | solution.py:841
  6.2 10.6 %collective-permute-start = (bf16[2,4,4,16,128]{4,3,2,1,0:T(8,128)(2,1)}, bf16[2,4,4,16,128]{4,3,2,1,0:T(8,128)(2,1)S(1)}, u32[]{:S(2)}, u32[]{:S(2)}) collective-permute-start(bf16[2,4,4,16,128]{4,3,2,1,0:T(8,128)(2,1)} %get-tuple-element.79), channel_id=1, source_target_pairs={{0,1},{1,0},{2,3},{3,2},{4,5},{5,4},{6,7},{7,6},{8,9},{9,8},{10,11... | collective-permute-start | bytes 393224 | tf_op jit(solution)/shard_map/ppermute | solution.py:841
  6.3 21.4 %collective-permute-start.8 = (bf16[1024,128]{1,0:T(8,128)(2,1)}, bf16[1024,128]{1,0:T(8,128)(2,1)S(1)}, u32[]{:S(2)}, u32[]{:S(2)}) collective-permute-start(bf16[1024,128]{1,0:T(8,128)(2,1)} %get-tuple-element.103), channel_id=1, source_target_pairs={{0,2},{4,6},{8,10},{12,14},{16,18},{20,22},{24,26},{28,30},{2,0},{... | collective-permute-start | bytes 786440 | tf_op jit(solution)/shard_map/ppermute | solution.py:826
  6.3 21.4 %collective-permute-start.9 = (bf16[1024,128]{1,0:T(8,128)(2,1)}, bf16[1024,128]{1,0:T(8,128)(2,1)S(1)}, u32[]{:S(2)}, u32[]{:S(2)}) collective-permute-start(bf16[1024,128]{1,0:T(8,128)(2,1)} %get-tuple-element.104), channel_id=1, source_target_pairs={{2,4},{6,8},{10,12},{14,16},{18,20},{22,24},{26,28},{4,2},{8,6},{1... | collective-permute-start | bytes 786440 | tf_op jit(solution)/shard_map/ppermute | solution.py:826
  10.8 10.6 %collective-permute-start.3 = (bf16[4,4,16,128]{3,2,1,0:T(8,128)(2,1)S(1)}, bf16[4,4,16,128]{3,2,1,0:T(8,128)(2,1)S(1)}, u32[]{:S(2)}, u32[]{:S(2)}) collective-permute-start(bf16[4,4,16,128]{3,2,1,0:T(8,128)(2,1)S(1)} %get-tuple-element.84), channel_id=1, source_target_pairs={{0,16},{2,18},{4,20},{6,22},{8,24},{10,26},{12,28},{14,30},{16,0},... | collective-permute-start | bytes 196616 | tf_op jit(solution)/shard_map/ppermute | solution.py:837
  15.5 6.4 %collective-permute-start.4 = (bf16[4,4,16,128]{3,2,1,0:T(8,128)(2,1)S(1)}, bf16[4,4,16,128]{3,2,1,0:T(8,128)(2,1)S(1)}, u32[]{:S(2)}, u32[]{:S(2)}) collective-permute-start(bf16[4,4,16,128]{3,2,1,0:T(8,128)(2,1)S(1)} %get-tuple-element.85), channel_id=1, source_target_pairs={{0,24},{2,26},{4,28},{6,30},{8,16},{10,18},{12,20},{14,22},{16,8},... | collective-permute-start | bytes 196616 | tf_op jit(solution)/shard_map/ppermute | solution.py:837
  16.9 5.4 %collective-permute-start.1 = (bf16[4,4,16,128]{3,2,1,0:T(8,128)(2,1)S(1)}, bf16[4,4,16,128]{3,2,1,0:T(8,128)(2,1)S(1)}, u32[]{:S(2)}, u32[]{:S(2)}) collective-permute-start(bf16[4,4,16,128]{3,2,1,0:T(8,128)(2,1)S(1)} %get-tuple-element.81), channel_id=1, source_target_pairs={{0,8},{2,10},{4,12},{6,14},{8,0},{10,2},{12,4},{14,6},{16,24},{18,... | collective-permute-start | bytes 196616 | tf_op jit(solution)/shard_map/ppermute | solution.py:837
  22.3 7.4 %copy-start.3 = (bf16[256,128]{1,0:T(8,128)(2,1)S(1)}, bf16[256,128]{1,0:T(8,128)(2,1)}, u32[]{:S(2)}) copy-start(bf16[256,128]{1,0:T(8,128)(2,1)} %constant.19.clone.refs_4_) | copy-start | bytes 196612
  22.3 7.4 %copy-start.4 = (bf16[128,128]{1,0:T(8,128)(2,1)S(1)}, bf16[128,128]{1,0:T(8,128)(2,1)}, u32[]{:S(2)}) copy-start(bf16[128,128]{1,0:T(8,128)(2,1)} %constant.20.clone.refs_5_) | copy-start | bytes 98308
  22.3 5.4 %collective-permute-start.5 = (bf16[4,4,16,128]{3,2,1,0:T(8,128)(2,1)S(1)}, bf16[4,4,16,128]{3,2,1,0:T(8,128)(2,1)S(1)}, u32[]{:S(2)}, u32[]{:S(2)}) collective-permute-start(bf16[4,4,16,128]{3,2,1,0:T(8,128)(2,1)S(1)} %get-tuple-element.96), channel_id=1, source_target_pairs={{0,6},{2,4},{4,2},{6,0},{8,14},{10,12},{12,10},{14,8},{16,22},{18,... | collective-permute-start | bytes 196616 | tf_op jit(solution)/shard_map/ppermute | solution.py:837
  22.8 5.0 %collective-permute-start.6 = (bf16[4,4,16,128]{3,2,1,0:T(8,128)(2,1)S(1)}, bf16[4,4,16,128]{3,2,1,0:T(8,128)(2,1)S(1)}, u32[]{:S(2)}, u32[]{:S(2)}) collective-permute-start(bf16[4,4,16,128]{3,2,1,0:T(8,128)(2,1)S(1)} %get-tuple-element.97), channel_id=1, source_target_pairs={{0,4},{2,6},{4,0},{6,2},{8,12},{10,14},{12,8},{14,10},{16,20},{18,... | collective-permute-start | bytes 196616 | tf_op jit(solution)/shard_map/ppermute | solution.py:837
  23.6 4.2 %collective-permute-start.7 = (bf16[4,4,16,128]{3,2,1,0:T(8,128)(2,1)S(1)}, bf16[4,4,16,128]{3,2,1,0:T(8,128)(2,1)S(1)}, u32[]{:S(2)}, u32[]{:S(2)}) collective-permute-start(bf16[4,4,16,128]{3,2,1,0:T(8,128)(2,1)S(1)} %get-tuple-element.98), channel_id=1, source_target_pairs={{0,2},{2,0},{4,6},{6,4},{8,10},{10,8},{12,14},{14,12},{16,18},{18,... | collective-permute-start | bytes 196616 | tf_op jit(solution)/shard_map/ppermute | solution.py:837
  27.8 9.8 %copy-start.6 = (bf16[3,3,3,128,128]{4,3,2,1,0:T(8,128)(2,1)S(1)}, bf16[3,3,3,128,128]{4,3,2,1,0:T(8,128)(2,1)}, u32[]{:S(2)}) copy-start(bf16[3,3,3,128,128]{4,3,2,1,0:T(8,128)(2,1)} %refs_5_.4) | copy-start | bytes 2654212
  27.9 7.8 %collective-permute-start.10 = (bf16[6,64,128]{2,1,0:T(8,128)(2,1)S(1)}, bf16[6,64,128]{2,1,0:T(8,128)(2,1)S(1)}, u32[]{:S(2)}, u32[]{:S(2)}) collective-permute-start(bf16[6,64,128]{2,1,0:T(8,128)(2,1)S(1)} %shard_map.91), channel_id=1, source_target_pairs={{0,1},{1,0},{2,3},{3,2},{4,5},{5,4},{6,7},{7,6},{8,9},{9,8},{10,11... | collective-permute-start | bytes 294920 | tf_op jit(solution)/shard_map/ppermute | solution.py:841
  35.7 4.4 %collective-permute-start.11 = (bf16[4,4,16,128]{3,2,1,0:T(8,128)(2,1)S(1)}, bf16[4,4,16,128]{3,2,1,0:T(8,128)(2,1)S(1)}, u32[]{:S(2)}, u32[]{:S(2)}) collective-permute-start(bf16[4,4,16,128]{3,2,1,0:T(8,128)(2,1)S(1)} %get-tuple-element.120), channel_id=1, source_target_pairs={{0,6},{2,4},{4,2},{6,0},{8,14},{10,12},{12,10},{14,8},{16,22},{18,... | collective-permute-start | bytes 196616 | tf_op jit(solution)/shard_map/ppermute | solution.py:837
  36.5 5.0 %collective-permute-start.12 = (bf16[4,4,16,128]{3,2,1,0:T(8,128)(2,1)S(1)}, bf16[4,4,16,128]{3,2,1,0:T(8,128)(2,1)S(1)}, u32[]{:S(2)}, u32[]{:S(2)}) collective-permute-start(bf16[4,4,16,128]{3,2,1,0:T(8,128)(2,1)S(1)} %get-tuple-element.121), channel_id=1, source_target_pairs={{0,4},{2,6},{4,0},{6,2},{8,12},{10,14},{12,8},{14,10},{16,20},{18,... | collective-permute-start | bytes 196616 | tf_op jit(solution)/shard_map/ppermute | solution.py:837
  37.2 4.3 %collective-permute-start.13 = (bf16[4,4,16,128]{3,2,1,0:T(8,128)(2,1)S(1)}, bf16[4,4,16,128]{3,2,1,0:T(8,128)(2,1)S(1)}, u32[]{:S(2)}, u32[]{:S(2)}) collective-permute-start(bf16[4,4,16,128]{3,2,1,0:T(8,128)(2,1)S(1)} %get-tuple-element.122), channel_id=1, source_target_pairs={{0,2},{2,0},{4,6},{6,4},{8,10},{10,8},{12,14},{14,12},{16,18},{18,... | collective-permute-start | bytes 196616 | tf_op jit(solution)/shard_map/ppermute | solution.py:837
  41.5 6.9 %collective-permute-start.14 = (bf16[4,4,16,128]{3,2,1,0:T(8,128)(2,1)S(1)}, bf16[4,4,16,128]{3,2,1,0:T(8,128)(2,1)S(1)}, u32[]{:S(2)}, u32[]{:S(2)}) collective-permute-start(bf16[4,4,16,128]{3,2,1,0:T(8,128)(2,1)S(1)} %get-tuple-element.131), channel_id=1, source_target_pairs={{0,24},{2,26},{4,28},{6,30},{8,16},{10,18},{12,20},{14,22},{16,8},... | collective-permute-start | bytes 196616 | tf_op jit(solution)/shard_map/ppermute | solution.py:837
  44.8 5.9 %collective-permute-start.16 = (bf16[4,4,16,128]{3,2,1,0:T(8,128)(2,1)S(1)}, bf16[4,4,16,128]{3,2,1,0:T(8,128)(2,1)S(1)}, u32[]{:S(2)}, u32[]{:S(2)}) collective-permute-start(bf16[4,4,16,128]{3,2,1,0:T(8,128)(2,1)S(1)} %get-tuple-element.133), channel_id=1, source_target_pairs={{0,16},{2,18},{4,20},{6,22},{8,24},{10,26},{12,28},{14,30},{16,0},... | collective-permute-start | bytes 196616 | tf_op jit(solution)/shard_map/ppermute | solution.py:837
  44.8 6.5 %copy-start = (bf16[4,1024,256]{2,1,0:T(8,128)(2,1)S(1)}, bf16[4,1024,256]{2,1,0:T(8,128)(2,1)}, u32[]{:S(2)}) copy-start(bf16[4,1024,256]{2,1,0:T(8,128)(2,1)} %constant.21.clone.table_ref) | copy-start | bytes 6291460
  44.8 6.5 %copy-start.5 = (f32[128]{0:T(128)S(1)}, f32[128]{0:T(128)}, u32[]{:S(2)}) copy-start(f32[128]{0:T(128)} %param.11) | copy-start | bytes 1540
  44.8 5.9 %collective-permute-start.17 = (bf16[4,4,16,128]{3,2,1,0:T(8,128)(2,1)S(1)}, bf16[4,4,16,128]{3,2,1,0:T(8,128)(2,1)S(1)}, u32[]{:S(2)}, u32[]{:S(2)}) collective-permute-start(bf16[4,4,16,128]{3,2,1,0:T(8,128)(2,1)S(1)} %get-tuple-element.134), channel_id=1, source_target_pairs={{0,8},{2,10},{4,12},{6,14},{8,0},{10,2},{12,4},{14,6},{16,24},{18,... | collective-permute-start | bytes 196616 | tf_op jit(solution)/shard_map/ppermute | solution.py:837
  48.5 5.1 %collective-permute-start.15 = (bf16[2,4,4,16,128]{4,3,2,1,0:T(8,128)(2,1)S(1)}, bf16[2,4,4,16,128]{4,3,2,1,0:T(8,128)(2,1)S(1)}, u32[]{:S(2)}, u32[]{:S(2)}) collective-permute-start(bf16[2,4,4,16,128]{4,3,2,1,0:T(8,128)(2,1)S(1)} %shard_map.95), channel_id=1, source_target_pairs={{0,1},{1,0},{2,3},{3,2},{4,5},{5,4},{6,7},{7,6},{8,9},{9,8},{10,11... | collective-permute-start | bytes 393224 | tf_op jit(solution)/shard_map/ppermute | solution.py:841
  50.7 5.6 %collective-permute-start.18 = (bf16[2,4,4,16,128]{4,3,2,1,0:T(8,128)(2,1)S(1)}, bf16[2,4,4,16,128]{4,3,2,1,0:T(8,128)(2,1)S(1)}, u32[]{:S(2)}, u32[]{:S(2)}) collective-permute-start(bf16[2,4,4,16,128]{4,3,2,1,0:T(8,128)(2,1)S(1)} %shard_map.96), channel_id=1, source_target_pairs={{0,1},{1,0},{2,3},{3,2},{4,5},{5,4},{6,7},{7,6},{8,9},{9,8},{10,11... | collective-permute-start | bytes 393224 | tf_op jit(solution)/shard_map/ppermute | solution.py:841

commit v16 on v15

--- a/solution.py
+++ b/solution.py
@@ -377,22 +377,28 @@
             at = rows_of(origin(own_outer, slot, outer), source)
             wide[at, :] = value.astype(jnp.float32)
     low = lax.broadcasted_iota(jnp.int32, (span, channels), 1) < half
-    for pair in range(pairs):
-        columns = [wide[pl.ds(2 * pair + p, full_x, stride=item_rows), :] for p in range(2)]
-        columns = jnp.concatenate(columns, axis=0).astype(jnp.bfloat16)
-        both = dot(forward_ref[...], columns)
-        value, turned = both[:span], both[span:]
-        first = jnp.where(low, value, pltpu.roll(turned, half, axis=1))
-        second = jnp.where(low, pltpu.roll(value, half, axis=1), turned)
-        left[pl.ds(pair * span, span), :channels] = first.astype(left.dtype)
-        left[pl.ds(pair * span, span), channels:] = second.astype(left.dtype)
+    width = 2 if pairs % 2 == 0 else 1
+    for first_pair in range(0, pairs, width):
+        columns = []
+        for pair in range(first_pair, first_pair + width):
+            parts = [wide[pl.ds(2 * pair + p, full_x, stride=item_rows), :] for p in range(2)]
+            columns.append(jnp.concatenate(parts, axis=0).astype(jnp.bfloat16))
+        both = dot(forward_ref[...], jnp.concatenate(columns, axis=1))
+        for i in range(width):
+            value = both[:span, i * channels : (i + 1) * channels]
+            turned = both[span:, i * channels : (i + 1) * channels]
+            first = jnp.where(low, value, pltpu.roll(turned, half, axis=1))
+            second = jnp.where(low, pltpu.roll(value, half, axis=1), turned)
+            rows = pl.ds((first_pair + i) * span, span)
+            left[rows, :channels] = first.astype(left.dtype)
+            left[rows, channels:] = second.astype(left.dtype)
 
     group = 16
     row = lax.broadcasted_iota(jnp.int32, (group, channels), 0) // 2
 
     def mix(pair, tile_of):
         for step in range(span // group):
-            start = pl.multiple_of(pair * span + step * group, group)
+            start = pair * span + step * group
             lhs = left[pl.ds(start, group), :]
             gathered = jnp.zeros((group, channels), jnp.float32)
             for i in range(0, group // 2, 2):
@@ -410,28 +416,24 @@
 
     pair = 0
     for ref in loaded_refs:
-        count = ref.shape[0] // 2
-
-        def ready(i, carry, ref=ref, pair=pair):
-            mix(pair + i, lambda h, mode: ref[2 * i + h, mode])
-            return carry
-
-        lax.fori_loop(0, count, ready, 0)
-        pair += count
-
-    def streamed(pair, carry):
+        for i in range(ref.shape[0] // 2):
+            mix(pair, lambda h, mode, ref=ref, i=i: ref[2 * i + h, mode])
+            pair += 1
+    for pair in range(loaded, pairs):
         copy(pair).wait()
-        mix(pair, lambda h, mode: held[pair - loaded, h, mode])
-        return carry
-
-    lax.fori_loop(loaded, pairs, streamed, 0)
-
-    for pair in range(pairs):
-        result = dot(backward_ref[...], mixed[pl.ds(pair * span, span), :])
-        for p in range(2):
-            wide[pl.ds(2 * pair + p, full_x, stride=item_rows), :] = result[
-                p * full_x : (p + 1) * full_x
-            ]
+        mix(pair, lambda h, mode, pair=pair: held[pair - loaded, h, mode])
+
+    for first_pair in range(0, pairs, width):
+        columns = [
+            mixed[pl.ds(pair * span, span), :] for pair in range(first_pair, first_pair + width)
+        ]
+        result = dot(backward_ref[...], jnp.concatenate(columns, axis=1))
+        for i in range(width):
+            for p in range(2):
+                rows = pl.ds(2 * (first_pair + i) + p, full_x, stride=item_rows)
+                wide[rows, :] = result[
+                    p * full_x : (p + 1) * full_x, i * channels : (i + 1) * channels
+                ]
     for step in range(inner):
         target = peer(own_inner, step, inner)
         for slot in range(outer):

time: 58.4 us -> 58.2 us (level)
  no operation moved by 1% of the time
where the time goes in v16:
time: 58.2 us; the launch traced here: 58 us
  Pallas kernels  26.3 us (45%)
  starting transfers between devices  21.2 us (36%)
  waiting for transfers between devices  10.3 us (18%)
    ppermute x12, starting transfers between devices, exchange(): return lax.ppermute(array, 'gx', pairs)  14.7 us
    pallas_call x3, Pallas kernels, preload(): pl.pallas_call(functools.partial(preload_kernel, 2 * pair), in_specs=[pl....  9.15 us
    ppermute x5, starting transfers between devices, over_y(): lax.ppermute(array, 'gy', [(i, (i + step) % shards_y) for i in range(shar...  5.82 us
    pallas_call x1, Pallas kernels, mixing(): pl.pallas_call(functools.partial(mixing_kernel, shards, len(loaded)), in_...  5.69 us
    ppermute x5, waiting for transfers between devices, over_y(): lax.ppermute(array, 'gy', [(i, (i + step) % shards_y) for i in range(shar...  5.19 us
    ppermute x12, waiting for transfers between devices, exchange(): return lax.ppermute(array, 'gx', pairs)  5.08 us
    pallas_call x2, Pallas kernels, convolution(): pl.pallas_call(functools.partial(convolution_kernel, x, cells_x, width, s...  4.84 us
    pallas_call x2, Pallas kernels, forward_yz(): pl.pallas_call(kernel, in_specs=[IN_SMEM] + specs, out_specs=in_vmem(len(...  3.58 us
  transfers between devices with their start and end apart: 19, of which 10 were waited for; matrix products, arithmetic and copies ran while one was open for 0% of the time, Pallas kernels for 37%

profile of v16, /device:TPU:0, one launch (start us, length us, event | category | flops | bytes accessed | tf_op | source)
XLA Modules:
  0.0 58.0 jit_solution(2590418781102400498)
XLA Ops:
  0.0 3.1 %shard_map.82 = (bf16[2,4,4,16,128]{4,3,2,1,0:T(8,128)(2,1)}, bf16[2,4,4,16,128]{4,3,2,1,0:T(8,128)(2,1)}, bf16[1024,128]{1,0:T(8,128)(2,1)}, bf16[1024,128]{1,0:T(8,128)(2,1)}) custom-call(s32[1]{0:T(128)} %bitcast.me_ref, bf16[2,512,1024]{2,1,0:T(8,128)(2,1)} %constant.18.clone.table_ref, bf16[4,1024,128]{2,1,0:T(8,128)(2,1)} %bitcast.6), custom_call_target="tpu_custom_call" | custom-call | flops 268435456 | bytes 1572864 | tf_op jit(solution)/shard_map/pallas_call | solution.py:217
  3.2 0.0 copy-start.1
  3.2 0.0 copy-start.2
  3.2 3.0 %collective-permute-start.2 = (bf16[2,4,4,16,128]{4,3,2,1,0:T(8,128)(2,1)}, bf16[2,4,4,16,128]{4,3,2,1,0:T(8,128)(2,1)S(1)}, u32[]{:S(2)}, u32[]{:S(2)}) collective-permute-start(bf16[2,4,4,16,128]{4,3,2,1,0:T(8,128)(2,1)} %get-tuple-element.83), channel_id=1, source_target_pairs={{0,1},{1,0},{2,3},{3,2},{4,5},{5,4},{6,7},{7,6},{8,9},{9,8},{10,11... | collective-permute-start | bytes 393224 | tf_op jit(solution)/shard_map/ppermute | solution.py:843
  6.2 0.1 collective-permute-start
  6.3 0.7 %collective-permute-start.9 = (bf16[1024,128]{1,0:T(8,128)(2,1)}, bf16[1024,128]{1,0:T(8,128)(2,1)S(1)}, u32[]{:S(2)}, u32[]{:S(2)}) collective-permute-start(bf16[1024,128]{1,0:T(8,128)(2,1)} %get-tuple-element.104), channel_id=1, source_target_pairs={{2,4},{6,8},{10,12},{14,16},{18,20},{22,24},{26,28},{4,2},{8,6},{1... | collective-permute-start | bytes 786440 | tf_op jit(solution)/shard_map/ppermute | solution.py:828
  7.0 2.2 %shard_map.83.refs_7_ = bf16[2,64,128,128]{3,2,1,0:T(8,128)(2,1)S(1)} custom-call(bf16[16,64,128,128]{3,2,1,0:T(8,128)(2,1)} %bitcast.13), custom_call_target="tpu_custom_call" | custom-call | bytes 4194304 | tf_op jit(solution)/shard_map/pallas_call | solution.py:330
  9.2 0.4 shard_map.84
  9.7 1.1 %collective-permute-done.2.refs_1_ = bf16[2,4,4,16,128]{4,3,2,1,0:T(8,128)(2,1)S(1)} collective-permute-done((bf16[2,4,4,16,128]{4,3,2,1,0:T(8,128)(2,1)}, bf16[2,4,4,16,128]{4,3,2,1,0:T(8,128)(2,1)S(1)}, u32[]{:S(2)}, u32[]{:S(2)}) %collective-permute-start.2) | collective-permute-done | bytes 131104 | tf_op jit(solution)/shard_map/ppermute | solution.py:843
  10.8 4.7 %collective-permute-start.3 = (bf16[4,4,16,128]{3,2,1,0:T(8,128)(2,1)S(1)}, bf16[4,4,16,128]{3,2,1,0:T(8,128)(2,1)S(1)}, u32[]{:S(2)}, u32[]{:S(2)}) collective-permute-start(bf16[4,4,16,128]{3,2,1,0:T(8,128)(2,1)S(1)} %get-tuple-element.84), channel_id=1, source_target_pairs={{0,16},{2,18},{4,20},{6,22},{8,24},{10,26},{12,28},{14,30},{16,0},... | collective-permute-start | bytes 196616 | tf_op jit(solution)/shard_map/ppermute | solution.py:839
  15.5 1.3 %collective-permute-start.4 = (bf16[4,4,16,128]{3,2,1,0:T(8,128)(2,1)S(1)}, bf16[4,4,16,128]{3,2,1,0:T(8,128)(2,1)S(1)}, u32[]{:S(2)}, u32[]{:S(2)}) collective-permute-start(bf16[4,4,16,128]{3,2,1,0:T(8,128)(2,1)S(1)} %get-tuple-element.85), channel_id=1, source_target_pairs={{0,24},{2,26},{4,28},{6,30},{8,16},{10,18},{12,20},{14,22},{16,8},... | collective-permute-start | bytes 196616 | tf_op jit(solution)/shard_map/ppermute | solution.py:839
  16.8 0.0 collective-permute-done.refs_1_
  16.9 0.3 collective-permute-start.1
  17.2 3.5 %shard_map.87.refs_8_ = bf16[4,64,128,128]{3,2,1,0:T(8,128)(2,1)S(1)} custom-call(bf16[16,64,128,128]{3,2,1,0:T(8,128)(2,1)} %bitcast.14), custom_call_target="tpu_custom_call" | custom-call | bytes 8388608 | tf_op jit(solution)/shard_map/pallas_call | solution.py:330
  20.7 0.8 %collective-permute-done.3.refs_1_ = bf16[4,4,16,128]{3,2,1,0:T(8,128)(2,1)S(1)} collective-permute-done((bf16[4,4,16,128]{3,2,1,0:T(8,128)(2,1)S(1)}, bf16[4,4,16,128]{3,2,1,0:T(8,128)(2,1)S(1)}, u32[]{:S(2)}, u32[]{:S(2)}) %collective-permute-start.3) | collective-permute-done | bytes 65568 | tf_op jit(solution)/shard_map/ppermute | solution.py:839
  21.4 0.5 collective-permute-done.4.refs_0_
  21.9 0.4 collective-permute-done.1.refs_2_
  22.3 0.0 copy-start.3
  22.3 0.0 copy-start.4
  22.3 0.5 collective-permute-start.5
  22.8 0.8 %collective-permute-start.6 = (bf16[4,4,16,128]{3,2,1,0:T(8,128)(2,1)S(1)}, bf16[4,4,16,128]{3,2,1,0:T(8,128)(2,1)S(1)}, u32[]{:S(2)}, u32[]{:S(2)}) collective-permute-start(bf16[4,4,16,128]{3,2,1,0:T(8,128)(2,1)S(1)} %get-tuple-element.97), channel_id=1, source_target_pairs={{0,4},{2,6},{4,0},{6,2},{8,12},{10,14},{12,8},{14,10},{16,20},{18,... | collective-permute-start | bytes 196616 | tf_op jit(solution)/shard_map/ppermute | solution.py:839
  23.6 0.6 %collective-permute-start.7 = (bf16[4,4,16,128]{3,2,1,0:T(8,128)(2,1)S(1)}, bf16[4,4,16,128]{3,2,1,0:T(8,128)(2,1)S(1)}, u32[]{:S(2)}, u32[]{:S(2)}) collective-permute-start(bf16[4,4,16,128]{3,2,1,0:T(8,128)(2,1)S(1)} %get-tuple-element.98), channel_id=1, source_target_pairs={{0,2},{2,0},{4,6},{6,4},{8,10},{10,8},{12,14},{14,12},{16,18},{18,... | collective-permute-start | bytes 196616 | tf_op jit(solution)/shard_map/ppermute | solution.py:839
  24.2 3.5 %shard_map.89.refs_9_ = bf16[4,64,128,128]{3,2,1,0:T(8,128)(2,1)S(1)} custom-call(bf16[16,64,128,128]{3,2,1,0:T(8,128)(2,1)} %bitcast.15), custom_call_target="tpu_custom_call" | custom-call | bytes 8388608 | tf_op jit(solution)/shard_map/pallas_call | solution.py:330
  27.7 0.0 collective-permute-done.8.paired_ref
  27.7 0.0 collective-permute-done.9.other_ref
  27.7 0.1 collective-permute-done.6.refs_1_
  27.8 0.0 collective-permute-done.7.refs_2_
  27.8 0.0 copy-start.6
  27.9 1.9 %collective-permute-start.10 = (bf16[6,64,128]{2,1,0:T(8,128)(2,1)S(1)}, bf16[6,64,128]{2,1,0:T(8,128)(2,1)S(1)}, u32[]{:S(2)}, u32[]{:S(2)}) collective-permute-start(bf16[6,64,128]{2,1,0:T(8,128)(2,1)S(1)} %shard_map.91), channel_id=1, source_target_pairs={{0,1},{1,0},{2,3},{3,2},{4,5},{5,4},{6,7},{7,6},{8,9},{9,8},{10,11... | collective-permute-start | bytes 294920 | tf_op jit(solution)/shard_map/ppermute | solution.py:843
  29.7 5.7 %shard_map.90 = (bf16[4,4,16,128]{3,2,1,0:T(8,128)(2,1)S(1)}, bf16[4,4,16,128]{3,2,1,0:T(8,128)(2,1)S(1)}, bf16[4,4,16,128]{3,2,1,0:T(8,128)(2,1)S(1)}, bf16[4,4,16,128]{3,2,1,0:T(8,128)(2,1)S(1)}) custom-call(s32[1]{0:T(128)} %bitcast.me_ref, bf16[4,4,16,128]{3,2,1,0:T(8,128)(2,1)S(1)} %collective-permute-done.5.refs_0_, ...), custom_call_target="tpu_custom_call" | custom-call | flops 134217728 | bytes 33554432 | tf_op jit(solution)/shard_map/pallas_call | solution.py:451
  35.4 0.9 %collective-permute-start.11 = (bf16[4,4,16,128]{3,2,1,0:T(8,128)(2,1)S(1)}, bf16[4,4,16,128]{3,2,1,0:T(8,128)(2,1)S(1)}, u32[]{:S(2)}, u32[]{:S(2)}) collective-permute-start(bf16[4,4,16,128]{3,2,1,0:T(8,128)(2,1)S(1)} %get-tuple-element.120), channel_id=1, source_target_pairs={{0,6},{2,4},{4,2},{6,0},{8,14},{10,12},{12,10},{14,8},{16,22},{18,... | collective-permute-start | bytes 196616 | tf_op jit(solution)/shard_map/ppermute | solution.py:839
  36.3 0.6 %collective-permute-start.12 = (bf16[4,4,16,128]{3,2,1,0:T(8,128)(2,1)S(1)}, bf16[4,4,16,128]{3,2,1,0:T(8,128)(2,1)S(1)}, u32[]{:S(2)}, u32[]{:S(2)}) collective-permute-start(bf16[4,4,16,128]{3,2,1,0:T(8,128)(2,1)S(1)} %get-tuple-element.121), channel_id=1, source_target_pairs={{0,4},{2,6},{4,0},{6,2},{8,12},{10,14},{12,8},{14,10},{16,20},{18,... | collective-permute-start | bytes 196616 | tf_op jit(solution)/shard_map/ppermute | solution.py:839
  36.9 0.4 collective-permute-start.13
  37.4 2.4 %shard_map.92.refs_4_ = bf16[2,16,64,128]{3,2,1,0:T(8,128)(2,1)S(1)} custom-call(s32[1]{0:T(128)} %bitcast.me_ref, bf16[4,16,64,128]{3,2,1,0:T(8,128)(2,1)S(1)} %copy-done.2, bf16[16,64,128]{2,1,0:T(8,128)(2,1)S(1)} %bitcast.8, bf16[16,64,128]{2,1,0:T(8,128)(2,1)S(1)} %bitcast.10, bf16[6,64,128]{2,1,0:T(8,128)(2,1)S(1)} %collective-permute-done.10.refs_3_.refs_4_, ...), custom_call_target="tpu_custom_call" | custom-call | flops 2717908992 | bytes 1310720 | tf_op jit(solution)/shard_map/pallas_call | solution.py:537
  39.8 0.1 collective-permute-done.11.refs_0_
  39.9 1.4 %collective-permute-done.12.refs_1_ = bf16[4,4,16,128]{3,2,1,0:T(8,128)(2,1)S(1)} collective-permute-done((bf16[4,4,16,128]{3,2,1,0:T(8,128)(2,1)S(1)}, bf16[4,4,16,128]{3,2,1,0:T(8,128)(2,1)S(1)}, u32[]{:S(2)}, u32[]{:S(2)}) %collective-permute-start.12) | collective-permute-done | bytes 65568 | tf_op jit(solution)/shard_map/ppermute | solution.py:839
  41.3 0.0 collective-permute-done.13.refs_2_
  41.3 3.2 %collective-permute-start.14 = (bf16[4,4,16,128]{3,2,1,0:T(8,128)(2,1)S(1)}, bf16[4,4,16,128]{3,2,1,0:T(8,128)(2,1)S(1)}, u32[]{:S(2)}, u32[]{:S(2)}) collective-permute-start(bf16[4,4,16,128]{3,2,1,0:T(8,128)(2,1)S(1)} %get-tuple-element.131), channel_id=1, source_target_pairs={{0,24},{2,26},{4,28},{6,30},{8,16},{10,18},{12,20},{14,22},{16,8},... | collective-permute-start | bytes 196616 | tf_op jit(solution)/shard_map/ppermute | solution.py:839
  44.5 0.0 collective-permute-start.16
  44.6 1.2 %collective-permute-start.17 = (bf16[4,4,16,128]{3,2,1,0:T(8,128)(2,1)S(1)}, bf16[4,4,16,128]{3,2,1,0:T(8,128)(2,1)S(1)}, u32[]{:S(2)}, u32[]{:S(2)}) collective-permute-start(bf16[4,4,16,128]{3,2,1,0:T(8,128)(2,1)S(1)} %get-tuple-element.134), channel_id=1, source_target_pairs={{0,8},{2,10},{4,12},{6,14},{8,0},{10,2},{12,4},{14,6},{16,24},{18,... | collective-permute-start | bytes 196616 | tf_op jit(solution)/shard_map/ppermute | solution.py:839
  45.8 2.4 %shard_map.94.refs_5_ = bf16[2,16,64,128]{3,2,1,0:T(8,128)(2,1)S(1)} custom-call(s32[1]{0:T(128)} %bitcast.me_ref, bf16[4,16,64,128]{3,2,1,0:T(8,128)(2,1)S(1)} %copy-done.2, bf16[16,64,128]{2,1,0:T(8,128)(2,1)S(1)} %bitcast.9, bf16[16,64,128]{2,1,0:T(8,128)(2,1)S(1)} %bitcast.11, bf16[6,64,128]{2,1,0:T(8,128)(2,1)S(1)} %collective-permute-done.10.refs_3_.refs_4_, ...), custom_call_target="tpu_custom_call" | custom-call | flops 2717908992 | bytes 1310720 | tf_op jit(solution)/shard_map/pallas_call | solution.py:537
  48.2 0.3 collective-permute-start.15
  48.5 1.9 %collective-permute-done.16.refs_0_.refs_1_ = bf16[4,4,16,128]{3,2,1,0:T(8,128)(2,1)S(1)} collective-permute-done((bf16[4,4,16,128]{3,2,1,0:T(8,128)(2,1)S(1)}, bf16[4,4,16,128]{3,2,1,0:T(8,128)(2,1)S(1)}, u32[]{:S(2)}, u32[]{:S(2)}) %collective-permute-start.16) | collective-permute-done | bytes 65568 | tf_op jit(solution)/shard_map/ppermute | solution.py:839
  50.5 0.5 collective-permute-start.18
  51.0 1.0 %shard_map.97.refs_2_ = f32[4,16,64,128]{3,2,1,0:T(8,128)S(1)} custom-call(s32[1]{0:T(128)} %bitcast.me_ref, bf16[4,1024,256]{2,1,0:T(8,128)(2,1)S(1)} %copy-done, bf16[4,4,16,128]{3,2,1,0:T(8,128)(2,1)S(1)} %collective-permute-done.14.refs_1_.refs_0_, bf16[4,4,16,128]{3,2,1,0:T(8,128)(2,1)S(1)} %collective-permute-done.16.refs_0_.refs_1_, ...), custom_call_target="tpu_custom_call" | custom-call | flops 268435456 | bytes 3145728 | tf_op jit(solution)/shard_map/pallas_call | solution.py:664
  52.0 1.4 %collective-permute-done.15.refs_0_ = bf16[2,4,4,16,128]{4,3,2,1,0:T(8,128)(2,1)S(1)} collective-permute-done((bf16[2,4,4,16,128]{4,3,2,1,0:T(8,128)(2,1)S(1)}, bf16[2,4,4,16,128]{4,3,2,1,0:T(8,128)(2,1)S(1)}, u32[]{:S(2)}, u32[]{:S(2)}) %collective-permute-start.15) | collective-permute-done | bytes 131104 | tf_op jit(solution)/shard_map/ppermute | solution.py:843
  53.3 2.7 %collective-permute-done.18.refs_1_ = bf16[2,4,4,16,128]{4,3,2,1,0:T(8,128)(2,1)S(1)} collective-permute-done((bf16[2,4,4,16,128]{4,3,2,1,0:T(8,128)(2,1)S(1)}, bf16[2,4,4,16,128]{4,3,2,1,0:T(8,128)(2,1)S(1)}, u32[]{:S(2)}, u32[]{:S(2)}) %collective-permute-start.18) | collective-permute-done | bytes 131104 | tf_op jit(solution)/shard_map/ppermute | solution.py:843
  56.1 1.9 %shard_map.98 = bf16[4,16,64,128]{3,2,1,0:T(8,128)(2,1)} custom-call(s32[1]{0:T(128)} %bitcast.me_ref, bf16[4,1024,256]{2,1,0:T(8,128)(2,1)S(1)} %copy-done, bf16[2,4,4,16,128]{4,3,2,1,0:T(8,128)(2,1)S(1)} %collective-permute-done.15.refs_0_, bf16[2,4,4,16,128]{4,3,2,1,0:T(8,128)(2,1)S(1)} %collective-permute-done.18.refs_1_, ...), custom_call_target="tpu_custom_call" | custom-call | flops 268435456 | bytes 3145728 | tf_op jit(solution)/shard_map/pallas_call | solution.py:684
  (21 shorter events, 0.2 us)
Async XLA Ops:
  3.2 6.0 %copy-start.1 = (bf16[2,512,1024]{2,1,0:T(8,128)(2,1)S(1)}, bf16[2,512,1024]{2,1,0:T(8,128)(2,1)}, u32[]{:S(2)}) copy-start(bf16[2,512,1024]{2,1,0:T(8,128)(2,1)} %constant.18.clone.table_ref) | copy-start | bytes 6291460
  3.2 6.0 %copy-start.2 = (bf16[4,16,64,128]{3,2,1,0:T(8,128)(2,1)S(1)}, bf16[4,16,64,128]{3,2,1,0:T(8,128)(2,1)}, u32[]{:S(2)}) copy-start(bf16[4,16,64,128]{3,2,1,0:T(8,128)(2,1)} %refs_0_.3) | copy-start | bytes 3145732
  3.2 7.6 %collective-permute-start.2 = (bf16[2,4,4,16,128]{4,3,2,1,0:T(8,128)(2,1)}, bf16[2,4,4,16,128]{4,3,2,1,0:T(8,128)(2,1)S(1)}, u32[]{:S(2)}, u32[]{:S(2)}) collective-permute-start(bf16[2,4,4,16,128]{4,3,2,1,0:T(8,128)(2,1)} %get-tuple-element.83), channel_id=1, source_target_pairs={{0,1},{1,0},{2,3},{3,2},{4,5},{5,4},{6,7},{7,6},{8,9},{9,8},{10,11... | collective-permute-start | bytes 393224 | tf_op jit(solution)/shard_map/ppermute | solution.py:843
  6.2 10.6 %collective-permute-start = (bf16[2,4,4,16,128]{4,3,2,1,0:T(8,128)(2,1)}, bf16[2,4,4,16,128]{4,3,2,1,0:T(8,128)(2,1)S(1)}, u32[]{:S(2)}, u32[]{:S(2)}) collective-permute-start(bf16[2,4,4,16,128]{4,3,2,1,0:T(8,128)(2,1)} %get-tuple-element.79), channel_id=1, source_target_pairs={{0,1},{1,0},{2,3},{3,2},{4,5},{5,4},{6,7},{7,6},{8,9},{9,8},{10,11... | collective-permute-start | bytes 393224 | tf_op jit(solution)/shard_map/ppermute | solution.py:843
  6.3 21.4 %collective-permute-start.8 = (bf16[1024,128]{1,0:T(8,128)(2,1)}, bf16[1024,128]{1,0:T(8,128)(2,1)S(1)}, u32[]{:S(2)}, u32[]{:S(2)}) collective-permute-start(bf16[1024,128]{1,0:T(8,128)(2,1)} %get-tuple-element.103), channel_id=1, source_target_pairs={{0,2},{4,6},{8,10},{12,14},{16,18},{20,22},{24,26},{28,30},{2,0},{... | collective-permute-start | bytes 786440 | tf_op jit(solution)/shard_map/ppermute | solution.py:828
  6.3 21.4 %collective-permute-start.9 = (bf16[1024,128]{1,0:T(8,128)(2,1)}, bf16[1024,128]{1,0:T(8,128)(2,1)S(1)}, u32[]{:S(2)}, u32[]{:S(2)}) collective-permute-start(bf16[1024,128]{1,0:T(8,128)(2,1)} %get-tuple-element.104), channel_id=1, source_target_pairs={{2,4},{6,8},{10,12},{14,16},{18,20},{22,24},{26,28},{4,2},{8,6},{1... | collective-permute-start | bytes 786440 | tf_op jit(solution)/shard_map/ppermute | solution.py:828
  10.8 10.6 %collective-permute-start.3 = (bf16[4,4,16,128]{3,2,1,0:T(8,128)(2,1)S(1)}, bf16[4,4,16,128]{3,2,1,0:T(8,128)(2,1)S(1)}, u32[]{:S(2)}, u32[]{:S(2)}) collective-permute-start(bf16[4,4,16,128]{3,2,1,0:T(8,128)(2,1)S(1)} %get-tuple-element.84), channel_id=1, source_target_pairs={{0,16},{2,18},{4,20},{6,22},{8,24},{10,26},{12,28},{14,30},{16,0},... | collective-permute-start | bytes 196616 | tf_op jit(solution)/shard_map/ppermute | solution.py:839
  15.5 6.4 %collective-permute-start.4 = (bf16[4,4,16,128]{3,2,1,0:T(8,128)(2,1)S(1)}, bf16[4,4,16,128]{3,2,1,0:T(8,128)(2,1)S(1)}, u32[]{:S(2)}, u32[]{:S(2)}) collective-permute-start(bf16[4,4,16,128]{3,2,1,0:T(8,128)(2,1)S(1)} %get-tuple-element.85), channel_id=1, source_target_pairs={{0,24},{2,26},{4,28},{6,30},{8,16},{10,18},{12,20},{14,22},{16,8},... | collective-permute-start | bytes 196616 | tf_op jit(solution)/shard_map/ppermute | solution.py:839
  16.9 5.4 %collective-permute-start.1 = (bf16[4,4,16,128]{3,2,1,0:T(8,128)(2,1)S(1)}, bf16[4,4,16,128]{3,2,1,0:T(8,128)(2,1)S(1)}, u32[]{:S(2)}, u32[]{:S(2)}) collective-permute-start(bf16[4,4,16,128]{3,2,1,0:T(8,128)(2,1)S(1)} %get-tuple-element.81), channel_id=1, source_target_pairs={{0,8},{2,10},{4,12},{6,14},{8,0},{10,2},{12,4},{14,6},{16,24},{18,... | collective-permute-start | bytes 196616 | tf_op jit(solution)/shard_map/ppermute | solution.py:839
  22.3 7.4 %copy-start.3 = (bf16[256,128]{1,0:T(8,128)(2,1)S(1)}, bf16[256,128]{1,0:T(8,128)(2,1)}, u32[]{:S(2)}) copy-start(bf16[256,128]{1,0:T(8,128)(2,1)} %constant.19.clone.refs_4_) | copy-start | bytes 196612
  22.3 7.4 %copy-start.4 = (bf16[128,128]{1,0:T(8,128)(2,1)S(1)}, bf16[128,128]{1,0:T(8,128)(2,1)}, u32[]{:S(2)}) copy-start(bf16[128,128]{1,0:T(8,128)(2,1)} %constant.20.clone.refs_5_) | copy-start | bytes 98308
  22.3 5.4 %collective-permute-start.5 = (bf16[4,4,16,128]{3,2,1,0:T(8,128)(2,1)S(1)}, bf16[4,4,16,128]{3,2,1,0:T(8,128)(2,1)S(1)}, u32[]{:S(2)}, u32[]{:S(2)}) collective-permute-start(bf16[4,4,16,128]{3,2,1,0:T(8,128)(2,1)S(1)} %get-tuple-element.96), channel_id=1, source_target_pairs={{0,6},{2,4},{4,2},{6,0},{8,14},{10,12},{12,10},{14,8},{16,22},{18,... | collective-permute-start | bytes 196616 | tf_op jit(solution)/shard_map/ppermute | solution.py:839
  22.8 5.0 %collective-permute-start.6 = (bf16[4,4,16,128]{3,2,1,0:T(8,128)(2,1)S(1)}, bf16[4,4,16,128]{3,2,1,0:T(8,128)(2,1)S(1)}, u32[]{:S(2)}, u32[]{:S(2)}) collective-permute-start(bf16[4,4,16,128]{3,2,1,0:T(8,128)(2,1)S(1)} %get-tuple-element.97), channel_id=1, source_target_pairs={{0,4},{2,6},{4,0},{6,2},{8,12},{10,14},{12,8},{14,10},{16,20},{18,... | collective-permute-start | bytes 196616 | tf_op jit(solution)/shard_map/ppermute | solution.py:839
  23.6 4.2 %collective-permute-start.7 = (bf16[4,4,16,128]{3,2,1,0:T(8,128)(2,1)S(1)}, bf16[4,4,16,128]{3,2,1,0:T(8,128)(2,1)S(1)}, u32[]{:S(2)}, u32[]{:S(2)}) collective-permute-start(bf16[4,4,16,128]{3,2,1,0:T(8,128)(2,1)S(1)} %get-tuple-element.98), channel_id=1, source_target_pairs={{0,2},{2,0},{4,6},{6,4},{8,10},{10,8},{12,14},{14,12},{16,18},{18,... | collective-permute-start | bytes 196616 | tf_op jit(solution)/shard_map/ppermute | solution.py:839
  27.8 9.5 %copy-start.6 = (bf16[3,3,3,128,128]{4,3,2,1,0:T(8,128)(2,1)S(1)}, bf16[3,3,3,128,128]{4,3,2,1,0:T(8,128)(2,1)}, u32[]{:S(2)}) copy-start(bf16[3,3,3,128,128]{4,3,2,1,0:T(8,128)(2,1)} %refs_5_.4) | copy-start | bytes 2654212
  27.9 7.6 %collective-permute-start.10 = (bf16[6,64,128]{2,1,0:T(8,128)(2,1)S(1)}, bf16[6,64,128]{2,1,0:T(8,128)(2,1)S(1)}, u32[]{:S(2)}, u32[]{:S(2)}) collective-permute-start(bf16[6,64,128]{2,1,0:T(8,128)(2,1)S(1)} %shard_map.91), channel_id=1, source_target_pairs={{0,1},{1,0},{2,3},{3,2},{4,5},{5,4},{6,7},{7,6},{8,9},{9,8},{10,11... | collective-permute-start | bytes 294920 | tf_op jit(solution)/shard_map/ppermute | solution.py:843
  35.4 4.4 %collective-permute-start.11 = (bf16[4,4,16,128]{3,2,1,0:T(8,128)(2,1)S(1)}, bf16[4,4,16,128]{3,2,1,0:T(8,128)(2,1)S(1)}, u32[]{:S(2)}, u32[]{:S(2)}) collective-permute-start(bf16[4,4,16,128]{3,2,1,0:T(8,128)(2,1)S(1)} %get-tuple-element.120), channel_id=1, source_target_pairs={{0,6},{2,4},{4,2},{6,0},{8,14},{10,12},{12,10},{14,8},{16,22},{18,... | collective-permute-start | bytes 196616 | tf_op jit(solution)/shard_map/ppermute | solution.py:839
  36.3 5.0 %collective-permute-start.12 = (bf16[4,4,16,128]{3,2,1,0:T(8,128)(2,1)S(1)}, bf16[4,4,16,128]{3,2,1,0:T(8,128)(2,1)S(1)}, u32[]{:S(2)}, u32[]{:S(2)}) collective-permute-start(bf16[4,4,16,128]{3,2,1,0:T(8,128)(2,1)S(1)} %get-tuple-element.121), channel_id=1, source_target_pairs={{0,4},{2,6},{4,0},{6,2},{8,12},{10,14},{12,8},{14,10},{16,20},{18,... | collective-permute-start | bytes 196616 | tf_op jit(solution)/shard_map/ppermute | solution.py:839
  36.9 4.3 %collective-permute-start.13 = (bf16[4,4,16,128]{3,2,1,0:T(8,128)(2,1)S(1)}, bf16[4,4,16,128]{3,2,1,0:T(8,128)(2,1)S(1)}, u32[]{:S(2)}, u32[]{:S(2)}) collective-permute-start(bf16[4,4,16,128]{3,2,1,0:T(8,128)(2,1)S(1)} %get-tuple-element.122), channel_id=1, source_target_pairs={{0,2},{2,0},{4,6},{6,4},{8,10},{10,8},{12,14},{14,12},{16,18},{18,... | collective-permute-start | bytes 196616 | tf_op jit(solution)/shard_map/ppermute | solution.py:839
  41.3 6.9 %collective-permute-start.14 = (bf16[4,4,16,128]{3,2,1,0:T(8,128)(2,1)S(1)}, bf16[4,4,16,128]{3,2,1,0:T(8,128)(2,1)S(1)}, u32[]{:S(2)}, u32[]{:S(2)}) collective-permute-start(bf16[4,4,16,128]{3,2,1,0:T(8,128)(2,1)S(1)} %get-tuple-element.131), channel_id=1, source_target_pairs={{0,24},{2,26},{4,28},{6,30},{8,16},{10,18},{12,20},{14,22},{16,8},... | collective-permute-start | bytes 196616 | tf_op jit(solution)/shard_map/ppermute | solution.py:839
  44.5 5.9 %collective-permute-start.16 = (bf16[4,4,16,128]{3,2,1,0:T(8,128)(2,1)S(1)}, bf16[4,4,16,128]{3,2,1,0:T(8,128)(2,1)S(1)}, u32[]{:S(2)}, u32[]{:S(2)}) collective-permute-start(bf16[4,4,16,128]{3,2,1,0:T(8,128)(2,1)S(1)} %get-tuple-element.133), channel_id=1, source_target_pairs={{0,16},{2,18},{4,20},{6,22},{8,24},{10,26},{12,28},{14,30},{16,0},... | collective-permute-start | bytes 196616 | tf_op jit(solution)/shard_map/ppermute | solution.py:839
  44.5 6.5 %copy-start = (bf16[4,1024,256]{2,1,0:T(8,128)(2,1)S(1)}, bf16[4,1024,256]{2,1,0:T(8,128)(2,1)}, u32[]{:S(2)}) copy-start(bf16[4,1024,256]{2,1,0:T(8,128)(2,1)} %constant.21.clone.table_ref) | copy-start | bytes 6291460
  44.5 6.5 %copy-start.5 = (f32[128]{0:T(128)S(1)}, f32[128]{0:T(128)}, u32[]{:S(2)}) copy-start(f32[128]{0:T(128)} %param.11) | copy-start | bytes 1540
  44.6 5.9 %collective-permute-start.17 = (bf16[4,4,16,128]{3,2,1,0:T(8,128)(2,1)S(1)}, bf16[4,4,16,128]{3,2,1,0:T(8,128)(2,1)S(1)}, u32[]{:S(2)}, u32[]{:S(2)}) collective-permute-start(bf16[4,4,16,128]{3,2,1,0:T(8,128)(2,1)S(1)} %get-tuple-element.134), channel_id=1, source_target_pairs={{0,8},{2,10},{4,12},{6,14},{8,0},{10,2},{12,4},{14,6},{16,24},{18,... | collective-permute-start | bytes 196616 | tf_op jit(solution)/shard_map/ppermute | solution.py:839
  48.2 5.1 %collective-permute-start.15 = (bf16[2,4,4,16,128]{4,3,2,1,0:T(8,128)(2,1)S(1)}, bf16[2,4,4,16,128]{4,3,2,1,0:T(8,128)(2,1)S(1)}, u32[]{:S(2)}, u32[]{:S(2)}) collective-permute-start(bf16[2,4,4,16,128]{4,3,2,1,0:T(8,128)(2,1)S(1)} %shard_map.95), channel_id=1, source_target_pairs={{0,1},{1,0},{2,3},{3,2},{4,5},{5,4},{6,7},{7,6},{8,9},{9,8},{10,11... | collective-permute-start | bytes 393224 | tf_op jit(solution)/shard_map/ppermute | solution.py:843
  50.5 5.6 %collective-permute-start.18 = (bf16[2,4,4,16,128]{4,3,2,1,0:T(8,128)(2,1)S(1)}, bf16[2,4,4,16,128]{4,3,2,1,0:T(8,128)(2,1)S(1)}, u32[]{:S(2)}, u32[]{:S(2)}) collective-permute-start(bf16[2,4,4,16,128]{4,3,2,1,0:T(8,128)(2,1)S(1)} %shard_map.96), channel_id=1, source_target_pairs={{0,1},{1,0},{2,3},{3,2},{4,5},{5,4},{6,7},{7,6},{8,9},{9,8},{10,11... | collective-permute-start | bytes 393224 | tf_op jit(solution)/shard_map/ppermute | solution.py:843
